TPU v7x, 32 devices: a whole 2x2x4 slice. The times are simulated.
32 devices in a mesh: dp: 2 (over y), row: 4 (over z), col: 4 (over x, core).
Axes of the slice: x: 2, y: 2, z: 4, core: 2. Of those that a mesh axis runs over, the one named last changes fastest.
Arguments:
- residual: bfloat16 [8192, 2048], P(('dp', 'col'), 'row'), may hold values from -6 to 6
- segments: int32 [8192], P(('dp', 'col')), may hold values from 0 to 127, never falling along the last dimension, each value on 1 to 512 neighbouring positions
- routes: int32 [8192, 8], P(('dp', 'col')), may hold values from 0 to 15, all different within a row; in each aligned block of 512 rows (0 to 511, 512 to 1023, ...) at most 320 rows name the same one
- norm_attention: float32 [2048], replicated, may hold values from 0.5 to 1.5
- query_weight: bfloat16 [2048, 4096], P('col', 'row'), may hold values from -0.125 to 0.125
- key_projection_matrix: bfloat16 [2048, 512], P('col'), may hold values from -0.125 to 0.125
- value_projection_matrix: bfloat16 [2048, 512], P('col'), may hold values from -0.125 to 0.125
- query_gain: float32 [128], replicated, may hold values from 0.5 to 1.5
- key_gain: float32 [128], replicated, may hold values from 0.5 to 1.5
- out_weight: bfloat16 [4096, 2048], P('row', 'col'), may hold values from -0.375 to 0.375
- norm_experts: float32 [2048], replicated, may hold values from 0.5 to 1.5
- router_weight: bfloat16 [2048, 16], replicated, may hold values from -0.0625 to 0.0625
- gate_weight: bfloat16 [16, 2048, 768], P(('row', 'col')), may hold values from -0.125 to 0.125
- up_weight: bfloat16 [16, 2048, 768], P(('row', 'col')), may hold values from -0.125 to 0.125
- down_weight: bfloat16 [16, 768, 2048], P(('row', 'col')), may hold values from -0.875 to 0.875
- grad_output: bfloat16 [8192, 2048], P(('dp', 'col'), 'row'), may hold values from -6 to 6
Outputs:
- output: bfloat16 [8192, 2048], P(('dp', 'col'), 'row')
- grad_residual: float32 [8192, 2048], P(('dp', 'col'), 'row')
- grad_norm_attention: float32 [2048], replicated
- grad_query: float32 [2048, 4096], P('col', 'row')
- grad_key: float32 [2048, 512], P('col')
- grad_value: float32 [2048, 512], P('col')
- grad_query_gain: float32 [128], replicated
- grad_key_gain: float32 [128], replicated
- grad_out_weight: float32 [4096, 2048], P('row', 'col')
- grad_norm_experts: float32 [2048], replicated
- grad_router: float32 [2048, 16], replicated
- grad_gate: float32 [16, 2048, 768], P(('row', 'col'))
- grad_up: float32 [16, 2048, 768], P(('row', 'col'))
- grad_down: float32 [16, 768, 2048], P(('row', 'col'))
Inputs may be any that keep to these rules, and one draw needn't show every extreme that they name: `routes`: in each aligned block of 512 rows (the rows of one device's micro-batch) no expert is named by more than 320 rows; the 8 experts of a row differ. `segments`: document numbers never fall along the whole array; a document has 1 to 512 tokens.
All inputs are finite; a program needn't handle non-finite values.
Results may differ from a plain program's by a relative error of at most 0.017.
Values may be sent and summed in bfloat16 or wider, within the bound.
No kernel may reach another device: no remote copies, remote signals or barrier semaphores. Data moves between devices by JAX's collectives and lax.ppermute only.
A program may use at most 320 MiB of HBM per device.

v0:
```python
import jax
import jax.numpy as jnp
from jax import lax
from jax.sharding import PartitionSpec as P

SEQUENCE_TOKENS = 512
MICRO = 2


EPSILON = 1e-06
ROPE_BASE = 1000000.0
MASKED = -1e30


def swapped(block, axis, apart):
    count = lax.axis_size(axis)
    route = []
    for low in range(count):
        high = low | 1 << apart
        if high != low and high < count:
            route += [(low, high), (high, low)]
    return lax.ppermute(block, axis, route)


def rms_scale(values, gain):
    return values * lax.rsqrt(jnp.mean(values * values, axis=-1, keepdims=True) + EPSILON) * gain


def rms_back(values, gain, upstream):
    factor = lax.rsqrt(jnp.mean(values * values, axis=-1, keepdims=True) + EPSILON)
    weighted = upstream * gain
    inner_sum = jnp.mean(weighted * values, axis=-1, keepdims=True)
    return (
        weighted * factor - values * (factor * factor * factor * inner_sum),
        upstream * values * factor,
    )


def positions(segment_ids):
    places = jnp.arange(segment_ids.shape[0], dtype=jnp.int32)
    earlier = jnp.concatenate([segment_ids[:1] - 1, segment_ids[:-1]])
    starts = jnp.logical_or(segment_ids != earlier, places % SEQUENCE_TOKENS == 0)
    opening = lax.cummax(jnp.where(starts, places, 0), axis=0)
    return places - opening


def rotary(places, head_size):
    halfway = head_size // 2
    frequency = ROPE_BASE ** (-2.0 * jnp.arange(halfway, dtype=jnp.float32) / head_size)
    angles = places.astype(jnp.float32)[:, None] * frequency[None, :]
    return (jnp.cos(angles), jnp.sin(angles))


def rotate(values, cos_table, sin_table):
    halfway = values.shape[-1] // 2
    front_part = values[..., :halfway]
    back_part = values[..., halfway:]
    cos_wide = cos_table[:, None, :]
    sin_wide = sin_table[:, None, :]
    return jnp.concatenate(
        [
            front_part * cos_wide - back_part * sin_wide,
            back_part * cos_wide + front_part * sin_wide,
        ],
        axis=-1,
    )


def unrotate(upstream, cos_table, sin_table):
    halfway = upstream.shape[-1] // 2
    front_part = upstream[..., :halfway]
    back_part = upstream[..., halfway:]
    cos_wide = cos_table[:, None, :]
    sin_wide = sin_table[:, None, :]
    return jnp.concatenate(
        [
            front_part * cos_wide + back_part * sin_wide,
            back_part * cos_wide - front_part * sin_wide,
        ],
        axis=-1,
    )


def slot_ranks(routes, experts):
    token_rows, chosen = routes.shape
    labels = jnp.arange(experts, dtype=jnp.int32)
    onehot = (routes.reshape(-1)[:, None] == labels[None, :]).astype(jnp.int32)
    before = jnp.cumsum(onehot, axis=0, dtype=jnp.int32) - onehot
    return jnp.sum(before * onehot, axis=1, dtype=jnp.int32).reshape(token_rows, chosen)


def row_total(values):
    return lax.psum(values, "row")


def full_features(values):
    return lax.all_gather(values, "row", axis=1, tiled=True)


def feature_share(values):
    return lax.psum_scatter(values, "row", scatter_dimension=1, tiled=True)


def from_experts(values, col_count):
    local_experts, slot_rows, model_width = values.shape
    capacity = slot_rows // col_count
    shaped = jnp.moveaxis(values.reshape(local_experts, col_count, capacity, model_width), 0, 1)
    shaped = shaped.reshape(1, col_count, local_experts * capacity, model_width)
    arrived = lax.all_to_all(
        lax.all_to_all(shaped, "row", split_axis=3, concat_axis=0, tiled=True),
        "col",
        split_axis=1,
        concat_axis=1,
        tiled=True,
    )
    return arrived.reshape(-1, arrived.shape[-1])


def to_owner_layout(arrived, col_count, local_experts):
    model_width = arrived.shape[-1]
    shaped = arrived.reshape(col_count, local_experts, -1, model_width)
    return jnp.moveaxis(shaped, 1, 0).reshape(local_experts, -1, model_width)


def block_scores(query_block, key_block, segment_ids, query_start, key_start, score_scale):
    block_rows = query_block.shape[0]
    scores = (
        jnp.einsum("qhd,kd->hqk", query_block, key_block, preferred_element_type=jnp.float32)
        * score_scale
    )
    query_places = query_start + jnp.arange(block_rows, dtype=jnp.int32)
    key_places = key_start + jnp.arange(SEQUENCE_TOKENS, dtype=jnp.int32)
    allowed = jnp.logical_and(
        segment_ids[:, None] == segment_ids[None, :], key_places[None, :] <= query_places[:, None]
    )
    return jnp.where(allowed[None], scores, MASKED)


def attention_forward(query_low, key_low, value_low, segment_ids, score_scale):
    token_rows, heads_here, head_size = query_low.shape
    block_rows = min(512, SEQUENCE_TOKENS)
    per_sequence = SEQUENCE_TOKENS // block_rows

    def one_block(block_number):
        query_start = block_number * block_rows
        key_start = block_number // per_sequence * SEQUENCE_TOKENS
        scores = block_scores(query_low, key_low, segment_ids, query_start, key_start, score_scale)
        top_score = jnp.max(scores, axis=-1, keepdims=True)
        weights = jnp.exp(scores - top_score)
        denominator = jnp.sum(weights, axis=-1, keepdims=True)
        probs_low = (weights / denominator).astype(jnp.bfloat16)
        expert_mixture_output = jnp.einsum(
            "hqk,kd->qhd", probs_low, value_low, preferred_element_type=jnp.float32
        )
        return (expert_mixture_output, (top_score + jnp.log(denominator))[..., 0])

    expert_mixture_output, log_totals = lax.map(
        one_block, jnp.arange(token_rows // block_rows, dtype=jnp.int32)
    )
    return (expert_mixture_output.reshape(token_rows, heads_here, head_size), log_totals)


def attention_backward(
    query_low, key_low, value_low, segment_ids, log_totals, mixed_grad, score_scale
):
    token_rows, heads_here, head_size = query_low.shape
    block_rows = min(512, SEQUENCE_TOKENS)
    per_sequence = SEQUENCE_TOKENS // block_rows

    def one_block(carry, block_number):
        key_acc, value_acc = carry
        query_start = block_number * block_rows
        key_start = block_number // per_sequence * SEQUENCE_TOKENS
        scores = block_scores(query_low, key_low, segment_ids, query_start, key_start, score_scale)
        probs = jnp.exp(scores - log_totals[block_number][:, :, None])
        probs_low = probs.astype(jnp.bfloat16)
        prob_grad = jnp.einsum(
            "qhd,kd->hqk", mixed_grad, value_low, preferred_element_type=jnp.float32
        )
        score_grad = (
            probs * (prob_grad - jnp.sum(probs * prob_grad, axis=-1, keepdims=True))
        ).astype(jnp.bfloat16)
        query_part = (
            jnp.einsum("hqk,kd->qhd", score_grad, key_low, preferred_element_type=jnp.float32)
            * score_scale
        )
        key_part = (
            jnp.einsum("hqk,qhd->kd", score_grad, query_low, preferred_element_type=jnp.float32)
            * score_scale
        )
        value_part = jnp.einsum(
            "hqk,qhd->kd", probs_low, mixed_grad, preferred_element_type=jnp.float32
        )
        key_acc = key_acc + key_part
        value_acc = value_acc + value_part
        return ((key_acc, value_acc), query_part)

    empty = jnp.zeros((token_rows, head_size), jnp.float32)
    sums, query_parts = lax.scan(
        one_block, (empty, empty), jnp.arange(token_rows // block_rows, dtype=jnp.int32)
    )
    return (query_parts.reshape(token_rows, heads_here, head_size), sums[0], sums[1])


def per_device(
    residual,
    segments,
    routes,
    norm_attention,
    query_weight,
    key_projection_matrix,
    value_projection_matrix,
    query_gain,
    key_gain,
    out_weight,
    norm_experts,
    router_weight,
    gate_weight,
    up_weight,
    down_weight,
    grad_output,
):
    row_count = lax.axis_size("row")
    col_count = lax.axis_size("col")
    row_place = lax.axis_index("row")
    col_place = lax.axis_index("col")
    model_width = norm_attention.shape[0]
    feature_width = model_width // row_count
    head_size = query_gain.shape[0]
    heads_here = query_weight.shape[1] // head_size
    kv_heads = key_projection_matrix.shape[1] // head_size
    query_group_width = heads_here * row_count // kv_heads
    members = query_group_width // heads_here
    kv_index = row_place * heads_here // query_group_width
    member_place = row_place % members
    share_width = head_size // members
    column_mask = (jnp.arange(head_size, dtype=jnp.int32) // share_width == member_place).astype(
        jnp.float32
    )
    local_experts = gate_weight.shape[0]
    experts = local_experts * row_count * col_count
    token_rows = residual.shape[0]
    micro_rows = token_rows // MICRO
    top_count = routes.shape[1]
    capacity = max(2, 5 * micro_rows * top_count // (4 * experts))
    score_scale = head_size ** (-0.5)
    row_start = row_place * feature_width
    gain_one = lax.dynamic_slice_in_dim(norm_attention, row_start, feature_width)
    gain_two = lax.dynamic_slice_in_dim(norm_experts, row_start, feature_width)
    router_rows = lax.dynamic_slice_in_dim(router_weight, row_start, feature_width, 0)
    labels = jnp.arange(experts, dtype=jnp.int32)
    key_part = lax.dynamic_slice_in_dim(key_projection_matrix, kv_index * head_size, head_size, 1)
    value_part = lax.dynamic_slice_in_dim(
        value_projection_matrix, kv_index * head_size, head_size, 1
    )
    query_full, key_full, value_full, out_full = (
        lax.all_gather(query_weight, "col", axis=0, tiled=True),
        lax.all_gather(key_part, "col", axis=0, tiled=True),
        lax.all_gather(value_part, "col", axis=0, tiled=True),
        lax.all_gather(out_weight, "col", axis=1, tiled=True),
    )
    acc_query = jnp.zeros((model_width, heads_here * head_size), jnp.float32)
    acc_key = jnp.zeros((model_width, head_size), jnp.float32)
    acc_value = jnp.zeros((model_width, head_size), jnp.float32)
    acc_out = jnp.zeros((heads_here * head_size, model_width), jnp.float32)
    acc_gate = jnp.zeros(gate_weight.shape, jnp.float32)
    acc_up = jnp.zeros(up_weight.shape, jnp.float32)
    acc_down = jnp.zeros(down_weight.shape, jnp.float32)
    acc_router = jnp.zeros((feature_width, experts), jnp.float32)
    acc_gain_one = jnp.zeros((feature_width,), jnp.float32)
    acc_gain_two = jnp.zeros((feature_width,), jnp.float32)
    acc_query_gain = jnp.zeros((head_size,), jnp.float32)
    acc_key_gain = jnp.zeros((head_size,), jnp.float32)
    output_blocks = []
    input_blocks = []
    for micro_number in range(MICRO):
        row_offset = micro_number * micro_rows
        block_in = residual[row_offset : row_offset + micro_rows].astype(jnp.float32)
        block_segs = segments[row_offset : row_offset + micro_rows]
        block_routes = routes[row_offset : row_offset + micro_rows]
        block_grad = grad_output[row_offset : row_offset + micro_rows].astype(jnp.float32)
        scale_one = lax.rsqrt(
            row_total(jnp.sum(block_in * block_in, axis=1)) / model_width + EPSILON
        )
        first_normalized = (block_in * scale_one[:, None] * gain_one).astype(jnp.bfloat16)
        normed_full = full_features(first_normalized)
        query_pre = jnp.dot(normed_full, query_full, preferred_element_type=jnp.float32).reshape(
            micro_rows, heads_here, head_size
        )
        key_pre = jnp.dot(normed_full, key_full, preferred_element_type=jnp.float32)[:, None, :]
        value_low = jnp.dot(normed_full, value_full, preferred_element_type=jnp.float32).astype(
            jnp.bfloat16
        )
        cos_table, sin_table = rotary(positions(block_segs), head_size)
        query_low = rotate(rms_scale(query_pre, query_gain), cos_table, sin_table).astype(
            jnp.bfloat16
        )
        key_low = rotate(rms_scale(key_pre, key_gain), cos_table, sin_table)[:, 0, :].astype(
            jnp.bfloat16
        )
        expert_mixture_output, log_totals = attention_forward(
            query_low, key_low, value_low, block_segs, score_scale
        )
        mixed_low = expert_mixture_output.reshape(micro_rows, heads_here * head_size).astype(
            jnp.bfloat16
        )
        hidden = block_in + feature_share(
            jnp.dot(mixed_low, out_full, preferred_element_type=jnp.float32)
        )
        scale_two = lax.rsqrt(row_total(jnp.sum(hidden * hidden, axis=1)) / model_width + EPSILON)
        normed_two = (hidden * scale_two[:, None] * gain_two).astype(jnp.bfloat16)
        slots = block_routes * capacity + slot_ranks(block_routes, experts)
        token_ids = jnp.broadcast_to(
            jnp.arange(micro_rows, dtype=jnp.int32)[:, None], block_routes.shape
        )
        source = (
            jnp.full((experts * capacity,), micro_rows, dtype=jnp.int32)
            .at[slots.reshape(-1)]
            .set(token_ids.reshape(-1))
        )
        normed_all = full_features(normed_two)
        logits = jnp.dot(normed_all, router_weight, preferred_element_type=jnp.float32)
        padded = jnp.concatenate([normed_all, jnp.zeros((1, model_width), jnp.bfloat16)], axis=0)
        own_slots = lax.dynamic_slice_in_dim(
            source.reshape(row_count, -1), row_place, 1, 0
        ).reshape(-1)
        outgoing = padded[own_slots].reshape(col_count, local_experts * capacity, model_width)
        arrived = lax.all_to_all(outgoing, "col", split_axis=0, concat_axis=0, tiled=True)
        expert_in = to_owner_layout(arrived, col_count, local_experts)
        gate_pre = jnp.einsum(
            "esd,edf->esf", expert_in, gate_weight, preferred_element_type=jnp.float32
        )
        up_pre = jnp.einsum(
            "esd,edf->esf", expert_in, up_weight, preferred_element_type=jnp.float32
        )
        sigmoid_gate = jax.nn.sigmoid(gate_pre)
        silu_gate = gate_pre * sigmoid_gate
        hidden_low = (silu_gate * up_pre).astype(jnp.bfloat16)
        expert_out = jnp.einsum(
            "esf,efd->esd", hidden_low, down_weight, preferred_element_type=jnp.float32
        ).astype(jnp.bfloat16)
        returned = from_experts(expert_out, col_count)
        gathered = returned[slots]
        picked = jnp.take_along_axis(logits, block_routes, axis=1)
        picked = jnp.exp(picked - jnp.max(picked, axis=1, keepdims=True))
        gates = picked / jnp.sum(picked, axis=1, keepdims=True)
        mixture = jnp.einsum("tk,tkd->td", gates, gathered, preferred_element_type=jnp.float32)
        output_blocks.append((hidden + mixture).astype(jnp.bfloat16))
        gate_dots = row_total(
            jnp.einsum("td,tkd->tk", block_grad, gathered, preferred_element_type=jnp.float32)
        )
        slot_grad = (gates[:, :, None] * block_grad[:, None, :]).astype(jnp.bfloat16)
        outgoing_grad = (
            jnp.zeros((experts * capacity, feature_width), jnp.bfloat16)
            .at[slots.reshape(-1)]
            .set(slot_grad.reshape(-1, feature_width))
        )
        outgoing_grad = outgoing_grad.reshape(
            row_count, col_count, local_experts * capacity, feature_width
        )
        expert_grad = to_owner_layout(
            lax.all_to_all(
                lax.all_to_all(outgoing_grad, "row", split_axis=0, concat_axis=3, tiled=True),
                "col",
                split_axis=1,
                concat_axis=1,
                tiled=True,
            ),
            col_count,
            local_experts,
        )
        hidden_grad = jnp.einsum(
            "esd,efd->esf", expert_grad, down_weight, preferred_element_type=jnp.float32
        ).astype(jnp.bfloat16)
        acc_down = acc_down + jnp.einsum(
            "esf,esd->efd", hidden_low, expert_grad, preferred_element_type=jnp.float32
        )
        gate_grad = (
            hidden_grad * up_pre * sigmoid_gate * (1.0 + gate_pre * (1.0 - sigmoid_gate))
        ).astype(jnp.bfloat16)
        up_grad = (hidden_grad * silu_gate).astype(jnp.bfloat16)
        acc_gate = acc_gate + jnp.einsum(
            "esd,esf->edf", expert_in, gate_grad, preferred_element_type=jnp.float32
        )
        acc_up = acc_up + jnp.einsum(
            "esd,esf->edf", expert_in, up_grad, preferred_element_type=jnp.float32
        )
        slot_input_grad = jnp.einsum(
            "esf,edf->esd", gate_grad, gate_weight, preferred_element_type=jnp.float32
        )
        slot_input_grad = slot_input_grad + jnp.einsum(
            "esf,edf->esd", up_grad, up_weight, preferred_element_type=jnp.float32
        )
        back_grad = from_experts(slot_input_grad.astype(jnp.bfloat16), col_count)
        normed_two_grad = jnp.einsum("tkd->td", back_grad[slots].astype(jnp.float32))
        pick_grad = gates * (gate_dots - jnp.sum(gates * gate_dots, axis=1, keepdims=True))
        logit_grad = jnp.einsum(
            "tk,tke->te",
            pick_grad,
            (block_routes[:, :, None] == labels[None, None, :]).astype(jnp.float32),
        ).astype(jnp.bfloat16)
        acc_router = acc_router + jnp.dot(
            normed_two.T, logit_grad, preferred_element_type=jnp.float32
        )
        normed_two_grad = normed_two_grad + jnp.dot(
            logit_grad, router_rows.T, preferred_element_type=jnp.float32
        )
        weighted_two = normed_two_grad * gain_two
        inner_two = row_total(jnp.sum(weighted_two * hidden, axis=1))
        hidden_total = (
            block_grad
            + weighted_two * scale_two[:, None]
            - hidden * (scale_two * scale_two * scale_two * inner_two / model_width)[:, None]
        )
        acc_gain_two = acc_gain_two + jnp.sum(normed_two_grad * hidden * scale_two[:, None], axis=0)
        branch_full = full_features(hidden_total.astype(jnp.bfloat16))
        acc_out = acc_out + jnp.dot(mixed_low.T, branch_full, preferred_element_type=jnp.float32)
        mixed_grad = (
            jnp.dot(branch_full, out_full.T, preferred_element_type=jnp.float32)
            .astype(jnp.bfloat16)
            .reshape(micro_rows, heads_here, head_size)
        )
        query_grad, key_grad, value_grad = attention_backward(
            query_low, key_low, value_low, block_segs, log_totals, mixed_grad, score_scale
        )
        for bit_number in range(members.bit_length() - 1):
            partner_key, partner_value = swapped((key_grad, value_grad), "row", bit_number)
            key_grad = key_grad + partner_key
            value_grad = value_grad + partner_value
        query_pre_grad, query_gain_terms = rms_back(
            query_pre, query_gain, unrotate(query_grad, cos_table, sin_table)
        )
        acc_query_gain = acc_query_gain + jnp.sum(query_gain_terms, axis=(0, 1))
        key_pre_grad, key_gain_terms = rms_back(
            key_pre, key_gain, unrotate(key_grad[:, None, :], cos_table, sin_table)
        )
        acc_key_gain = acc_key_gain + column_mask * jnp.sum(key_gain_terms, axis=(0, 1))
        query_low_grad = query_pre_grad.reshape(micro_rows, heads_here * head_size).astype(
            jnp.bfloat16
        )
        key_low_grad = (column_mask * key_pre_grad[:, 0, :]).astype(jnp.bfloat16)
        value_low_grad = (column_mask * value_grad).astype(jnp.bfloat16)
        normed_one_full = jnp.dot(query_low_grad, query_full.T, preferred_element_type=jnp.float32)
        normed_one_full = normed_one_full + jnp.dot(
            key_low_grad, key_full.T, preferred_element_type=jnp.float32
        )
        normed_one_full = normed_one_full + jnp.dot(
            value_low_grad, value_full.T, preferred_element_type=jnp.float32
        )
        acc_query = acc_query + jnp.dot(
            normed_full.T, query_low_grad, preferred_element_type=jnp.float32
        )
        acc_key = acc_key + jnp.dot(normed_full.T, key_low_grad, preferred_element_type=jnp.float32)
        acc_value = acc_value + jnp.dot(
            normed_full.T, value_low_grad, preferred_element_type=jnp.float32
        )
        normed_one_grad = feature_share(normed_one_full)
        weighted_one = normed_one_grad * gain_one
        inner_one = row_total(jnp.sum(weighted_one * block_in, axis=1))
        input_blocks.append(
            hidden_total
            + weighted_one * scale_one[:, None]
            - block_in * (scale_one * scale_one * scale_one * inner_one / model_width)[:, None]
        )
        acc_gain_one = acc_gain_one + jnp.sum(
            normed_one_grad * block_in * scale_one[:, None], axis=0
        )
    query_share, out_share = (
        lax.psum_scatter(acc_query, "col", scatter_dimension=0, tiled=True),
        lax.psum_scatter(acc_out, "col", scatter_dimension=1, tiled=True),
    )
    grad_gate, grad_up, grad_down, grad_query, grad_out_weight = lax.psum(
        (acc_gate, acc_up, acc_down, query_share, out_share), "dp"
    )
    gain_one_full = lax.dynamic_update_slice_in_dim(
        jnp.zeros((model_width,), jnp.float32), acc_gain_one, row_start, 0
    )
    gain_two_full = lax.dynamic_update_slice_in_dim(
        jnp.zeros((model_width,), jnp.float32), acc_gain_two, row_start, 0
    )
    router_full = lax.dynamic_update_slice_in_dim(
        jnp.zeros((model_width, experts), jnp.float32), acc_router, row_start, 0
    )
    col_width = model_width // col_count
    key_whole = lax.dynamic_update_slice_in_dim(
        jnp.zeros((model_width, kv_heads * head_size), jnp.float32),
        acc_key,
        kv_index * head_size,
        1,
    )
    value_whole = lax.dynamic_update_slice_in_dim(
        jnp.zeros((model_width, kv_heads * head_size), jnp.float32),
        acc_value,
        kv_index * head_size,
        1,
    )
    totals = lax.psum(
        (
            gain_one_full,
            gain_two_full,
            acc_query_gain,
            acc_key_gain,
            router_full,
            key_whole,
            value_whole,
        ),
        ("dp", "row", "col"),
    )
    grad_key = lax.dynamic_slice_in_dim(totals[5], col_place * col_width, col_width, 0)
    grad_value = lax.dynamic_slice_in_dim(totals[6], col_place * col_width, col_width, 0)
    output = jnp.concatenate(output_blocks, axis=0)
    grad_residual = jnp.concatenate(input_blocks, axis=0)
    return (
        output,
        grad_residual,
        totals[0],
        grad_query,
        grad_key,
        grad_value,
        totals[2],
        totals[3],
        grad_out_weight,
        totals[1],
        totals[4],
        grad_gate,
        grad_up,
        grad_down,
    )


def solution(mesh):
    in_specs = (
        P(("dp", "col"), "row"),
        P(("dp", "col")),
        P(("dp", "col"), None),
        P(),
        P("col", "row"),
        P("col", None),
        P("col", None),
        P(),
        P(),
        P("row", "col"),
        P(),
        P(),
        P(("row", "col"), None, None),
        P(("row", "col"), None, None),
        P(("row", "col"), None, None),
        P(("dp", "col"), "row"),
    )
    out_specs = (
        P(("dp", "col"), "row"),
        P(("dp", "col"), "row"),
        P(),
        P("col", "row"),
        P("col", None),
        P("col", None),
        P(),
        P(),
        P("row", "col"),
        P(),
        P(),
        P(("row", "col"), None, None),
        P(("row", "col"), None, None),
        P(("row", "col"), None, None),
    )
    return jax.shard_map(
        per_device, mesh=mesh, in_specs=in_specs, out_specs=out_specs, check_vma=False
    )
```

profile of v0, /device:TPU:0, one launch (start us, length us, event | category | flops | bytes accessed | tf_op | source)
XLA Modules:
  0.0 3051.1 jit_solution(7067747617094922909)
XLA Ops:
  9.7 13.4 all-reduce.8
  40.9 7.9 all_gather.32
  52.9 17.6 all-gather.17.cloned.1.call-done
  73.0 44.2 %all-gather.9.cloned.1.call-done = bf16[512,2048]{1,0:T(8,128)(2,1)} async-done(((bf16[512,512]{1,0:T(8,128)(2,1)}), bf16[512,2048]{1,0:T(8,128)(2,1)}) %all-gather.9.cloned.1.call-update) | async-done | bytes 2097168 | tf_op jit(solution)/shard_map/all_gather | solution.py:97
  124.0 28.0 all-gather.11.cloned.1.call-done
  214.6 58.4 %reduce-scatter.9.cloned.1.call-done = f32[512,512]{1,0:T(8,128)} async-done(((f32[512,2048]{1,0:T(8,128)}), f32[512,512]{1,0:T(8,128)}) %reduce-scatter.9.cloned.1.call-update) | async-done | bytes 1048592 | tf_op jit(solution)/shard_map/reduce_scatter | solution.py:101
  273.0 80.1 %reduce-scatter.7.cloned.1.call-done = f32[512,512]{1,0:T(8,128)} async-done(((f32[512,2048]{1,0:T(8,128)}), f32[512,512]{1,0:T(8,128)}) %reduce-scatter.7.cloned.1.call-update) | async-done | bytes 1048592 | tf_op jit(solution)/shard_map/reduce_scatter | solution.py:101
  356.5 10.9 all-reduce.7
  372.0 9.6 reduce-window.48
  390.7 15.7 scatter_custom_fusion.1
  406.6 8.7 all-gather.19.cloned.1.call-done
  418.4 12.7 gather_fusion.2
  440.7 9.6 reduce-window.34
  457.7 15.5 scatter_custom_fusion
  473.3 10.5 all-gather.15.cloned.1.call-done
  487.0 12.7 gather_fusion
  512.2 10.6 multiply_convert_fusion
  528.8 10.3 copy.393
  539.1 25.3 all-to-all-done
  577.4 10.5 multiply_convert_fusion.1
  593.9 10.3 copy.384
  604.2 104.2 %all-to-all-done.4 = bf16[1,4,320,2048]{2,1,0,3:T(4,128)(2,1)} async-done(((bf16[1,4,320,2048]{2,1,0,3:T(4,128)(2,1)}), bf16[1,4,320,2048]{2,1,0,3:T(4,128)(2,1)}, u32[]{:S(2)}, u32[]{:S(2)}) %all-to-all-start.4) | async-done | bytes 5242912 | tf_op jit(solution)/shard_map/all_to_all | solution.py:110
  713.6 10.4 copy.394
  723.9 127.3 %all-to-all-done.1 = bf16[1,4,320,2048]{2,1,0,3:T(4,128)(2,1)} async-done(((bf16[1,4,320,2048]{2,1,0,3:T(4,128)(2,1)}), bf16[1,4,320,2048]{2,1,0,3:T(4,128)(2,1)}, u32[]{:S(2)}, u32[]{:S(2)}) %all-to-all-start.1) | async-done | bytes 5242912 | tf_op jit(solution)/shard_map/all_to_all | solution.py:110
  856.4 10.4 copy.385
  866.7 49.1 %all-to-all-done.5 = bf16[4,4,320,512]{3,2,0,1:T(8,128)(2,1)} async-done(((bf16[4,4,320,512]{3,2,0,1:T(8,128)(2,1)}), bf16[4,4,320,512]{3,2,0,1:T(8,128)(2,1)}, u32[]{:S(2)}, u32[]{:S(2)}) %all-to-all-start.5) | async-done | bytes 5242912 | tf_op jit(solution)/shard_map/all_to_all | solution.py:109
  929.1 33.0 %gather_fusion.7 = f32[4096]{0:T(1024)S(1)} fusion(f32[512,16]{0,1:T(8,128)S(1)} %fusion.244, s32[4096]{0:T(1024)S(1)} %reshape.1151), kind=kCustom, calls=%fused_computation.1.clone | custom fusion | bytes 65536 | tf_op jit(solution)/shard_map/jit(take_along_axis)/gather | solution.py:344
  970.6 20.6 gather_fusion.3
  1001.3 20.6 gather_fusion.1
  1026.8 30.2 all-reduce.6
  1060.6 23.4 scatter_custom_fusion.3
  1093.3 33.0 %gather_fusion.6 = f32[4096]{0:T(1024)S(1)} fusion(f32[512,16]{0,1:T(8,128)S(1)} %fusion.241, s32[4096]{0:T(1024)S(1)} %reshape.1146), kind=kCustom, calls=%fused_computation.clone | custom fusion | bytes 65536 | tf_op jit(solution)/shard_map/jit(take_along_axis)/gather | solution.py:344
  1133.2 23.8 scatter_custom_fusion.2
  1157.0 43.1 %all-to-all-done.10 = bf16[4,4,320,512]{3,2,1,0:T(8,128)(2,1)} async-done(((bf16[4,4,320,512]{3,2,1,0:T(8,128)(2,1)}), bf16[4,4,320,512]{3,2,1,0:T(8,128)(2,1)}, u32[]{:S(2)}, u32[]{:S(2)}) %all-to-all-start.10) | async-done | bytes 5242912 | tf_op jit(solution)/shard_map/all_to_all | solution.py:363
  1210.9 109.5 %all-to-all-done.6 = bf16[4,4,320,512]{3,2,1,0:T(8,128)(2,1)} async-done(((bf16[4,4,320,512]{3,2,1,0:T(8,128)(2,1)}), bf16[4,4,320,512]{3,2,1,0:T(8,128)(2,1)}, u32[]{:S(2)}, u32[]{:S(2)}) %all-to-all-start.6) | async-done | bytes 5242912 | tf_op jit(solution)/shard_map/all_to_all | solution.py:363
  1331.1 53.8 %all-to-all-done.11 = bf16[1,4,320,2048]{3,2,0,1:T(8,128)(2,1)} async-done(((bf16[1,4,320,2048]{3,2,0,1:T(8,128)(2,1)}), bf16[1,4,320,2048]{3,2,0,1:T(8,128)(2,1)}, u32[]{:S(2)}, u32[]{:S(2)}) %all-to-all-start.11) | async-done | bytes 5242912 | tf_op jit(solution)/shard_map/all_to_all | solution.py:362
  1389.9 9.0 fusion.42
  1406.3 8.8 add_convert_fusion
  1415.1 10.2 copy.415
  1425.4 24.0 all-to-all-done.7
  1454.8 9.0 fusion.38
  1471.2 8.8 add_convert_fusion.1
  1480.0 10.2 copy.398
  1490.2 102.8 %all-to-all-done.12 = bf16[1,4,320,2048]{2,1,0,3:T(4,128)(2,1)} async-done(((bf16[1,4,320,2048]{2,1,0,3:T(4,128)(2,1)}), bf16[1,4,320,2048]{2,1,0,3:T(4,128)(2,1)}, u32[]{:S(2)}, u32[]{:S(2)}) %all-to-all-start.12) | async-done | bytes 5242912 | tf_op jit(solution)/shard_map/all_to_all | solution.py:110
  1598.3 10.4 copy.416
  1608.6 127.3 %all-to-all-done.8 = bf16[1,4,320,2048]{2,1,0,3:T(4,128)(2,1)} async-done(((bf16[1,4,320,2048]{2,1,0,3:T(4,128)(2,1)}), bf16[1,4,320,2048]{2,1,0,3:T(4,128)(2,1)}, u32[]{:S(2)}, u32[]{:S(2)}) %all-to-all-start.8) | async-done | bytes 5242912 | tf_op jit(solution)/shard_map/all_to_all | solution.py:110
  1741.0 10.4 copy.399
  1751.3 49.1 %all-to-all-done.13 = bf16[4,4,320,512]{3,2,0,1:T(8,128)(2,1)} async-done(((bf16[4,4,320,512]{3,2,0,1:T(8,128)(2,1)}), bf16[4,4,320,512]{3,2,0,1:T(8,128)(2,1)}, u32[]{:S(2)}, u32[]{:S(2)}) %all-to-all-start.13) | async-done | bytes 5242912 | tf_op jit(solution)/shard_map/all_to_all | solution.py:109
  1824.0 21.0 gather_fusion.5
  1851.0 14.1 all-to-all-done.9
  1870.4 20.6 gather_fusion.4
  1898.9 9.8 all-reduce.5
  1913.9 42.7 %all-gather.21.cloned.1.call-done = bf16[512,2048]{1,0:T(8,128)(2,1)} async-done(((bf16[512,512]{1,0:T(8,128)(2,1)}), bf16[512,2048]{1,0:T(8,128)(2,1)}) %all-gather.21.cloned.1.call-update) | async-done | bytes 2097168 | tf_op jit(solution)/shard_map/all_gather | solution.py:97
  1964.2 39.1 %all-gather.23.cloned.1.call-done = bf16[512,2048]{1,0:T(8,128)(2,1)} async-done(((bf16[512,512]{1,0:T(8,128)(2,1)}), bf16[512,2048]{1,0:T(8,128)(2,1)}) %all-gather.23.cloned.1.call-update) | async-done | bytes 2097168 | tf_op jit(solution)/shard_map/all_gather | solution.py:97
  2003.3 10.0 convolution_add_fusion
  2134.5 9.4 add_bitcast_fusion
  2143.9 9.1 add_bitcast_fusion.2
  2160.2 9.6 add_bitcast_fusion.1
  2175.8 170.9 %all-reduce.13.cloned.1.call-done = (f32[2048,512]{1,0:T(8,128)}, f32[2048,512]{1,0:T(8,128)}, f32[2048,16]{0,1:T(8,128)}) async-done(((f32[2048,512]{1,0:T(8,128)}, f32[2048,512]{1,0:T(8,128)}, f32[2048,16]{0,1:T(8,128)}), (f32[2048,512]{1,0:T(8,128)}, f32[2048,512]{1,0:T(8,128)}, f32[2048,16]{0,1:T(8,128)})) %all-reduce.13.cloned.1.call-update) | async-done | bytes 8519696 | tf_op jit(solution)/shard_map/psum | solution.py:497
  2351.2 74.6 %reduce-scatter.11.cloned.1.call-done = f32[512,512]{1,0:T(8,128)} async-done(((f32[512,2048]{1,0:T(8,128)}), f32[512,512]{1,0:T(8,128)}) %reduce-scatter.11.cloned.1.call-update) | async-done | bytes 1048592 | tf_op jit(solution)/shard_map/reduce_scatter | solution.py:101
  2425.8 79.4 %reduce-scatter.13.cloned.1.call-done = f32[512,512]{1,0:T(8,128)} async-done(((f32[512,2048]{1,0:T(8,128)}), f32[512,512]{1,0:T(8,128)}) %reduce-scatter.13.cloned.1.call-update) | async-done | bytes 1048592 | tf_op jit(solution)/shard_map/reduce_scatter | solution.py:101
  2507.9 10.9 all-reduce.4
  2519.0 39.4 %all-reduce.2 = (f32[2048]{0:T(1024)}, f32[128]{0:T(128)}, f32[128]{0:T(128)}, f32[2048]{0:T(1024)}) all-reduce(f32[2048]{0:T(1024)S(1)} %add_dynamic-update-slice_fusion.1, f32[128]{0:T(128)S(1)} %add.495, f32[128]{0:T(128)S(1)} %select_add_fusion, ...), channel_id=1, replica_groups=mesh['dp'=2,'row'=4,'col'=4] {'dp','row','col'}, use_global_device_ids=true, to_apply=%region_60.62 | all-reduce | flops 4352 | bytes 34816 | tf_op jit(solution)/shard_map/psum | solution.py:497
  2565.4 462.4 %all-reduce.15.cloned.1.call-done = (f32[512,1024]{1,0:T(8,128)}, f32[1024,512]{1,0:T(8,128)}, f32[1,2048,768]{2,1,0:T(8,128)}, f32[1,2048,768]{2,1,0:T(8,128)}, f32[1,768,2048]{2,1,0:T(8,128)}) async-done(((f32[512,1024]{1,0:T(8,128)}, f32[1024,512]{1,0:T(8,128)}, f32[1,2048,768]{2,1,0:T(8,128)}, f32[1,2048,768]{2,1,0:T(8,128)}, f32[1,768,2048]{2,1,0:T(8,128)}), (f32[512,1024]{1,0:T(8,128)}, ...) | async-done | bytes 23068688 | tf_op jit(solution)/shard_map/psum | solution.py:472
  (690 shorter events, 514.7 us)
Async XLA Ops:
  7.2 515.7 %copy-start = (bf16[1,768,2048]{2,1,0:T(8,128)(2,1)S(1)}, bf16[1,768,2048]{2,1,0:T(8,128)(2,1)}, u32[]{:S(2)}) copy-start(bf16[1,768,2048]{2,1,0:T(8,128)(2,1)} %param.32) | copy-start | bytes 9437188
  7.2 21.1 copy-start.129
  7.2 63.3 %all-gather.17.cloned.1.call-start = ((), (), s32[]{:S(2)}) async-start(), calls=%async_computation.25 | async-start | bytes 2621440 | tf_op jit(solution)/shard_map/all_gather | solution.py:97
  9.7 43.2 %copy-start.121 = (f32[512]{0:T(512)}, f32[512]{0:T(512)S(1)}, u32[]{:S(2)}) copy-start(f32[512]{0:T(512)S(1)} %dynamic_slice.40) | copy-start | bytes 6148
  26.2 91.1 %all-gather.9.cloned.1.call-start = ((), (), s32[]{:S(2)}) async-start(), calls=%async_computation.20 | async-start | bytes 2621440 | tf_op jit(solution)/shard_map/all_gather | solution.py:97
  26.9 125.1 %all-gather.11.cloned.1.call-start = ((), (), s32[]{:S(2)}) async-start(), calls=%async_computation.21 | async-start | bytes 5242880 | tf_op jit(solution)/shard_map/all_gather | solution.py:257
  27.7 161.8 %all-gather.13.cloned.1.call-start = ((), (), s32[]{:S(2)}) async-start(), calls=%async_computation.22 | async-start | bytes 5242880 | tf_op jit(solution)/shard_map/all_gather | solution.py:260
  28.2 244.8 %reduce-scatter.9.cloned.1.call-start = ((), (), s32[]{:S(2)}) async-start(), calls=%async_computation.26 | async-start | bytes 5242880 | tf_op jit(solution)/shard_map/reduce_scatter | solution.py:101
  28.3 92.4 %copy-start.168 = (f32[64]{0:T(128)}, f32[64]{0:T(128)S(1)}, u32[]{:S(2)}) copy-start(f32[64]{0:T(128)S(1)} %multiply_power_fusion) | copy-start | bytes 772
  31.3 89.5 %copy-start.130 = (f32[512]{0:T(512)}, f32[512]{0:T(512)S(1)}, u32[]{:S(2)}) copy-start(f32[512]{0:T(512)S(1)} %fusion.210) | copy-start | bytes 6148
  31.4 89.4 %copy-start.132 = (f32[512]{0:T(512)}, f32[512]{0:T(512)S(1)}, u32[]{:S(2)}) copy-start(f32[512]{0:T(512)S(1)} %fusion.211) | copy-start | bytes 6148
  40.9 79.8 %copy-start.166 = (f32[128]{0:T(128)S(1)}, f32[128]{0:T(128)}, u32[]{:S(2)}) copy-start(f32[128]{0:T(128)} %param.26) | copy-start | bytes 1540
  73.0 46.9 %copy-start.147 = (f32[512]{0:T(512)}, f32[512]{0:T(512)S(1)}, u32[]{:S(2)}) copy-start(f32[512]{0:T(512)S(1)} %get-tuple-element.238) | copy-start | bytes 6148
  73.0 85.5 %copy-start.49 = (f32[512,128]{0,1:T(8,128)}, f32[512,128]{0,1:T(8,128)S(1)}, u32[]{:S(2)}) copy-start(f32[512,128]{0,1:T(8,128)S(1)} %get-tuple-element.239) | copy-start | bytes 786436
  73.0 47.7 %copy-start.134 = (f32[512]{0:T(512)}, f32[512]{0:T(512)S(1)}, u32[]{:S(2)}) copy-start(f32[512]{0:T(512)S(1)} %add_rsqrt_fusion.3) | copy-start | bytes 6148
  122.6 57.8 %copy-start.81 = (bf16[512,1,64]{0,2,1:T(8,128)(2,1)}, bf16[512,1,64]{0,2,1:T(8,128)(2,1)S(1)}, u32[]{:S(2)}) copy-start(bf16[512,1,64]{0,2,1:T(8,128)(2,1)S(1)} %get-tuple-element.228) | copy-start | bytes 196612
  122.6 57.8 %copy-start.83 = (bf16[512,1,64]{0,2,1:T(8,128)(2,1)}, bf16[512,1,64]{0,2,1:T(8,128)(2,1)S(1)}, u32[]{:S(2)}) copy-start(bf16[512,1,64]{0,2,1:T(8,128)(2,1)S(1)} %get-tuple-element.229) | copy-start | bytes 196612
  196.4 156.8 %reduce-scatter.7.cloned.1.call-start = ((), (), s32[]{:S(2)}) async-start(), calls=%async_computation.23 | async-start | bytes 5242880 | tf_op jit(solution)/shard_map/reduce_scatter | solution.py:101
  213.8 201.4 %all-gather.19.cloned.1.call-start = ((), (), s32[]{:S(2)}) async-start(), calls=%async_computation.27 | async-start | bytes 2621440 | tf_op jit(solution)/shard_map/all_gather | solution.py:97
  214.6 156.1 %copy-start.114 = (f32[512]{0:T(512)}, f32[512]{0:T(512)S(1)}, u32[]{:S(2)}) copy-start(f32[512]{0:T(512)S(1)} %dynamic_slice.43) | copy-start | bytes 6148
  214.6 156.2 %copy-start.138 = (s32[1024,8]{0,1:T(8,128)S(1)}, s32[1024,8]{0,1:T(8,128)}, u32[]{:S(2)}) copy-start(s32[1024,8]{0,1:T(8,128)} %param.20) | copy-start | bytes 98308
  370.8 47.6 %copy-start.110 = (s32[512,8]{0,1:T(8,128)}, s32[512,8]{0,1:T(8,128)S(1)}, u32[]{:S(2)}) copy-start(s32[512,8]{0,1:T(8,128)S(1)} %get-tuple-element.204) | copy-start | bytes 49156
  370.8 66.1 %copy-start.112 = (s32[512,8]{0,1:T(8,128)}, s32[512,8]{0,1:T(8,128)S(1)}, u32[]{:S(2)}) copy-start(s32[512,8]{0,1:T(8,128)S(1)} %get-tuple-element.205) | copy-start | bytes 49156
  431.1 68.5 %all-to-all-start.3 = ((bf16[4,320,2048]{2,1,0:T(8,128)(2,1)}), bf16[4,320,2048]{2,1,0:T(8,128)(2,1)}, u32[]{:S(2)}, u32[]{:S(2)}) async-start(bf16[4,320,2048]{2,1,0:T(8,128)(2,1)} %bitcast.500), calls=%async_computation.5 | async-start | bytes 10485760 | tf_op jit(solution)/shard_map/all_to_all | solution.py:328
  436.2 47.6 %all-gather.15.cloned.1.call-start = ((), (), s32[]{:S(2)}) async-start(), calls=%async_computation.24 | async-start | bytes 2621440 | tf_op jit(solution)/shard_map/all_gather | solution.py:97
  499.7 64.7 %all-to-all-start = ((bf16[4,320,2048]{2,1,0:T(8,128)(2,1)}), bf16[4,320,2048]{2,1,0:T(8,128)(2,1)}, u32[]{:S(2)}, u32[]{:S(2)}) async-start(bf16[4,320,2048]{2,1,0:T(8,128)(2,1)} %bitcast.501), calls=%async_computation.1 | async-start | bytes 10485760 | tf_op jit(solution)/shard_map/all_to_all | solution.py:328
  512.2 10.6 copy-start.179
  564.4 143.9 %all-to-all-start.4 = ((bf16[1,4,320,2048]{2,1,0,3:T(4,128)(2,1)}), bf16[1,4,320,2048]{2,1,0,3:T(4,128)(2,1)}, u32[]{:S(2)}, u32[]{:S(2)}) async-start(bf16[1,4,320,2048]{2,1,0,3:T(4,128)(2,1)} %copy.393), calls=%async_computation.6 | async-start | bytes 12582912 | tf_op jit(solution)/shard_map/all_to_all | solution.py:110
  577.4 10.6 copy-start.182
  708.3 142.9 %all-to-all-start.1 = ((bf16[1,4,320,2048]{2,1,0,3:T(4,128)(2,1)}), bf16[1,4,320,2048]{2,1,0,3:T(4,128)(2,1)}, u32[]{:S(2)}, u32[]{:S(2)}) async-start(bf16[1,4,320,2048]{2,1,0,3:T(4,128)(2,1)} %copy.384), calls=%async_computation.2 | async-start | bytes 12582912 | tf_op jit(solution)/shard_map/all_to_all | solution.py:110
  851.2 64.6 %all-to-all-start.5 = ((bf16[4,4,320,512]{3,2,0,1:T(8,128)(2,1)}), bf16[4,4,320,512]{3,2,0,1:T(8,128)(2,1)}, u32[]{:S(2)}, u32[]{:S(2)}) async-start(bf16[4,4,320,512]{3,2,0,1:T(8,128)(2,1)} %bitcast.507), calls=%async_computation.7 | async-start | bytes 10485760 | tf_op jit(solution)/shard_map/all_to_all | solution.py:109
  915.8 80.2 %all-to-all-start.2 = ((bf16[4,4,320,512]{3,2,0,1:T(8,128)(2,1)}), bf16[4,4,320,512]{3,2,0,1:T(8,128)(2,1)}, u32[]{:S(2)}, u32[]{:S(2)}) async-start(bf16[4,4,320,512]{3,2,0,1:T(8,128)(2,1)} %bitcast.503), calls=%async_computation.3 | async-start | bytes 10485760 | tf_op jit(solution)/shard_map/all_to_all | solution.py:109
  925.2 76.2 %copy-start.22 = (s32[4096]{0:T(1024)}, s32[4096]{0:T(1024)S(1)}, u32[]{:S(2)}) copy-start(s32[4096]{0:T(1024)S(1)} %broadcast_clamp_fusion.1) | copy-start | bytes 49156
  925.2 45.4 %copy-start.24 = (s32[4096]{0:T(1024)}, s32[4096]{0:T(1024)S(1)}, u32[]{:S(2)}) copy-start(s32[4096]{0:T(1024)S(1)} %broadcast_clamp_fusion) | copy-start | bytes 49156
  1084.0 116.1 %all-to-all-start.10 = ((bf16[4,4,320,512]{3,2,1,0:T(8,128)(2,1)}), bf16[4,4,320,512]{3,2,1,0:T(8,128)(2,1)}, u32[]{:S(2)}, u32[]{:S(2)}) async-start(bf16[4,4,320,512]{3,2,1,0:T(8,128)(2,1)} %bitcast.504), calls=%async_computation.13 | async-start | bytes 10485760 | tf_op jit(solution)/shard_map/all_to_all | solution.py:363
  1200.1 120.3 %all-to-all-start.6 = ((bf16[4,4,320,512]{3,2,1,0:T(8,128)(2,1)}), bf16[4,4,320,512]{3,2,1,0:T(8,128)(2,1)}, u32[]{:S(2)}, u32[]{:S(2)}) async-start(bf16[4,4,320,512]{3,2,1,0:T(8,128)(2,1)} %bitcast.506), calls=%async_computation.8 | async-start | bytes 10485760 | tf_op jit(solution)/shard_map/all_to_all | solution.py:363
  1320.4 64.5 %all-to-all-start.11 = ((bf16[1,4,320,2048]{3,2,0,1:T(8,128)(2,1)}), bf16[1,4,320,2048]{3,2,0,1:T(8,128)(2,1)}, u32[]{:S(2)}, u32[]{:S(2)}) async-start(bf16[1,4,320,2048]{3,2,0,1:T(8,128)(2,1)} %bitcast.508), calls=%async_computation.14 | async-start | bytes 10485760 | tf_op jit(solution)/shard_map/all_to_all | solution.py:362
  1384.9 64.5 %all-to-all-start.7 = ((bf16[1,4,320,2048]{3,2,0,1:T(8,128)(2,1)}), bf16[1,4,320,2048]{3,2,0,1:T(8,128)(2,1)}, u32[]{:S(2)}, u32[]{:S(2)}) async-start(bf16[1,4,320,2048]{3,2,0,1:T(8,128)(2,1)} %bitcast.505), calls=%async_computation.9 | async-start | bytes 10485760 | tf_op jit(solution)/shard_map/all_to_all | solution.py:362
  1449.4 143.6 %all-to-all-start.12 = ((bf16[1,4,320,2048]{2,1,0,3:T(4,128)(2,1)}), bf16[1,4,320,2048]{2,1,0,3:T(4,128)(2,1)}, u32[]{:S(2)}, u32[]{:S(2)}) async-start(bf16[1,4,320,2048]{2,1,0,3:T(4,128)(2,1)} %copy.415), calls=%async_computation.15 | async-start | bytes 12582912 | tf_op jit(solution)/shard_map/all_to_all | solution.py:110
  1593.0 142.9 %all-to-all-start.8 = ((bf16[1,4,320,2048]{2,1,0,3:T(4,128)(2,1)}), bf16[1,4,320,2048]{2,1,0,3:T(4,128)(2,1)}, u32[]{:S(2)}, u32[]{:S(2)}) async-start(bf16[1,4,320,2048]{2,1,0,3:T(4,128)(2,1)} %copy.398), calls=%async_computation.10 | async-start | bytes 12582912 | tf_op jit(solution)/shard_map/all_to_all | solution.py:110
  1735.9 64.5 %all-to-all-start.13 = ((bf16[4,4,320,512]{3,2,0,1:T(8,128)(2,1)}), bf16[4,4,320,512]{3,2,0,1:T(8,128)(2,1)}, u32[]{:S(2)}, u32[]{:S(2)}) async-start(bf16[4,4,320,512]{3,2,0,1:T(8,128)(2,1)} %bitcast.509), calls=%async_computation.16 | async-start | bytes 10485760 | tf_op jit(solution)/shard_map/all_to_all | solution.py:109
  1800.4 10.5 copy-start.56
  1800.4 64.6 %all-to-all-start.9 = ((bf16[4,4,320,512]{3,2,0,1:T(8,128)(2,1)}), bf16[4,4,320,512]{3,2,0,1:T(8,128)(2,1)}, u32[]{:S(2)}, u32[]{:S(2)}) async-start(bf16[4,4,320,512]{3,2,0,1:T(8,128)(2,1)} %bitcast.502), calls=%async_computation.11 | async-start | bytes 10485760 | tf_op jit(solution)/shard_map/all_to_all | solution.py:109
  1805.6 151.0 %all-gather.21.cloned.1.call-start = ((), (), s32[]{:S(2)}) async-start(), calls=%async_computation.28 | async-start | bytes 2621440 | tf_op jit(solution)/shard_map/all_gather | solution.py:97
  1813.9 82.6 %copy-start.73 = (f32[512,1,16]{2,1,0:T(1,128)}, f32[512,1,16]{2,1,0:T(1,128)S(1)}, u32[]{:S(2)}) copy-start(f32[512,1,16]{2,1,0:T(1,128)S(1)} %fusion.248) | copy-start | bytes 98308
  1851.0 19.4 copy-start.23
  1896.2 12.5 copy-start.160
  1896.3 12.5 copy-start.158
  1913.3 90.0 %all-gather.23.cloned.1.call-start = ((), (), s32[]{:S(2)}) async-start(), calls=%async_computation.30 | async-start | bytes 2621440 | tf_op jit(solution)/shard_map/all_gather | solution.py:97
  1913.9 255.9 %reduce-scatter.17.cloned.1.call-start = ((), (), s32[]{:S(2)}) async-start(), calls=%async_computation.33 | async-start | bytes 10485760 | tf_op jit(solution)/shard_map/reduce_scatter | solution.py:470
  2013.4 156.5 %reduce-scatter.15.cloned.1.call-start = ((), (), s32[]{:S(2)}) async-start(), calls=%async_computation.32 | async-start | bytes 10485760 | tf_op jit(solution)/shard_map/reduce_scatter | solution.py:469
  2015.8 13.6 copy-start.96
  2015.8 13.6 slice-start.4
  2071.6 275.1 %all-reduce.13.cloned.1.call-start = ((), (), s32[]{:S(2)}) async-start(), calls=%async_computation.34 | async-start | bytes 17039360 | tf_op jit(solution)/shard_map/psum | solution.py:497
  2101.5 324.3 %reduce-scatter.11.cloned.1.call-start = ((), (), s32[]{:S(2)}) async-start(), calls=%async_computation.29 | async-start | bytes 5242880 | tf_op jit(solution)/shard_map/reduce_scatter | solution.py:101
  2111.0 394.2 %reduce-scatter.13.cloned.1.call-start = ((), (), s32[]{:S(2)}) async-start(), calls=%async_computation.31 | async-start | bytes 5242880 | tf_op jit(solution)/shard_map/reduce_scatter | solution.py:101
  2120.3 907.5 %all-reduce.15.cloned.1.call-start = ((), (), s32[]{:S(2)}) async-start(), calls=%async_computation.35 | async-start | bytes 46137344 | tf_op jit(solution)/shard_map/psum | solution.py:472
  2170.9 334.3 %copy-start.122 = (f32[512]{0:T(512)S(1)}, f32[512]{0:T(512)}, u32[]{:S(2)}) copy-start(f32[512]{0:T(512)} %copy-done.121) | copy-start | bytes 6148
  2170.9 334.3 %copy-start.140 = (f32[512]{0:T(512)S(1)}, f32[512]{0:T(512)}, u32[]{:S(2)}) copy-start(f32[512]{0:T(512)} %copy-done.139) | copy-start | bytes 6148
  2170.9 334.3 %copy-start.142 = (f32[512]{0:T(512)S(1)}, f32[512]{0:T(512)}, u32[]{:S(2)}) copy-start(f32[512]{0:T(512)} %copy-done.141) | copy-start | bytes 6148
  2175.5 382.9 %copy-start.164 = (f32[512]{0:T(512)S(1)}, f32[512]{0:T(512)}, u32[]{:S(2)}) copy-start(f32[512]{0:T(512)} %copy-done.163) | copy-start | bytes 6148
  2175.5 382.9 %copy-start.116 = (f32[512]{0:T(512)S(1)}, f32[512]{0:T(512)}, u32[]{:S(2)}) copy-start(f32[512]{0:T(512)} %copy-done.114) | copy-start | bytes 6148
  2175.5 382.9 %copy-start.128 = (f32[512]{0:T(512)S(1)}, f32[512]{0:T(512)}, u32[]{:S(2)}) copy-start(f32[512]{0:T(512)} %copy-done.126) | copy-start | bytes 6148
  2175.5 382.9 %copy-start.146 = (f32[512]{0:T(512)S(1)}, f32[512]{0:T(512)}, u32[]{:S(2)}) copy-start(f32[512]{0:T(512)} %copy-done.145) | copy-start | bytes 6148
  (171 other events, 718.4 us)
Sparse Core Ops, SparseCore 0:
  26.3 44.1 all-gather.16
  72.6 44.5 all-gather.8
  118.8 33.1 all-gather.10
  153.4 34.4 all-gather.12
  196.5 76.4 reduce-scatter.8
  275.9 77.2 reduce-scatter.6
  370.9 44.2 all-gather.18
  438.6 45.1 all-gather.14
  1913.4 43.1 all-gather.20
  1958.6 44.6 all-gather.22
  2013.5 70.3 reduce-scatter.16
  2086.5 71.7 reduce-scatter.14
  2165.0 181.5 all-reduce.12
  2348.9 76.8 reduce-scatter.10
  2427.9 77.2 reduce-scatter.12
  2508.7 519.0 all-reduce.14
where the time goes:
time: 3070 us; the launch traced here: 3050 us
  waiting for transfers between devices  1950 us (64%)
  local copies, waits for them, and re-layouts  416 us (14%)
  matrix products  299 us (10%)
  other arithmetic  163 us (5%)
  blocking collectives  130 us (4%)
  starting transfers between devices  74.3 us (2%)
    psum x1, waiting for transfers between devices, per_device(): lax.psum((acc_gate, acc_up, acc_down, query_share, out_share), 'dp')  462 us
    all_to_all x4, waiting for transfers between devices, from_experts(): lax.all_to_all(shaped, 'row', split_axis=3, concat_axis=0, tiled=True)  462 us
    reduce_scatter x4, waiting for transfers between devices, feature_share(): return lax.psum_scatter(values, 'row', scatter_dimension=1, tiled=True)  293 us
    psum x1, waiting for transfers between devices, per_device(): lax.psum((gain_one_full, gain_two_full, acc_query_gain, acc_key_gain, rou...  171 us
    all_gather x6, waiting for transfers between devices, full_features(): return lax.all_gather(values, 'row', axis=1, tiled=True)  163 us
    all_to_all x2, waiting for transfers between devices, per_device(): lax.all_to_all(outgoing_grad, 'row', split_axis=0, concat_axis=3, tiled=T...  153 us
    all_to_all x4, waiting for transfers between devices, from_experts(): lax.all_to_all(lax.all_to_all(shaped, 'row', split_axis=3, concat_axis=0,...  112 us
    all_to_all x2, waiting for transfers between devices, per_device(): lax.all_to_all(lax.all_to_all(outgoing_grad, 'row', split_axis=0, concat_...  77.8 us
  transfers between devices with their start and end apart: 30, of which 25 were waited for; matrix products, arithmetic and copies ran while one was open for 23% of the time, Pallas kernels for 0%

commit v1 on v0

v1 whole, which is shorter than its diff:
```python
import jax
import jax.numpy as jnp
from jax import lax
from jax.sharding import PartitionSpec as P

SEQUENCE_TOKENS = 512
EPSILON = 1e-06
ROPE_BASE = 1000000.0
MASKED = -1e30
BF16 = jnp.bfloat16
F32 = jnp.float32


def dot(left, right):
    return jnp.dot(left, right, preferred_element_type=F32)


def moved(block, axis, by):
    count = lax.axis_size(axis)
    return lax.ppermute(block, axis, [(i, (i + by) % count) for i in range(count)])


def swapped(block, axis, bit):
    count = lax.axis_size(axis)
    return lax.ppermute(block, axis, [(i, i ^ (1 << bit)) for i in range(count)])


def butterfly(values, axis):
    for bit in range(lax.axis_size(axis).bit_length() - 1):
        values = values + swapped(values, axis, bit)
    return values


def ring_pieces(block):
    count = lax.axis_size("row")
    pieces = [block] + [None] * (count - 1)
    from_left = from_right = block
    half = block.shape[0] // 2
    for step in range(1, count // 2):
        from_left = moved(from_left, "row", 1)
        from_right = moved(from_right, "row", -1)
        pieces[count - step] = from_left
        pieces[step] = from_right
    if count > 1:
        pieces[count // 2] = jnp.concatenate(
            [moved(from_left[:half], "row", 1), moved(from_right[half:], "row", -1)], axis=0
        )
    return pieces


def ring_gather(block):
    count = lax.axis_size("row")
    place = lax.axis_index("row")
    width = block.shape[-1]
    whole = jnp.zeros(block.shape[:-1] + (width * count,), block.dtype)
    for distance, piece in enumerate(ring_pieces(block)):
        start = (place + distance) % count * width
        whole = lax.dynamic_update_slice_in_dim(whole, piece, start, block.ndim - 1)
    return whole


def ring_scatter(partial):
    count = lax.axis_size("row")
    place = lax.axis_index("row")
    width = partial.shape[1] // count
    half = partial.shape[0] // 2

    def piece(distance):
        start = (place + distance) % count * width
        return lax.dynamic_slice_in_dim(partial, start, width, 1)

    total = piece(0).astype(F32)
    if count == 1:
        return total
    middle = piece(count // 2)
    to_right = moved(middle[:half], "row", 1)
    to_left = moved(middle[half:], "row", -1)
    for step in range(count // 2 - 1, 0, -1):
        right, left = piece(step), piece(count - step)
        if step == count // 2 - 1:
            right = jnp.concatenate([right[:half] + to_right, right[half:]], axis=0)
            left = jnp.concatenate([left[:half], left[half:] + to_left], axis=0)
        else:
            right = right + to_right
            left = left + to_left
        to_right = moved(right, "row", 1)
        to_left = moved(left, "row", -1)
    if count == 2:
        return total + jnp.concatenate([to_right, to_left], axis=0).astype(F32)
    return total + to_right.astype(F32) + to_left.astype(F32)


def col_gather(block):
    count = lax.axis_size("col")
    pieces = []
    for step in range(count // 2):
        same = block if step == 0 else moved(block, "col", 2 * step)
        pieces += [same, swapped(same, "col", 0)]
    return pieces


def col_scatter(pieces):
    count = lax.axis_size("col")
    total = None
    for step in range(count // 2 - 1, -1, -1):
        here = pieces[2 * step].astype(F32) + swapped(pieces[2 * step + 1], "col", 0).astype(F32)
        if step > 0:
            here = moved(here.astype(pieces[0].dtype), "col", -2 * step).astype(F32)
        total = here if total is None else total + here
    return total


def col_order():
    count = lax.axis_size("col")
    place = lax.axis_index("col")
    chip, core = place // 2, place % 2
    order = []
    for step in range(count // 2):
        back = (chip - step) % (count // 2) * 2
        order += [back + core, back + 1 - core]
    return order


def col_assemble(block, axis):
    count = lax.axis_size("col")
    width = block.shape[axis]
    shape = list(block.shape)
    shape[axis] = width * count
    whole = jnp.zeros(shape, block.dtype)
    for piece, place in zip(col_gather(block), col_order()):
        whole = lax.dynamic_update_slice_in_dim(whole, piece, place * width, axis)
    return whole


def col_share(partial, axis):
    width = partial.shape[axis] // lax.axis_size("col")
    return col_scatter(
        [lax.dynamic_slice_in_dim(partial, place * width, width, axis) for place in col_order()]
    )


def pair_total(values):
    low = values.astype(BF16)
    total = low.astype(F32)
    for bit in range(lax.axis_size("dp").bit_length() - 1):
        total = total + swapped(low, "dp", bit).astype(F32)
        low = total.astype(BF16)
    return total


def rms_factor(values):
    return lax.rsqrt(jnp.mean(values * values, axis=-1, keepdims=True) + EPSILON)


def rms_back(values, gain, upstream):
    factor = rms_factor(values)
    weighted = upstream * gain
    inner_sum = jnp.mean(weighted * values, axis=-1, keepdims=True)
    return (
        weighted * factor - values * (factor * factor * factor * inner_sum),
        upstream * values * factor,
    )


def positions(segment_ids):
    places = jnp.arange(segment_ids.shape[0], dtype=jnp.int32)
    earlier = jnp.concatenate([segment_ids[:1] - 1, segment_ids[:-1]])
    starts = jnp.logical_or(segment_ids != earlier, places % SEQUENCE_TOKENS == 0)
    opening = lax.cummax(jnp.where(starts, places, 0), axis=0)
    return places - opening


def rotary(places, head_size):
    halfway = head_size // 2
    frequency = ROPE_BASE ** (-2.0 * jnp.arange(halfway, dtype=F32) / head_size)
    angles = places.astype(F32)[:, None] * frequency[None, :]
    return (jnp.cos(angles), jnp.sin(angles))


def rotate(values, cos_table, sin_table):
    halfway = values.shape[-1] // 2
    front, back = values[..., :halfway], values[..., halfway:]
    cos_wide, sin_wide = cos_table[:, None, :], sin_table[:, None, :]
    return jnp.concatenate(
        [front * cos_wide - back * sin_wide, back * cos_wide + front * sin_wide], axis=-1
    )


def unrotate(upstream, cos_table, sin_table):
    return rotate(upstream, cos_table, -sin_table)


def sequence_scores(query_low, key_low, segment_ids, score_scale):
    scores = jnp.einsum("qhd,kd->hqk", query_low, key_low, preferred_element_type=F32) * score_scale
    places = jnp.arange(segment_ids.shape[0], dtype=jnp.int32)
    allowed = jnp.logical_and(
        segment_ids[:, None] == segment_ids[None, :], places[None, :] <= places[:, None]
    )
    return jnp.where(allowed[None], scores, MASKED)


def attention_forward(query_low, key_low, value_low, segment_ids, score_scale):
    scores = sequence_scores(query_low, key_low, segment_ids, score_scale)
    top_score = jnp.max(scores, axis=-1, keepdims=True)
    weights = jnp.exp(scores - top_score)
    denominator = jnp.sum(weights, axis=-1, keepdims=True)
    probs_low = (weights / denominator).astype(BF16)
    mixed = jnp.einsum("hqk,kd->qhd", probs_low, value_low, preferred_element_type=F32)
    return mixed, (top_score + jnp.log(denominator))[..., 0]


def attention_backward(
    query_low, key_low, value_low, segment_ids, log_totals, mixed_grad, score_scale
):
    scores = sequence_scores(query_low, key_low, segment_ids, score_scale)
    probs = jnp.exp(scores - log_totals[:, :, None])
    probs_low = probs.astype(BF16)
    prob_grad = jnp.einsum("qhd,kd->hqk", mixed_grad, value_low, preferred_element_type=F32)
    score_grad = (
        probs * (prob_grad - jnp.sum(probs * prob_grad, axis=-1, keepdims=True))
    ).astype(BF16)
    query_grad = (
        jnp.einsum("hqk,kd->qhd", score_grad, key_low, preferred_element_type=F32) * score_scale
    )
    key_grad = (
        jnp.einsum("hqk,qhd->kd", score_grad, query_low, preferred_element_type=F32) * score_scale
    )
    value_grad = jnp.einsum("hqk,qhd->kd", probs_low, mixed_grad, preferred_element_type=F32)
    return query_grad, key_grad, value_grad


def per_device(
    residual,
    segments,
    routes,
    norm_attention,
    query_weight,
    key_projection_matrix,
    value_projection_matrix,
    query_gain,
    key_gain,
    out_weight,
    norm_experts,
    router_weight,
    gate_weight,
    up_weight,
    down_weight,
    grad_output,
):
    row_count = lax.axis_size("row")
    col_count = lax.axis_size("col")
    row_place = lax.axis_index("row")
    col_place = lax.axis_index("col")
    model_width = norm_attention.shape[0]
    feature_width = model_width // row_count
    head_size = query_gain.shape[0]
    heads_here = query_weight.shape[1] // head_size
    query_width = heads_here * head_size
    kv_heads = key_projection_matrix.shape[1] // head_size
    query_group_width = heads_here * row_count // kv_heads
    members = query_group_width // heads_here
    kv_index = row_place * heads_here // query_group_width
    member_place = row_place % members
    share_width = head_size // members
    column_mask = (jnp.arange(head_size, dtype=jnp.int32) // share_width == member_place).astype(
        F32
    )
    experts = gate_weight.shape[0] * row_count * col_count
    expert = row_place * col_count + col_place
    gate_here, up_here, down_here = gate_weight[0], up_weight[0], down_weight[0]
    token_rows = residual.shape[0]
    chunks = token_rows // SEQUENCE_TOKENS
    rows = SEQUENCE_TOKENS
    top_count = routes.shape[1]
    capacity = max(2, 5 * rows * top_count // (4 * experts))
    score_scale = head_size ** (-0.5)
    row_start = row_place * feature_width
    gain_one = lax.dynamic_slice_in_dim(norm_attention, row_start, feature_width)
    gain_two = lax.dynamic_slice_in_dim(norm_experts, row_start, feature_width)
    router_rows = lax.dynamic_slice_in_dim(router_weight, row_start, feature_width, 0)
    labels = jnp.arange(experts, dtype=jnp.int32)
    key_part = lax.dynamic_slice_in_dim(key_projection_matrix, kv_index * head_size, head_size, 1)
    value_part = lax.dynamic_slice_in_dim(
        value_projection_matrix, kv_index * head_size, head_size, 1
    )

    def chunk(array, number):
        return array[number * rows : (number + 1) * rows]

    blocks = [chunk(residual, n) for n in range(chunks)]
    grads = [chunk(grad_output, n) for n in range(chunks)]
    segs = [chunk(segments, n) for n in range(chunks)]
    picks = [chunk(routes, n) for n in range(chunks)]

    inputs_full = [ring_gather(block) for block in blocks]
    projection = col_assemble(jnp.concatenate([query_weight, key_part, value_part], axis=1), 0)
    out_full = col_assemble(out_weight, 1)
    picks_all = [jnp.stack(col_gather(pick)) for pick in picks]
    grads_cols = [jnp.stack(col_gather(grad)) for grad in grads]

    state = [{} for _ in range(chunks)]

    for n in range(chunks):
        s = state[n]
        wide = inputs_full[n].astype(F32)
        s["scale_one"] = rms_factor(wide)
        s["normed_full"] = (wide * s["scale_one"] * norm_attention).astype(BF16)
        projected = dot(s["normed_full"], projection)
        s["query_pre"] = projected[:, :query_width].reshape(rows, heads_here, head_size)
        s["key_pre"] = projected[:, None, query_width : query_width + head_size]
        s["value_pre"] = projected[:, query_width + head_size :]
        s["value_low"] = s["value_pre"].astype(BF16)
        s["tables"] = rotary(positions(segs[n]), head_size)
        s["query_low"] = rotate(
            s["query_pre"] * rms_factor(s["query_pre"]) * query_gain, *s["tables"]
        ).astype(BF16)
        s["key_low"] = rotate(s["key_pre"] * rms_factor(s["key_pre"]) * key_gain, *s["tables"])[
            :, 0, :
        ].astype(BF16)
        mixed, s["log_totals"] = attention_forward(
            s["query_low"], s["key_low"], s["value_low"], segs[n], score_scale
        )
        s["mixed_low"] = mixed.reshape(rows, query_width).astype(BF16)
        partial = dot(s["mixed_low"], out_full).astype(BF16)
        s["hidden"] = blocks[n].astype(F32) + ring_scatter(partial)

    for n in range(chunks):
        s = state[n]
        wide = ring_gather(s["hidden"].astype(BF16)).astype(F32)
        s["scale_two"] = rms_factor(wide)
        normed_full = (wide * s["scale_two"] * norm_experts).astype(BF16)
        s["normed_two"] = lax.dynamic_slice_in_dim(normed_full, row_start, feature_width, 1)
        s["tokens"] = jnp.stack(col_gather(normed_full))

    grads_full = [ring_gather(g) for g in grads_cols]

    acc_gate = acc_up = acc_down = None
    for n in range(chunks):
        s = state[n]
        chosen = jnp.any(picks_all[n][:, :, :, None] == labels, axis=2)
        s["chosen"] = chosen[0]
        logits = jnp.einsum("gtd,de->gte", s["tokens"], router_weight, preferred_element_type=F32)
        shifted = jnp.where(chosen, logits, MASKED)
        weights = jnp.exp(shifted - jnp.max(shifted, axis=-1, keepdims=True))
        gates = weights / jnp.sum(weights, axis=-1, keepdims=True)
        s["logits"], s["gates"] = logits[0], gates[0]
        mine = jnp.any(picks_all[n] == expert, axis=2)
        ranks = jnp.cumsum(mine.astype(jnp.int32), axis=1) - 1
        slots = jnp.arange(capacity, dtype=jnp.int32)
        onehot = jnp.logical_and(ranks[:, None, :] == slots[None, :, None], mine[:, None, :])
        gates_here = lax.dynamic_index_in_dim(gates, expert, 2, keepdims=False)
        slot_gates = jnp.sum(jnp.where(onehot, gates_here[:, None, :], 0.0), axis=2).reshape(-1, 1)
        choose = onehot.astype(BF16)

        def gather(values):
            found = jnp.einsum("gst,gtd->gsd", choose, values, preferred_element_type=F32)
            return found.astype(BF16).reshape(-1, model_width)

        def scatter(values):
            values = values.reshape(col_count, capacity, model_width)
            spread = jnp.einsum("gst,gsd->gtd", choose, values, preferred_element_type=F32)
            spread = spread.astype(BF16)
            return ring_scatter(
                col_scatter([spread[g] for g in range(col_count)]).astype(BF16)
            )

        expert_in = gather(s["tokens"])
        gate_pre = dot(expert_in, gate_here)
        up_pre = dot(expert_in, up_here)
        sigmoid_gate = jax.nn.sigmoid(gate_pre)
        silu_gate = gate_pre * sigmoid_gate
        hidden_low = (silu_gate * up_pre).astype(BF16)
        expert_out = dot(hidden_low, down_here).astype(BF16).astype(F32)
        s["mixture"] = scatter((slot_gates * expert_out).astype(BF16))

        out_grad = gather(grads_full[n]).astype(F32)
        gate_dots = jnp.sum(out_grad * expert_out, axis=1)
        expert_grad = (slot_gates * out_grad).astype(BF16)
        hidden_grad = dot(expert_grad, down_here.T).astype(BF16).astype(F32)
        gate_grad = (
            hidden_grad * up_pre * sigmoid_gate * (1.0 + gate_pre * (1.0 - sigmoid_gate))
        ).astype(BF16)
        up_grad = (hidden_grad * silu_gate).astype(BF16)
        slot_grad = dot(gate_grad, gate_here.T) + dot(up_grad, up_here.T)
        slot_low = slot_grad.astype(BF16)
        slot_inner = jnp.sum(slot_grad * expert_in.astype(F32), axis=1)
        s["spread_grad"] = scatter(slot_low)

        def by_token(values):
            values = values.reshape(col_count, capacity, 1)
            return jnp.sum(jnp.where(onehot, values, 0.0), axis=1)

        dots_here = by_token(gate_dots)
        inner_here = by_token(slot_inner)
        small = jnp.concatenate(
            [
                jnp.where((labels == expert)[None, :, None], dots_here[:, None, :], 0.0),
                inner_here[:, None, :],
            ],
            axis=1,
        )
        s["small"] = butterfly(col_scatter([small[g] for g in range(col_count)]), "row")
        here = (
            dot(expert_in.T, gate_grad),
            dot(expert_in.T, up_grad),
            dot(hidden_low.T, expert_grad),
        )
        if n == 0:
            acc_gate, acc_up, acc_down = here
        else:
            acc_gate, acc_up, acc_down = acc_gate + here[0], acc_up + here[1], acc_down + here[2]
    grad_gate, grad_up, grad_down = pair_total(acc_gate), pair_total(acc_up), pair_total(acc_down)

    acc_projection = acc_out = None
    acc_router = jnp.zeros((feature_width, experts), F32)
    acc_gain_one = jnp.zeros((model_width,), F32)
    acc_gain_two = jnp.zeros((feature_width,), F32)
    acc_query_gain = jnp.zeros((head_size,), F32)
    acc_key_gain = jnp.zeros((head_size,), F32)
    output_blocks, input_blocks = [], []
    for n in range(chunks):
        s = state[n]
        output_blocks.append((s["hidden"] + s["mixture"]).astype(BF16))
        block_grad = grads[n].astype(F32)
        gate_dots = s["small"][:experts].T
        slot_inner = s["small"][experts]
        pick_grad = s["gates"] * (
            gate_dots - jnp.sum(s["gates"] * gate_dots, axis=1, keepdims=True)
        )
        logit_grad = pick_grad.astype(BF16)
        acc_router = acc_router + dot(s["normed_two"].T, logit_grad)
        normed_two_grad = s["spread_grad"] + dot(logit_grad, router_rows.T)
        inner_two = slot_inner[:, None] + jnp.sum(
            logit_grad.astype(F32) * s["logits"], axis=1, keepdims=True
        )
        scale_two = s["scale_two"]
        hidden_total = (
            block_grad
            + normed_two_grad * gain_two * scale_two
            - s["hidden"] * (scale_two * scale_two * inner_two / model_width)
        )
        acc_gain_two = acc_gain_two + jnp.sum(normed_two_grad * s["hidden"] * scale_two, axis=0)
        branch_full = ring_gather(hidden_total.astype(BF16))
        out_here = dot(s["mixed_low"].T, branch_full)
        acc_out = out_here if n == 0 else acc_out + out_here
        mixed_grad = dot(branch_full, out_full.T).astype(BF16)
        mixed_grad = mixed_grad.reshape(rows, heads_here, head_size)
        query_grad, key_grad, value_grad = attention_backward(
            s["query_low"],
            s["key_low"],
            s["value_low"],
            segs[n],
            s["log_totals"],
            mixed_grad,
            score_scale,
        )
        for bit in range(members.bit_length() - 1):
            key_grad = key_grad + swapped(key_grad, "row", bit)
            value_grad = value_grad + swapped(value_grad, "row", bit)
        query_pre_grad, query_terms = rms_back(
            s["query_pre"], query_gain, unrotate(query_grad, *s["tables"])
        )
        acc_query_gain = acc_query_gain + jnp.sum(query_terms, axis=(0, 1))
        key_pre_grad, key_terms = rms_back(
            s["key_pre"], key_gain, unrotate(key_grad[:, None, :], *s["tables"])
        )
        acc_key_gain = acc_key_gain + column_mask * jnp.sum(key_terms, axis=(0, 1))
        projected_grad = jnp.concatenate(
            [
                query_pre_grad.reshape(rows, query_width).astype(BF16),
                (column_mask * key_pre_grad[:, 0, :]).astype(BF16),
                (column_mask * value_grad).astype(BF16),
            ],
            axis=1,
        )
        projected = jnp.concatenate(
            [s["query_pre"].reshape(rows, query_width), s["key_pre"][:, 0, :], s["value_pre"]],
            axis=1,
        )
        inner_one = butterfly(
            jnp.sum(projected_grad.astype(F32) * projected, axis=1), "row"
        )[:, None]
        partial = dot(projected_grad, projection.T)
        acc_gain_one = acc_gain_one + jnp.sum(
            partial * inputs_full[n].astype(F32) * s["scale_one"], axis=0
        )
        projection_here = dot(s["normed_full"].T, projected_grad)
        acc_projection = projection_here if n == 0 else acc_projection + projection_here
        normed_one_grad = ring_scatter(partial.astype(BF16))
        scale_one = s["scale_one"]
        input_blocks.append(
            hidden_total
            + normed_one_grad * gain_one * scale_one
            - blocks[n].astype(F32) * (scale_one * scale_one * inner_one / model_width)
        )

    grad_out_weight = pair_total(col_share(acc_out.astype(BF16), 1))
    projection_share = pair_total(col_share(acc_projection.astype(BF16), 0))
    grad_query = projection_share[:, :query_width]
    shares = ring_gather(projection_share[:, query_width:].astype(BF16))
    shares = shares.astype(F32).reshape(-1, kv_heads, members, 2, head_size).sum(axis=2)
    grad_key = shares[:, :, 0].reshape(-1, kv_heads * head_size)
    grad_value = shares[:, :, 1].reshape(-1, kv_heads * head_size)

    gain_two_full = lax.dynamic_update_slice_in_dim(
        jnp.zeros((model_width,), F32), acc_gain_two, row_start, 0
    )
    router_full = lax.dynamic_update_slice_in_dim(
        jnp.zeros((model_width, experts), F32), acc_router, row_start, 0
    )
    sizes = (model_width, model_width, head_size, head_size, model_width * experts)
    flat = jnp.concatenate(
        [acc_gain_one, gain_two_full, acc_query_gain, acc_key_gain, router_full.reshape(-1)]
    )
    for axis in ("dp", "col", "row"):
        flat = butterfly(flat, axis)
    totals, start = [], 0
    for size in sizes:
        totals.append(flat[start : start + size])
        start += size
    return (
        jnp.concatenate(output_blocks, axis=0),
        jnp.concatenate(input_blocks, axis=0),
        totals[0],
        grad_query,
        grad_key,
        grad_value,
        totals[2],
        totals[3],
        grad_out_weight,
        totals[1],
        totals[4].reshape(model_width, experts),
        grad_gate[None],
        grad_up[None],
        grad_down[None],
    )


def solution(mesh):
    in_specs = (
        P(("dp", "col"), "row"),
        P(("dp", "col")),
        P(("dp", "col"), None),
        P(),
        P("col", "row"),
        P("col", None),
        P("col", None),
        P(),
        P(),
        P("row", "col"),
        P(),
        P(),
        P(("row", "col"), None, None),
        P(("row", "col"), None, None),
        P(("row", "col"), None, None),
        P(("dp", "col"), "row"),
    )
    out_specs = (
        P(("dp", "col"), "row"),
        P(("dp", "col"), "row"),
        P(),
        P("col", "row"),
        P("col", None),
        P("col", None),
        P(),
        P(),
        P("row", "col"),
        P(),
        P(),
        P(("row", "col"), None, None),
        P(("row", "col"), None, None),
        P(("row", "col"), None, None),
    )
    return jax.shard_map(
        per_device, mesh=mesh, in_specs=in_specs, out_specs=out_specs, check_vma=False
    )
```

time: 3070 us -> 1590 us (0.52)
  waiting for transfers between devices: 1950 us -> 770 us
  local copies, waits for them, and re-layouts: 416 us -> 146 us
  blocking collectives: 130 us -> 0 us
  starting transfers between devices: 74.3 us -> 203 us
    all_to_all x14 -> x0, waiting for transfers between devices: 830 us -> none  [the longest x4 462 us: from_experts(): lax.all_to_all(shaped, 'row', split_axis=3, concat_axis=0, tiled=True)]
    ppermute x0 -> x134, waiting for transfers between devices: none -> 770 us  [the longest x84 581 us: moved(): lax.ppermute(block, axis, [(i, (i + by) % count) for i in range(count)])]
    psum x2 -> x0, waiting for transfers between devices: 633 us -> none  [the longest x1 462 us: per_device(): lax.psum((acc_gate, acc_up, acc_down, query_share, out_share), 'dp')]
    reduce_scatter x6 -> x0, waiting for transfers between devices: 293 us -> none  [the longest x4 293 us: feature_share(): return lax.psum_scatter(values, 'row', scatter_dimension=1, tiled=True)]
    ppermute x0 -> x134, starting transfers between devices: none -> 203 us  [the longest x84 175 us: moved(): lax.ppermute(block, axis, [(i, (i + by) % count) for i in range(count)])]
    all_gather x8 -> x0, waiting for transfers between devices: 191 us -> none  [the longest x6 163 us: full_features(): return lax.all_gather(values, 'row', axis=1, tiled=True)]
    gather x12 -> x0, local copies, waits for them, and re-layouts: 178 us -> none  [the longest x6 70 us: per_device(): picked = jnp.take_along_axis(logits, block_routes, axis=1)]
    psum x6 -> x0, blocking collectives: 115 us -> none  [the longest x5 75.2 us: row_total(): return lax.psum(values, 'row')]
  transfers between devices with their start and end apart: 30 -> 134, of which waited for: 25 -> 59; matrix products, arithmetic and copies ran while one was open for 23% -> 29% of each run, Pallas kernels for 0% -> 0%
where the time goes in v1:
time: 1590 us; the launch traced here: 1580 us
  waiting for transfers between devices  770 us (48%)
  matrix products  311 us (20%)
  starting transfers between devices  203 us (13%)
  other arithmetic  148 us (9%)
  local copies, waits for them, and re-layouts  146 us (9%)
    ppermute x84, waiting for transfers between devices, moved(): lax.ppermute(block, axis, [(i, (i + by) % count) for i in range(count)])  581 us
    dot_general x34, matrix products, dot(): return jnp.dot(left, right, preferred_element_type=F32)  212 us
    ppermute x50, waiting for transfers between devices, swapped(): return lax.ppermute(block, axis, [(i, i ^ 1 << bit) for i in range(count)])  189 us
    ppermute x84, starting transfers between devices, moved(): lax.ppermute(block, axis, [(i, (i + by) % count) for i in range(count)])  175 us
    unnamed x449, local copies, waits for them, and re-layouts  44.4 us
    dot_general x4, matrix products, scatter(): jnp.einsum('gst,gsd->gtd', choose, values, preferred_element_type=F32)  31.8 us
  transfers between devices with their start and end apart: 134, of which 59 were waited for; matrix products, arithmetic and copies ran while one was open for 29% of the time, Pallas kernels for 0%

profile of v1, /device:TPU:0, one launch (start us, length us, event | category | flops | bytes accessed | tf_op | source)
XLA Modules:
  0.0 1583.3 jit_solution(7630216765957893277)
XLA Ops:
  23.1 17.3 %collective-permute-done.1 = bf16[512,512]{1,0:T(8,128)(2,1)} collective-permute-done((bf16[512,512]{1,0:T(8,128)(2,1)}, bf16[512,512]{1,0:T(8,128)(2,1)}, u32[]{:S(2)}, u32[]{:S(2)}) %collective-permute-start.1) | collective-permute-done | bytes 524320 | tf_op jit(solution)/shard_map/ppermute | solution.py:20
  45.9 5.9 collective-permute-done.2
  74.0 6.6 fusion.163
  106.6 7.2 collective-permute-done.10
  121.0 12.8 collective-permute-done.11
  133.8 8.6 collective-permute-done.13
  148.0 12.9 collective-permute-done.32
  161.0 11.2 collective-permute-done.31
  228.0 11.9 collective-permute-start.38
  240.5 10.6 collective-permute-done.18
  255.1 7.2 collective-permute-done.36
  262.2 11.2 collective-permute-done.38
  283.9 21.9 %collective-permute-done.43 = bf16[512,512]{1,0:T(8,128)(2,1)S(1)} collective-permute-done((bf16[512,512]{1,0:T(8,128)(2,1)S(1)}, bf16[512,512]{1,0:T(8,128)(2,1)S(1)}, u32[]{:S(2)}, u32[]{:S(2)}) %collective-permute-start.43) | collective-permute-done | bytes 524320 | tf_op jit(solution)/shard_map/ppermute | solution.py:20
  309.9 7.1 collective-permute-done.44
  335.7 32.8 %collective-permute-done.15 = s32[512,8]{0,1:T(8,128)S(1)} collective-permute-done((s32[512,8]{0,1:T(8,128)S(1)}, s32[512,8]{0,1:T(8,128)S(1)}, u32[]{:S(2)}, u32[]{:S(2)}) %collective-permute-start.15) | collective-permute-done | bytes 16416 | tf_op jit(solution)/shard_map/ppermute | solution.py:20
  382.5 39.2 %collective-permute-start.61 = (bf16[2,512,512]{2,1,0:T(8,128)(2,1)}, bf16[2,512,512]{2,1,0:T(8,128)(2,1)}, u32[]{:S(2)}, u32[]{:S(2)}) collective-permute-start(bf16[2,512,512]{2,1,0:T(8,128)(2,1)} %slice.666), channel_id=1, source_target_pairs={{0,4},{4,8},{8,12},{12,0},{1,5},{5,9},{9,13},{13,1},{2,6},{6,10},{... | collective-permute-start | bytes 3145736 | tf_op jit(solution)/shard_map/ppermute | solution.py:20
  433.9 13.8 collective-permute-done.61
  447.7 19.0 %collective-permute-done.62 = bf16[2,512,512]{2,1,0:T(8,128)(2,1)} collective-permute-done((bf16[2,512,512]{2,1,0:T(8,128)(2,1)}, bf16[2,512,512]{2,1,0:T(8,128)(2,1)}, u32[]{:S(2)}, u32[]{:S(2)}) %collective-permute-start.62) | collective-permute-done | bytes 1048608 | tf_op jit(solution)/shard_map/ppermute | solution.py:20
  480.0 7.0 convolution_convert_fusion.9
  487.7 7.2 fusion.8
  503.8 5.8 fusion.58
  509.7 7.0 fusion.78
  516.6 6.4 fusion.295
  523.1 6.8 fusion.9
  529.8 6.2 fusion.296
  536.0 12.0 fusion.281
  548.0 7.5 convolution_convert_fusion.3
  561.9 11.4 fusion.276
  579.2 9.7 convolution_convert_fusion.5
  588.9 6.2 fusion.80
  615.6 32.9 %collective-permute-done.64 = bf16[512,2048]{1,0:T(8,128)(2,1)S(1)} collective-permute-done((bf16[512,2048]{1,0:T(8,128)(2,1)S(1)}, bf16[512,2048]{1,0:T(8,128)(2,1)S(1)}, u32[]{:S(2)}, u32[]{:S(2)}) %collective-permute-start.64) | collective-permute-done | bytes 2097184 | tf_op jit(solution)/shard_map/ppermute | solution.py:20
  656.1 6.4 collective-permute-done.66
  668.5 24.2 %collective-permute-done.25 = bf16[512,2048]{1,0:T(8,128)(2,1)S(1)} collective-permute-done((bf16[512,2048]{1,0:T(8,128)(2,1)S(1)}, bf16[512,2048]{1,0:T(8,128)(2,1)S(1)}, u32[]{:S(2)}, u32[]{:S(2)}) %collective-permute-start.25) | collective-permute-done | bytes 2097184 | tf_op jit(solution)/shard_map/ppermute | solution.py:20
  712.0 20.8 %collective-permute-done.76 = bf16[512,512]{1,0:T(8,128)(2,1)} collective-permute-done((bf16[512,512]{1,0:T(8,128)(2,1)}, bf16[512,512]{1,0:T(8,128)(2,1)}, u32[]{:S(2)}, u32[]{:S(2)}) %collective-permute-start.76) | collective-permute-done | bytes 524320 | tf_op jit(solution)/shard_map/ppermute | solution.py:20
  776.1 76.0 %collective-permute-done.89 = bf16[4,512,512]{2,1,0:T(8,128)(2,1)S(1)} collective-permute-done((bf16[4,512,512]{2,1,0:T(8,128)(2,1)}, bf16[4,512,512]{2,1,0:T(8,128)(2,1)S(1)}, u32[]{:S(2)}, u32[]{:S(2)}) %collective-permute-start.89) | collective-permute-done | bytes 2097184 | tf_op jit(solution)/shard_map/ppermute | solution.py:20
  860.8 19.3 %collective-permute-done.90 = bf16[2,512,512]{2,1,0:T(8,128)(2,1)S(1)} collective-permute-done((bf16[2,512,512]{2,1,0:T(8,128)(2,1)S(1)}, bf16[2,512,512]{2,1,0:T(8,128)(2,1)S(1)}, u32[]{:S(2)}, u32[]{:S(2)}) %collective-permute-start.90) | collective-permute-done | bytes 1048608 | tf_op jit(solution)/shard_map/ppermute | solution.py:20
  880.1 19.0 %collective-permute-done.91 = bf16[2,512,512]{2,1,0:T(8,128)(2,1)S(1)} collective-permute-done((bf16[2,512,512]{2,1,0:T(8,128)(2,1)S(1)}, bf16[2,512,512]{2,1,0:T(8,128)(2,1)S(1)}, u32[]{:S(2)}, u32[]{:S(2)}) %collective-permute-start.91) | collective-permute-done | bytes 1048608 | tf_op jit(solution)/shard_map/ppermute | solution.py:20
  916.7 7.0 fusion.76
  923.8 15.3 fusion.282
  939.0 7.3 convolution_convert_fusion.2
  951.0 9.4 fusion.7
  962.3 7.4 convolution_convert_fusion.4
  973.4 10.7 add_convert_fusion.3
  985.3 11.4 add_convert_fusion.4
  1007.5 9.0 add_convert_fusion.2
  1017.6 34.3 %collective-permute-done.93 = bf16[512,2048]{1,0:T(8,128)(2,1)} collective-permute-done((bf16[512,2048]{1,0:T(8,128)(2,1)}, bf16[512,2048]{1,0:T(8,128)(2,1)}, u32[]{:S(2)}, u32[]{:S(2)}) %collective-permute-start.93) | collective-permute-done | bytes 2097184 | tf_op jit(solution)/shard_map/ppermute | solution.py:20
  1071.6 24.0 %collective-permute-done.50 = bf16[512,2048]{1,0:T(8,128)(2,1)} collective-permute-done((bf16[512,2048]{1,0:T(8,128)(2,1)S(1)}, bf16[512,2048]{1,0:T(8,128)(2,1)}, u32[]{:S(2)}, u32[]{:S(2)}) %collective-permute-start.50) | collective-permute-done | bytes 2097184 | tf_op jit(solution)/shard_map/ppermute | solution.py:20
  1116.9 20.3 %collective-permute-done.105 = bf16[512,512]{1,0:T(8,128)(2,1)} collective-permute-done((bf16[512,512]{1,0:T(8,128)(2,1)}, bf16[512,512]{1,0:T(8,128)(2,1)}, u32[]{:S(2)}, u32[]{:S(2)}) %collective-permute-start.105) | collective-permute-done | bytes 524320 | tf_op jit(solution)/shard_map/ppermute | solution.py:20
  1198.8 7.5 fusion.161
  1206.3 7.6 fusion.30
  1221.7 6.2 fusion.35
  1230.5 5.8 add_convert_fusion.1
  1236.4 6.1 add_convert_fusion
  1253.0 6.8 collective-permute-done.83
  1265.8 18.2 %collective-permute-done.84 = f32[512]{0:T(512)S(1)} collective-permute-done((f32[512]{0:T(512)S(1)}, f32[512]{0:T(512)S(1)}, u32[]{:S(2)}, u32[]{:S(2)}) %collective-permute-start.84) | collective-permute-done | bytes 2080 | tf_op jit(solution)/shard_map/ppermute | solution.py:25
  1290.3 10.4 collective-permute-done.53
  1302.3 18.0 %collective-permute-done.113 = f32[512]{0:T(512)S(1)} collective-permute-done((f32[512]{0:T(512)S(1)}, f32[512]{0:T(512)S(1)}, u32[]{:S(2)}, u32[]{:S(2)}) %collective-permute-start.113) | collective-permute-done | bytes 2080 | tf_op jit(solution)/shard_map/ppermute | solution.py:25
  1328.8 17.5 %collective-permute-done.55 = bf16[512,512]{1,0:T(8,128)(2,1)S(1)} collective-permute-done((bf16[512,512]{1,0:T(8,128)(2,1)}, bf16[512,512]{1,0:T(8,128)(2,1)S(1)}, u32[]{:S(2)}, u32[]{:S(2)}) %collective-permute-start.55) | collective-permute-done | bytes 524320 | tf_op jit(solution)/shard_map/ppermute | solution.py:20
  1347.9 8.8 collective-permute-done.111
  1363.4 108.3 %collective-permute-done.114 = f32[37120]{0:T(1024)S(1)} collective-permute-done((f32[37120]{0:T(1024)S(1)}, f32[37120]{0:T(1024)S(1)}, u32[]{:S(2)}, u32[]{:S(2)}) %collective-permute-start.114) | collective-permute-done | bytes 148512 | tf_op jit(solution)/shard_map/ppermute | solution.py:25
  1485.4 18.9 %collective-permute-done.116 = f32[37120]{0:T(1024)S(1)} collective-permute-done((f32[37120]{0:T(1024)S(1)}, f32[37120]{0:T(1024)S(1)}, u32[]{:S(2)}, u32[]{:S(2)}) %collective-permute-start.116) | collective-permute-done | bytes 148512 | tf_op jit(solution)/shard_map/ppermute | solution.py:25
  1521.3 5.8 collective-permute-done.128
  1530.2 9.9 collective-permute-done.122
  1551.6 5.7 collective-permute-done.124
  (1010 shorter events, 610.8 us)
Async XLA Ops:
  6.2 61.4 %collective-permute-start.4 = (bf16[512,1280]{1,0:T(8,128)(2,1)}, bf16[512,1280]{1,0:T(8,128)(2,1)}, u32[]{:S(2)}, u32[]{:S(2)}) collective-permute-start(bf16[512,1280]{1,0:T(8,128)(2,1)} %get-tuple-element.228), channel_id=1, source_target_pairs={{0,1},{1,0},{2,3},{3,2},{4,5},{5,4},{6,7},{7,6},{8,9},{9,8},{10,11... | collective-permute-start | bytes 3932168 | tf_op jit(solution)/shard_map/ppermute | solution.py:25
  6.6 55.6 %collective-permute-start.5 = (bf16[512,1280]{1,0:T(8,128)(2,1)}, bf16[512,1280]{1,0:T(8,128)(2,1)}, u32[]{:S(2)}, u32[]{:S(2)}) collective-permute-start(bf16[512,1280]{1,0:T(8,128)(2,1)} %get-tuple-element.228), channel_id=1, source_target_pairs={{0,2},{1,3},{2,0},{3,1},{4,6},{5,7},{6,4},{7,5},{8,10},{9,11},{10,... | collective-permute-start | bytes 3932168 | tf_op jit(solution)/shard_map/ppermute | solution.py:20
  12.7 30.9 %collective-permute-start = (bf16[512,512]{1,0:T(8,128)(2,1)}, bf16[512,512]{1,0:T(8,128)(2,1)}, u32[]{:S(2)}, u32[]{:S(2)}) collective-permute-start(bf16[512,512]{1,0:T(8,128)(2,1)} %get-tuple-element.239), channel_id=1, source_target_pairs={{0,12},{4,0},{8,4},{12,8},{1,13},{5,1},{9,5},{13,9},{2,14},{6,2},{... | collective-permute-start | bytes 1572872 | tf_op jit(solution)/shard_map/ppermute | solution.py:20
  16.3 47.9 %collective-permute-start.8 = (bf16[1024,512]{1,0:T(8,128)(2,1)}, bf16[1024,512]{1,0:T(8,128)(2,1)}, u32[]{:S(2)}, u32[]{:S(2)}) collective-permute-start(bf16[1024,512]{1,0:T(8,128)(2,1)} %param.25), channel_id=1, source_target_pairs={{0,2},{1,3},{2,0},{3,1},{4,6},{5,7},{6,4},{7,5},{8,10},{9,11},{10,... | collective-permute-start | bytes 3145736 | tf_op jit(solution)/shard_map/ppermute | solution.py:20
  215.6 35.5 %collective-permute-start.17 = (bf16[512,512]{1,0:T(8,128)(2,1)S(1)}, bf16[512,512]{1,0:T(8,128)(2,1)S(1)}, u32[]{:S(2)}, u32[]{:S(2)}) collective-permute-start(bf16[512,512]{1,0:T(8,128)(2,1)S(1)} %copy-done.99), channel_id=1, source_target_pairs={{0,12},{4,0},{8,4},{12,8},{1,13},{5,1},{9,5},{13,9},{2,14},{6,2},{... | collective-permute-start | bytes 1572872 | tf_op jit(solution)/shard_map/ppermute | solution.py:20
  215.7 35.4 %collective-permute-start.18 = (bf16[512,512]{1,0:T(8,128)(2,1)S(1)}, bf16[512,512]{1,0:T(8,128)(2,1)S(1)}, u32[]{:S(2)}, u32[]{:S(2)}) collective-permute-start(bf16[512,512]{1,0:T(8,128)(2,1)S(1)} %copy-done.99), channel_id=1, source_target_pairs={{0,4},{4,8},{8,12},{12,0},{1,5},{5,9},{9,13},{13,1},{2,6},{6,10},{... | collective-permute-start | bytes 1572872 | tf_op jit(solution)/shard_map/ppermute | solution.py:20
  227.3 35.0 %collective-permute-start.36 = (bf16[512,512]{1,0:T(8,128)(2,1)S(1)}, bf16[512,512]{1,0:T(8,128)(2,1)S(1)}, u32[]{:S(2)}, u32[]{:S(2)}) collective-permute-start(bf16[512,512]{1,0:T(8,128)(2,1)S(1)} %pad_maximum_fusion.21), channel_id=1, source_target_pairs={{0,4},{4,8},{8,12},{12,0},{1,5},{5,9},{9,13},{13,1},{2,6},{6,10},{... | collective-permute-start | bytes 1572872 | tf_op jit(solution)/shard_map/ppermute | solution.py:20
  228.0 45.4 %collective-permute-start.38 = (bf16[512,512]{1,0:T(8,128)(2,1)S(1)}, bf16[512,512]{1,0:T(8,128)(2,1)S(1)}, u32[]{:S(2)}, u32[]{:S(2)}) collective-permute-start(bf16[512,512]{1,0:T(8,128)(2,1)S(1)} %pad_maximum_fusion.22), channel_id=1, source_target_pairs={{0,12},{4,0},{8,4},{12,8},{1,13},{5,1},{9,5},{13,9},{2,14},{6,2},{... | collective-permute-start | bytes 1572872 | tf_op jit(solution)/shard_map/ppermute | solution.py:20
  240.1 38.9 %collective-permute-start.57 = (bf16[512,512]{1,0:T(8,128)(2,1)S(1)}, bf16[512,512]{1,0:T(8,128)(2,1)S(1)}, u32[]{:S(2)}, u32[]{:S(2)}) collective-permute-start(bf16[512,512]{1,0:T(8,128)(2,1)S(1)} %get-tuple-element.237), channel_id=1, source_target_pairs={{0,2},{1,3},{2,0},{3,1},{4,6},{5,7},{6,4},{7,5},{8,10},{9,11},{10,... | collective-permute-start | bytes 1572872 | tf_op jit(solution)/shard_map/ppermute | solution.py:20
  251.2 32.1 %collective-permute-start.20 = (bf16[256,512]{1,0:T(8,128)(2,1)S(1)}, bf16[256,512]{1,0:T(8,128)(2,1)S(1)}, u32[]{:S(2)}, u32[]{:S(2)}) collective-permute-start(bf16[256,512]{1,0:T(8,128)(2,1)S(1)} %slice.645), channel_id=1, source_target_pairs={{0,12},{4,0},{8,4},{12,8},{1,13},{5,1},{9,5},{13,9},{2,14},{6,2},{... | collective-permute-start | bytes 786440 | tf_op jit(solution)/shard_map/ppermute | solution.py:20
  275.1 30.8 %collective-permute-start.42 = (bf16[512,512]{1,0:T(8,128)(2,1)S(1)}, bf16[512,512]{1,0:T(8,128)(2,1)S(1)}, u32[]{:S(2)}, u32[]{:S(2)}) collective-permute-start(bf16[512,512]{1,0:T(8,128)(2,1)S(1)} %get-tuple-element.122), channel_id=1, source_target_pairs={{0,12},{4,0},{8,4},{12,8},{1,13},{5,1},{9,5},{13,9},{2,14},{6,2},{... | collective-permute-start | bytes 1572872 | tf_op jit(solution)/shard_map/ppermute | solution.py:20
  275.4 30.4 %collective-permute-start.43 = (bf16[512,512]{1,0:T(8,128)(2,1)S(1)}, bf16[512,512]{1,0:T(8,128)(2,1)S(1)}, u32[]{:S(2)}, u32[]{:S(2)}) collective-permute-start(bf16[512,512]{1,0:T(8,128)(2,1)S(1)} %get-tuple-element.122), channel_id=1, source_target_pairs={{0,4},{4,8},{8,12},{12,0},{1,5},{5,9},{9,13},{13,1},{2,6},{6,10},{... | collective-permute-start | bytes 1572872 | tf_op jit(solution)/shard_map/ppermute | solution.py:20
  279.0 43.8 %collective-permute-start.56 = (bf16[512,512]{1,0:T(8,128)(2,1)S(1)}, bf16[512,512]{1,0:T(8,128)(2,1)S(1)}, u32[]{:S(2)}, u32[]{:S(2)}) collective-permute-start(bf16[512,512]{1,0:T(8,128)(2,1)S(1)} %get-tuple-element.237), channel_id=1, source_target_pairs={{0,1},{1,0},{2,3},{3,2},{4,5},{5,4},{6,7},{7,6},{8,9},{9,8},{10,11... | collective-permute-start | bytes 1572872 | tf_op jit(solution)/shard_map/ppermute | solution.py:25
  279.1 43.6 %collective-permute-start.58 = (bf16[512,512]{1,0:T(8,128)(2,1)S(1)}, bf16[512,512]{1,0:T(8,128)(2,1)S(1)}, u32[]{:S(2)}, u32[]{:S(2)}) collective-permute-start(bf16[512,512]{1,0:T(8,128)(2,1)S(1)} %collective-permute-done.57), channel_id=1, source_target_pairs={{0,1},{1,0},{2,3},{3,2},{4,5},{5,4},{6,7},{7,6},{8,9},{9,8},{10,11... | collective-permute-start | bytes 1572872 | tf_op jit(solution)/shard_map/ppermute | solution.py:25
  322.3 54.2 %collective-permute-start.22 = (bf16[512,2048]{1,0:T(8,128)(2,1)}, bf16[512,2048]{1,0:T(8,128)(2,1)}, u32[]{:S(2)}, u32[]{:S(2)}) collective-permute-start(bf16[512,2048]{1,0:T(8,128)(2,1)} %get-tuple-element.261), channel_id=1, source_target_pairs={{0,2},{1,3},{2,0},{3,1},{4,6},{5,7},{6,4},{7,5},{8,10},{9,11},{10,... | collective-permute-start | bytes 6291464 | tf_op jit(solution)/shard_map/ppermute | solution.py:20
  329.6 50.7 %collective-permute-start.60 = (bf16[4,512,512]{2,1,0:T(8,128)(2,1)}, bf16[4,512,512]{2,1,0:T(8,128)(2,1)}, u32[]{:S(2)}, u32[]{:S(2)}) collective-permute-start(bf16[4,512,512]{2,1,0:T(8,128)(2,1)} %get-tuple-element.194), channel_id=1, source_target_pairs={{0,4},{4,8},{8,12},{12,0},{1,5},{5,9},{9,13},{13,1},{2,6},{6,10},{... | collective-permute-start | bytes 6291464 | tf_op jit(solution)/shard_map/ppermute | solution.py:20
  329.6 93.6 %collective-permute-start.59 = (bf16[4,512,512]{2,1,0:T(8,128)(2,1)}, bf16[4,512,512]{2,1,0:T(8,128)(2,1)}, u32[]{:S(2)}, u32[]{:S(2)}) collective-permute-start(bf16[4,512,512]{2,1,0:T(8,128)(2,1)} %get-tuple-element.194), channel_id=1, source_target_pairs={{0,12},{4,0},{8,4},{12,8},{1,13},{5,1},{9,5},{13,9},{2,14},{6,2},{... | collective-permute-start | bytes 6291464 | tf_op jit(solution)/shard_map/ppermute | solution.py:20
  333.4 35.1 %collective-permute-start.15 = (s32[512,8]{0,1:T(8,128)S(1)}, s32[512,8]{0,1:T(8,128)S(1)}, u32[]{:S(2)}, u32[]{:S(2)}) collective-permute-start(s32[512,8]{0,1:T(8,128)S(1)} %get-tuple-element.260), channel_id=1, source_target_pairs={{0,2},{1,3},{2,0},{3,1},{4,6},{5,7},{6,4},{7,5},{8,10},{9,11},{10,... | collective-permute-start | bytes 49160 | tf_op jit(solution)/shard_map/ppermute | solution.py:20
  335.1 33.9 %collective-permute-start.14 = (s32[512,8]{0,1:T(8,128)S(1)}, s32[512,8]{0,1:T(8,128)S(1)}, u32[]{:S(2)}, u32[]{:S(2)}) collective-permute-start(s32[512,8]{0,1:T(8,128)S(1)} %get-tuple-element.260), channel_id=1, source_target_pairs={{0,1},{1,0},{2,3},{3,2},{4,5},{5,4},{6,7},{7,6},{8,9},{9,8},{10,11... | collective-permute-start | bytes 49160 | tf_op jit(solution)/shard_map/ppermute | solution.py:25
  376.0 98.1 %collective-permute-start.21 = (bf16[512,2048]{1,0:T(8,128)(2,1)}, bf16[512,2048]{1,0:T(8,128)(2,1)}, u32[]{:S(2)}, u32[]{:S(2)}) collective-permute-start(bf16[512,2048]{1,0:T(8,128)(2,1)} %get-tuple-element.261), channel_id=1, source_target_pairs={{0,1},{1,0},{2,3},{3,2},{4,5},{5,4},{6,7},{7,6},{8,9},{9,8},{10,11... | collective-permute-start | bytes 6291464 | tf_op jit(solution)/shard_map/ppermute | solution.py:25
  376.1 97.5 %collective-permute-start.47 = (bf16[512,2048]{1,0:T(8,128)(2,1)}, bf16[512,2048]{1,0:T(8,128)(2,1)}, u32[]{:S(2)}, u32[]{:S(2)}) collective-permute-start(bf16[512,2048]{1,0:T(8,128)(2,1)} %get-tuple-element.262), channel_id=1, source_target_pairs={{0,2},{1,3},{2,0},{3,1},{4,6},{5,7},{6,4},{7,5},{8,10},{9,11},{10,... | collective-permute-start | bytes 6291464 | tf_op jit(solution)/shard_map/ppermute | solution.py:20
  376.6 97.5 %collective-permute-start.23 = (bf16[512,2048]{1,0:T(8,128)(2,1)}, bf16[512,2048]{1,0:T(8,128)(2,1)}, u32[]{:S(2)}, u32[]{:S(2)}) collective-permute-start(bf16[512,2048]{1,0:T(8,128)(2,1)} %collective-permute-done.22), channel_id=1, source_target_pairs={{0,1},{1,0},{2,3},{3,2},{4,5},{5,4},{6,7},{7,6},{8,9},{9,8},{10,11... | collective-permute-start | bytes 6291464 | tf_op jit(solution)/shard_map/ppermute | solution.py:25
  382.5 65.2 %collective-permute-start.61 = (bf16[2,512,512]{2,1,0:T(8,128)(2,1)}, bf16[2,512,512]{2,1,0:T(8,128)(2,1)}, u32[]{:S(2)}, u32[]{:S(2)}) collective-permute-start(bf16[2,512,512]{2,1,0:T(8,128)(2,1)} %slice.666), channel_id=1, source_target_pairs={{0,4},{4,8},{8,12},{12,0},{1,5},{5,9},{9,13},{13,1},{2,6},{6,10},{... | collective-permute-start | bytes 3145736 | tf_op jit(solution)/shard_map/ppermute | solution.py:20
  425.4 41.3 %collective-permute-start.62 = (bf16[2,512,512]{2,1,0:T(8,128)(2,1)}, bf16[2,512,512]{2,1,0:T(8,128)(2,1)}, u32[]{:S(2)}, u32[]{:S(2)}) collective-permute-start(bf16[2,512,512]{2,1,0:T(8,128)(2,1)} %slice.667), channel_id=1, source_target_pairs={{0,12},{4,0},{8,4},{12,8},{1,13},{5,1},{9,5},{13,9},{2,14},{6,2},{... | collective-permute-start | bytes 3145736 | tf_op jit(solution)/shard_map/ppermute | solution.py:20
  473.5 99.7 %collective-permute-start.46 = (bf16[512,2048]{1,0:T(8,128)(2,1)}, bf16[512,2048]{1,0:T(8,128)(2,1)}, u32[]{:S(2)}, u32[]{:S(2)}) collective-permute-start(bf16[512,2048]{1,0:T(8,128)(2,1)} %get-tuple-element.262), channel_id=1, source_target_pairs={{0,1},{1,0},{2,3},{3,2},{4,5},{5,4},{6,7},{7,6},{8,9},{9,8},{10,11... | collective-permute-start | bytes 6291464 | tf_op jit(solution)/shard_map/ppermute | solution.py:25
  473.6 100.1 %collective-permute-start.48 = (bf16[512,2048]{1,0:T(8,128)(2,1)}, bf16[512,2048]{1,0:T(8,128)(2,1)}, u32[]{:S(2)}, u32[]{:S(2)}) collective-permute-start(bf16[512,2048]{1,0:T(8,128)(2,1)} %collective-permute-done.47), channel_id=1, source_target_pairs={{0,1},{1,0},{2,3},{3,2},{4,5},{5,4},{6,7},{7,6},{8,9},{9,8},{10,11... | collective-permute-start | bytes 6291464 | tf_op jit(solution)/shard_map/ppermute | solution.py:25
  560.0 37.5 %collective-permute-start.63 = (bf16[512,2048]{1,0:T(8,128)(2,1)}, bf16[512,2048]{1,0:T(8,128)(2,1)}, u32[]{:S(2)}, u32[]{:S(2)}) collective-permute-start(bf16[512,2048]{1,0:T(8,128)(2,1)} %get-tuple-element.128), channel_id=1, source_target_pairs={{0,1},{1,0},{2,3},{3,2},{4,5},{5,4},{6,7},{7,6},{8,9},{9,8},{10,11... | collective-permute-start | bytes 6291464 | tf_op jit(solution)/shard_map/ppermute | solution.py:25
  560.1 55.5 %collective-permute-start.65 = (bf16[512,2048]{1,0:T(8,128)(2,1)}, bf16[512,2048]{1,0:T(8,128)(2,1)}, u32[]{:S(2)}, u32[]{:S(2)}) collective-permute-start(bf16[512,2048]{1,0:T(8,128)(2,1)} %get-tuple-element.129), channel_id=1, source_target_pairs={{0,1},{1,0},{2,3},{3,2},{4,5},{5,4},{6,7},{7,6},{8,9},{9,8},{10,11... | collective-permute-start | bytes 6291464 | tf_op jit(solution)/shard_map/ppermute | solution.py:25
  561.8 34.1 %collective-permute-start.70 = (f32[17,512]{1,0:T(8,128)S(1)}, f32[17,512]{1,0:T(8,128)S(1)}, u32[]{:S(2)}, u32[]{:S(2)}) collective-permute-start(f32[17,512]{1,0:T(8,128)S(1)} %get-tuple-element.254), channel_id=1, source_target_pairs={{0,1},{1,0},{2,3},{3,2},{4,5},{5,4},{6,7},{7,6},{8,9},{9,8},{10,11... | collective-permute-start | bytes 104456 | tf_op jit(solution)/shard_map/ppermute | solution.py:25
  573.3 32.3 %collective-permute-start.72 = (f32[17,512]{1,0:T(8,128)S(1)}, f32[17,512]{1,0:T(8,128)S(1)}, u32[]{:S(2)}, u32[]{:S(2)}) collective-permute-start(f32[17,512]{1,0:T(8,128)S(1)} %get-tuple-element.253), channel_id=1, source_target_pairs={{0,1},{1,0},{2,3},{3,2},{4,5},{5,4},{6,7},{7,6},{8,9},{9,8},{10,11... | collective-permute-start | bytes 104456 | tf_op jit(solution)/shard_map/ppermute | solution.py:25
  600.0 48.5 %collective-permute-start.64 = (bf16[512,2048]{1,0:T(8,128)(2,1)S(1)}, bf16[512,2048]{1,0:T(8,128)(2,1)S(1)}, u32[]{:S(2)}, u32[]{:S(2)}) collective-permute-start(bf16[512,2048]{1,0:T(8,128)(2,1)S(1)} %fusion.45), channel_id=1, source_target_pairs={{0,2},{1,3},{2,0},{3,1},{4,6},{5,7},{6,4},{7,5},{8,10},{9,11},{10,... | collective-permute-start | bytes 6291464 | tf_op jit(solution)/shard_map/ppermute | solution.py:20
  605.6 62.9 %collective-permute-start.26 = (bf16[512,2048]{1,0:T(8,128)(2,1)S(1)}, bf16[512,2048]{1,0:T(8,128)(2,1)S(1)}, u32[]{:S(2)}, u32[]{:S(2)}) collective-permute-start(bf16[512,2048]{1,0:T(8,128)(2,1)S(1)} %get-tuple-element.133), channel_id=1, source_target_pairs={{0,1},{1,0},{2,3},{3,2},{4,5},{5,4},{6,7},{7,6},{8,9},{9,8},{10,11... | collective-permute-start | bytes 6291464 | tf_op jit(solution)/shard_map/ppermute | solution.py:25
  611.5 81.2 %collective-permute-start.25 = (bf16[512,2048]{1,0:T(8,128)(2,1)S(1)}, bf16[512,2048]{1,0:T(8,128)(2,1)S(1)}, u32[]{:S(2)}, u32[]{:S(2)}) collective-permute-start(bf16[512,2048]{1,0:T(8,128)(2,1)S(1)} %fusion.51), channel_id=1, source_target_pairs={{0,2},{1,3},{2,0},{3,1},{4,6},{5,7},{6,4},{7,5},{8,10},{9,11},{10,... | collective-permute-start | bytes 6291464 | tf_op jit(solution)/shard_map/ppermute | solution.py:20
  664.5 34.3 %collective-permute-start.67 = (bf16[512,512]{1,0:T(8,128)(2,1)S(1)}, bf16[512,512]{1,0:T(8,128)(2,1)S(1)}, u32[]{:S(2)}, u32[]{:S(2)}) collective-permute-start(bf16[512,512]{1,0:T(8,128)(2,1)S(1)} %pad_maximum_fusion.25), channel_id=1, source_target_pairs={{0,4},{4,8},{8,12},{12,0},{1,5},{5,9},{9,13},{13,1},{2,6},{6,10},{... | collective-permute-start | bytes 1572872 | tf_op jit(solution)/shard_map/ppermute | solution.py:20
  665.3 33.5 %collective-permute-start.69 = (bf16[512,512]{1,0:T(8,128)(2,1)S(1)}, bf16[512,512]{1,0:T(8,128)(2,1)S(1)}, u32[]{:S(2)}, u32[]{:S(2)}) collective-permute-start(bf16[512,512]{1,0:T(8,128)(2,1)S(1)} %pad_maximum_fusion.26), channel_id=1, source_target_pairs={{0,12},{4,0},{8,4},{12,8},{1,13},{5,1},{9,5},{13,9},{2,14},{6,2},{... | collective-permute-start | bytes 1572872 | tf_op jit(solution)/shard_map/ppermute | solution.py:20
  703.0 30.8 %collective-permute-start.75 = (bf16[512,512]{1,0:T(8,128)(2,1)}, bf16[512,512]{1,0:T(8,128)(2,1)}, u32[]{:S(2)}, u32[]{:S(2)}) collective-permute-start(bf16[512,512]{1,0:T(8,128)(2,1)} %get-tuple-element.111), channel_id=1, source_target_pairs={{0,12},{4,0},{8,4},{12,8},{1,13},{5,1},{9,5},{13,9},{2,14},{6,2},{... | collective-permute-start | bytes 1572872 | tf_op jit(solution)/shard_map/ppermute | solution.py:20
  703.0 29.8 %collective-permute-start.76 = (bf16[512,512]{1,0:T(8,128)(2,1)}, bf16[512,512]{1,0:T(8,128)(2,1)}, u32[]{:S(2)}, u32[]{:S(2)}) collective-permute-start(bf16[512,512]{1,0:T(8,128)(2,1)} %get-tuple-element.111), channel_id=1, source_target_pairs={{0,4},{4,8},{8,12},{12,0},{1,5},{5,9},{9,13},{13,1},{2,6},{6,10},{... | collective-permute-start | bytes 1572872 | tf_op jit(solution)/shard_map/ppermute | solution.py:20
  705.2 35.2 %collective-permute-start.86 = (bf16[512,512]{1,0:T(8,128)(2,1)}, bf16[512,512]{1,0:T(8,128)(2,1)}, u32[]{:S(2)}, u32[]{:S(2)}) collective-permute-start(bf16[512,512]{1,0:T(8,128)(2,1)} %get-tuple-element.235), channel_id=1, source_target_pairs={{0,2},{1,3},{2,0},{3,1},{4,6},{5,7},{6,4},{7,5},{8,10},{9,11},{10,... | collective-permute-start | bytes 1572872 | tf_op jit(solution)/shard_map/ppermute | solution.py:20
  759.6 92.7 %collective-permute-start.88 = (bf16[4,512,512]{2,1,0:T(8,128)(2,1)}, bf16[4,512,512]{2,1,0:T(8,128)(2,1)S(1)}, u32[]{:S(2)}, u32[]{:S(2)}) collective-permute-start(bf16[4,512,512]{2,1,0:T(8,128)(2,1)} %get-tuple-element.202), channel_id=1, source_target_pairs={{0,12},{4,0},{8,4},{12,8},{1,13},{5,1},{9,5},{13,9},{2,14},{6,2},{... | collective-permute-start | bytes 6291464 | tf_op jit(solution)/shard_map/ppermute | solution.py:20
  760.6 91.5 %collective-permute-start.89 = (bf16[4,512,512]{2,1,0:T(8,128)(2,1)}, bf16[4,512,512]{2,1,0:T(8,128)(2,1)S(1)}, u32[]{:S(2)}, u32[]{:S(2)}) collective-permute-start(bf16[4,512,512]{2,1,0:T(8,128)(2,1)} %get-tuple-element.202), channel_id=1, source_target_pairs={{0,4},{4,8},{8,12},{12,0},{1,5},{5,9},{9,13},{13,1},{2,6},{6,10},{... | collective-permute-start | bytes 6291464 | tf_op jit(solution)/shard_map/ppermute | solution.py:20
  852.3 46.8 %collective-permute-start.91 = (bf16[2,512,512]{2,1,0:T(8,128)(2,1)S(1)}, bf16[2,512,512]{2,1,0:T(8,128)(2,1)S(1)}, u32[]{:S(2)}, u32[]{:S(2)}) collective-permute-start(bf16[2,512,512]{2,1,0:T(8,128)(2,1)S(1)} %slice.689), channel_id=1, source_target_pairs={{0,12},{4,0},{8,4},{12,8},{1,13},{5,1},{9,5},{13,9},{2,14},{6,2},{... | collective-permute-start | bytes 3145736 | tf_op jit(solution)/shard_map/ppermute | solution.py:20
  951.0 48.2 %collective-permute-start.92 = (bf16[512,2048]{1,0:T(8,128)(2,1)}, bf16[512,2048]{1,0:T(8,128)(2,1)}, u32[]{:S(2)}, u32[]{:S(2)}) collective-permute-start(bf16[512,2048]{1,0:T(8,128)(2,1)} %get-tuple-element.130), channel_id=1, source_target_pairs={{0,1},{1,0},{2,3},{3,2},{4,5},{5,4},{6,7},{7,6},{8,9},{9,8},{10,11... | collective-permute-start | bytes 6291464 | tf_op jit(solution)/shard_map/ppermute | solution.py:25
  972.5 31.5 %collective-permute-start.49 = (bf16[512,2048]{1,0:T(8,128)(2,1)}, bf16[512,2048]{1,0:T(8,128)(2,1)}, u32[]{:S(2)}, u32[]{:S(2)}) collective-permute-start(bf16[512,2048]{1,0:T(8,128)(2,1)} %get-tuple-element.134), channel_id=1, source_target_pairs={{0,1},{1,0},{2,3},{3,2},{4,5},{5,4},{6,7},{7,6},{8,9},{9,8},{10,11... | collective-permute-start | bytes 6291464 | tf_op jit(solution)/shard_map/ppermute | solution.py:25
  996.7 74.9 %collective-permute-start.51 = (bf16[512,2048]{1,0:T(8,128)(2,1)}, bf16[512,2048]{1,0:T(8,128)(2,1)}, u32[]{:S(2)}, u32[]{:S(2)}) collective-permute-start(bf16[512,2048]{1,0:T(8,128)(2,1)} %get-tuple-element.135), channel_id=1, source_target_pairs={{0,1},{1,0},{2,3},{3,2},{4,5},{5,4},{6,7},{7,6},{8,9},{9,8},{10,11... | collective-permute-start | bytes 6291464 | tf_op jit(solution)/shard_map/ppermute | solution.py:25
  1003.1 48.9 %collective-permute-start.93 = (bf16[512,2048]{1,0:T(8,128)(2,1)}, bf16[512,2048]{1,0:T(8,128)(2,1)}, u32[]{:S(2)}, u32[]{:S(2)}) collective-permute-start(bf16[512,2048]{1,0:T(8,128)(2,1)} %fusion.42), channel_id=1, source_target_pairs={{0,2},{1,3},{2,0},{3,1},{4,6},{5,7},{6,4},{7,5},{8,10},{9,11},{10,... | collective-permute-start | bytes 6291464 | tf_op jit(solution)/shard_map/ppermute | solution.py:20
  1006.3 89.2 %collective-permute-start.50 = (bf16[512,2048]{1,0:T(8,128)(2,1)S(1)}, bf16[512,2048]{1,0:T(8,128)(2,1)}, u32[]{:S(2)}, u32[]{:S(2)}) collective-permute-start(bf16[512,2048]{1,0:T(8,128)(2,1)S(1)} %fusion.48), channel_id=1, source_target_pairs={{0,2},{1,3},{2,0},{3,1},{4,6},{5,7},{6,4},{7,5},{8,10},{9,11},{10,... | collective-permute-start | bytes 6291464 | tf_op jit(solution)/shard_map/ppermute | solution.py:20
  1016.6 247.6 %collective-permute-start.28 = (bf16[512,512]{1,0:T(8,128)(2,1)}, bf16[512,512]{1,0:T(8,128)(2,1)}, u32[]{:S(2)}, u32[]{:S(2)}) collective-permute-start(bf16[512,512]{1,0:T(8,128)(2,1)} %pad_maximum_fusion.19), channel_id=1, source_target_pairs={{0,4},{4,8},{8,12},{12,0},{1,5},{5,9},{9,13},{13,1},{2,6},{6,10},{... | collective-permute-start | bytes 1572872 | tf_op jit(solution)/shard_map/ppermute | solution.py:20
  1067.6 36.1 %collective-permute-start.96 = (bf16[512,512]{1,0:T(8,128)(2,1)S(1)}, bf16[512,512]{1,0:T(8,128)(2,1)S(1)}, u32[]{:S(2)}, u32[]{:S(2)}) collective-permute-start(bf16[512,512]{1,0:T(8,128)(2,1)S(1)} %pad_maximum_fusion.29), channel_id=1, source_target_pairs={{0,4},{4,8},{8,12},{12,0},{1,5},{5,9},{9,13},{13,1},{2,6},{6,10},{... | collective-permute-start | bytes 1572872 | tf_op jit(solution)/shard_map/ppermute | solution.py:20
  1068.9 34.8 %collective-permute-start.98 = (bf16[512,512]{1,0:T(8,128)(2,1)S(1)}, bf16[512,512]{1,0:T(8,128)(2,1)S(1)}, u32[]{:S(2)}, u32[]{:S(2)}) collective-permute-start(bf16[512,512]{1,0:T(8,128)(2,1)S(1)} %pad_maximum_fusion.30), channel_id=1, source_target_pairs={{0,12},{4,0},{8,4},{12,8},{1,13},{5,1},{9,5},{13,9},{2,14},{6,2},{... | collective-permute-start | bytes 1572872 | tf_op jit(solution)/shard_map/ppermute | solution.py:20
  1107.9 30.4 %collective-permute-start.104 = (bf16[512,512]{1,0:T(8,128)(2,1)}, bf16[512,512]{1,0:T(8,128)(2,1)}, u32[]{:S(2)}, u32[]{:S(2)}) collective-permute-start(bf16[512,512]{1,0:T(8,128)(2,1)} %get-tuple-element.115), channel_id=1, source_target_pairs={{0,12},{4,0},{8,4},{12,8},{1,13},{5,1},{9,5},{13,9},{2,14},{6,2},{... | collective-permute-start | bytes 1572872 | tf_op jit(solution)/shard_map/ppermute | solution.py:20
  1264.2 99.1 %collective-permute-start.133 = (bf16[768,2048]{1,0:T(8,128)(2,1)S(1)}, bf16[768,2048]{1,0:T(8,128)(2,1)S(1)}, u32[]{:S(2)}, u32[]{:S(2)}) collective-permute-start(bf16[768,2048]{1,0:T(8,128)(2,1)S(1)} %copy-done.15), channel_id=1, source_target_pairs={{0,16},{16,0},{1,17},{17,1},{2,18},{18,2},{3,19},{19,3},{4,20},{20... | collective-permute-start | bytes 9437192 | tf_op jit(solution)/shard_map/ppermute | solution.py:25
  1284.0 38.5 %collective-permute-start.80 = (bf16[512,512]{1,0:T(8,128)(2,1)S(1)}, bf16[512,512]{1,0:T(8,128)(2,1)S(1)}, u32[]{:S(2)}, u32[]{:S(2)}) collective-permute-start(bf16[512,512]{1,0:T(8,128)(2,1)S(1)} %pad_maximum_fusion.27), channel_id=1, source_target_pairs={{0,4},{4,8},{8,12},{12,0},{1,5},{5,9},{9,13},{13,1},{2,6},{6,10},{... | collective-permute-start | bytes 1572872 | tf_op jit(solution)/shard_map/ppermute | solution.py:20
  1286.8 35.8 %collective-permute-start.82 = (bf16[512,512]{1,0:T(8,128)(2,1)S(1)}, bf16[512,512]{1,0:T(8,128)(2,1)S(1)}, u32[]{:S(2)}, u32[]{:S(2)}) collective-permute-start(bf16[512,512]{1,0:T(8,128)(2,1)S(1)} %pad_maximum_fusion.28), channel_id=1, source_target_pairs={{0,12},{4,0},{8,4},{12,8},{1,13},{5,1},{9,5},{13,9},{2,14},{6,2},{... | collective-permute-start | bytes 1572872 | tf_op jit(solution)/shard_map/ppermute | solution.py:20
  1289.0 31.3 %collective-permute-start.113 = (f32[512]{0:T(512)S(1)}, f32[512]{0:T(512)S(1)}, u32[]{:S(2)}, u32[]{:S(2)}) collective-permute-start(f32[512]{0:T(512)S(1)} %add.905), channel_id=1, source_target_pairs={{0,8},{4,12},{8,0},{12,4},{1,9},{5,13},{9,1},{13,5},{2,10},{6,14},... | collective-permute-start | bytes 6152 | tf_op jit(solution)/shard_map/ppermute | solution.py:25
  1300.8 175.8 %collective-permute-start.132 = (bf16[2048,768]{1,0:T(8,128)(2,1)S(1)}, bf16[2048,768]{1,0:T(8,128)(2,1)}, u32[]{:S(2)}, u32[]{:S(2)}) collective-permute-start(bf16[2048,768]{1,0:T(8,128)(2,1)S(1)} %copy-done.56), channel_id=1, source_target_pairs={{0,16},{16,0},{1,17},{17,1},{2,18},{18,2},{3,19},{19,3},{4,20},{20... | collective-permute-start | bytes 9437192 | tf_op jit(solution)/shard_map/ppermute | solution.py:25
  1322.5 34.1 %collective-permute-start.111 = (bf16[512,512]{1,0:T(8,128)(2,1)}, bf16[512,512]{1,0:T(8,128)(2,1)}, u32[]{:S(2)}, u32[]{:S(2)}) collective-permute-start(bf16[512,512]{1,0:T(8,128)(2,1)} %pad_maximum_fusion.32), channel_id=1, source_target_pairs={{0,12},{4,0},{8,4},{12,8},{1,13},{5,1},{9,5},{13,9},{2,14},{6,2},{... | collective-permute-start | bytes 1572872 | tf_op jit(solution)/shard_map/ppermute | solution.py:20
  1346.3 163.6 %collective-permute-start.131 = (bf16[2048,768]{1,0:T(8,128)(2,1)S(1)}, bf16[2048,768]{1,0:T(8,128)(2,1)S(1)}, u32[]{:S(2)}, u32[]{:S(2)}) collective-permute-start(bf16[2048,768]{1,0:T(8,128)(2,1)S(1)} %copy-done.55), channel_id=1, source_target_pairs={{0,16},{16,0},{1,17},{17,1},{2,18},{18,2},{3,19},{19,3},{4,20},{20... | collective-permute-start | bytes 9437192 | tf_op jit(solution)/shard_map/ppermute | solution.py:25
  1347.9 134.7 %collective-permute-start.127 = (bf16[1024,512]{1,0:T(8,128)(2,1)}, bf16[1024,512]{1,0:T(8,128)(2,1)}, u32[]{:S(2)}, u32[]{:S(2)}) collective-permute-start(bf16[1024,512]{1,0:T(8,128)(2,1)} %get-tuple-element.152), channel_id=1, source_target_pairs={{0,1},{1,0},{2,3},{3,2},{4,5},{5,4},{6,7},{7,6},{8,9},{9,8},{10,11... | collective-permute-start | bytes 3145736 | tf_op jit(solution)/shard_map/ppermute | solution.py:25
  1360.0 111.7 %collective-permute-start.114 = (f32[37120]{0:T(1024)S(1)}, f32[37120]{0:T(1024)S(1)}, u32[]{:S(2)}, u32[]{:S(2)}) collective-permute-start(f32[37120]{0:T(1024)S(1)} %constant_dynamic-update-slice_fusion.36), channel_id=1, source_target_pairs={{0,16},{16,0},{1,17},{17,1},{2,18},{18,2},{3,19},{19,3},{4,20},{20... | collective-permute-start | bytes 445448 | tf_op jit(solution)/shard_map/ppermute | solution.py:25
  1363.2 142.0 %collective-permute-start.121 = (bf16[512,1280]{0,1:T(8,128)(2,1)}, bf16[512,1280]{0,1:T(8,128)(2,1)}, u32[]{:S(2)}, u32[]{:S(2)}) collective-permute-start(bf16[512,1280]{0,1:T(8,128)(2,1)} %get-tuple-element.151), channel_id=1, source_target_pairs={{0,1},{1,0},{2,3},{3,2},{4,5},{5,4},{6,7},{7,6},{8,9},{9,8},{10,11... | collective-permute-start | bytes 3932168 | tf_op jit(solution)/shard_map/ppermute | solution.py:25
  1471.7 34.2 %collective-permute-start.120 = (bf16[512,1280]{0,1:T(8,128)(2,1)}, bf16[512,1280]{0,1:T(8,128)(2,1)}, u32[]{:S(2)}, u32[]{:S(2)}) collective-permute-start(bf16[512,1280]{0,1:T(8,128)(2,1)} %add_convert_fusion.6), channel_id=1, source_target_pairs={{0,2},{1,3},{2,0},{3,1},{4,6},{5,7},{6,4},{7,5},{8,10},{9,11},{10,... | collective-permute-start | bytes 3932168 | tf_op jit(solution)/shard_map/ppermute | solution.py:20
  1482.2 39.1 %collective-permute-start.129 = (bf16[1024,512]{1,0:T(8,128)(2,1)S(1)}, bf16[1024,512]{1,0:T(8,128)(2,1)S(1)}, u32[]{:S(2)}, u32[]{:S(2)}) collective-permute-start(bf16[1024,512]{1,0:T(8,128)(2,1)S(1)} %copy-done.80), channel_id=1, source_target_pairs={{0,1},{1,0},{2,3},{3,2},{4,5},{5,4},{6,7},{7,6},{8,9},{9,8},{10,11... | collective-permute-start | bytes 3145736 | tf_op jit(solution)/shard_map/ppermute | solution.py:25
  1508.3 31.8 %collective-permute-start.122 = (bf16[512,1280]{0,1:T(8,128)(2,1)S(1)}, bf16[512,1280]{0,1:T(8,128)(2,1)S(1)}, u32[]{:S(2)}, u32[]{:S(2)}) collective-permute-start(bf16[512,1280]{0,1:T(8,128)(2,1)S(1)} %add_convert_fusion.5), channel_id=1, source_target_pairs={{0,16},{16,0},{1,17},{17,1},{2,18},{18,2},{3,19},{19,3},{4,20},{20... | collective-permute-start | bytes 3932168 | tf_op jit(solution)/shard_map/ppermute | solution.py:25
  1528.6 35.1 %collective-permute-start.130 = (bf16[1024,512]{1,0:T(8,128)(2,1)}, bf16[1024,512]{1,0:T(8,128)(2,1)}, u32[]{:S(2)}, u32[]{:S(2)}) collective-permute-start(bf16[1024,512]{1,0:T(8,128)(2,1)} %add_convert_fusion.7), channel_id=1, source_target_pairs={{0,16},{16,0},{1,17},{17,1},{2,18},{18,2},{3,19},{19,3},{4,20},{20... | collective-permute-start | bytes 3145736 | tf_op jit(solution)/shard_map/ppermute | solution.py:25
  (287 other events, 4860.6 us)

commit v2 on v1

v2 whole, which is shorter than its diff:
```python
import functools

import jax
import jax.numpy as jnp
from jax import lax
from jax.experimental import pallas as pl
from jax.experimental.pallas import tpu as pltpu
from jax.sharding import PartitionSpec as P

SEQUENCE_TOKENS = 512
EPSILON = 1e-06
ROPE_BASE = 1000000.0
MASKED = -1e30
LANES = 128
BF16 = jnp.bfloat16
F32 = jnp.float32
NT = (((1,), (1,)), ((), ()))
TN = (((0,), (0,)), ((), ()))

def mm(left, right):
    return jnp.dot(left, right, preferred_element_type=F32)

def mm_nt(left, right):
    return lax.dot_general(left, right, NT, preferred_element_type=F32)

def mm_tn(left, right):
    return lax.dot_general(left, right, (((0,), (0,)), ((), ())), preferred_element_type=F32)

def turn(values, cos_wide, sin_wide):
    return values * cos_wide + pltpu.roll(values, values.shape[1] // 2, 1) * sin_wide

def unit(values):
    return lax.rsqrt(jnp.mean(values * values, axis=1, keepdims=True) + EPSILON)

def sequence_bias(segs_ref, segs_t_ref):
    rows = segs_ref.shape[1]
    before = lax.broadcasted_iota(jnp.int32, (rows, rows), 1) <= lax.broadcasted_iota(jnp.int32, (rows, rows), 0)
    same = segs_t_ref[...] == segs_ref[...]
    return jnp.where(jnp.logical_and(same, before), 0.0, MASKED)

def block_probs(query, key, bias, scale):
    scores = mm_nt(query, key) * scale + bias
    weights = jnp.exp(scores - jnp.max(scores, axis=1, keepdims=True))
    return weights * (1.0 / jnp.sum(weights, axis=1, keepdims=True))

def attention_forward_kernel(scale, q_ref, k_ref, v_ref, segs_ref, segs_t_ref, cos_ref, sin_ref, q_gain_ref, k_gain_ref, out_ref, bias, key, value):
    head = k_ref.shape[1]
    rows = q_ref.shape[0]
    half = rows // 2
    cos_wide, sin_wide = cos_ref[...], sin_ref[...]

    @pl.when(pl.program_id(0) == 0)
    def _():
        bias[...] = sequence_bias(segs_ref, segs_t_ref)
        k_pre = k_ref[...]
        key[...] = turn(k_pre * unit(k_pre) * k_gain_ref[...], cos_wide, sin_wide).astype(BF16)
        value[...] = v_ref[...].astype(BF16)

    for h in range(q_ref.shape[1] // head):
        lanes = slice(h * head, (h + 1) * head)
        q_pre = q_ref[:, lanes]
        query = turn(q_pre * unit(q_pre) * q_gain_ref[...], cos_wide, sin_wide).astype(BF16)
        for part in range(2):
            at, keys = slice(part * half, (part + 1) * half), slice(0, (part + 1) * half)
            probs = block_probs(query[at], key[keys, :], bias[at, keys], scale)
            out_ref[at, lanes] = mm(probs.astype(BF16), value[keys, :]).astype(BF16)

def attention_forward(projected, heads, segs, segs_t, cos_wide, sin_wide, q_gain, k_gain):
    rows = projected.shape[0]
    head = q_gain.shape[1]
    pair = 2 if heads % 2 == 0 else 1
    fixed = lambda *shape: pl.BlockSpec(shape, lambda i: (0,) * len(shape))
    return pl.pallas_call(
        functools.partial(attention_forward_kernel, head ** -0.5),
        grid=(heads // pair,),
        out_shape=jax.ShapeDtypeStruct((rows, heads * head), BF16),
        in_specs=[
            pl.BlockSpec((rows, pair * head), lambda i: (0, i)),
            pl.BlockSpec((rows, head), lambda i: (0, heads)),
            pl.BlockSpec((rows, head), lambda i: (0, heads + 1)),
            fixed(1, rows), fixed(rows, 1), fixed(rows, head), fixed(rows, head), fixed(1, head), fixed(1, head),
        ],
        out_specs=pl.BlockSpec((rows, pair * head), lambda i: (0, i)),
        scratch_shapes=[pltpu.VMEM((rows, rows), F32), pltpu.VMEM((rows, head), BF16), pltpu.VMEM((rows, head), BF16)],
        compiler_params=pltpu.CompilerParams(vmem_limit_bytes=48 << 20),
        cost_estimate=pl.CostEstimate(flops=10**10, bytes_accessed=10**7, transcendentals=0),
        name="attention_forward",
    )(projected, projected, projected, segs, segs_t, cos_wide, sin_wide, q_gain, k_gain)

def norm_back(values, gain, upstream):
    factor = unit(values)
    weighted = upstream * gain
    inner = jnp.mean(weighted * values, axis=1, keepdims=True)
    return weighted * factor - values * (factor * factor * factor * inner), upstream * values * factor

def attention_backward_kernel(scale, finish, q_ref, k_ref, v_ref, g_ref, segs_ref, segs_t_ref, cos_ref, sin_ref, q_gain_ref, k_gain_ref,
                              out_ref, key_ref, value_ref, inner_ref, gains_ref, bias, key, value, inner):
    head = k_ref.shape[1]
    rows = q_ref.shape[0]
    half = rows // 2
    cos_wide, sin_wide = cos_ref[...], sin_ref[...]
    step, steps = pl.program_id(0), pl.num_programs(0)
    pair = q_ref.shape[1] // head

    @pl.when(step == 0)
    def _():
        bias[...] = sequence_bias(segs_ref, segs_t_ref)
        k_pre = k_ref[...]
        key[...] = turn(k_pre * unit(k_pre) * k_gain_ref[...], cos_wide, sin_wide).astype(BF16)
        value[...] = v_ref[...].astype(BF16)
        key_ref[...] = jnp.zeros_like(key_ref)
        value_ref[...] = jnp.zeros_like(value_ref)
        inner[...] = jnp.zeros_like(inner)
        gains_ref[...] = jnp.zeros_like(gains_ref)

    for h in range(pair):
        lanes = slice(h * head, (h + 1) * head)
        q_pre = q_ref[:, lanes]
        query = turn(q_pre * unit(q_pre) * q_gain_ref[...], cos_wide, sin_wide).astype(BF16)
        grads = []
        for part in range(2):
            at, keys = slice(part * half, (part + 1) * half), slice(0, (part + 1) * half)
            probs = block_probs(query[at], key[keys, :], bias[at, keys], scale)
            upstream = g_ref[at, lanes]
            prob_grad = mm_nt(upstream, value[keys, :])
            score_grad = (probs * (prob_grad - jnp.sum(probs * prob_grad, axis=1, keepdims=True))).astype(BF16)
            grads.append(mm(score_grad, key[keys, :]) * scale)
            key_ref[keys, :] += mm_tn(score_grad, query[at]) * scale
            value_ref[keys, :] += mm_tn(probs.astype(BF16), upstream)
        query_grad = turn(jnp.concatenate(grads, axis=0), cos_wide, -sin_wide)
        q_grad, terms = norm_back(q_pre, q_gain_ref[...], query_grad)
        low = q_grad.astype(BF16)
        out_ref[:, pl.ds(pl.multiple_of((step * pair + h) * head, head), head)] = low
        inner[...] += low.astype(F32) * q_pre
        gains_ref[0:1, :] += jnp.sum(terms, axis=0, keepdims=True)

    @pl.when(step == steps - 1)
    def _():
        total = jnp.sum(inner[...], axis=1, keepdims=True)
        if finish:
            k_pre, v_pre = k_ref[...], v_ref[...]
            k_grad, terms = norm_back(k_pre, k_gain_ref[...], turn(key_ref[...], cos_wide, -sin_wide))
            k_low, v_low = k_grad.astype(BF16), value_ref[...].astype(BF16)
            width = steps * pair * head
            out_ref[:, pl.ds(out_ref.shape[1] - 2 * head, head)] = k_low
            out_ref[:, pl.ds(out_ref.shape[1] - head, head)] = v_low
            gains_ref[1:2, :] = jnp.sum(terms, axis=0, keepdims=True)
            total = total + jnp.sum(k_low.astype(F32) * k_pre + v_low.astype(F32) * v_pre, axis=1, keepdims=True)
        inner_ref[...] = total

def attention_backward(finish, projected, upstream, heads, segs, segs_t, cos_wide, sin_wide, q_gain, k_gain):
    rows = projected.shape[0]
    head = q_gain.shape[1]
    pair = 2 if heads % 2 == 0 else 1
    fixed = lambda *shape: pl.BlockSpec(shape, lambda i: (0,) * len(shape))
    return pl.pallas_call(
        functools.partial(attention_backward_kernel, head ** -0.5, finish),
        grid=(heads // pair,),
        out_shape=[
            jax.ShapeDtypeStruct((rows, (heads + 2) * head), BF16),
            jax.ShapeDtypeStruct((rows, head), F32),
            jax.ShapeDtypeStruct((rows, head), F32),
            jax.ShapeDtypeStruct((rows, 1), F32),
            jax.ShapeDtypeStruct((2, head), F32),
        ],
        in_specs=[
            pl.BlockSpec((rows, pair * head), lambda i: (0, i)),
            pl.BlockSpec((rows, head), lambda i: (0, heads)),
            pl.BlockSpec((rows, head), lambda i: (0, heads + 1)),
            pl.BlockSpec((rows, pair * head), lambda i: (0, i)),
            fixed(1, rows), fixed(rows, 1), fixed(rows, head), fixed(rows, head), fixed(1, head), fixed(1, head),
        ],
        out_specs=[fixed(rows, (heads + 2) * head), fixed(rows, head), fixed(rows, head), fixed(rows, 1), fixed(2, head)],
        scratch_shapes=[pltpu.VMEM((rows, rows), F32), pltpu.VMEM((rows, head), BF16), pltpu.VMEM((rows, head), BF16), pltpu.VMEM((rows, head), F32)],
        compiler_params=pltpu.CompilerParams(vmem_limit_bytes=48 << 20),
        cost_estimate=pl.CostEstimate(flops=2 * 10**10, bytes_accessed=10**7, transcendentals=0),
        name="attention_backward",
    )(projected, projected, projected, upstream, segs, segs_t, cos_wide, sin_wide, q_gain, k_gain)

def norm_kernel(count, *refs):
    pieces, gain_ref, out_ref, scale_ref = refs[:count], refs[count], refs[count + 1], refs[count + 2]
    width = pieces[0].shape[1]
    total = None
    for piece in pieces:
        wide = piece[...].astype(F32)
        part = jnp.sum(wide * wide, axis=1, keepdims=True)
        total = part if total is None else total + part
    scale = lax.rsqrt(total / (width * count) + EPSILON)
    scale_ref[...] = scale
    for i, piece in enumerate(pieces):
        at = slice(i * width, (i + 1) * width)
        out_ref[:, at] = (piece[...].astype(F32) * scale * gain_ref[:, at]).astype(BF16)

def assemble_norm(pieces, offsets, rows, gain):
    count = len(pieces)
    width = pieces[0].shape[1]
    block = min(128, rows)
    return pl.pallas_call(
        functools.partial(norm_kernel, count),
        grid=(rows // block,),
        out_shape=[jax.ShapeDtypeStruct((rows, width * count), BF16), jax.ShapeDtypeStruct((rows, 1), F32)],
        in_specs=[pl.BlockSpec((block, width), lambda i, o=o: (o // block + i, 0)) for o in offsets]
        + [pl.BlockSpec((1, width * count), lambda i: (0, 0))],
        out_specs=[pl.BlockSpec((block, width * count), lambda i: (i, 0)), pl.BlockSpec((block, 1), lambda i: (i, 0))],
        compiler_params=pltpu.CompilerParams(vmem_limit_bytes=32 << 20),
        cost_estimate=pl.CostEstimate(flops=2 * 10**9, bytes_accessed=8 * 10**6, transcendentals=0),
        name="assemble_norm",
    )(*pieces, gain)


def pair_kernel(first, place, scalars_ref, slots_ref, slots_t_ref, mask_ref, router_ref, *refs):
    refs = list(refs)
    token_in, grad_in = refs[0:2], refs[2:4]
    weights_in = refs[4:7]
    del refs[:7]
    if not first:
        del refs[:5]
    y_out, x_out = refs[0:2], refs[2:4]
    small_out, logits_out, gates_out = refs[4:7]
    kept_out = refs[7:12]
    (token, grad, gate_w, up_w, down_w, y_buf, x_buf, rows_in, rows_grad, rows_dy, rows_u, rows_da, rows_db, in_sem, w_sem, out_sem, kept_sem) = refs[12:]
    capacity = rows_in.shape[0] // 2
    tokens, width = token.shape[1:]
    hidden = gate_w.shape[1]
    load_tok = [pltpu.make_async_copy(token_in[g], token.at[g], in_sem.at[0, g]) for g in range(2)]
    load_grad = [pltpu.make_async_copy(grad_in[g], grad.at[g], in_sem.at[1, g]) for g in range(2)]
    parts = w_sem.shape[1]
    strip = width // parts
    load_w = []
    for d in range(parts):
        there = pl.multiple_of((scalars_ref[1] + d) % parts * strip, strip)
        here = slice(d * strip, (d + 1) * strip)
        for i, (src, dst) in enumerate(zip(weights_in, (gate_w, up_w, down_w))):
            if i < 2:
                src, dst = src.at[pl.ds(there, strip), :], dst.at[here, :]
            else:
                src, dst = src.at[:, pl.ds(there, strip)], dst.at[:, here]
            load_w.append(pltpu.make_async_copy(src, dst, w_sem.at[i, d]))
    load_tok[0].start()
    load_grad[0].start()
    for load in load_w:
        load.start()
    load_tok[1].start()
    load_grad[1].start()
    expert = scalars_ref[0]
    stores = []
    wide = min(512, width)
    step = 256 if hidden % 256 == 0 else hidden
    chosen_rows, spreads, gate_cols = [], [], []
    for g in range(2):
        load_tok[g].wait()
        logits = mm(token[g], router_ref[...])
        shifted = logits + mask_ref[g].astype(F32)
        weights = jnp.exp(shifted - jnp.max(shifted, axis=1, keepdims=True))
        gates = weights / jnp.sum(weights, axis=1, keepdims=True)
        if g == 0:
            logits_out[...] = logits
            gates_out[...] = gates
        gates_t = gates.T
        lane = lax.broadcasted_iota(jnp.int32, gates_t.shape, 0)
        gate_row = jnp.sum(jnp.where(lane == expert, gates_t, 0.0), axis=0, keepdims=True)
        chosen = lax.broadcasted_iota(jnp.int32, (capacity, tokens), 0) == slots_ref[g]
        slot_gates = jnp.sum(jnp.where(chosen, gate_row, 0.0), axis=1, keepdims=True)
        pick = jnp.where(chosen, 1.0, 0.0).astype(BF16)
        here = slice(g * capacity, (g + 1) * capacity)
        gate_cols.append(slot_gates)
        load_grad[g].wait()

        def gather(j, _):
            at = pl.ds(pl.multiple_of(j * wide, wide), wide)
            rows_in[here, at] = mm(pick, token[g, :, at]).astype(BF16)
            found = mm(pick, grad[g, :, at])
            rows_grad[here, at] = found.astype(BF16)
            rows_dy[here, at] = (slot_gates * found).astype(BF16)
            return 0

        lax.fori_loop(0, width // wide, gather, 0)
    for load in load_w:
        load.wait()
    slot_gates = jnp.concatenate(gate_cols, axis=0)

    def middle(j, _):
        at = pl.ds(pl.multiple_of(j * step, step), step)
        a = mm(rows_in[...], gate_w[:, at])
        b = mm(rows_in[...], up_w[:, at])
        du = mm_nt(rows_dy[...], down_w[at, :]).astype(BF16).astype(F32)
        sig = 1.0 / (1.0 + jnp.exp(-a))
        silu = a * sig
        rows_u[:, at] = (silu * b).astype(BF16)
        rows_da[:, at] = (du * b * sig * (1.0 + a * (1.0 - sig))).astype(BF16)
        rows_db[:, at] = (du * silu).astype(BF16)
        return 0

    lax.fori_loop(0, hidden // step, middle, 0)
    kept_here = pl.ds(place * 2 * capacity, 2 * capacity)
    for i, kept_rows in enumerate((rows_in, rows_dy, rows_u, rows_da, rows_db)):
        store = pltpu.make_async_copy(kept_rows, kept_out[i].at[kept_here, :], kept_sem.at[i])
        store.start()
        stores.append(store)
    spreads = [
        jnp.where(
            lax.broadcasted_iota(jnp.int32, (tokens, capacity), 1) == slots_t_ref[g], 1.0, 0.0
        ).astype(BF16)
        for g in range(2)
    ]

    def back(j, carry):
        dots, inner = carry
        at = pl.ds(pl.multiple_of(j * wide, wide), wide)
        y = mm(rows_u[...], down_w[:, at]).astype(BF16).astype(F32)
        dots = dots + jnp.sum(rows_grad[:, at].astype(F32) * y, axis=1, keepdims=True)
        low = (slot_gates * y).astype(BF16)
        dx = mm_nt(rows_da[...], gate_w[at, :]) + mm_nt(rows_db[...], up_w[at, :])
        inner = inner + jnp.sum(rows_in[:, at].astype(F32) * dx, axis=1, keepdims=True)
        dx_low = dx.astype(BF16)
        for g in range(2):
            here = slice(g * capacity, (g + 1) * capacity)
            y_buf[g, :, at] = mm(spreads[g], low[here]).astype(BF16)
            x_buf[g, :, at] = mm(spreads[g], dx_low[here]).astype(BF16)
        return dots, inner

    nothing = jnp.zeros((2 * capacity, 1), F32)
    dots, inner = lax.fori_loop(0, width // wide, back, (nothing, nothing))
    for g in range(2):
        here = slice(g * capacity, (g + 1) * capacity)
        chosen = lax.broadcasted_iota(jnp.int32, (capacity, tokens), 0) == slots_ref[g]
        small_out[g, 0:1, :] = jnp.sum(jnp.where(chosen, dots[here], 0.0), axis=0, keepdims=True)
        small_out[g, 1:2, :] = jnp.sum(jnp.where(chosen, inner[here], 0.0), axis=0, keepdims=True)
        for i, (buf, out) in enumerate(((x_buf, x_out), (y_buf, y_out))):
            store = pltpu.make_async_copy(buf.at[g], out[g], out_sem.at[i, g])
            store.start()
            stores.append(store)
    for store in stores:
        store.wait()


def expert_pair(
    place, places, capacity, scalars, slots, slots_t, mask, router, tokens, grads, weights, kept
):
    rows, width = tokens[0].shape
    hidden = weights[0].shape[1]
    parts = lax.axis_size("row")
    total = places * 2 * capacity
    anywhere = pl.BlockSpec(memory_space=pl.ANY)
    inside = pl.BlockSpec(memory_space=pltpu.VMEM)
    first = kept is None
    dense = jax.ShapeDtypeStruct((rows, width), BF16)
    kept_shapes = [jax.ShapeDtypeStruct((total, w), BF16) for w in (width, width, hidden, hidden, hidden)]
    flat = jax.ShapeDtypeStruct((rows, router.shape[1]), F32)
    out = pl.pallas_call(
        functools.partial(pair_kernel, first, place),
        out_shape=[dense] * 4 + [jax.ShapeDtypeStruct((2, 2, rows), F32), flat, flat] + kept_shapes,
        in_specs=[pl.BlockSpec(memory_space=pltpu.SMEM)] + [inside] * 4 + [anywhere] * (7 if first else 12),
        out_specs=[anywhere] * 4 + [inside] * 3 + [anywhere] * 5,
        input_output_aliases={} if first else {12 + i: 7 + i for i in range(5)},
        scratch_shapes=[
            pltpu.VMEM((2, rows, width), BF16),
            pltpu.VMEM((2, rows, width), BF16),
            pltpu.VMEM((width, hidden), BF16),
            pltpu.VMEM((width, hidden), BF16),
            pltpu.VMEM((hidden, width), BF16),
            pltpu.VMEM((2, rows, width), BF16),
            pltpu.VMEM((2, rows, width), BF16),
            pltpu.VMEM((2 * capacity, width), BF16),
            pltpu.VMEM((2 * capacity, width), BF16),
            pltpu.VMEM((2 * capacity, width), BF16),
            pltpu.VMEM((2 * capacity, hidden), BF16),
            pltpu.VMEM((2 * capacity, hidden), BF16),
            pltpu.VMEM((2 * capacity, hidden), BF16),
            pltpu.SemaphoreType.DMA((2, 2)),
            pltpu.SemaphoreType.DMA((3, parts)),
            pltpu.SemaphoreType.DMA((2, 2)),
            pltpu.SemaphoreType.DMA((5,)),
        ],
        compiler_params=pltpu.CompilerParams(vmem_limit_bytes=56 << 20),
        cost_estimate=pl.CostEstimate(flops=36 * 10**9, bytes_accessed=10**7, transcendentals=0),
        name="expert_pair",
    )(scalars, slots, slots_t, mask, router, *tokens, *grads, *weights, *([] if first else kept))
    return out


def route_kernel(expert_ref, routes_ref, mask_ref, slots_ref, slots_t_ref):
    rows, top_count = routes_ref.shape[1:]
    routes = routes_ref[0]
    lanes = lax.broadcasted_iota(jnp.int32, (rows, LANES), 1)
    chosen = routes[:, 0:1] == lanes
    for k in range(1, top_count):
        chosen = jnp.logical_or(chosen, routes[:, k : k + 1] == lanes)
    mask_ref[0] = jnp.where(chosen, 0.0, MASKED).astype(BF16)
    below = lax.broadcasted_iota(jnp.int32, (rows, rows), 1) <= lax.broadcasted_iota(
        jnp.int32, (rows, rows), 0
    )
    ones = jnp.where(chosen, 1.0, 0.0)
    ranks = mm(jnp.where(below, 1.0, 0.0).astype(BF16), ones.astype(BF16))
    slots = jnp.where(chosen, ranks - 1.0, -1.0)
    here = lanes == expert_ref[0]
    slots_t_ref[0] = jnp.max(jnp.where(here, slots, -1.0), axis=1, keepdims=True).astype(jnp.int32)
    lane_first = lax.broadcasted_iota(jnp.int32, (LANES, rows), 0)
    slots_ref[0] = jnp.max(
        jnp.where(lane_first == expert_ref[0], slots.T, -1.0), axis=0, keepdims=True
    ).astype(jnp.int32)


def route_tables(scalars, routes):
    blocks, rows, top_count = routes.shape
    return pl.pallas_call(
        route_kernel,
        grid=(blocks,),
        out_shape=[
            jax.ShapeDtypeStruct((blocks, rows, LANES), BF16),
            jax.ShapeDtypeStruct((blocks, 1, rows), jnp.int32),
            jax.ShapeDtypeStruct((blocks, rows, 1), jnp.int32),
        ],
        in_specs=[
            pl.BlockSpec(memory_space=pltpu.SMEM),
            pl.BlockSpec((1, rows, top_count), lambda i: (i, 0, 0)),
        ],
        out_specs=[
            pl.BlockSpec((1, rows, LANES), lambda i: (i, 0, 0)),
            pl.BlockSpec((1, 1, rows), lambda i: (i, 0, 0)),
            pl.BlockSpec((1, rows, 1), lambda i: (i, 0, 0)),
        ],
        compiler_params=pltpu.CompilerParams(vmem_limit_bytes=32 << 20),
        cost_estimate=pl.CostEstimate(flops=10**9, bytes_accessed=10**6, transcendentals=0),
        name="route_tables",
    )(scalars, routes)


def place_kernel(axis, starts_ref, *refs):
    out = refs[-1]
    for i, piece in enumerate(refs[:-1]):
        width = piece.shape[axis]
        at = pl.ds(pl.multiple_of(starts_ref[i] * width, width), width)
        if axis == 0:
            out[at, :] = piece[...]
        else:
            out[:, at] = piece[...]


def placed(pieces, starts, axis):
    shape = list(pieces[0].shape)
    shape[axis] *= len(pieces)
    inside = pl.BlockSpec(memory_space=pltpu.VMEM)
    return pl.pallas_call(
        functools.partial(place_kernel, axis),
        out_shape=jax.ShapeDtypeStruct(tuple(shape), pieces[0].dtype),
        in_specs=[pl.BlockSpec(memory_space=pltpu.SMEM)] + [inside] * len(pieces),
        out_specs=inside,
        compiler_params=pltpu.CompilerParams(vmem_limit_bytes=32 << 20),
        cost_estimate=pl.CostEstimate(flops=10**6, bytes_accessed=10**7, transcendentals=0),
        name="placed",
    )(starts, *pieces)


def add_kernel(place_ref, one_ref, two_ref, out_ref):
    out_ref[...] = one_ref[...].astype(F32) + two_ref[...].astype(F32)


def unrolled_sum(one, two, place, parts, axis):
    shape = one.shape
    block = tuple(s // parts if d == axis else s for d, s in enumerate(shape))
    if axis == 0:
        at_in, at_out = lambda i, p: (i, 0), lambda i, p: ((i + p[0]) % parts, 0)
    else:
        at_in, at_out = lambda i, p: (0, i), lambda i, p: (0, (i + p[0]) % parts)
    return pl.pallas_call(
        add_kernel,
        grid_spec=pltpu.PrefetchScalarGridSpec(
            num_scalar_prefetch=1,
            grid=(parts,),
            in_specs=[pl.BlockSpec(block, at_in)] * 2,
            out_specs=pl.BlockSpec(block, at_out),
        ),
        out_shape=jax.ShapeDtypeStruct(shape, F32),
        compiler_params=pltpu.CompilerParams(vmem_limit_bytes=40 << 20),
        cost_estimate=pl.CostEstimate(flops=10**6, bytes_accessed=10**6, transcendentals=0),
        name="unrolled_sum",
    )(place, one, two)


def moved(block, axis, by):
    count = lax.axis_size(axis)
    return lax.ppermute(block, axis, [(i, (i + by) % count) for i in range(count)])


def swapped(block, axis, bit):
    count = lax.axis_size(axis)
    return lax.ppermute(block, axis, [(i, i ^ (1 << bit)) for i in range(count)])


def butterfly(values, axis):
    for bit in range(lax.axis_size(axis).bit_length() - 1):
        values = values + swapped(values, axis, bit)
    return values


def ring_pieces(block):
    count = lax.axis_size("row")
    pieces = [[block]] + [None] * (count - 1)
    from_left = from_right = block
    half = block.shape[0] // 2
    for step in range(1, count // 2):
        from_left = moved(from_left, "row", 1)
        from_right = moved(from_right, "row", -1)
        pieces[count - step] = [from_left]
        pieces[step] = [from_right]
    if count > 1:
        pieces[count // 2] = [
            moved(from_left[:half], "row", 1),
            moved(from_right[half:], "row", -1),
        ]
    return pieces


def chunk_pieces(pieces, number, rows):
    blocks, offsets = [], []
    for piece in pieces:
        tall = piece[0].shape[0]
        if len(piece) == 1:
            blocks.append(piece[0])
            offsets.append(number * rows)
        elif tall >= rows:
            blocks.append(piece[number * rows // tall])
            offsets.append(number * rows % tall)
        else:
            blocks.append(jnp.concatenate(piece, axis=0))
            offsets.append(number * rows)
    return blocks, offsets


def joined(pieces, number, rows):
    blocks, offsets = chunk_pieces(pieces, number, rows)
    return jnp.concatenate([b[o : o + rows] for b, o in zip(blocks, offsets)], axis=1)


def ring_scatter(partial):
    count = lax.axis_size("row")
    width = partial.shape[1] // count
    half = partial.shape[0] // 2

    def piece(distance):
        return partial[:, distance * width : (distance + 1) * width]

    total = piece(0).astype(F32)
    if count == 1:
        return total
    middle = piece(count // 2)
    to_right = moved(middle[:half], "row", 1)
    to_left = moved(middle[half:], "row", -1)
    for step in range(count // 2 - 1, 0, -1):
        right, left = piece(step), piece(count - step)
        if step == count // 2 - 1:
            right = jnp.concatenate([right[:half] + to_right, right[half:]], axis=0)
            left = jnp.concatenate([left[:half], left[half:] + to_left], axis=0)
        else:
            right = right + to_right
            left = left + to_left
        to_right = moved(right, "row", 1)
        to_left = moved(left, "row", -1)
    if count == 2:
        return total + jnp.concatenate([to_right, to_left], axis=0).astype(F32)
    return total + to_right.astype(F32) + to_left.astype(F32)


def after(value, *others):
    return lax.optimization_barrier((value,) + others)[0]


class Link:
    def __init__(self):
        self.last = ()

    def moved(self, block, by):
        block = moved(after(block, *self.last), "col", by)
        self.last = (block,)
        return block


def col_gather(block, link):
    count = lax.axis_size("col")
    pieces = []
    for step in range(count // 2):
        same = block if step == 0 else link.moved(block, 2 * step)
        pieces += [same, swapped(same, "col", 0)]
    return pieces


def chip_total(same, other):
    return (same.astype(F32) + swapped(other, "col", 0).astype(F32)).astype(same.dtype)


def chips_total(totals, link):
    total = totals[0].astype(F32)
    for step in range(1, len(totals)):
        total = total + link.moved(totals[step], -2 * step).astype(F32)
    return total


def col_order():
    count = lax.axis_size("col")
    place = lax.axis_index("col")
    chip, core = place // 2, place % 2
    order = []
    for step in range(count // 2):
        back = (chip - step) % (count // 2) * 2
        order += [back + core, back + 1 - core]
    return order


def col_assemble(block, axis, shift, link):
    count = lax.axis_size("col")
    width = block.shape[axis]
    starts = [(place - shift // width) % count for place in col_order()]
    return placed(col_gather(block, link), jnp.stack(starts).astype(jnp.int32), axis)


def col_share(partial, axis, shift, link):
    count = lax.axis_size("col")
    width = partial.shape[axis] // count
    pieces = [
        lax.dynamic_slice_in_dim(
            partial, (place * width - shift) % (width * count), width, axis
        )
        for place in col_order()
    ]
    return chips_total(
        [chip_total(pieces[2 * s], pieces[2 * s + 1]) for s in range(count // 2)], link
    )


def pair_total(values):
    low = values.astype(BF16)
    total = low.astype(F32)
    for bit in range(lax.axis_size("dp").bit_length() - 1):
        total = total + swapped(low, "dp", bit).astype(F32)
        low = total.astype(BF16)
    return total


def rolled(values, shift, axis=0):
    size = values.shape[axis]
    twice = jnp.concatenate([values, values], axis=axis)
    return lax.dynamic_slice_in_dim(twice, shift % size, size, axis)


def positions(segment_ids):
    places = jnp.arange(segment_ids.shape[0], dtype=jnp.int32)
    earlier = jnp.concatenate([segment_ids[:1] - 1, segment_ids[:-1]])
    starts = jnp.logical_or(segment_ids != earlier, places % SEQUENCE_TOKENS == 0)
    opening = lax.cummax(jnp.where(starts, places, 0), axis=0)
    return places - opening


def rotary(places, head_size):
    halfway = head_size // 2
    frequency = ROPE_BASE ** (-2.0 * jnp.arange(halfway, dtype=F32) / head_size)
    angles = places.astype(F32)[:, None] * frequency[None, :]
    cos_part, sin_part = jnp.cos(angles), jnp.sin(angles)
    return (
        jnp.concatenate([cos_part, cos_part], axis=1),
        jnp.concatenate([-sin_part, sin_part], axis=1),
    )


def turn_plain(values, cos_wide, sin_wide):
    return values * cos_wide + jnp.roll(values, values.shape[1] // 2, 1) * sin_wide


def per_device(
    residual,
    segments,
    routes,
    norm_attention,
    query_weight,
    key_projection_matrix,
    value_projection_matrix,
    query_gain,
    key_gain,
    out_weight,
    norm_experts,
    router_weight,
    gate_weight,
    up_weight,
    down_weight,
    grad_output,
):
    row_count = lax.axis_size("row")
    col_count = lax.axis_size("col")
    row_place = lax.axis_index("row")
    col_place = lax.axis_index("col")
    model_width = norm_attention.shape[0]
    feature_width = model_width // row_count
    head_size = query_gain.shape[0]
    heads_here = query_weight.shape[1] // head_size
    query_width = heads_here * head_size
    kv_heads = key_projection_matrix.shape[1] // head_size
    query_group_width = heads_here * row_count // kv_heads
    members = query_group_width // heads_here
    kv_index = row_place * heads_here // query_group_width
    member_place = row_place % members
    share_width = head_size // members
    column_mask = (jnp.arange(head_size, dtype=jnp.int32) // share_width == member_place).astype(
        F32
    )
    experts = gate_weight.shape[0] * row_count * col_count
    expert = row_place * col_count + col_place
    chips = col_count // 2
    token_rows = residual.shape[0]
    rows = SEQUENCE_TOKENS
    chunks = token_rows // rows
    top_count = routes.shape[1]
    capacity = max(2, 5 * rows * top_count // (4 * experts))
    row_start = row_place * feature_width
    labels = jnp.arange(experts, dtype=jnp.int32)
    scalars = jnp.stack([expert, row_place]).astype(jnp.int32)
    row_scalar = row_place.astype(jnp.int32).reshape(1)
    key_part = lax.dynamic_slice_in_dim(key_projection_matrix, kv_index * head_size, head_size, 1)
    value_part = lax.dynamic_slice_in_dim(
        value_projection_matrix, kv_index * head_size, head_size, 1
    )

    def chunk(array, number):
        return array[number * rows : (number + 1) * rows]

    link = Link()
    input_pieces = ring_pieces(residual)
    projection = col_assemble(
        jnp.concatenate([query_weight, key_part, value_part], axis=1), 0, row_start, link
    )
    routes_all = jnp.stack(col_gather(routes, link)).reshape(col_count * chunks, rows, top_count)
    out_full = col_assemble(out_weight, 1, row_start, link)
    arrived = [block for piece in input_pieces[1:] for block in piece]
    grad_pieces = ring_pieces(after(grad_output, *arrived))
    grads_cols = [col_gather(joined(grad_pieces, n, rows), link) for n in range(chunks)]

    gain_one = rolled(norm_attention, row_start)
    gain_two = rolled(norm_experts, row_start)
    router = rolled(router_weight, row_start)
    router = jnp.pad(router, ((0, 0), (0, LANES - experts)))
    cos_all, sin_all = rotary(positions(segments), head_size)
    tables = [(chunk(cos_all, n), chunk(sin_all, n)) for n in range(chunks)]
    segs = [(chunk(segments, n)[None, :], chunk(segments, n)[:, None]) for n in range(chunks)]
    head_gains = (query_gain[None, :], key_gain[None, :])
    masks, slots, slots_t = (
        table.reshape(col_count, chunks, *table.shape[1:])
        for table in route_tables(scalars, routes_all)
    )

    state = [{} for _ in range(chunks)]

    for n in range(chunks):
        s = state[n]
        s["normed_full"], s["scale_one"] = assemble_norm(
            *chunk_pieces(input_pieces, n, rows), rows, gain_one[None, :]
        )
        s["projected"] = mm(s["normed_full"], projection)
        s["mixed"] = attention_forward(
            s["projected"], heads_here, *segs[n], *tables[n], *head_gains
        )
        partial = mm(s["mixed"], out_full).astype(BF16)
        s["hidden"] = chunk(residual, n).astype(F32) + ring_scatter(partial)

    for n in range(chunks):
        s = state[n]
        pieces = ring_pieces(s["hidden"].astype(BF16))
        s["normed_two"], s["scale_two"] = assemble_norm(
            *chunk_pieces(pieces, 0, rows), rows, gain_two[None, :]
        )
        s["tokens"] = col_gather(s["normed_two"], link)

    kept = None
    for place in range(chips):
        for n in range(chunks):
            s = state[n]
            two = slice(2 * place, 2 * place + 2)
            found = expert_pair(
                n * chips + place,
                chunks * chips,
                capacity,
                scalars,
                slots[two, n],
                slots_t[two, n],
                masks[two, n],
                router,
                s["tokens"][two],
                grads_cols[n][two],
                (gate_weight[0], up_weight[0], down_weight[0]),
                kept,
            )
            kept = found[7:]
            s.setdefault("y", []).append(chip_total(found[0], found[1]))
            s.setdefault("x", []).append(chip_total(found[2], found[3]))
            s.setdefault("small", []).append(found[4])
            if place == 0:
                s["logits"], s["gates"] = found[5][:, :experts], found[6][:, :experts]
    grad_gate = lax.dot_general(kept[0], kept[3], TN, preferred_element_type=F32).astype(BF16)
    grad_up = lax.dot_general(kept[0], kept[4], TN, preferred_element_type=F32).astype(BF16)
    grad_down = lax.dot_general(kept[2], kept[1], TN, preferred_element_type=F32).astype(BF16)
    own_grads = (grad_gate, grad_up, grad_down)
    other_grads = []
    for own in own_grads:
        other_grads.append(swapped(after(own, *other_grads[-1:]), "dp", 0))

    for n in range(chunks):
        s = state[n]
        small = jnp.stack(s["small"])
        small = jnp.concatenate(
            [
                jnp.where((labels == expert)[:, None], small[:, :, 0, None, :], 0.0),
                small[:, :, 1, None, :],
            ],
            axis=2,
        )
        small = small[:, 0] + swapped(small[:, 1], "col", 0)
        total = chips_total(s["x"], link).astype(BF16)
        s["small"] = butterfly(chips_total([small[p] for p in range(chips)], link), "row")
        if n == chunks - 1:
            total = after(total, *own_grads)
        s["normed_two_grad"] = ring_scatter(total)
    for n in range(chunks):
        s = state[n]
        s["mixture"] = ring_scatter(chips_total(s["y"], link).astype(BF16))

    acc_projection = acc_out = None
    acc_router = jnp.zeros((feature_width, experts), F32)
    acc_gain_one = jnp.zeros((model_width,), F32)
    acc_gain_two = jnp.zeros((feature_width,), F32)
    acc_query_gain = jnp.zeros((head_size,), F32)
    acc_key_gain = jnp.zeros((head_size,), F32)
    output_blocks, input_blocks = [], []
    for n in range(chunks):
        s = state[n]
        hidden = s["hidden"]
        output_blocks.append((hidden + s["mixture"]).astype(BF16))
        gate_dots = s["small"][:experts].T
        slot_inner = s["small"][experts]
        pick_grad = s["gates"] * (
            gate_dots - jnp.sum(s["gates"] * gate_dots, axis=1, keepdims=True)
        )
        logit_grad = pick_grad.astype(BF16)
        acc_router = acc_router + lax.dot_general(
            s["normed_two"][:, :feature_width], logit_grad, TN, preferred_element_type=F32
        )
        normed_two_grad = s["normed_two_grad"] + lax.dot_general(
            logit_grad, router[:feature_width, :experts], NT, preferred_element_type=F32
        )
        inner_two = slot_inner[:, None] + jnp.sum(
            logit_grad.astype(F32) * s["logits"], axis=1, keepdims=True
        )
        scale_two = s["scale_two"]
        hidden_total = (
            chunk(grad_output, n).astype(F32)
            + normed_two_grad * gain_two[:feature_width] * scale_two
            - hidden * (scale_two * scale_two * inner_two / model_width)
        )
        acc_gain_two = acc_gain_two + jnp.sum(normed_two_grad * hidden * scale_two, axis=0)
        branch_full = joined(ring_pieces(hidden_total.astype(BF16)), 0, rows)
        if n == chunks - 1:
            branch_full = after(branch_full, other_grads[0])
        mixed_grad = lax.dot_general(
            branch_full, out_full, NT, preferred_element_type=F32
        ).astype(BF16)
        projected_grad, key_grad, value_grad, inner_one, head_terms = attention_backward(
            members == 1, s["projected"], mixed_grad, heads_here, *segs[n], *tables[n], *head_gains
        )
        acc_query_gain = acc_query_gain + head_terms[0]
        if members == 1:
            acc_key_gain = acc_key_gain + head_terms[1]
        else:
            for bit in range(members.bit_length() - 1):
                key_grad = key_grad + swapped(key_grad, "row", bit)
                value_grad = value_grad + swapped(value_grad, "row", bit)
            key_pre = s["projected"][:, query_width : query_width + head_size]
            value_pre = s["projected"][:, query_width + head_size :]
            key_grad, key_terms = norm_back(
                key_pre, head_gains[1], turn_plain(key_grad, tables[n][0], -tables[n][1])
            )
            acc_key_gain = acc_key_gain + column_mask * jnp.sum(key_terms, axis=0)
            key_low = (column_mask * key_grad).astype(BF16)
            value_low = (column_mask * value_grad).astype(BF16)
            projected_grad = jnp.concatenate(
                [projected_grad[:, :query_width], key_low, value_low], axis=1
            )
            inner_one = inner_one + jnp.sum(
                key_low.astype(F32) * key_pre + value_low.astype(F32) * value_pre,
                axis=1,
                keepdims=True,
            )
        partial = lax.dot_general(
            projected_grad, projection, NT, preferred_element_type=F32
        ).astype(BF16)
        normed_one_grad = ring_scatter(partial)
        inner_one = butterfly(inner_one[:, 0], "row")[:, None]
        out_here = lax.dot_general(s["mixed"], branch_full, TN, preferred_element_type=F32)
        acc_out = out_here if n == 0 else acc_out + out_here
        acc_gain_one = acc_gain_one + jnp.sum(
            partial.astype(F32) * s["normed_full"].astype(F32), axis=0
        )
        if n == chunks - 1:
            projected_grad = after(projected_grad, other_grads[1])
        projection_here = lax.dot_general(
            s["normed_full"], projected_grad, TN, preferred_element_type=F32
        )
        acc_projection = projection_here if n == 0 else acc_projection + projection_here
        scale_one = s["scale_one"]
        input_blocks.append(
            hidden_total
            + normed_one_grad * gain_one[:feature_width] * scale_one
            - chunk(residual, n).astype(F32)
            * (scale_one * scale_one * inner_one / model_width)
        )

    grad_gate, grad_up, grad_down = (
        unrolled_sum(own, other, row_scalar, row_count, axis)[None]
        for own, other, axis in zip(own_grads, other_grads, (0, 0, 1))
    )
    grad_out_weight = pair_total(col_share(acc_out.astype(BF16), 1, row_start, link))
    projection_share = pair_total(col_share(acc_projection.astype(BF16), 0, row_start, link))
    grad_query = projection_share[:, :query_width]
    share = projection_share[:, query_width:].astype(BF16)
    shares = rolled(joined(ring_pieces(share), 0, share.shape[0]), -row_place * 2 * head_size, 1)
    shares = shares.astype(F32).reshape(-1, kv_heads, members, 2, head_size).sum(axis=2)
    grad_key = shares[:, :, 0].reshape(-1, kv_heads * head_size)
    grad_value = shares[:, :, 1].reshape(-1, kv_heads * head_size)

    gain_two_full = lax.dynamic_update_slice_in_dim(
        jnp.zeros((model_width,), F32), acc_gain_two, row_start, 0
    )
    router_full = lax.dynamic_update_slice_in_dim(
        jnp.zeros((model_width, experts), F32), acc_router, row_start, 0
    )
    sizes = (model_width, model_width, head_size, head_size, model_width * experts)
    flat = jnp.concatenate(
        [
            rolled(acc_gain_one / gain_one, -row_start),
            gain_two_full,
            acc_query_gain,
            acc_key_gain,
            router_full.reshape(-1),
        ]
    )
    for axis in ("col", "row", "dp"):
        flat = butterfly(flat, axis)
    totals, start = [], 0
    for size in sizes:
        totals.append(flat[start : start + size])
        start += size
    return (
        jnp.concatenate(output_blocks, axis=0),
        jnp.concatenate(input_blocks, axis=0),
        totals[0],
        grad_query,
        grad_key,
        grad_value,
        totals[2],
        totals[3],
        grad_out_weight,
        totals[1],
        totals[4].reshape(model_width, experts),
        grad_gate,
        grad_up,
        grad_down,
    )


def solution(mesh):
    in_specs = (
        P(("dp", "col"), "row"),
        P(("dp", "col")),
        P(("dp", "col"), None),
        P(),
        P("col", "row"),
        P("col", None),
        P("col", None),
        P(),
        P(),
        P("row", "col"),
        P(),
        P(),
        P(("row", "col"), None, None),
        P(("row", "col"), None, None),
        P(("row", "col"), None, None),
        P(("dp", "col"), "row"),
    )
    out_specs = (
        P(("dp", "col"), "row"),
        P(("dp", "col"), "row"),
        P(),
        P("col", "row"),
        P("col", None),
        P("col", None),
        P(),
        P(),
        P("row", "col"),
        P(),
        P(),
        P(("row", "col"), None, None),
        P(("row", "col"), None, None),
        P(("row", "col"), None, None),
    )
    return jax.shard_map(
        per_device, mesh=mesh, in_specs=in_specs, out_specs=out_specs, check_vma=False
    )
```

time: 1590 us -> 1130 us (0.71)
  waiting for transfers between devices: 770 us -> 450 us
  Pallas kernels: 0 us -> 234 us
  matrix products: 311 us -> 86.5 us
  local copies, waits for them, and re-layouts: 146 us -> 66.5 us
  other arithmetic: 148 us -> 108 us
  starting transfers between devices: 203 us -> 171 us
    pallas_call x0 -> x18, Pallas kernels: none -> 234 us  [the longest x4 137 us: expert_pair(): pl.pallas_call(functools.partial(pair_kernel, first, place), out_shape=[d...]
    dot_general x56 -> x19, matrix products: 311 us -> 86.5 us  [the longest x1 13.8 us: per_device(): lax.dot_general(kept[0], kept[4], TN, preferred_element_type=F32)]
    ppermute x84 -> x75, waiting for transfers between devices: 581 us -> 389 us  [moved(): lax.ppermute(block, axis, [(i, (i + by) % count) for i in range(count)])]
    ppermute x50 -> x46, waiting for transfers between devices: 189 us -> 60.9 us  [swapped(): return lax.ppermute(block, axis, [(i, i ^ 1 << bit) for i in range(count)])]
    ppermute x84 -> x75, starting transfers between devices: 175 us -> 136 us  [moved(): lax.ppermute(block, axis, [(i, (i + by) % count) for i in range(count)])]
    unnamed x449 -> x329, local copies, waits for them, and re-layouts: 44.4 us -> 13.8 us
    dynamic_update_slice x27 -> x0, local copies, waits for them, and re-layouts: 30.1 us -> none  [the longest x20 19.6 us: ring_gather(): whole = lax.dynamic_update_slice_in_dim(whole, piece, start, block.ndim - 1)]
    reduce_sum x24 -> x2, other arithmetic: 28.1 us -> 6.98 us  [per_device(): jnp.sum(normed_two_grad * hidden * scale_two, axis=0)]
  transfers between devices with their start and end apart: 134 -> 121, of which waited for: 59 -> 62; matrix products, arithmetic and copies ran while one was open for 29% -> 22% of each run, Pallas kernels for 0% -> 21%
where the time goes in v2:
time: 1130 us; the launch traced here: 1120 us
  waiting for transfers between devices  450 us (40%)
  Pallas kernels  234 us (21%)
  starting transfers between devices  171 us (15%)
  other arithmetic  108 us (10%)
  matrix products  86.5 us (8%)
  local copies, waits for them, and re-layouts  66.5 us (6%)
    ppermute x75, waiting for transfers between devices, moved(): lax.ppermute(block, axis, [(i, (i + by) % count) for i in range(count)])  389 us
    pallas_call x4, Pallas kernels, expert_pair(): pl.pallas_call(functools.partial(pair_kernel, first, place), out_shape=[d...  137 us
    ppermute x75, starting transfers between devices, moved(): lax.ppermute(block, axis, [(i, (i + by) % count) for i in range(count)])  136 us
    ppermute x46, waiting for transfers between devices, swapped(): return lax.ppermute(block, axis, [(i, i ^ 1 << bit) for i in range(count)])  60.9 us
    ppermute x46, starting transfers between devices, swapped(): return lax.ppermute(block, axis, [(i, i ^ 1 << bit) for i in range(count)])  35.7 us
    pallas_call x2, Pallas kernels, attention_backward(): pl.pallas_call(functools.partial(attention_backward_kernel, head ** (-0.5...  35.5 us
  transfers between devices with their start and end apart: 121, of which 62 were waited for; matrix products, arithmetic and copies ran while one was open for 22% of the time, Pallas kernels for 21%

profile of v2, /device:TPU:0, one launch (start us, length us, event | category | flops | bytes accessed | tf_op | source)
XLA Modules:
  0.0 1121.0 jit_solution(9340942161406678639)
XLA Ops:
  0.7 5.1 collective-permute-start
  12.0 17.6 %collective-permute-done.refs_1_ = bf16[1024,512]{1,0:T(8,128)(2,1)} collective-permute-done((bf16[1024,512]{1,0:T(8,128)(2,1)}, bf16[1024,512]{1,0:T(8,128)(2,1)}, u32[]{:S(2)}, u32[]{:S(2)}) %collective-permute-start) | collective-permute-done | bytes 1048608 | tf_op jit(solution)/shard_map/ppermute | solution.py:483
  35.8 17.3 %collective-permute-done.1.refs_3_ = bf16[1024,512]{1,0:T(8,128)(2,1)} collective-permute-done((bf16[1024,512]{1,0:T(8,128)(2,1)}, bf16[1024,512]{1,0:T(8,128)(2,1)}, u32[]{:S(2)}, u32[]{:S(2)}) %collective-permute-start.1) | collective-permute-done | bytes 1048608 | tf_op jit(solution)/shard_map/ppermute | solution.py:483
  66.4 8.0 collective-permute-done.2.refs_2_
  91.7 10.9 collective-permute-done.23
  104.9 20.5 %collective-permute-start.24 = (bf16[512,512]{1,0:T(8,128)(2,1)}, bf16[512,512]{1,0:T(8,128)(2,1)}, u32[]{:S(2)}, u32[]{:S(2)}) collective-permute-start(bf16[512,512]{1,0:T(8,128)(2,1)} %get-tuple-element.322), channel_id=1, source_target_pairs={{0,4},{4,8},{8,12},{12,0},{1,5},{5,9},{9,13},{13,1},{2,6},{6,10},{... | collective-permute-start | bytes 1572872 | tf_op jit(solution)/shard_map/ppermute | solution.py:483
  130.4 8.9 attention_forward.3
  142.3 9.0 attention_forward.2
  168.7 4.5 collective-permute-done.33
  183.1 12.9 %collective-permute-done.35 = bf16[256,512]{1,0:T(8,128)(2,1)S(1)} collective-permute-done((bf16[256,512]{1,0:T(8,128)(2,1)S(1)}, bf16[256,512]{1,0:T(8,128)(2,1)S(1)}, u32[]{:S(2)}, u32[]{:S(2)}) %collective-permute-start.35) | collective-permute-done | bytes 262176 | tf_op jit(solution)/shard_map/ppermute | solution.py:483
  198.5 13.3 %collective-permute-done.12 = bf16[256,512]{1,0:T(8,128)(2,1)S(1)} collective-permute-done((bf16[256,512]{1,0:T(8,128)(2,1)S(1)}, bf16[256,512]{1,0:T(8,128)(2,1)S(1)}, u32[]{:S(2)}, u32[]{:S(2)}) %collective-permute-start.12) | collective-permute-done | bytes 262176 | tf_op jit(solution)/shard_map/ppermute | solution.py:483
  215.4 7.7 collective-permute-done.36
  223.1 11.1 collective-permute-done.13
  240.6 11.9 %collective-permute-done.17.refs_3_ = bf16[512,512]{1,0:T(8,128)(2,1)S(1)} collective-permute-done((bf16[512,512]{1,0:T(8,128)(2,1)S(1)}, bf16[512,512]{1,0:T(8,128)(2,1)S(1)}, u32[]{:S(2)}, u32[]{:S(2)}) %collective-permute-start.17) | collective-permute-done | bytes 524320 | tf_op jit(solution)/shard_map/ppermute | solution.py:483
  252.7 9.9 collective-permute-done.16.refs_1_
  264.6 10.0 collective-permute-done.27
  297.7 10.1 route_tables.1
  310.1 7.1 collective-permute-start.39
  333.8 34.2 %expert_pair.4 = (bf16[512,2048]{1,0:T(8,128)(2,1)}, bf16[512,2048]{1,0:T(8,128)(2,1)}, bf16[512,2048]{1,0:T(8,128)(2,1)}, bf16[512,2048]{1,0:T(8,128)(2,1)}, f3...) custom-call(s32[2]{0:T(128)} %copy-done.38, ...), custom_call_target="tpu_custom_call" | custom-call | flops 35999997952 | bytes 10000000 | tf_op jit(solution)/shard_map/expert_pair/pallas_call | solution.py:350
  368.0 13.2 %collective-permute-done.30.refs_0_ = bf16[512,2048]{1,0:T(8,128)(2,1)} collective-permute-done((bf16[512,2048]{1,0:T(8,128)(2,1)}, bf16[512,2048]{1,0:T(8,128)(2,1)}, u32[]{:S(2)}, u32[]{:S(2)}) %collective-permute-start.30) | collective-permute-done | bytes 2097184 | tf_op jit(solution)/shard_map/ppermute | solution.py:483
  381.9 34.4 %expert_pair.5 = (bf16[512,2048]{1,0:T(8,128)(2,1)}, bf16[512,2048]{1,0:T(8,128)(2,1)}, bf16[512,2048]{1,0:T(8,128)(2,1)}, bf16[512,2048]{1,0:T(8,128)(2,1)}, f3...) custom-call(s32[2]{0:T(128)} %copy-done.38, ...), custom_call_target="tpu_custom_call", output_to_operand_aliasing={{7}: (12, {}), {8}: (13, {}), {9}: (14, {}), {10}: (15, {})... | custom-call | flops 35999997952 | bytes 10000000 | tf_op jit(solution)/shard_map/expert_pair/pallas_call | solution.py:350
  416.7 12.6 %collective-permute-done.44.refs_0_ = bf16[512,2048]{1,0:T(8,128)(2,1)} collective-permute-done((bf16[512,2048]{1,0:T(8,128)(2,1)S(1)}, bf16[512,2048]{1,0:T(8,128)(2,1)}, u32[]{:S(2)}, u32[]{:S(2)}) %collective-permute-start.44) | collective-permute-done | bytes 2097184 | tf_op jit(solution)/shard_map/ppermute | solution.py:483
  429.3 34.2 %expert_pair.6 = (bf16[512,2048]{1,0:T(8,128)(2,1)}, bf16[512,2048]{1,0:T(8,128)(2,1)}, bf16[512,2048]{1,0:T(8,128)(2,1)}, bf16[512,2048]{1,0:T(8,128)(2,1)}, f3...) custom-call(s32[2]{0:T(128)} %copy-done.38, ...), custom_call_target="tpu_custom_call", output_to_operand_aliasing={{7}: (12, {}), {8}: (13, {}), {9}: (14, {}), {10}: (15, {})... | custom-call | flops 35999997952 | bytes 10000000 | tf_op jit(solution)/shard_map/expert_pair/pallas_call | solution.py:350
  465.4 34.7 %expert_pair.7 = (bf16[512,2048]{1,0:T(8,128)(2,1)}, bf16[512,2048]{1,0:T(8,128)(2,1)}, bf16[512,2048]{1,0:T(8,128)(2,1)}, bf16[512,2048]{1,0:T(8,128)(2,1)}, f3...) custom-call(s32[2]{0:T(128)} %copy-done.38, ...), custom_call_target="tpu_custom_call", output_to_operand_aliasing={{7}: (12, {}), {8}: (13, {}), {9}: (14, {}), {10}: (15, {})... | custom-call | flops 35999997952 | bytes 10000000 | tf_op jit(solution)/shard_map/expert_pair/pallas_call | solution.py:350
  506.4 11.8 %convolution_convert_fusion.1.one_ref = bf16[2048,768]{1,0:T(8,128)(2,1)S(1)} fusion(bf16[2560,2048]{1,0:T(8,128)(2,1)} %get-tuple-element.156, bf16[2560,768]{1,0:T(8,128)(2,1)S(1)} %copy-done.151), kind=kOutput, calls=%fused_computation.17 | convolution fusion | flops 8054636544 | bytes 17563648 | tf_op jit(solution)/shard_map/dot_general | solution.py:796
  518.3 13.8 %convolution_convert_fusion.one_ref = bf16[2048,768]{1,0:T(8,128)(2,1)} fusion(bf16[2560,2048]{1,0:T(8,128)(2,1)} %get-tuple-element.156, bf16[2560,768]{1,0:T(8,128)(2,1)S(1)} %copy-done.152), kind=kOutput, calls=%fused_computation.16 | convolution fusion | flops 8054636544 | bytes 17563648 | tf_op jit(solution)/shard_map/dot_general | solution.py:797
  532.5 18.6 %collective-permute-done.51 = bf16[512,2048]{1,0:T(8,128)(2,1)S(1)} collective-permute-done((bf16[512,2048]{1,0:T(8,128)(2,1)S(1)}, bf16[512,2048]{1,0:T(8,128)(2,1)S(1)}, u32[]{:S(2)}, u32[]{:S(2)}) %collective-permute-start.51) | collective-permute-done | bytes 2097184 | tf_op jit(solution)/shard_map/ppermute | solution.py:483
  553.9 6.0 collective-permute-done.52
  561.1 10.3 convolution_convert_fusion.2.one_ref
  580.4 27.6 %collective-permute-done.53 = bf16[512,2048]{1,0:T(8,128)(2,1)} collective-permute-done((bf16[512,2048]{1,0:T(8,128)(2,1)}, bf16[512,2048]{1,0:T(8,128)(2,1)}, u32[]{:S(2)}, u32[]{:S(2)}) %collective-permute-start.53) | collective-permute-done | bytes 2097184 | tf_op jit(solution)/shard_map/ppermute | solution.py:483
  608.6 6.4 collective-permute-done.54
  630.3 9.9 collective-permute-done.73
  656.8 5.5 collective-permute-done.55
  666.7 16.8 %collective-permute-done.56 = bf16[256,512]{1,0:T(8,128)(2,1)S(1)} collective-permute-done((bf16[256,512]{1,0:T(8,128)(2,1)S(1)}, bf16[256,512]{1,0:T(8,128)(2,1)S(1)}, u32[]{:S(2)}, u32[]{:S(2)}) %collective-permute-start.56) | collective-permute-done | bytes 262176 | tf_op jit(solution)/shard_map/ppermute | solution.py:483
  686.8 5.9 collective-permute-done.89
  694.7 5.5 collective-permute-done.58
  706.4 13.4 %collective-permute-done.90 = f32[17,512]{0,1:T(8,128)S(1)} collective-permute-done((f32[17,512]{0,1:T(8,128)S(1)}, f32[17,512]{0,1:T(8,128)S(1)}, u32[]{:S(2)}, u32[]{:S(2)}) %collective-permute-start.90) | collective-permute-done | bytes 34848 | tf_op jit(solution)/shard_map/ppermute | solution.py:488
  719.9 14.7 %collective-permute-done.59 = bf16[512,512]{1,0:T(8,128)(2,1)S(1)} collective-permute-done((bf16[512,512]{1,0:T(8,128)(2,1)S(1)}, bf16[512,512]{1,0:T(8,128)(2,1)S(1)}, u32[]{:S(2)}, u32[]{:S(2)}) %collective-permute-start.59) | collective-permute-done | bytes 524320 | tf_op jit(solution)/shard_map/ppermute | solution.py:483
  743.5 10.2 collective-permute-done.75
  754.8 8.9 collective-permute-done.74
  768.0 5.5 collective-permute-done.87
  779.3 5.0 convolution_convert_fusion.8.g_ref
  784.4 17.6 %attention_backward.2 = (bf16[512,1280]{1,0:T(8,128)(2,1)S(1)}, f32[512,128]{1,0:T(8,128)}, f32[512,128]{1,0:T(8,128)}, f32[512,1]{1,0:T(8,128)S(1)}, f32[2,128]{1,0:T(2,128)S(1)}) custom-call(f32[512,1280]{1,0:T(8,128)} %copy-done.51, f32[512,1280]{1,0:T(8,128)} %copy-done.51, f32[512,1280]{1,0:T(8,128)} %copy-done.51, ...), custom_call_target="tpu_custom_call" | custom-call | flops 20000000000 | bytes 10000000 | tf_op jit(solution)/shard_map/attention_backward/pallas_call | solution.py:156
  814.0 4.9 collective-permute-start.88
  825.0 9.8 collective-permute-start.83
  840.0 6.2 collective-permute-done.80
  855.9 6.1 collective-permute-done.81
  876.9 11.2 collective-permute-done.107.two_ref
  901.3 6.9 collective-permute-done.94
  908.3 6.6 pad_maximum_fusion.3
  926.1 17.9 %attention_backward.3 = (bf16[512,1280]{1,0:T(8,128)(2,1)S(1)}, f32[512,128]{1,0:T(8,128)}, f32[512,128]{1,0:T(8,128)}, f32[512,1]{1,0:T(8,128)S(1)}, f32[2,128]{1,0:T(2,128)S(1)}) custom-call(f32[512,1280]{1,0:T(8,128)} %copy-done.50, f32[512,1280]{1,0:T(8,128)} %copy-done.50, f32[512,1280]{1,0:T(8,128)} %copy-done.50, ...), custom_call_target="tpu_custom_call" | custom-call | flops 20000000000 | bytes 10000000 | tf_op jit(solution)/shard_map/attention_backward/pallas_call | solution.py:156
  944.0 5.6 fusion.65
  949.6 5.8 add_convert_fusion
  978.4 5.1 collective-permute-done.101
  1000.5 11.3 %collective-permute-done.66 = bf16[512,512]{1,0:T(8,128)(2,1)S(1)} collective-permute-done((bf16[512,512]{1,0:T(8,128)(2,1)}, bf16[512,512]{1,0:T(8,128)(2,1)S(1)}, u32[]{:S(2)}, u32[]{:S(2)}) %collective-permute-start.66) | collective-permute-done | bytes 524320 | tf_op jit(solution)/shard_map/ppermute | solution.py:483
  1012.5 10.4 collective-permute-done.97
  1022.9 8.1 collective-permute-done.99
  1034.4 7.6 collective-permute-done.112
  1047.7 5.5 collective-permute-done.103
  1053.9 4.7 collective-permute-done.104
  1059.3 5.1 unrolled_sum.3
  1064.5 6.2 unrolled_sum.4
  1070.7 5.4 unrolled_sum.5
  1097.6 4.8 collective-permute-done.115
  (731 shorter events, 389.0 us)
Async XLA Ops:
  0.7 29.0 %collective-permute-start = (bf16[1024,512]{1,0:T(8,128)(2,1)}, bf16[1024,512]{1,0:T(8,128)(2,1)}, u32[]{:S(2)}, u32[]{:S(2)}) collective-permute-start(bf16[1024,512]{1,0:T(8,128)(2,1)} %refs_0_.5), channel_id=1, source_target_pairs={{0,12},{4,0},{8,4},{12,8},{1,13},{5,1},{9,5},{13,9},{2,14},{6,2},{... | collective-permute-start | bytes 3145736 | tf_op jit(solution)/shard_map/ppermute | solution.py:483
  5.8 47.3 %collective-permute-start.1 = (bf16[1024,512]{1,0:T(8,128)(2,1)}, bf16[1024,512]{1,0:T(8,128)(2,1)}, u32[]{:S(2)}, u32[]{:S(2)}) collective-permute-start(bf16[1024,512]{1,0:T(8,128)(2,1)} %refs_0_.5), channel_id=1, source_target_pairs={{0,4},{4,8},{8,12},{12,0},{1,5},{5,9},{9,13},{13,1},{2,6},{6,10},{... | collective-permute-start | bytes 3145736 | tf_op jit(solution)/shard_map/ppermute | solution.py:483
  8.1 48.4 %collective-permute-start.4 = (bf16[512,1280]{1,0:T(8,128)(2,1)S(1)}, bf16[512,1280]{1,0:T(8,128)(2,1)S(1)}, u32[]{:S(2)}, u32[]{:S(2)}) collective-permute-start(bf16[512,1280]{1,0:T(8,128)(2,1)S(1)} %pad_maximum_fusion.5.refs_0_), channel_id=1, source_target_pairs={{0,2},{1,3},{2,0},{3,1},{4,6},{5,7},{6,4},{7,5},{8,10},{9,11},{10,... | collective-permute-start | bytes 3932168 | tf_op jit(solution)/shard_map/ppermute | solution.py:483
  9.7 95.2 %collective-permute-start.3 = (bf16[512,1280]{1,0:T(8,128)(2,1)S(1)}, bf16[512,1280]{1,0:T(8,128)(2,1)}, u32[]{:S(2)}, u32[]{:S(2)}) collective-permute-start(bf16[512,1280]{1,0:T(8,128)(2,1)S(1)} %pad_maximum_fusion.5.refs_0_), channel_id=1, source_target_pairs={{0,1},{1,0},{2,3},{3,2},{4,5},{5,4},{6,7},{7,6},{8,9},{9,8},{10,11... | collective-permute-start | bytes 3932168 | tf_op jit(solution)/shard_map/ppermute | solution.py:488
  9.7 147.7 %collective-permute-start.6 = (bf16[1024,512]{1,0:T(8,128)(2,1)}, bf16[1024,512]{1,0:T(8,128)(2,1)}, u32[]{:S(2)}, u32[]{:S(2)}) collective-permute-start(bf16[1024,512]{1,0:T(8,128)(2,1)} %refs_0_.4), channel_id=1, source_target_pairs={{0,1},{1,0},{2,3},{3,2},{4,5},{5,4},{6,7},{7,6},{8,9},{9,8},{10,11... | collective-permute-start | bytes 3145736 | tf_op jit(solution)/shard_map/ppermute | solution.py:488
  31.5 32.6 %collective-permute-start.21 = (bf16[512,512]{1,0:T(8,128)(2,1)}, bf16[512,512]{1,0:T(8,128)(2,1)S(1)}, u32[]{:S(2)}, u32[]{:S(2)}) collective-permute-start(bf16[512,512]{1,0:T(8,128)(2,1)} %slice.665), channel_id=1, source_target_pairs={{0,12},{4,0},{8,4},{12,8},{1,13},{5,1},{9,5},{13,9},{2,14},{6,2},{... | collective-permute-start | bytes 1572872 | tf_op jit(solution)/shard_map/ppermute | solution.py:483
  60.5 64.8 %collective-permute-start.5 = (bf16[512,1280]{1,0:T(8,128)(2,1)S(1)}, bf16[512,1280]{1,0:T(8,128)(2,1)}, u32[]{:S(2)}, u32[]{:S(2)}) collective-permute-start(bf16[512,1280]{1,0:T(8,128)(2,1)S(1)} %collective-permute-done.4.refs_2_), channel_id=1, source_target_pairs={{0,1},{1,0},{2,3},{3,2},{4,5},{5,4},{6,7},{7,6},{8,9},{9,8},{10,11... | collective-permute-start | bytes 3932168 | tf_op jit(solution)/shard_map/ppermute | solution.py:488
  74.4 28.2 %collective-permute-start.23 = (bf16[1024,512]{1,0:T(8,128)(2,1)}, bf16[1024,512]{1,0:T(8,128)(2,1)}, u32[]{:S(2)}, u32[]{:S(2)}) collective-permute-start(bf16[1024,512]{1,0:T(8,128)(2,1)} %param.31), channel_id=1, source_target_pairs={{0,4},{4,8},{8,12},{12,0},{1,5},{5,9},{9,13},{13,1},{2,6},{6,10},{... | collective-permute-start | bytes 3145736 | tf_op jit(solution)/shard_map/ppermute | solution.py:483
  90.2 61.2 %collective-permute-start.22 = (bf16[1024,512]{1,0:T(8,128)(2,1)}, bf16[1024,512]{1,0:T(8,128)(2,1)}, u32[]{:S(2)}, u32[]{:S(2)}) collective-permute-start(bf16[1024,512]{1,0:T(8,128)(2,1)} %param.31), channel_id=1, source_target_pairs={{0,12},{4,0},{8,4},{12,8},{1,13},{5,1},{9,5},{13,9},{2,14},{6,2},{... | collective-permute-start | bytes 3145736 | tf_op jit(solution)/shard_map/ppermute | solution.py:483
  102.6 54.8 %collective-permute-start.9 = (bf16[1024,512]{1,0:T(8,128)(2,1)}, bf16[1024,512]{1,0:T(8,128)(2,1)S(1)}, u32[]{:S(2)}, u32[]{:S(2)}) collective-permute-start(bf16[1024,512]{1,0:T(8,128)(2,1)} %collective-permute-done.8.refs_2_), channel_id=1, source_target_pairs={{0,1},{1,0},{2,3},{3,2},{4,5},{5,4},{6,7},{7,6},{8,9},{9,8},{10,11... | collective-permute-start | bytes 3145736 | tf_op jit(solution)/shard_map/ppermute | solution.py:488
  104.9 48.2 %collective-permute-start.24 = (bf16[512,512]{1,0:T(8,128)(2,1)}, bf16[512,512]{1,0:T(8,128)(2,1)}, u32[]{:S(2)}, u32[]{:S(2)}) collective-permute-start(bf16[512,512]{1,0:T(8,128)(2,1)} %get-tuple-element.322), channel_id=1, source_target_pairs={{0,4},{4,8},{8,12},{12,0},{1,5},{5,9},{9,13},{13,1},{2,6},{6,10},{... | collective-permute-start | bytes 1572872 | tf_op jit(solution)/shard_map/ppermute | solution.py:483
  155.9 120.3 %collective-permute-start.28 = (bf16[512,2048]{1,0:T(8,128)(2,1)}, bf16[512,2048]{1,0:T(8,128)(2,1)S(1)}, u32[]{:S(2)}, u32[]{:S(2)}) collective-permute-start(bf16[512,2048]{1,0:T(8,128)(2,1)} %pad_maximum_fusion.refs_2_), channel_id=1, source_target_pairs={{0,2},{1,3},{2,0},{3,1},{4,6},{5,7},{6,4},{7,5},{8,10},{9,11},{10,... | collective-permute-start | bytes 6291464 | tf_op jit(solution)/shard_map/ppermute | solution.py:483
  173.4 42.0 %collective-permute-start.34 = (bf16[512,512]{1,0:T(8,128)(2,1)S(1)}, bf16[512,512]{1,0:T(8,128)(2,1)S(1)}, u32[]{:S(2)}, u32[]{:S(2)}) collective-permute-start(bf16[512,512]{1,0:T(8,128)(2,1)S(1)} %pad_maximum_fusion.12), channel_id=1, source_target_pairs={{0,4},{4,8},{8,12},{12,0},{1,5},{5,9},{9,13},{13,1},{2,6},{6,10},{... | collective-permute-start | bytes 1572872 | tf_op jit(solution)/shard_map/ppermute | solution.py:483
  179.2 36.2 %collective-permute-start.11 = (bf16[512,512]{1,0:T(8,128)(2,1)S(1)}, bf16[512,512]{1,0:T(8,128)(2,1)S(1)}, u32[]{:S(2)}, u32[]{:S(2)}) collective-permute-start(bf16[512,512]{1,0:T(8,128)(2,1)S(1)} %pad_maximum_fusion.9), channel_id=1, source_target_pairs={{0,4},{4,8},{8,12},{12,0},{1,5},{5,9},{9,13},{13,1},{2,6},{6,10},{... | collective-permute-start | bytes 1572872 | tf_op jit(solution)/shard_map/ppermute | solution.py:483
  179.9 32.0 %collective-permute-start.12 = (bf16[256,512]{1,0:T(8,128)(2,1)S(1)}, bf16[256,512]{1,0:T(8,128)(2,1)S(1)}, u32[]{:S(2)}, u32[]{:S(2)}) collective-permute-start(bf16[256,512]{1,0:T(8,128)(2,1)S(1)} %get-tuple-element.301), channel_id=1, source_target_pairs={{0,12},{4,0},{8,4},{12,8},{1,13},{5,1},{9,5},{13,9},{2,14},{6,2},{... | collective-permute-start | bytes 786440 | tf_op jit(solution)/shard_map/ppermute | solution.py:483
  196.0 27.1 %collective-permute-start.36 = (bf16[512,512]{1,0:T(8,128)(2,1)S(1)}, bf16[512,512]{1,0:T(8,128)(2,1)S(1)}, u32[]{:S(2)}, u32[]{:S(2)}) collective-permute-start(bf16[512,512]{1,0:T(8,128)(2,1)S(1)} %pad_maximum_fusion.13), channel_id=1, source_target_pairs={{0,12},{4,0},{8,4},{12,8},{1,13},{5,1},{9,5},{13,9},{2,14},{6,2},{... | collective-permute-start | bytes 1572872 | tf_op jit(solution)/shard_map/ppermute | solution.py:483
  239.8 34.8 %collective-permute-start.27 = (bf16[512,512]{1,0:T(8,128)(2,1)S(1)}, bf16[512,512]{1,0:T(8,128)(2,1)S(1)}, u32[]{:S(2)}, u32[]{:S(2)}) collective-permute-start(bf16[512,512]{1,0:T(8,128)(2,1)S(1)} %get-tuple-element.321), channel_id=1, source_target_pairs={{0,12},{4,0},{8,4},{12,8},{1,13},{5,1},{9,5},{13,9},{2,14},{6,2},{... | collective-permute-start | bytes 1572872 | tf_op jit(solution)/shard_map/ppermute | solution.py:483
  240.6 92.6 %collective-permute-start.25 = (bf16[512,2048]{1,0:T(8,128)(2,1)}, bf16[512,2048]{1,0:T(8,128)(2,1)}, u32[]{:S(2)}, u32[]{:S(2)}) collective-permute-start(bf16[512,2048]{1,0:T(8,128)(2,1)} %pad_maximum_fusion.refs_2_), channel_id=1, source_target_pairs={{0,1},{1,0},{2,3},{3,2},{4,5},{5,4},{6,7},{7,6},{8,9},{9,8},{10,11... | collective-permute-start | bytes 6291464 | tf_op jit(solution)/shard_map/ppermute | solution.py:488
  252.6 28.1 %collective-permute-start.18 = (bf16[256,512]{1,0:T(8,128)(2,1)S(1)}, bf16[256,512]{1,0:T(8,128)(2,1)S(1)}, u32[]{:S(2)}, u32[]{:S(2)}) collective-permute-start(bf16[256,512]{1,0:T(8,128)(2,1)S(1)} %slice.663), channel_id=1, source_target_pairs={{0,4},{4,8},{8,12},{12,0},{1,5},{5,9},{9,13},{13,1},{2,6},{6,10},{... | collective-permute-start | bytes 786440 | tf_op jit(solution)/shard_map/ppermute | solution.py:483
  276.2 56.5 %collective-permute-start.29 = (bf16[512,2048]{1,0:T(8,128)(2,1)}, bf16[512,2048]{1,0:T(8,128)(2,1)}, u32[]{:S(2)}, u32[]{:S(2)}) collective-permute-start(bf16[512,2048]{1,0:T(8,128)(2,1)} %pad_maximum_fusion.1.refs_2_), channel_id=1, source_target_pairs={{0,2},{1,3},{2,0},{3,1},{4,6},{5,7},{6,4},{7,5},{8,10},{9,11},{10,... | collective-permute-start | bytes 6291464 | tf_op jit(solution)/shard_map/ppermute | solution.py:483
  286.4 47.4 %collective-permute-start.20 = (bf16[512,2048]{1,0:T(8,128)(2,1)}, bf16[512,2048]{1,0:T(8,128)(2,1)}, u32[]{:S(2)}, u32[]{:S(2)}) collective-permute-start(bf16[512,2048]{1,0:T(8,128)(2,1)} %get-tuple-element.107.refs_0_), channel_id=1, source_target_pairs={{0,1},{1,0},{2,3},{3,2},{4,5},{5,4},{6,7},{7,6},{8,9},{9,8},{10,11... | collective-permute-start | bytes 6291464 | tf_op jit(solution)/shard_map/ppermute | solution.py:488
  290.7 26.6 %collective-permute-start.37 = (bf16[512,512]{1,0:T(8,128)(2,1)}, bf16[512,512]{1,0:T(8,128)(2,1)}, u32[]{:S(2)}, u32[]{:S(2)}) collective-permute-start(bf16[512,512]{1,0:T(8,128)(2,1)} %get-tuple-element.324.refs_0_), channel_id=1, source_target_pairs={{0,12},{4,0},{8,4},{12,8},{1,13},{5,1},{9,5},{13,9},{2,14},{6,2},{... | collective-permute-start | bytes 1572872 | tf_op jit(solution)/shard_map/ppermute | solution.py:483
  325.2 56.0 %collective-permute-start.42 = (bf16[512,2048]{1,0:T(8,128)(2,1)}, bf16[512,2048]{1,0:T(8,128)(2,1)}, u32[]{:S(2)}, u32[]{:S(2)}) collective-permute-start(bf16[512,2048]{1,0:T(8,128)(2,1)} %pad_maximum_fusion.1.refs_2_), channel_id=1, source_target_pairs={{0,1},{1,0},{2,3},{3,2},{4,5},{5,4},{6,7},{7,6},{8,9},{9,8},{10,11... | collective-permute-start | bytes 6291464 | tf_op jit(solution)/shard_map/ppermute | solution.py:488
  329.0 87.3 %collective-permute-start.32 = (bf16[512,2048]{1,0:T(8,128)(2,1)S(1)}, bf16[512,2048]{1,0:T(8,128)(2,1)S(1)}, u32[]{:S(2)}, u32[]{:S(2)}) collective-permute-start(bf16[512,2048]{1,0:T(8,128)(2,1)S(1)} %copy-done.142), channel_id=1, source_target_pairs={{0,1},{1,0},{2,3},{3,2},{4,5},{5,4},{6,7},{7,6},{8,9},{9,8},{10,11... | collective-permute-start | bytes 6291464 | tf_op jit(solution)/shard_map/ppermute | solution.py:488
  332.7 49.0 %collective-permute-start.41 = (bf16[512,2048]{1,0:T(8,128)(2,1)S(1)}, bf16[512,2048]{1,0:T(8,128)(2,1)}, u32[]{:S(2)}, u32[]{:S(2)}) collective-permute-start(bf16[512,2048]{1,0:T(8,128)(2,1)S(1)} %get-tuple-element.123.refs_0_), channel_id=1, source_target_pairs={{0,1},{1,0},{2,3},{3,2},{4,5},{5,4},{6,7},{7,6},{8,9},{9,8},{10,11... | collective-permute-start | bytes 6291464 | tf_op jit(solution)/shard_map/ppermute | solution.py:488
  333.2 47.9 %collective-permute-start.30 = (bf16[512,2048]{1,0:T(8,128)(2,1)}, bf16[512,2048]{1,0:T(8,128)(2,1)}, u32[]{:S(2)}, u32[]{:S(2)}) collective-permute-start(bf16[512,2048]{1,0:T(8,128)(2,1)} %get-tuple-element.107.refs_0_), channel_id=1, source_target_pairs={{0,2},{1,3},{2,0},{3,1},{4,6},{5,7},{6,4},{7,5},{8,10},{9,11},{10,... | collective-permute-start | bytes 6291464 | tf_op jit(solution)/shard_map/ppermute | solution.py:483
  333.8 131.6 %collective-permute-start.46 = (bf16[512,2048]{1,0:T(8,128)(2,1)}, bf16[512,2048]{1,0:T(8,128)(2,1)}, u32[]{:S(2)}, u32[]{:S(2)}) collective-permute-start(bf16[512,2048]{1,0:T(8,128)(2,1)} %collective-permute-done.29.refs_2_), channel_id=1, source_target_pairs={{0,1},{1,0},{2,3},{3,2},{4,5},{5,4},{6,7},{7,6},{8,9},{9,8},{10,11... | collective-permute-start | bytes 6291464 | tf_op jit(solution)/shard_map/ppermute | solution.py:488
  381.2 271.4 %collective-permute-start.26 = (bf16[512,2048]{1,0:T(8,128)(2,1)}, bf16[512,2048]{1,0:T(8,128)(2,1)}, u32[]{:S(2)}, u32[]{:S(2)}) collective-permute-start(bf16[512,2048]{1,0:T(8,128)(2,1)} %get-tuple-element.104), channel_id=1, source_target_pairs={{0,1},{1,0},{2,3},{3,2},{4,5},{5,4},{6,7},{7,6},{8,9},{9,8},{10,11... | collective-permute-start | bytes 6291464 | tf_op jit(solution)/shard_map/ppermute | solution.py:488
  381.2 48.1 %collective-permute-start.44 = (bf16[512,2048]{1,0:T(8,128)(2,1)S(1)}, bf16[512,2048]{1,0:T(8,128)(2,1)}, u32[]{:S(2)}, u32[]{:S(2)}) collective-permute-start(bf16[512,2048]{1,0:T(8,128)(2,1)S(1)} %get-tuple-element.123.refs_0_), channel_id=1, source_target_pairs={{0,2},{1,3},{2,0},{3,1},{4,6},{5,7},{6,4},{7,5},{8,10},{9,11},{10,... | collective-permute-start | bytes 6291464 | tf_op jit(solution)/shard_map/ppermute | solution.py:483
  381.8 47.5 %collective-permute-start.31 = (bf16[512,2048]{1,0:T(8,128)(2,1)}, bf16[512,2048]{1,0:T(8,128)(2,1)}, u32[]{:S(2)}, u32[]{:S(2)}) collective-permute-start(bf16[512,2048]{1,0:T(8,128)(2,1)} %collective-permute-done.30.refs_0_), channel_id=1, source_target_pairs={{0,1},{1,0},{2,3},{3,2},{4,5},{5,4},{6,7},{7,6},{8,9},{9,8},{10,11... | collective-permute-start | bytes 6291464 | tf_op jit(solution)/shard_map/ppermute | solution.py:488
  416.3 200.4 %collective-permute-start.67 = (bf16[512,2048]{1,0:T(8,128)(2,1)}, bf16[512,2048]{1,0:T(8,128)(2,1)}, u32[]{:S(2)}, u32[]{:S(2)}) collective-permute-start(bf16[512,2048]{1,0:T(8,128)(2,1)} %get-tuple-element.147), channel_id=1, source_target_pairs={{0,1},{1,0},{2,3},{3,2},{4,5},{5,4},{6,7},{7,6},{8,9},{9,8},{10,11... | collective-permute-start | bytes 6291464 | tf_op jit(solution)/shard_map/ppermute | solution.py:488
  429.3 36.1 %collective-permute-start.45 = (bf16[512,2048]{1,0:T(8,128)(2,1)}, bf16[512,2048]{1,0:T(8,128)(2,1)}, u32[]{:S(2)}, u32[]{:S(2)}) collective-permute-start(bf16[512,2048]{1,0:T(8,128)(2,1)} %collective-permute-done.44.refs_0_), channel_id=1, source_target_pairs={{0,1},{1,0},{2,3},{3,2},{4,5},{5,4},{6,7},{7,6},{8,9},{9,8},{10,11... | collective-permute-start | bytes 6291464 | tf_op jit(solution)/shard_map/ppermute | solution.py:488
  464.4 36.5 %collective-permute-start.50 = (bf16[512,2048]{1,0:T(8,128)(2,1)}, bf16[512,2048]{1,0:T(8,128)(2,1)}, u32[]{:S(2)}, u32[]{:S(2)}) collective-permute-start(bf16[512,2048]{1,0:T(8,128)(2,1)} %get-tuple-element.135), channel_id=1, source_target_pairs={{0,1},{1,0},{2,3},{3,2},{4,5},{5,4},{6,7},{7,6},{8,9},{9,8},{10,11... | collective-permute-start | bytes 6291464 | tf_op jit(solution)/shard_map/ppermute | solution.py:488
  503.5 47.6 %collective-permute-start.51 = (bf16[512,2048]{1,0:T(8,128)(2,1)S(1)}, bf16[512,2048]{1,0:T(8,128)(2,1)S(1)}, u32[]{:S(2)}, u32[]{:S(2)}) collective-permute-start(bf16[512,2048]{1,0:T(8,128)(2,1)S(1)} %add_convert_fusion.10), channel_id=1, source_target_pairs={{0,2},{1,3},{2,0},{3,1},{4,6},{5,7},{6,4},{7,5},{8,10},{9,11},{10,... | collective-permute-start | bytes 6291464 | tf_op jit(solution)/shard_map/ppermute | solution.py:483
  505.8 26.3 %collective-permute-start.49 = (f32[2,17,512]{1,2,0:T(8,128)S(1)}, f32[2,17,512]{1,2,0:T(8,128)S(1)}, u32[]{:S(2)}, u32[]{:S(2)}) collective-permute-start(f32[2,17,512]{1,2,0:T(8,128)S(1)} %fusion.8), channel_id=1, source_target_pairs={{0,1},{1,0},{2,3},{3,2},{4,5},{5,4},{6,7},{7,6},{8,9},{9,8},{10,11... | collective-permute-start | bytes 208904 | tf_op jit(solution)/shard_map/ppermute | solution.py:488
  505.9 45.2 %collective-permute-start.48 = (bf16[512,2048]{1,0:T(8,128)(2,1)S(1)}, bf16[512,2048]{1,0:T(8,128)(2,1)S(1)}, u32[]{:S(2)}, u32[]{:S(2)}) collective-permute-start(bf16[512,2048]{1,0:T(8,128)(2,1)S(1)} %copy-done.144), channel_id=1, source_target_pairs={{0,1},{1,0},{2,3},{3,2},{4,5},{5,4},{6,7},{7,6},{8,9},{9,8},{10,11... | collective-permute-start | bytes 6291464 | tf_op jit(solution)/shard_map/ppermute | solution.py:488
  532.1 42.2 %collective-permute-start.43 = (bf16[512,2048]{1,0:T(8,128)(2,1)}, bf16[512,2048]{1,0:T(8,128)(2,1)}, u32[]{:S(2)}, u32[]{:S(2)}) collective-permute-start(bf16[512,2048]{1,0:T(8,128)(2,1)} %get-tuple-element.121), channel_id=1, source_target_pairs={{0,1},{1,0},{2,3},{3,2},{4,5},{5,4},{6,7},{7,6},{8,9},{9,8},{10,11... | collective-permute-start | bytes 6291464 | tf_op jit(solution)/shard_map/ppermute | solution.py:488
  551.1 72.2 %collective-permute-start.61 = (bf16[512,2048]{1,0:T(8,128)(2,1)}, bf16[512,2048]{1,0:T(8,128)(2,1)}, u32[]{:S(2)}, u32[]{:S(2)}) collective-permute-start(bf16[512,2048]{1,0:T(8,128)(2,1)} %get-tuple-element.144), channel_id=1, source_target_pairs={{0,1},{1,0},{2,3},{3,2},{4,5},{5,4},{6,7},{7,6},{8,9},{9,8},{10,11... | collective-permute-start | bytes 6291464 | tf_op jit(solution)/shard_map/ppermute | solution.py:488
  560.5 47.5 %collective-permute-start.53 = (bf16[512,2048]{1,0:T(8,128)(2,1)}, bf16[512,2048]{1,0:T(8,128)(2,1)}, u32[]{:S(2)}, u32[]{:S(2)}) collective-permute-start(bf16[512,2048]{1,0:T(8,128)(2,1)} %add_convert_fusion.11), channel_id=1, source_target_pairs={{0,2},{1,3},{2,0},{3,1},{4,6},{5,7},{6,4},{7,5},{8,10},{9,11},{10,... | collective-permute-start | bytes 6291464 | tf_op jit(solution)/shard_map/ppermute | solution.py:483
  578.6 108.2 %collective-permute-start.95 = (bf16[2048,768]{1,0:T(8,128)(2,1)S(1)}, bf16[2048,768]{1,0:T(8,128)(2,1)}, u32[]{:S(2)}, u32[]{:S(2)}) collective-permute-start(bf16[2048,768]{1,0:T(8,128)(2,1)S(1)} %convolution_convert_fusion.1.one_ref), channel_id=1, source_target_pairs={{0,16},{16,0},{1,17},{17,1},{2,18},{18,2},{3,19},{19,3},{4,20},{20... | collective-permute-start | bytes 9437192 | tf_op jit(solution)/shard_map/ppermute | solution.py:488
  616.7 45.5 %collective-permute-start.55 = (bf16[512,2048]{1,0:T(8,128)(2,1)}, bf16[512,2048]{1,0:T(8,128)(2,1)}, u32[]{:S(2)}, u32[]{:S(2)}) collective-permute-start(bf16[512,2048]{1,0:T(8,128)(2,1)} %add_convert_fusion.12), channel_id=1, source_target_pairs={{0,2},{1,3},{2,0},{3,1},{4,6},{5,7},{6,4},{7,5},{8,10},{9,11},{10,... | collective-permute-start | bytes 6291464 | tf_op jit(solution)/shard_map/ppermute | solution.py:483
  640.2 60.8 %collective-permute-start.84 = (bf16[512,2048]{1,0:T(8,128)(2,1)}, bf16[512,2048]{1,0:T(8,128)(2,1)}, u32[]{:S(2)}, u32[]{:S(2)}) collective-permute-start(bf16[512,2048]{1,0:T(8,128)(2,1)} %get-tuple-element.155), channel_id=1, source_target_pairs={{0,1},{1,0},{2,3},{3,2},{4,5},{5,4},{6,7},{7,6},{8,9},{9,8},{10,11... | collective-permute-start | bytes 6291464 | tf_op jit(solution)/shard_map/ppermute | solution.py:488
  650.5 33.0 %collective-permute-start.69 = (bf16[512,512]{1,0:T(8,128)(2,1)S(1)}, bf16[512,512]{1,0:T(8,128)(2,1)S(1)}, u32[]{:S(2)}, u32[]{:S(2)}) collective-permute-start(bf16[512,512]{1,0:T(8,128)(2,1)S(1)} %pad_maximum_fusion.19), channel_id=1, source_target_pairs={{0,4},{4,8},{8,12},{12,0},{1,5},{5,9},{9,13},{13,1},{2,6},{6,10},{... | collective-permute-start | bytes 1572872 | tf_op jit(solution)/shard_map/ppermute | solution.py:483
  652.6 31.0 %collective-permute-start.71 = (bf16[512,512]{1,0:T(8,128)(2,1)S(1)}, bf16[512,512]{1,0:T(8,128)(2,1)S(1)}, u32[]{:S(2)}, u32[]{:S(2)}) collective-permute-start(bf16[512,512]{1,0:T(8,128)(2,1)S(1)} %pad_maximum_fusion.20), channel_id=1, source_target_pairs={{0,12},{4,0},{8,4},{12,8},{1,13},{5,1},{9,5},{13,9},{2,14},{6,2},{... | collective-permute-start | bytes 1572872 | tf_op jit(solution)/shard_map/ppermute | solution.py:483
  683.4 164.1 %collective-permute-start.60 = (bf16[512,2048]{1,0:T(8,128)(2,1)}, bf16[512,2048]{1,0:T(8,128)(2,1)}, u32[]{:S(2)}, u32[]{:S(2)}) collective-permute-start(bf16[512,2048]{1,0:T(8,128)(2,1)} %get-tuple-element.142), channel_id=1, source_target_pairs={{0,1},{1,0},{2,3},{3,2},{4,5},{5,4},{6,7},{7,6},{8,9},{9,8},{10,11... | collective-permute-start | bytes 6291464 | tf_op jit(solution)/shard_map/ppermute | solution.py:488
  692.7 27.1 %collective-permute-start.90 = (f32[17,512]{0,1:T(8,128)S(1)}, f32[17,512]{0,1:T(8,128)S(1)}, u32[]{:S(2)}, u32[]{:S(2)}) collective-permute-start(f32[17,512]{0,1:T(8,128)S(1)} %add.495), channel_id=1, source_target_pairs={{0,8},{4,12},{8,0},{12,4},{1,9},{5,13},{9,1},{13,5},{2,10},{6,14},... | collective-permute-start | bytes 104456 | tf_op jit(solution)/shard_map/ppermute | solution.py:488
  693.1 26.8 %collective-permute-start.57 = (bf16[512,512]{1,0:T(8,128)(2,1)S(1)}, bf16[512,512]{1,0:T(8,128)(2,1)S(1)}, u32[]{:S(2)}, u32[]{:S(2)}) collective-permute-start(bf16[512,512]{1,0:T(8,128)(2,1)S(1)} %pad_maximum_fusion.15), channel_id=1, source_target_pairs={{0,4},{4,8},{8,12},{12,0},{1,5},{5,9},{9,13},{13,1},{2,6},{6,10},{... | collective-permute-start | bytes 1572872 | tf_op jit(solution)/shard_map/ppermute | solution.py:483
  700.2 34.3 %collective-permute-start.59 = (bf16[512,512]{1,0:T(8,128)(2,1)S(1)}, bf16[512,512]{1,0:T(8,128)(2,1)S(1)}, u32[]{:S(2)}, u32[]{:S(2)}) collective-permute-start(bf16[512,512]{1,0:T(8,128)(2,1)S(1)} %pad_maximum_fusion.16), channel_id=1, source_target_pairs={{0,12},{4,0},{8,4},{12,8},{1,13},{5,1},{9,5},{13,9},{2,14},{6,2},{... | collective-permute-start | bytes 1572872 | tf_op jit(solution)/shard_map/ppermute | solution.py:483
  704.5 36.5 %collective-permute-start.85 = (bf16[256,512]{1,0:T(8,128)(2,1)S(1)}, bf16[256,512]{1,0:T(8,128)(2,1)S(1)}, u32[]{:S(2)}, u32[]{:S(2)}) collective-permute-start(bf16[256,512]{1,0:T(8,128)(2,1)S(1)} %slice.610), channel_id=1, source_target_pairs={{0,4},{4,8},{8,12},{12,0},{1,5},{5,9},{9,13},{13,1},{2,6},{6,10},{... | collective-permute-start | bytes 786440 | tf_op jit(solution)/shard_map/ppermute | solution.py:483
  741.8 31.7 %collective-permute-start.87 = (bf16[256,512]{1,0:T(8,128)(2,1)}, bf16[256,512]{1,0:T(8,128)(2,1)}, u32[]{:S(2)}, u32[]{:S(2)}) collective-permute-start(bf16[256,512]{1,0:T(8,128)(2,1)} %get-tuple-element.289), channel_id=1, source_target_pairs={{0,12},{4,0},{8,4},{12,8},{1,13},{5,1},{9,5},{13,9},{2,14},{6,2},{... | collective-permute-start | bytes 786440 | tf_op jit(solution)/shard_map/ppermute | solution.py:483
  768.0 56.9 %collective-permute-start.86 = (bf16[512,512]{1,0:T(8,128)(2,1)}, bf16[512,512]{1,0:T(8,128)(2,1)}, u32[]{:S(2)}, u32[]{:S(2)}) collective-permute-start(bf16[512,512]{1,0:T(8,128)(2,1)} %pad_maximum_fusion.23), channel_id=1, source_target_pairs={{0,4},{4,8},{8,12},{12,0},{1,5},{5,9},{9,13},{13,1},{2,6},{6,10},{... | collective-permute-start | bytes 1572872 | tf_op jit(solution)/shard_map/ppermute | solution.py:483
  775.3 72.2 %collective-permute-start.62 = (bf16[512,2048]{1,0:T(8,128)(2,1)}, bf16[512,2048]{1,0:T(8,128)(2,1)}, u32[]{:S(2)}, u32[]{:S(2)}) collective-permute-start(bf16[512,2048]{1,0:T(8,128)(2,1)} %add_convert_fusion.7), channel_id=1, source_target_pairs={{0,2},{1,3},{2,0},{3,1},{4,6},{5,7},{6,4},{7,5},{8,10},{9,11},{10,... | collective-permute-start | bytes 6291464 | tf_op jit(solution)/shard_map/ppermute | solution.py:483
  819.8 68.3 %collective-permute-start.107 = (bf16[2048,768]{1,0:T(8,128)(2,1)}, bf16[2048,768]{1,0:T(8,128)(2,1)}, u32[]{:S(2)}, u32[]{:S(2)}) collective-permute-start(bf16[2048,768]{1,0:T(8,128)(2,1)} %convolution_convert_fusion.one_ref), channel_id=1, source_target_pairs={{0,16},{16,0},{1,17},{17,1},{2,18},{18,2},{3,19},{19,3},{4,20},{20... | collective-permute-start | bytes 9437192 | tf_op jit(solution)/shard_map/ppermute | solution.py:488
  870.7 26.7 %collective-permute-start.65 = (bf16[256,512]{1,0:T(8,128)(2,1)}, bf16[256,512]{1,0:T(8,128)(2,1)}, u32[]{:S(2)}, u32[]{:S(2)}) collective-permute-start(bf16[256,512]{1,0:T(8,128)(2,1)} %get-tuple-element.297), channel_id=1, source_target_pairs={{0,12},{4,0},{8,4},{12,8},{1,13},{5,1},{9,5},{13,9},{2,14},{6,2},{... | collective-permute-start | bytes 786440 | tf_op jit(solution)/shard_map/ppermute | solution.py:483
  888.1 182.6 %collective-permute-start.120 = (bf16[768,2048]{1,0:T(8,128)(2,1)}, bf16[768,2048]{1,0:T(8,128)(2,1)}, u32[]{:S(2)}, u32[]{:S(2)}) collective-permute-start(bf16[768,2048]{1,0:T(8,128)(2,1)} %convolution_convert_fusion.2.one_ref), channel_id=1, source_target_pairs={{0,16},{16,0},{1,17},{17,1},{2,18},{18,2},{3,19},{19,3},{4,20},{20... | collective-permute-start | bytes 9437192 | tf_op jit(solution)/shard_map/ppermute | solution.py:488
  926.1 39.7 %collective-permute-start.110 = (bf16[1024,512]{1,0:T(8,128)(2,1)}, bf16[1024,512]{1,0:T(8,128)(2,1)}, u32[]{:S(2)}, u32[]{:S(2)}) collective-permute-start(bf16[1024,512]{1,0:T(8,128)(2,1)} %get-tuple-element.271), channel_id=1, source_target_pairs={{0,1},{1,0},{2,3},{3,2},{4,5},{5,4},{6,7},{7,6},{8,9},{9,8},{10,11... | collective-permute-start | bytes 3145736 | tf_op jit(solution)/shard_map/ppermute | solution.py:488
  958.6 32.1 %collective-permute-start.109 = (bf16[512,1280]{0,1:T(8,128)(2,1)}, bf16[512,1280]{0,1:T(8,128)(2,1)}, u32[]{:S(2)}, u32[]{:S(2)}) collective-permute-start(bf16[512,1280]{0,1:T(8,128)(2,1)} %get-tuple-element.269), channel_id=1, source_target_pairs={{0,1},{1,0},{2,3},{3,2},{4,5},{5,4},{6,7},{7,6},{8,9},{9,8},{10,11... | collective-permute-start | bytes 3932168 | tf_op jit(solution)/shard_map/ppermute | solution.py:488
  985.2 26.5 %collective-permute-start.66 = (bf16[512,512]{1,0:T(8,128)(2,1)}, bf16[512,512]{1,0:T(8,128)(2,1)S(1)}, u32[]{:S(2)}, u32[]{:S(2)}) collective-permute-start(bf16[512,512]{1,0:T(8,128)(2,1)} %pad_maximum_fusion.18), channel_id=1, source_target_pairs={{0,12},{4,0},{8,4},{12,8},{1,13},{5,1},{9,5},{13,9},{2,14},{6,2},{... | collective-permute-start | bytes 1572872 | tf_op jit(solution)/shard_map/ppermute | solution.py:483
  990.7 32.2 %collective-permute-start.97 = (bf16[512,512]{1,0:T(8,128)(2,1)S(1)}, bf16[512,512]{1,0:T(8,128)(2,1)S(1)}, u32[]{:S(2)}, u32[]{:S(2)}) collective-permute-start(bf16[512,512]{1,0:T(8,128)(2,1)S(1)} %pad_maximum_fusion.25), channel_id=1, source_target_pairs={{0,4},{4,8},{8,12},{12,0},{1,5},{5,9},{9,13},{13,1},{2,6},{6,10},{... | collective-permute-start | bytes 1572872 | tf_op jit(solution)/shard_map/ppermute | solution.py:483
  994.2 36.9 %collective-permute-start.99 = (bf16[512,512]{1,0:T(8,128)(2,1)S(1)}, bf16[512,512]{1,0:T(8,128)(2,1)S(1)}, u32[]{:S(2)}, u32[]{:S(2)}) collective-permute-start(bf16[512,512]{1,0:T(8,128)(2,1)S(1)} %pad_maximum_fusion.26), channel_id=1, source_target_pairs={{0,12},{4,0},{8,4},{12,8},{1,13},{5,1},{9,5},{13,9},{2,14},{6,2},{... | collective-permute-start | bytes 1572872 | tf_op jit(solution)/shard_map/ppermute | solution.py:483
  1000.5 34.0 %collective-permute-start.108 = (bf16[512,1280]{0,1:T(8,128)(2,1)S(1)}, bf16[512,1280]{0,1:T(8,128)(2,1)S(1)}, u32[]{:S(2)}, u32[]{:S(2)}) collective-permute-start(bf16[512,1280]{0,1:T(8,128)(2,1)S(1)} %copy-done.97), channel_id=1, source_target_pairs={{0,1},{1,0},{2,3},{3,2},{4,5},{5,4},{6,7},{7,6},{8,9},{9,8},{10,11... | collective-permute-start | bytes 3932168 | tf_op jit(solution)/shard_map/ppermute | solution.py:488
  1011.8 30.2 %collective-permute-start.112 = (bf16[512,1280]{0,1:T(8,128)(2,1)S(1)}, bf16[512,1280]{0,1:T(8,128)(2,1)S(1)}, u32[]{:S(2)}, u32[]{:S(2)}) collective-permute-start(bf16[512,1280]{0,1:T(8,128)(2,1)S(1)} %add_convert_fusion.15), channel_id=1, source_target_pairs={{0,2},{1,3},{2,0},{3,1},{4,6},{5,7},{6,4},{7,5},{8,10},{9,11},{10,... | collective-permute-start | bytes 3932168 | tf_op jit(solution)/shard_map/ppermute | solution.py:483
  1022.9 58.5 %collective-permute-start.118 = (bf16[1024,512]{1,0:T(8,128)(2,1)}, bf16[1024,512]{1,0:T(8,128)(2,1)}, u32[]{:S(2)}, u32[]{:S(2)}) collective-permute-start(bf16[1024,512]{1,0:T(8,128)(2,1)} %get-tuple-element.270), channel_id=1, source_target_pairs={{0,1},{1,0},{2,3},{3,2},{4,5},{5,4},{6,7},{7,6},{8,9},{9,8},{10,11... | collective-permute-start | bytes 3145736 | tf_op jit(solution)/shard_map/ppermute | solution.py:488
  1045.7 41.4 %collective-permute-start.113 = (bf16[512,1280]{0,1:T(8,128)(2,1)}, bf16[512,1280]{0,1:T(8,128)(2,1)}, u32[]{:S(2)}, u32[]{:S(2)}) collective-permute-start(bf16[512,1280]{0,1:T(8,128)(2,1)} %add_convert_fusion.14), channel_id=1, source_target_pairs={{0,16},{16,0},{1,17},{17,1},{2,18},{18,2},{3,19},{19,3},{4,20},{20... | collective-permute-start | bytes 3932168 | tf_op jit(solution)/shard_map/ppermute | solution.py:488
  (217 other events, 3863.5 us)

commit v3 on v2

--- a/solution.py
+++ b/solution.py
@@ -83,7 +83,7 @@
         out_specs=pl.BlockSpec((rows, pair * head), lambda i: (0, i)),
         scratch_shapes=[pltpu.VMEM((rows, rows), F32), pltpu.VMEM((rows, head), BF16), pltpu.VMEM((rows, head), BF16)],
         compiler_params=pltpu.CompilerParams(vmem_limit_bytes=48 << 20),
-        cost_estimate=pl.CostEstimate(flops=10**10, bytes_accessed=10**7, transcendentals=0),
+        cost_estimate=pl.CostEstimate(flops=10000000000, bytes_accessed=10000000, transcendentals=0),
         name="attention_forward",
     )(projected, projected, projected, segs, segs_t, cos_wide, sin_wide, q_gain, k_gain)
 
@@ -173,11 +173,39 @@
         out_specs=[fixed(rows, (heads + 2) * head), fixed(rows, head), fixed(rows, head), fixed(rows, 1), fixed(2, head)],
         scratch_shapes=[pltpu.VMEM((rows, rows), F32), pltpu.VMEM((rows, head), BF16), pltpu.VMEM((rows, head), BF16), pltpu.VMEM((rows, head), F32)],
         compiler_params=pltpu.CompilerParams(vmem_limit_bytes=48 << 20),
-        cost_estimate=pl.CostEstimate(flops=2 * 10**10, bytes_accessed=10**7, transcendentals=0),
+        cost_estimate=pl.CostEstimate(flops=20000000000, bytes_accessed=10000000, transcendentals=0),
         name="attention_backward",
     )(projected, projected, projected, upstream, segs, segs_t, cos_wide, sin_wide, q_gain, k_gain)
 
-def norm_kernel(count, *refs):
+def norm_kernel(in_ref, gain_ref, out_ref, scale_ref):
+    wide = in_ref[...].astype(F32)
+    scale = unit(wide)
+    scale_ref[...] = scale
+    out_ref[...] = (wide * scale * gain_ref[...]).astype(BF16)
+
+
+def normalized(values, gain):
+    rows, width = values.shape
+    block = min(128, rows)
+    return pl.pallas_call(
+        norm_kernel,
+        grid=(rows // block,),
+        out_shape=[jax.ShapeDtypeStruct((rows, width), BF16), jax.ShapeDtypeStruct((rows, 1), F32)],
+        in_specs=[
+            pl.BlockSpec((block, width), lambda i: (i, 0)),
+            pl.BlockSpec((1, width), lambda i: (0, 0)),
+        ],
+        out_specs=[
+            pl.BlockSpec((block, width), lambda i: (i, 0)),
+            pl.BlockSpec((block, 1), lambda i: (i, 0)),
+        ],
+        compiler_params=pltpu.CompilerParams(vmem_limit_bytes=32 << 20),
+        cost_estimate=pl.CostEstimate(flops=2000000000, bytes_accessed=8000000, transcendentals=0),
+        name="normalized",
+    )(values, gain)
+
+
+def norm_pieces_kernel(count, scalars_ref, *refs):
     pieces, gain_ref, out_ref, scale_ref = refs[:count], refs[count], refs[count + 1], refs[count + 2]
     width = pieces[0].shape[1]
     total = None
@@ -188,27 +216,35 @@
     scale = lax.rsqrt(total / (width * count) + EPSILON)
     scale_ref[...] = scale
     for i, piece in enumerate(pieces):
-        at = slice(i * width, (i + 1) * width)
+        at = pl.ds(pl.multiple_of((scalars_ref[1] + i) % count * width, width), width)
         out_ref[:, at] = (piece[...].astype(F32) * scale * gain_ref[:, at]).astype(BF16)
 
-def assemble_norm(pieces, offsets, rows, gain):
+
+def normalized_pieces(pieces, offsets, rows, scalars, gain):
     count = len(pieces)
     width = pieces[0].shape[1]
     block = min(128, rows)
     return pl.pallas_call(
-        functools.partial(norm_kernel, count),
+        functools.partial(norm_pieces_kernel, count),
         grid=(rows // block,),
-        out_shape=[jax.ShapeDtypeStruct((rows, width * count), BF16), jax.ShapeDtypeStruct((rows, 1), F32)],
-        in_specs=[pl.BlockSpec((block, width), lambda i, o=o: (o // block + i, 0)) for o in offsets]
+        out_shape=[
+            jax.ShapeDtypeStruct((rows, width * count), BF16),
+            jax.ShapeDtypeStruct((rows, 1), F32),
+        ],
+        in_specs=[pl.BlockSpec(memory_space=pltpu.SMEM)]
+        + [pl.BlockSpec((block, width), lambda i, o=o: (o // block + i, 0)) for o in offsets]
         + [pl.BlockSpec((1, width * count), lambda i: (0, 0))],
-        out_specs=[pl.BlockSpec((block, width * count), lambda i: (i, 0)), pl.BlockSpec((block, 1), lambda i: (i, 0))],
+        out_specs=[
+            pl.BlockSpec((block, width * count), lambda i: (i, 0)),
+            pl.BlockSpec((block, 1), lambda i: (i, 0)),
+        ],
         compiler_params=pltpu.CompilerParams(vmem_limit_bytes=32 << 20),
-        cost_estimate=pl.CostEstimate(flops=2 * 10**9, bytes_accessed=8 * 10**6, transcendentals=0),
-        name="assemble_norm",
-    )(*pieces, gain)
-
-
-def pair_kernel(first, place, scalars_ref, slots_ref, slots_t_ref, mask_ref, router_ref, *refs):
+        cost_estimate=pl.CostEstimate(flops=2000000000, bytes_accessed=8000000, transcendentals=0),
+        name="normalized_pieces",
+    )(scalars, *pieces, gain)
+
+
+def pair_kernel(first, place, experts, scalars_ref, slots_ref, slots_t_ref, mask_ref, router_ref, *refs):
     refs = list(refs)
     token_in, grad_in = refs[0:2], refs[2:4]
     weights_in = refs[4:7]
@@ -218,24 +254,16 @@
     y_out, x_out = refs[0:2], refs[2:4]
     small_out, logits_out, gates_out = refs[4:7]
     kept_out = refs[7:12]
-    (token, grad, gate_w, up_w, down_w, y_buf, x_buf, rows_in, rows_grad, rows_dy, rows_u, rows_da, rows_db, in_sem, w_sem, out_sem, kept_sem) = refs[12:]
+    (token, grad, gate_w, up_w, down_w, y_buf, x_buf, rows_in, rows_grad, rows_dy, rows_u, rows_da, rows_db, in_sem, grad_sem, w_sem, out_sem, kept_sem) = refs[12:]
     capacity = rows_in.shape[0] // 2
     tokens, width = token.shape[1:]
     hidden = gate_w.shape[1]
-    load_tok = [pltpu.make_async_copy(token_in[g], token.at[g], in_sem.at[0, g]) for g in range(2)]
-    load_grad = [pltpu.make_async_copy(grad_in[g], grad.at[g], in_sem.at[1, g]) for g in range(2)]
-    parts = w_sem.shape[1]
-    strip = width // parts
-    load_w = []
-    for d in range(parts):
-        there = pl.multiple_of((scalars_ref[1] + d) % parts * strip, strip)
-        here = slice(d * strip, (d + 1) * strip)
-        for i, (src, dst) in enumerate(zip(weights_in, (gate_w, up_w, down_w))):
-            if i < 2:
-                src, dst = src.at[pl.ds(there, strip), :], dst.at[here, :]
-            else:
-                src, dst = src.at[:, pl.ds(there, strip)], dst.at[:, here]
-            load_w.append(pltpu.make_async_copy(src, dst, w_sem.at[i, d]))
+    load_tok = [pltpu.make_async_copy(token_in[g], token.at[g], in_sem.at[g]) for g in range(2)]
+    load_grad = [pltpu.make_async_copy(grad_in[g], grad.at[g], grad_sem.at[g]) for g in range(2)]
+    load_w = [
+        pltpu.make_async_copy(src, dst, w_sem.at[i])
+        for i, (src, dst) in enumerate(zip(weights_in, (gate_w, up_w, down_w)))
+    ]
     load_tok[0].start()
     load_grad[0].start()
     for load in load_w:
@@ -324,8 +352,12 @@
     for g in range(2):
         here = slice(g * capacity, (g + 1) * capacity)
         chosen = lax.broadcasted_iota(jnp.int32, (capacity, tokens), 0) == slots_ref[g]
-        small_out[g, 0:1, :] = jnp.sum(jnp.where(chosen, dots[here], 0.0), axis=0, keepdims=True)
-        small_out[g, 1:2, :] = jnp.sum(jnp.where(chosen, inner[here], 0.0), axis=0, keepdims=True)
+        small_row = lax.broadcasted_iota(jnp.int32, small_out.shape[1:], 0)
+        dots_row = jnp.sum(jnp.where(chosen, dots[here], 0.0), axis=0, keepdims=True)
+        inner_row = jnp.sum(jnp.where(chosen, inner[here], 0.0), axis=0, keepdims=True)
+        small_out[g] = jnp.where(small_row == expert, dots_row, 0.0) + jnp.where(
+            small_row == experts, inner_row, 0.0
+        )
         for i, (buf, out) in enumerate(((x_buf, x_out), (y_buf, y_out))):
             store = pltpu.make_async_copy(buf.at[g], out[g], out_sem.at[i, g])
             store.start()
@@ -335,21 +367,21 @@
 
 
 def expert_pair(
-    place, places, capacity, scalars, slots, slots_t, mask, router, tokens, grads, weights, kept
+    place, places, capacity, experts, scalars, slots, slots_t, mask, router, tokens, grads, weights, kept
 ):
     rows, width = tokens[0].shape
     hidden = weights[0].shape[1]
-    parts = lax.axis_size("row")
     total = places * 2 * capacity
     anywhere = pl.BlockSpec(memory_space=pl.ANY)
     inside = pl.BlockSpec(memory_space=pltpu.VMEM)
     first = kept is None
+    small_rows = (experts + 8) // 8 * 8
     dense = jax.ShapeDtypeStruct((rows, width), BF16)
     kept_shapes = [jax.ShapeDtypeStruct((total, w), BF16) for w in (width, width, hidden, hidden, hidden)]
     flat = jax.ShapeDtypeStruct((rows, router.shape[1]), F32)
     out = pl.pallas_call(
-        functools.partial(pair_kernel, first, place),
-        out_shape=[dense] * 4 + [jax.ShapeDtypeStruct((2, 2, rows), F32), flat, flat] + kept_shapes,
+        functools.partial(pair_kernel, first, place, experts),
+        out_shape=[dense] * 4 + [jax.ShapeDtypeStruct((2, small_rows, rows), F32), flat, flat] + kept_shapes,
         in_specs=[pl.BlockSpec(memory_space=pltpu.SMEM)] + [inside] * 4 + [anywhere] * (7 if first else 12),
         out_specs=[anywhere] * 4 + [inside] * 3 + [anywhere] * 5,
         input_output_aliases={} if first else {12 + i: 7 + i for i in range(5)},
@@ -367,13 +399,14 @@
             pltpu.VMEM((2 * capacity, hidden), BF16),
             pltpu.VMEM((2 * capacity, hidden), BF16),
             pltpu.VMEM((2 * capacity, hidden), BF16),
-            pltpu.SemaphoreType.DMA((2, 2)),
-            pltpu.SemaphoreType.DMA((3, parts)),
+            pltpu.SemaphoreType.DMA((2,)),
+            pltpu.SemaphoreType.DMA((2,)),
+            pltpu.SemaphoreType.DMA((3,)),
             pltpu.SemaphoreType.DMA((2, 2)),
             pltpu.SemaphoreType.DMA((5,)),
         ],
         compiler_params=pltpu.CompilerParams(vmem_limit_bytes=56 << 20),
-        cost_estimate=pl.CostEstimate(flops=36 * 10**9, bytes_accessed=10**7, transcendentals=0),
+        cost_estimate=pl.CostEstimate(flops=36000000000, bytes_accessed=10000000, transcendentals=0),
         name="expert_pair",
     )(scalars, slots, slots_t, mask, router, *tokens, *grads, *weights, *([] if first else kept))
     return out
@@ -421,7 +454,7 @@
             pl.BlockSpec((1, rows, 1), lambda i: (i, 0, 0)),
         ],
         compiler_params=pltpu.CompilerParams(vmem_limit_bytes=32 << 20),
-        cost_estimate=pl.CostEstimate(flops=10**9, bytes_accessed=10**6, transcendentals=0),
+        cost_estimate=pl.CostEstimate(flops=1000000000, bytes_accessed=1000000, transcendentals=0),
         name="route_tables",
     )(scalars, routes)
 
@@ -447,35 +480,41 @@
         in_specs=[pl.BlockSpec(memory_space=pltpu.SMEM)] + [inside] * len(pieces),
         out_specs=inside,
         compiler_params=pltpu.CompilerParams(vmem_limit_bytes=32 << 20),
-        cost_estimate=pl.CostEstimate(flops=10**6, bytes_accessed=10**7, transcendentals=0),
+        cost_estimate=pl.CostEstimate(flops=1000000, bytes_accessed=10000000, transcendentals=0),
         name="placed",
     )(starts, *pieces)
 
 
-def add_kernel(place_ref, one_ref, two_ref, out_ref):
-    out_ref[...] = one_ref[...].astype(F32) + two_ref[...].astype(F32)
-
-
-def unrolled_sum(one, two, place, parts, axis):
-    shape = one.shape
-    block = tuple(s // parts if d == axis else s for d, s in enumerate(shape))
-    if axis == 0:
-        at_in, at_out = lambda i, p: (i, 0), lambda i, p: ((i + p[0]) % parts, 0)
-    else:
-        at_in, at_out = lambda i, p: (0, i), lambda i, p: (0, (i + p[0]) % parts)
+def halves_kernel(own_ref, one_ref, two_ref, out_ref):
+    early = pl.program_id(0) < pl.num_programs(0) // 2
+
+    @pl.when(early)
+    def _():
+        out_ref[...] = own_ref[...].astype(F32) + one_ref[...].astype(F32)
+
+    @pl.when(jnp.logical_not(early))
+    def _():
+        out_ref[...] = own_ref[...].astype(F32) + two_ref[...].astype(F32)
+
+
+def halves_sum(own, one, two):
+    rows, width = own.shape
+    half = 2
+    block = rows // (2 * half)
     return pl.pallas_call(
-        add_kernel,
-        grid_spec=pltpu.PrefetchScalarGridSpec(
-            num_scalar_prefetch=1,
-            grid=(parts,),
-            in_specs=[pl.BlockSpec(block, at_in)] * 2,
-            out_specs=pl.BlockSpec(block, at_out),
-        ),
-        out_shape=jax.ShapeDtypeStruct(shape, F32),
-        compiler_params=pltpu.CompilerParams(vmem_limit_bytes=40 << 20),
-        cost_estimate=pl.CostEstimate(flops=10**6, bytes_accessed=10**6, transcendentals=0),
-        name="unrolled_sum",
-    )(place, one, two)
+        halves_kernel,
+        grid=(2 * half,),
+        out_shape=jax.ShapeDtypeStruct((rows, width), F32),
+        in_specs=[
+            pl.BlockSpec((block, width), lambda i: (i, 0)),
+            pl.BlockSpec((block, width), lambda i: (jnp.minimum(i, half - 1), 0)),
+            pl.BlockSpec((block, width), lambda i: (jnp.maximum(i - half, 0), 0)),
+        ],
+        out_specs=pl.BlockSpec((block, width), lambda i: (i, 0)),
+        compiler_params=pltpu.CompilerParams(vmem_limit_bytes=32 << 20),
+        cost_estimate=pl.CostEstimate(flops=4000000000, bytes_accessed=12000000, transcendentals=0),
+        name="halves_sum",
+    )(own, one, two)
 
 
 def moved(block, axis, by):
@@ -528,38 +567,12 @@
     return blocks, offsets
 
 
-def joined(pieces, number, rows):
-    blocks, offsets = chunk_pieces(pieces, number, rows)
-    return jnp.concatenate([b[o : o + rows] for b, o in zip(blocks, offsets)], axis=1)
-
-
-def ring_scatter(partial):
-    count = lax.axis_size("row")
-    width = partial.shape[1] // count
-    half = partial.shape[0] // 2
-
-    def piece(distance):
-        return partial[:, distance * width : (distance + 1) * width]
-
-    total = piece(0).astype(F32)
-    if count == 1:
-        return total
-    middle = piece(count // 2)
-    to_right = moved(middle[:half], "row", 1)
-    to_left = moved(middle[half:], "row", -1)
-    for step in range(count // 2 - 1, 0, -1):
-        right, left = piece(step), piece(count - step)
-        if step == count // 2 - 1:
-            right = jnp.concatenate([right[:half] + to_right, right[half:]], axis=0)
-            left = jnp.concatenate([left[:half], left[half:] + to_left], axis=0)
-        else:
-            right = right + to_right
-            left = left + to_left
-        to_right = moved(right, "row", 1)
-        to_left = moved(left, "row", -1)
-    if count == 2:
-        return total + jnp.concatenate([to_right, to_left], axis=0).astype(F32)
-    return total + to_right.astype(F32) + to_left.astype(F32)
+def row_gather(block):
+    return lax.all_gather(block, "row", axis=block.ndim - 1, tiled=True)
+
+
+def row_scatter(partial):
+    return lax.psum_scatter(partial, "row", scatter_dimension=1, tiled=True).astype(F32)
 
 
 def after(value, *others):
@@ -572,6 +585,16 @@
 
     def moved(self, block, by):
         block = moved(after(block, *self.last), "col", by)
+        self.last = (block,)
+        return block
+
+
+class PairLink:
+    def __init__(self):
+        self.last = ()
+
+    def swapped(self, block):
+        block = swapped(after(block, *self.last), "dp", 0)
         self.last = (block,)
         return block
 
@@ -585,15 +608,18 @@
     return pieces
 
 
-def chip_total(same, other):
-    return (same.astype(F32) + swapped(other, "col", 0).astype(F32)).astype(same.dtype)
-
-
-def chips_total(totals, link):
-    total = totals[0].astype(F32)
+def added(*parts):
+    total = parts[0].astype(F32)
+    for part in parts[1:]:
+        total = total + part.astype(F32)
+    return total.astype(parts[0].dtype)
+
+
+def chips_total(totals, link, *others):
+    parts = list(totals[0])
     for step in range(1, len(totals)):
-        total = total + link.moved(totals[step], -2 * step).astype(F32)
-    return total
+        parts.append(after(link.moved(added(*totals[step]), -2 * step), *others))
+    return added(*parts)
 
 
 def col_order():
@@ -607,40 +633,24 @@
     return order
 
 
-def col_assemble(block, axis, shift, link):
-    count = lax.axis_size("col")
-    width = block.shape[axis]
-    starts = [(place - shift // width) % count for place in col_order()]
-    return placed(col_gather(block, link), jnp.stack(starts).astype(jnp.int32), axis)
-
-
-def col_share(partial, axis, shift, link):
+def col_assemble(block, axis, link):
+    return placed(col_gather(block, link), jnp.stack(col_order()).astype(jnp.int32), axis)
+
+
+def col_share(partial, axis, link):
     count = lax.axis_size("col")
     width = partial.shape[axis] // count
     pieces = [
-        lax.dynamic_slice_in_dim(
-            partial, (place * width - shift) % (width * count), width, axis
-        )
+        lax.dynamic_slice_in_dim(partial, place * width, width, axis)
         for place in col_order()
     ]
     return chips_total(
-        [chip_total(pieces[2 * s], pieces[2 * s + 1]) for s in range(count // 2)], link
-    )
-
-
-def pair_total(values):
-    low = values.astype(BF16)
-    total = low.astype(F32)
-    for bit in range(lax.axis_size("dp").bit_length() - 1):
-        total = total + swapped(low, "dp", bit).astype(F32)
-        low = total.astype(BF16)
-    return total
-
-
-def rolled(values, shift, axis=0):
-    size = values.shape[axis]
-    twice = jnp.concatenate([values, values], axis=axis)
-    return lax.dynamic_slice_in_dim(twice, shift % size, size, axis)
+        [
+            (pieces[2 * step], swapped(pieces[2 * step + 1], "col", 0))
+            for step in range(count // 2)
+        ],
+        link,
+    )
 
 
 def positions(segment_ids):
@@ -713,7 +723,6 @@
     row_start = row_place * feature_width
     labels = jnp.arange(experts, dtype=jnp.int32)
     scalars = jnp.stack([expert, row_place]).astype(jnp.int32)
-    row_scalar = row_place.astype(jnp.int32).reshape(1)
     key_part = lax.dynamic_slice_in_dim(key_projection_matrix, kv_index * head_size, head_size, 1)
     value_part = lax.dynamic_slice_in_dim(
         value_projection_matrix, kv_index * head_size, head_size, 1
@@ -724,142 +733,188 @@
 
     link = Link()
     input_pieces = ring_pieces(residual)
+    grads_full = [row_gather(chunk(grad_output, n)) for n in range(chunks)]
     projection = col_assemble(
-        jnp.concatenate([query_weight, key_part, value_part], axis=1), 0, row_start, link
+        jnp.concatenate([query_weight, key_part, value_part], axis=1), 0, link
     )
     routes_all = jnp.stack(col_gather(routes, link)).reshape(col_count * chunks, rows, top_count)
-    out_full = col_assemble(out_weight, 1, row_start, link)
-    arrived = [block for piece in input_pieces[1:] for block in piece]
-    grad_pieces = ring_pieces(after(grad_output, *arrived))
-    grads_cols = [col_gather(joined(grad_pieces, n, rows), link) for n in range(chunks)]
-
-    gain_one = rolled(norm_attention, row_start)
-    gain_two = rolled(norm_experts, row_start)
-    router = rolled(router_weight, row_start)
-    router = jnp.pad(router, ((0, 0), (0, LANES - experts)))
+    out_full = col_assemble(out_weight, 1, link)
+    grads_cols = [None] * chunks
+    for n in range(chunks):
+        grads_cols[n] = col_gather(grads_full[n], link)
+    grads_far = [[g for g in grads_cols[n][2::2]] for n in range(chunks)]
+
+    gain_one = lax.dynamic_slice_in_dim(norm_attention, row_start, feature_width)
+    gain_two = lax.dynamic_slice_in_dim(norm_experts, row_start, feature_width)
+    router_rows = lax.dynamic_slice_in_dim(router_weight, row_start, feature_width, 0)
+    router = jnp.pad(router_weight, ((0, 0), (0, LANES - experts)))
     cos_all, sin_all = rotary(positions(segments), head_size)
     tables = [(chunk(cos_all, n), chunk(sin_all, n)) for n in range(chunks)]
     segs = [(chunk(segments, n)[None, :], chunk(segments, n)[:, None]) for n in range(chunks)]
     head_gains = (query_gain[None, :], key_gain[None, :])
+    state = [{} for _ in range(chunks)]
+
+    for n in range(chunks):
+        s = state[n]
+        s["normed_full"], s["scale_one"] = normalized_pieces(
+            *chunk_pieces(input_pieces, n, rows), rows, scalars, norm_attention[None, :]
+        )
+        normed = s["normed_full"] if n == 0 else after(s["normed_full"], *grads_far[n - 1])
+        s["projected"] = mm(normed, projection)
+        s["mixed"] = attention_forward(
+            s["projected"], heads_here, *segs[n], *tables[n], *head_gains
+        )
+        partial = mm(s["mixed"], out_full).astype(BF16)
+        partial = after(partial, grads_full[n])
+        summed = row_scatter(partial)
+        if n == chunks - 1:
+            summed = after(summed, *grads_far[n])
+        s["hidden"] = chunk(residual, n).astype(F32) + summed
     masks, slots, slots_t = (
         table.reshape(col_count, chunks, *table.shape[1:])
-        for table in route_tables(scalars, routes_all)
-    )
-
-    state = [{} for _ in range(chunks)]
-
+        for table in route_tables(scalars, after(routes_all, partial))
+    )
+
+    kept = None
+
+    def run_pair(n, place, *others):
+        nonlocal kept
+        s = state[n]
+        two = slice(2 * place, 2 * place + 2)
+        found = expert_pair(
+            n * chips + place,
+            chunks * chips,
+            capacity,
+            experts,
+            scalars,
+            slots[two, n],
+            slots_t[two, n],
+            masks[two, n],
+            after(router, *others),
+            s["tokens"][two],
+            grads_cols[n][two],
+            (gate_weight[0], up_weight[0], down_weight[0]),
+            kept,
+        )
+        kept = found[7:]
+        for name, same, other in (
+            ("y", found[0], found[1]),
+            ("x", found[2], found[3]),
+            ("small", found[4][0], found[4][1]),
+        ):
+            other = swapped(other, "col", 0)
+            s.setdefault(name, []).append(
+                (same, other) if place == 0 else (added(same, other),)
+            )
+        if place == 0:
+            s["logits"], s["gates"] = found[5][:, :experts], found[6][:, :experts]
+
+    def second_norm(n, *others):
+        s = state[n]
+        hidden_low = s["hidden"].astype(BF16)
+        if n == 0:
+            hidden_low = after(hidden_low, masks)
+        wide = row_gather(hidden_low)
+        s["normed_two"], s["scale_two"] = normalized(
+            after(wide, *others), norm_experts[None, :]
+        )
+        own = s["normed_two"]
+        s["tokens"] = [own, swapped(own, "col", 0)]
+        s["far"] = [link.moved(own, 2 * step) for step in range(1, chips)]
+
+    def far_tokens(n, *others):
+        for block in state[n]["far"]:
+            same = after(block, *others)
+            state[n]["tokens"] += [same, swapped(same, "col", 0)]
+
+    def to_row(n, *others):
+        s = state[n]
+        s["small"] = butterfly(chips_total(s["small"], link), "row")
+        s["total"] = chips_total(s["x"], link, *others)
+
+    second_norm(0)
     for n in range(chunks):
         s = state[n]
-        s["normed_full"], s["scale_one"] = assemble_norm(
-            *chunk_pieces(input_pieces, n, rows), rows, gain_one[None, :]
-        )
-        s["projected"] = mm(s["normed_full"], projection)
-        s["mixed"] = attention_forward(
-            s["projected"], heads_here, *segs[n], *tables[n], *head_gains
-        )
-        partial = mm(s["mixed"], out_full).astype(BF16)
-        s["hidden"] = chunk(residual, n).astype(F32) + ring_scatter(partial)
-
+        run_pair(n, 0, *([state[n - 1]["x"][-1][0]] if n > 0 else []))
+        spacer = s["small"][0][1]
+        if n + 1 < chunks:
+            second_norm(n + 1, spacer)
+            ahead = (state[n + 1]["normed_two"], spacer)
+        else:
+            ahead = (spacer,)
+        far_tokens(n, spacer)
+        if n > 0:
+            to_row(n - 1)
+            ahead += (state[n - 1]["total"],)
+        for place in range(1, chips):
+            run_pair(n, place, *ahead)
+    acc_router = jnp.zeros((feature_width, experts), F32)
+    acc_gain_two = jnp.zeros((feature_width,), F32)
     for n in range(chunks):
         s = state[n]
-        pieces = ring_pieces(s["hidden"].astype(BF16))
-        s["normed_two"], s["scale_two"] = assemble_norm(
-            *chunk_pieces(pieces, 0, rows), rows, gain_two[None, :]
-        )
-        s["tokens"] = col_gather(s["normed_two"], link)
-
-    kept = None
-    for place in range(chips):
-        for n in range(chunks):
-            s = state[n]
-            two = slice(2 * place, 2 * place + 2)
-            found = expert_pair(
-                n * chips + place,
-                chunks * chips,
-                capacity,
-                scalars,
-                slots[two, n],
-                slots_t[two, n],
-                masks[two, n],
-                router,
-                s["tokens"][two],
-                grads_cols[n][two],
-                (gate_weight[0], up_weight[0], down_weight[0]),
-                kept,
-            )
-            kept = found[7:]
-            s.setdefault("y", []).append(chip_total(found[0], found[1]))
-            s.setdefault("x", []).append(chip_total(found[2], found[3]))
-            s.setdefault("small", []).append(found[4])
-            if place == 0:
-                s["logits"], s["gates"] = found[5][:, :experts], found[6][:, :experts]
-    grad_gate = lax.dot_general(kept[0], kept[3], TN, preferred_element_type=F32).astype(BF16)
-    grad_up = lax.dot_general(kept[0], kept[4], TN, preferred_element_type=F32).astype(BF16)
-    grad_down = lax.dot_general(kept[2], kept[1], TN, preferred_element_type=F32).astype(BF16)
-    own_grads = (grad_gate, grad_up, grad_down)
-    other_grads = []
-    for own in own_grads:
-        other_grads.append(swapped(after(own, *other_grads[-1:]), "dp", 0))
-
-    for n in range(chunks):
-        s = state[n]
-        small = jnp.stack(s["small"])
-        small = jnp.concatenate(
-            [
-                jnp.where((labels == expert)[:, None], small[:, :, 0, None, :], 0.0),
-                small[:, :, 1, None, :],
-            ],
-            axis=2,
-        )
-        small = small[:, 0] + swapped(small[:, 1], "col", 0)
-        total = chips_total(s["x"], link).astype(BF16)
-        s["small"] = butterfly(chips_total([small[p] for p in range(chips)], link), "row")
         if n == chunks - 1:
-            total = after(total, *own_grads)
-        s["normed_two_grad"] = ring_scatter(total)
-    for n in range(chunks):
-        s = state[n]
-        s["mixture"] = ring_scatter(chips_total(s["y"], link).astype(BF16))
-
-    acc_projection = acc_out = None
-    acc_router = jnp.zeros((feature_width, experts), F32)
-    acc_gain_one = jnp.zeros((model_width,), F32)
-    acc_gain_two = jnp.zeros((feature_width,), F32)
-    acc_query_gain = jnp.zeros((head_size,), F32)
-    acc_key_gain = jnp.zeros((head_size,), F32)
-    output_blocks, input_blocks = [], []
-    for n in range(chunks):
-        s = state[n]
+            to_row(n, *([state[n - 1]["hidden_total"]] if n > 0 else []))
+        normed_two_grad = row_scatter(s["total"])
         hidden = s["hidden"]
-        output_blocks.append((hidden + s["mixture"]).astype(BF16))
         gate_dots = s["small"][:experts].T
         slot_inner = s["small"][experts]
         pick_grad = s["gates"] * (
             gate_dots - jnp.sum(s["gates"] * gate_dots, axis=1, keepdims=True)
         )
         logit_grad = pick_grad.astype(BF16)
+        shard = lax.dynamic_slice_in_dim(s["normed_two"], row_start, feature_width, 1)
         acc_router = acc_router + lax.dot_general(
-            s["normed_two"][:, :feature_width], logit_grad, TN, preferred_element_type=F32
-        )
-        normed_two_grad = s["normed_two_grad"] + lax.dot_general(
-            logit_grad, router[:feature_width, :experts], NT, preferred_element_type=F32
+            shard, logit_grad, TN, preferred_element_type=F32
+        )
+        normed_two_grad = normed_two_grad + lax.dot_general(
+            logit_grad, router_rows, NT, preferred_element_type=F32
         )
         inner_two = slot_inner[:, None] + jnp.sum(
             logit_grad.astype(F32) * s["logits"], axis=1, keepdims=True
         )
         scale_two = s["scale_two"]
-        hidden_total = (
+        s["hidden_total"] = (
             chunk(grad_output, n).astype(F32)
-            + normed_two_grad * gain_two[:feature_width] * scale_two
+            + normed_two_grad * gain_two * scale_two
             - hidden * (scale_two * scale_two * inner_two / model_width)
         )
         acc_gain_two = acc_gain_two + jnp.sum(normed_two_grad * hidden * scale_two, axis=0)
-        branch_full = joined(ring_pieces(hidden_total.astype(BF16)), 0, rows)
+
+    rows_in = after(kept[0], state[-1]["total"])
+    rows_u = after(kept[2], state[-1]["total"])
+    own_grads = lax.optimization_barrier(
+        (
+            lax.dot_general(rows_in, kept[3], TN, preferred_element_type=F32).astype(BF16),
+            lax.dot_general(rows_in, kept[4], TN, preferred_element_type=F32).astype(BF16),
+            lax.dot_general(rows_u, kept[1], TN, preferred_element_type=F32).astype(BF16),
+        )
+    )
+    pair = PairLink()
+    halves = [
+        pair.swapped(own[half * own.shape[0] // 2 : (half + 1) * own.shape[0] // 2])
+        for own in own_grads
+        for half in range(2)
+    ]
+    for n in range(chunks):
+        state[n]["mixed_total"] = chips_total(state[n]["y"], link)
+
+    acc_out = acc_query = acc_key = None
+    acc_gain_one = jnp.zeros((model_width,), F32)
+    acc_query_gain = jnp.zeros((head_size,), F32)
+    acc_key_gain = jnp.zeros((head_size,), F32)
+    input_blocks = []
+    for n in range(chunks):
+        s = state[n]
+        branch_full = row_gather(s["hidden_total"].astype(BF16))
         if n == chunks - 1:
-            branch_full = after(branch_full, other_grads[0])
+            branch_full = after(branch_full, halves[0], state[0]["mixed_total"])
         mixed_grad = lax.dot_general(
             branch_full, out_full, NT, preferred_element_type=F32
         ).astype(BF16)
+        out_here = lax.dot_general(s["mixed"], branch_full, TN, preferred_element_type=F32)
+        acc_out = out_here if n == 0 else acc_out + out_here
+        if n == chunks - 1:
+            out_share = col_share(acc_out.astype(BF16), 1, link)
         projected_grad, key_grad, value_grad, inner_one, head_terms = attention_backward(
             members == 1, s["projected"], mixed_grad, heads_here, *segs[n], *tables[n], *head_gains
         )
@@ -886,43 +941,51 @@
                 axis=1,
                 keepdims=True,
             )
+        key_here = lax.dot_general(
+            s["normed_full"], projected_grad[:, query_width:], TN, preferred_element_type=F32
+        )
+        acc_key = key_here if n == 0 else acc_key + key_here
         partial = lax.dot_general(
             projected_grad, projection, NT, preferred_element_type=F32
         ).astype(BF16)
-        normed_one_grad = ring_scatter(partial)
+        s["partial"] = partial
+        normed_one_grad = row_scatter(partial)
         inner_one = butterfly(inner_one[:, 0], "row")[:, None]
-        out_here = lax.dot_general(s["mixed"], branch_full, TN, preferred_element_type=F32)
-        acc_out = out_here if n == 0 else acc_out + out_here
         acc_gain_one = acc_gain_one + jnp.sum(
             partial.astype(F32) * s["normed_full"].astype(F32), axis=0
         )
+        query_here = lax.dot_general(
+            s["normed_full"], projected_grad[:, :query_width], TN, preferred_element_type=F32
+        )
+        acc_query = query_here if n == 0 else acc_query + query_here
+        scale_one = s["scale_one"]
+        if n == 0:
+            normed_one_grad = after(normed_one_grad, halves[1], state[-1]["mixed_total"])
         if n == chunks - 1:
-            projected_grad = after(projected_grad, other_grads[1])
-        projection_here = lax.dot_general(
-            s["normed_full"], projected_grad, TN, preferred_element_type=F32
-        )
-        acc_projection = projection_here if n == 0 else acc_projection + projection_here
-        scale_one = s["scale_one"]
+            normed_one_grad = after(normed_one_grad, halves[3])
         input_blocks.append(
-            hidden_total
-            + normed_one_grad * gain_one[:feature_width] * scale_one
+            s["hidden_total"]
+            + normed_one_grad * gain_one * scale_one
             - chunk(residual, n).astype(F32)
             * (scale_one * scale_one * inner_one / model_width)
         )
 
-    grad_gate, grad_up, grad_down = (
-        unrolled_sum(own, other, row_scalar, row_count, axis)[None]
-        for own, other, axis in zip(own_grads, other_grads, (0, 0, 1))
-    )
-    grad_out_weight = pair_total(col_share(acc_out.astype(BF16), 1, row_start, link))
-    projection_share = pair_total(col_share(acc_projection.astype(BF16), 0, row_start, link))
-    grad_query = projection_share[:, :query_width]
-    share = projection_share[:, query_width:].astype(BF16)
-    shares = rolled(joined(ring_pieces(share), 0, share.shape[0]), -row_place * 2 * head_size, 1)
+    for n in range(chunks):
+        s = state[n]
+        s["mixture"] = row_scatter(after(s["mixed_total"], state[-1]["partial"]))
+    state[0]["mixture"] = after(state[0]["mixture"], halves[4])
+
+    out_other = pair.swapped(out_share)
+    key_share = col_share(acc_key.astype(BF16), 0, link)
+    key_share = added(key_share, pair.swapped(key_share))
+    shares = [jnp.concatenate(piece, axis=0) for piece in ring_pieces(key_share)]
+    shares = jnp.concatenate(shares + shares, axis=1)
+    shares = lax.dynamic_slice_in_dim(
+        shares, (row_count - row_place) * 2 * head_size, row_count * 2 * head_size, 1
+    )
     shares = shares.astype(F32).reshape(-1, kv_heads, members, 2, head_size).sum(axis=2)
     grad_key = shares[:, :, 0].reshape(-1, kv_heads * head_size)
     grad_value = shares[:, :, 1].reshape(-1, kv_heads * head_size)
-
     gain_two_full = lax.dynamic_update_slice_in_dim(
         jnp.zeros((model_width,), F32), acc_gain_two, row_start, 0
     )
@@ -932,19 +995,27 @@
     sizes = (model_width, model_width, head_size, head_size, model_width * experts)
     flat = jnp.concatenate(
         [
-            rolled(acc_gain_one / gain_one, -row_start),
+            acc_gain_one / norm_attention,
             gain_two_full,
             acc_query_gain,
             acc_key_gain,
             router_full.reshape(-1),
         ]
     )
-    for axis in ("col", "row", "dp"):
+    for axis in ("col", "row"):
         flat = butterfly(flat, axis)
+    flat = flat + pair.swapped(flat)
     totals, start = [], 0
     for size in sizes:
         totals.append(flat[start : start + size])
         start += size
+    query_share = col_share(acc_query.astype(BF16), 0, link)
+    grad_query = query_share.astype(F32) + pair.swapped(query_share).astype(F32)
+    grad_out_weight = out_share.astype(F32) + out_other.astype(F32)
+    grad_gate, grad_up, grad_down = (
+        halves_sum(own, halves[2 * i], halves[2 * i + 1])[None] for i, own in enumerate(own_grads)
+    )
+    output_blocks = [(s["hidden"] + s["mixture"]).astype(BF16) for s in state]
     return (
         jnp.concatenate(output_blocks, axis=0),
         jnp.concatenate(input_blocks, axis=0),

time: 1130 us -> 991 us (0.88)
  starting transfers between devices: 171 us -> 72.5 us
  waiting for transfers between devices: 450 us -> 406 us
  other arithmetic: 108 us -> 78.8 us
  matrix products: 86.5 us -> 102 us
  between operations: 4.33 us -> 16.2 us
    ppermute x75 -> x24, waiting for transfers between devices: 389 us -> 196 us  [moved(): lax.ppermute(block, axis, [(i, (i + by) % count) for i in range(count)])]
    ppermute x75 -> x24, starting transfers between devices: 136 us -> 43.8 us  [moved(): lax.ppermute(block, axis, [(i, (i + by) % count) for i in range(count)])]
    all_gather x0 -> x6, waiting for transfers between devices: none -> 86.9 us  [row_gather(): return lax.all_gather(block, 'row', axis=block.ndim - 1, tiled=True)]
    ppermute x46 -> x54, waiting for transfers between devices: 60.9 us -> 102 us  [swapped(): return lax.ppermute(block, axis, [(i, i ^ 1 << bit) for i in range(count)])]
    reduce_scatter x0 -> x8, waiting for transfers between devices: none -> 21.4 us  [row_scatter(): lax.psum_scatter(partial, 'row', scatter_dimension=1, tiled=True)]
    concatenate x24 -> x0, other arithmetic: 20.4 us -> none  [the longest x3 11.1 us: joined(): jnp.concatenate([b[o:o + rows] for b, o in zip(blocks, offsets)], axis=1)]
    add x22 -> x7, other arithmetic: 18.5 us -> 5.74 us  [the longest x1 3.25 us: per_device(): grad_query = query_share.astype(F32) + pair.swapped(query_share).astype(F32)]
    unnamed x329 -> x215, local copies, waits for them, and re-layouts: 13.8 us -> 23.5 us
  transfers between devices with their start and end apart: 121 -> 92, of which waited for: 62 -> 43; matrix products, arithmetic and copies ran while one was open for 22% -> 23% of each run, Pallas kernels for 21% -> 20%
where the time goes in v3:
time: 991 us; the launch traced here: 981 us
  waiting for transfers between devices  406 us (41%)
  Pallas kernels  231 us (23%)
  matrix products  102 us (10%)
  other arithmetic  78.8 us (8%)
  local copies, waits for them, and re-layouts  74.3 us (7%)
  starting transfers between devices  72.5 us (7%)
  between operations  16.2 us (2%)
    ppermute x24, waiting for transfers between devices, moved(): lax.ppermute(block, axis, [(i, (i + by) % count) for i in range(count)])  196 us
    pallas_call x4, Pallas kernels, expert_pair(): pl.pallas_call(functools.partial(pair_kernel, first, place, experts), out...  135 us
    ppermute x54, waiting for transfers between devices, swapped(): return lax.ppermute(block, axis, [(i, i ^ 1 << bit) for i in range(count)])  102 us
    all_gather x6, waiting for transfers between devices, row_gather(): return lax.all_gather(block, 'row', axis=block.ndim - 1, tiled=True)  86.9 us
    ppermute x24, starting transfers between devices, moved(): lax.ppermute(block, axis, [(i, (i + by) % count) for i in range(count)])  43.8 us
    convert_element_type x14, other arithmetic, added(): return total.astype(parts[0].dtype)  41.1 us
    pallas_call x2, Pallas kernels, attention_backward(): pl.pallas_call(functools.partial(attention_backward_kernel, head ** (-0.5...  35.6 us
    ppermute x54, starting transfers between devices, swapped(): return lax.ppermute(block, axis, [(i, i ^ 1 << bit) for i in range(count)])  27.8 us
  transfers between devices with their start and end apart: 92, of which 43 were waited for; matrix products, arithmetic and copies ran while one was open for 23% of the time, Pallas kernels for 20%

profile of v3, /device:TPU:0, one launch (start us, length us, event | category | flops | bytes accessed | tf_op | source)
XLA Modules:
  0.0 980.8 jit_solution(6137734958741169083)
XLA Ops:
  15.0 28.8 %collective-permute-done.4.refs_2_ = bf16[512,1280]{1,0:T(8,128)(2,1)S(1)} collective-permute-done((bf16[512,1280]{1,0:T(8,128)(2,1)S(1)}, bf16[512,1280]{1,0:T(8,128)(2,1)S(1)}, u32[]{:S(2)}, u32[]{:S(2)}) %collective-permute-start.4) | collective-permute-done | bytes 1310752 | tf_op jit(solution)/shard_map/ppermute | solution.py:522
  49.5 3.6 collective-permute-start
  53.1 18.5 %collective-permute-done.8.refs_2_ = bf16[1024,512]{1,0:T(8,128)(2,1)} collective-permute-done((bf16[1024,512]{1,0:T(8,128)(2,1)S(1)}, bf16[1024,512]{1,0:T(8,128)(2,1)}, u32[]{:S(2)}, u32[]{:S(2)}) %collective-permute-start.8) | collective-permute-done | bytes 1048608 | tf_op jit(solution)/shard_map/ppermute | solution.py:522
  74.2 5.4 collective-permute-done.refs_1_
  81.4 9.1 collective-permute-start.12
  90.9 20.9 %collective-permute-done.1.refs_3_ = bf16[1024,512]{1,0:T(8,128)(2,1)} collective-permute-done((bf16[1024,512]{1,0:T(8,128)(2,1)S(1)}, bf16[1024,512]{1,0:T(8,128)(2,1)}, u32[]{:S(2)}, u32[]{:S(2)}) %collective-permute-start.1) | collective-permute-done | bytes 1048608 | tf_op jit(solution)/shard_map/ppermute | solution.py:522
  111.8 25.5 %collective-permute-done.12.refs_2_ = bf16[512,512]{1,0:T(8,128)(2,1)} collective-permute-done((bf16[512,512]{1,0:T(8,128)(2,1)}, bf16[512,512]{1,0:T(8,128)(2,1)}, u32[]{:S(2)}, u32[]{:S(2)}) %collective-permute-start.12) | collective-permute-done | bytes 524320 | tf_op jit(solution)/shard_map/ppermute | solution.py:522
  148.8 4.1 placed.3
  153.0 4.4 fusion.52.q_ref.k_ref.v_ref
  159.2 8.9 attention_forward.3
  168.1 3.7 convolution_convert_fusion.3
  174.5 24.7 %collective-permute-done.2.refs_2_ = bf16[512,512]{1,0:T(8,128)(2,1)S(1)} collective-permute-done((bf16[512,512]{1,0:T(8,128)(2,1)S(1)}, bf16[512,512]{1,0:T(8,128)(2,1)S(1)}, u32[]{:S(2)}, u32[]{:S(2)}) %collective-permute-start.2) | collective-permute-done | bytes 524320 | tf_op jit(solution)/shard_map/ppermute | solution.py:522
  205.2 8.9 attention_forward.2
  215.1 3.7 convolution_convert_fusion.4
  225.3 10.1 %route_tables.1 = (bf16[8,512,128]{2,1,0:T(8,128)(2,1)S(1)}, s32[8,1,512]{2,1,0:T(1,128)S(1)}, s32[8,512,1]{2,1,0:T(8,128)S(1)}) custom-call(s32[2]{0:T(128)S(1)} %pad_add_fusion.1.scalars_ref.expert_ref, s32[8,512,8]{2,1,0:T(8,128)S(1)} %bitcast.145), custom_call_target="tpu_custom_call" | custom-call | flops 1000000000 | bytes 1000000 | tf_op jit(solution)/shard_map/route_tables/pallas_call | solution.py:439
  238.6 27.0 %collective-permute-done.17.refs_2_ = bf16[512,2048]{1,0:T(8,128)(2,1)} collective-permute-done((bf16[512,2048]{1,0:T(8,128)(2,1)}, bf16[512,2048]{1,0:T(8,128)(2,1)}, u32[]{:S(2)}, u32[]{:S(2)}) %collective-permute-start.17) | collective-permute-done | bytes 2097184 | tf_op jit(solution)/shard_map/ppermute | solution.py:522
  265.6 4.2 reduce-scatter.9.cloned.1.call-done
  272.6 45.4 %all-gather.11.cloned.1.call-done.in_ref = bf16[512,2048]{1,0:T(8,128)(2,1)} async-done(((bf16[512,512]{1,0:T(8,128)(2,1)}), bf16[512,2048]{1,0:T(8,128)(2,1)}) %all-gather.11.cloned.1.call-update) | async-done | bytes 2097168 | tf_op jit(solution)/shard_map/all_gather | solution.py:571
  329.7 35.0 %expert_pair.4 = (bf16[512,2048]{1,0:T(8,128)(2,1)}, bf16[512,2048]{1,0:T(8,128)(2,1)}, bf16[512,2048]{1,0:T(8,128)(2,1)}, bf16[512,2048]{1,0:T(8,128)(2,1)}, f3...) custom-call(s32[2]{0:T(128)} %copy-done.60, ...), custom_call_target="tpu_custom_call" | custom-call | flops 35999997952 | bytes 10000000 | tf_op jit(solution)/shard_map/expert_pair/pallas_call | solution.py:382
  366.1 10.6 %collective-permute-done.19.refs_0_ = bf16[512,2048]{1,0:T(8,128)(2,1)} collective-permute-done((bf16[512,2048]{1,0:T(8,128)(2,1)}, bf16[512,2048]{1,0:T(8,128)(2,1)}, u32[]{:S(2)}, u32[]{:S(2)}) %collective-permute-start.19) | collective-permute-done | bytes 2097184 | tf_op jit(solution)/shard_map/ppermute | solution.py:522
  381.7 33.5 %expert_pair.5 = (bf16[512,2048]{1,0:T(8,128)(2,1)}, bf16[512,2048]{1,0:T(8,128)(2,1)}, bf16[512,2048]{1,0:T(8,128)(2,1)}, bf16[512,2048]{1,0:T(8,128)(2,1)}, f3...) custom-call(s32[2]{0:T(128)} %copy-done.60, ...), custom_call_target="tpu_custom_call", output_to_operand_aliasing={{7}: (12, {}), {8}: (13, {}), {9}: (14, {}), {10}: (15, {})... | custom-call | flops 35999997952 | bytes 10000000 | tf_op jit(solution)/shard_map/expert_pair/pallas_call | solution.py:382
  418.1 7.4 collective-permute-done.28
  435.8 33.4 %expert_pair.6 = (bf16[512,2048]{1,0:T(8,128)(2,1)}, bf16[512,2048]{1,0:T(8,128)(2,1)}, bf16[512,2048]{1,0:T(8,128)(2,1)}, bf16[512,2048]{1,0:T(8,128)(2,1)}, f3...) custom-call(s32[2]{0:T(128)} %copy-done.60, ...), custom_call_target="tpu_custom_call", output_to_operand_aliasing={{7}: (12, {}), {8}: (13, {}), {9}: (14, {}), {10}: (15, {})... | custom-call | flops 35999997952 | bytes 10000000 | tf_op jit(solution)/shard_map/expert_pair/pallas_call | solution.py:382
  472.4 7.0 collective-permute-done.31
  479.4 4.9 add_convert_fusion.7
  484.3 33.1 %expert_pair.7 = (bf16[512,2048]{1,0:T(8,128)(2,1)}, bf16[512,2048]{1,0:T(8,128)(2,1)}, bf16[512,2048]{1,0:T(8,128)(2,1)}, bf16[512,2048]{1,0:T(8,128)(2,1)}, f3...) custom-call(s32[2]{0:T(128)} %copy-done.60, ...), custom_call_target="tpu_custom_call", output_to_operand_aliasing={{7}: (12, {}), {8}: (13, {}), {9}: (14, {}), {10}: (15, {})... | custom-call | flops 35999997952 | bytes 10000000 | tf_op jit(solution)/shard_map/expert_pair/pallas_call | solution.py:382
  523.4 4.5 add_convert_fusion.6
  528.8 6.7 collective-permute-done.40
  536.0 8.8 collective-permute-done.41
  545.4 17.2 %reduce-scatter.13.cloned.1.call-done = bf16[512,512]{1,0:T(8,128)(2,1)} async-done(((bf16[512,2048]{1,0:T(8,128)(2,1)}), bf16[512,512]{1,0:T(8,128)(2,1)}) %reduce-scatter.13.cloned.1.call-update) | async-done | bytes 524304 | tf_op jit(solution)/shard_map/reduce_scatter | solution.py:575
  565.9 9.8 %collective-permute-done.37 = bf16[512,2048]{1,0:T(8,128)(2,1)} collective-permute-done((bf16[512,2048]{1,0:T(8,128)(2,1)}, bf16[512,2048]{1,0:T(8,128)(2,1)}, u32[]{:S(2)}, u32[]{:S(2)}) %collective-permute-start.37) | collective-permute-done | bytes 2097184 | tf_op jit(solution)/shard_map/ppermute | solution.py:522
  575.7 4.8 add_convert_fusion.4
  581.7 3.9 collective-permute-done.42
  587.1 3.8 add_convert_fusion.9
  594.6 14.2 %convolution_convert_fusion.own_ref = bf16[2048,768]{1,0:T(8,128)(2,1)} fusion(bf16[2560,2048]{1,0:T(8,128)(2,1)} %get-tuple-element.192, bf16[2560,768]{1,0:T(8,128)(2,1)} %get-tuple-element.194), kind=kOutput, calls=%fused_computation.12 | convolution fusion | flops 8054636544 | bytes 17563648 | tf_op jit(solution)/shard_map/dot_general | solution.py:888
  608.8 12.7 %convolution_convert_fusion.2.own_ref = bf16[768,2048]{1,0:T(8,128)(2,1)} fusion(bf16[2560,768]{1,0:T(8,128)(2,1)S(1)} %copy-done.95, bf16[2560,2048]{1,0:T(8,128)(2,1)} %get-tuple-element.197), kind=kOutput, calls=%fused_computation.14 | convolution fusion | flops 8054636544 | bytes 17563648 | tf_op jit(solution)/shard_map/dot_general | solution.py:889
  621.6 9.4 convolution_convert_fusion.1.own_ref
  640.1 30.3 %all-gather.17.cloned.1.call-done = bf16[512,2048]{1,0:T(8,128)(2,1)} async-done(((bf16[512,512]{1,0:T(8,128)(2,1)}), bf16[512,2048]{1,0:T(8,128)(2,1)}) %all-gather.17.cloned.1.call-update) | async-done | bytes 2097168 | tf_op jit(solution)/shard_map/all_gather | solution.py:571
  670.4 5.3 convolution_convert_fusion.7.g_ref
  675.8 17.7 %attention_backward.3 = (bf16[512,1280]{1,0:T(8,128)(2,1)S(1)}, f32[512,128]{1,0:T(8,128)}, f32[512,128]{1,0:T(8,128)}, f32[512,1]{1,0:T(8,128)S(1)}, f32[2,128]{1,0:T(2,128)S(1)}) custom-call(f32[512,1280]{1,0:T(8,128)} %copy-done.65, f32[512,1280]{1,0:T(8,128)} %copy-done.65, f32[512,1280]{1,0:T(8,128)} %copy-done.65, ...), custom_call_target="tpu_custom_call" | custom-call | flops 20000000000 | bytes 10000000 | tf_op jit(solution)/shard_map/attention_backward/pallas_call | solution.py:156
  693.6 4.2 multiply_reduce_fusion.1
  700.5 4.8 add_convert_fusion.5
  705.3 11.2 %all-gather.15.cloned.1.call-done = bf16[512,2048]{1,0:T(8,128)(2,1)} async-done(((bf16[512,512]{1,0:T(8,128)(2,1)}), bf16[512,2048]{1,0:T(8,128)(2,1)}) %all-gather.15.cloned.1.call-update) | async-done | bytes 2097168 | tf_op jit(solution)/shard_map/all_gather | solution.py:571
  716.5 5.3 convolution_convert_fusion.8.g_ref
  721.9 17.9 %attention_backward.2 = (bf16[512,1280]{1,0:T(8,128)(2,1)S(1)}, f32[512,128]{1,0:T(8,128)}, f32[512,128]{1,0:T(8,128)}, f32[512,1]{1,0:T(8,128)S(1)}, f32[2,128]{1,0:T(2,128)S(1)}) custom-call(f32[512,1280]{1,0:T(8,128)} %fusion.52.q_ref.k_ref.v_ref, f32[512,1280]{1,0:T(8,128)} %fusion.52.q_ref.k_ref.v_ref, f32[512,1280]{1,0:T(8,128)} %fusion.52.q_ref.k_ref.v_ref, ...), custom_call_target="tpu_custom_call" | custom-call | flops 20000000000 | bytes 10000000 | tf_op jit(solution)/shard_map/attention_backward/pallas_call | solution.py:156
  739.8 4.1 multiply_reduce_fusion
  744.0 3.9 fusion.45
  750.6 3.7 add_convert_fusion.3
  763.0 4.1 fusion.43
  769.0 15.4 %collective-permute-done.46.one_ref = bf16[1024,768]{1,0:T(8,128)(2,1)} collective-permute-done((bf16[1024,768]{1,0:T(8,128)(2,1)}, bf16[1024,768]{1,0:T(8,128)(2,1)}, u32[]{:S(2)}, u32[]{:S(2)}) %collective-permute-start.46) | collective-permute-done | bytes 1572896 | tf_op jit(solution)/shard_map/ppermute | solution.py:527
  785.8 5.8 fusion.53
  795.5 5.4 halves_sum.3
  802.7 5.0 add_convert_fusion.2
  807.7 12.2 %collective-permute-done.47.two_ref = bf16[1024,768]{1,0:T(8,128)(2,1)} collective-permute-done((bf16[1024,768]{1,0:T(8,128)(2,1)}, bf16[1024,768]{1,0:T(8,128)(2,1)}, u32[]{:S(2)}, u32[]{:S(2)}) %collective-permute-start.47) | collective-permute-done | bytes 1572896 | tf_op jit(solution)/shard_map/ppermute | solution.py:527
  823.2 5.3 halves_sum.4
  831.2 6.8 add_convert_fusion.1
  846.0 4.6 add_convert_fusion
  850.7 3.7 collective-permute-done.48.one_ref
  872.7 9.9 %collective-permute-done.57 = f32[37120]{0:T(1024)S(1)} collective-permute-done((f32[37120]{0:T(1024)S(1)}, f32[37120]{0:T(1024)S(1)}, u32[]{:S(2)}, u32[]{:S(2)}) %collective-permute-start.57) | collective-permute-done | bytes 148512 | tf_op jit(solution)/shard_map/ppermute | solution.py:527
  889.7 10.8 %collective-permute-done.58 = f32[37120]{0:T(1024)S(1)} collective-permute-done((f32[37120]{0:T(1024)S(1)}, f32[37120]{0:T(1024)S(1)}, u32[]{:S(2)}, u32[]{:S(2)}) %collective-permute-start.58) | collective-permute-done | bytes 148512 | tf_op jit(solution)/shard_map/ppermute | solution.py:527
  904.2 5.3 collective-permute-done.64
  910.5 8.6 collective-permute-done.59
  919.2 5.5 halves_sum.5
  939.9 3.8 collective-permute-done.75
  (524 shorter events, 226.4 us)
Async XLA Ops:
  7.2 64.4 %all-gather.7.cloned.1.call-start = ((), (), s32[]{:S(2)}) async-start(), calls=%async_computation.8 | async-start | bytes 2621440 | tf_op jit(solution)/shard_map/all_gather | solution.py:571
  9.5 162.3 %all-gather.9.cloned.1.call-start = ((), (), s32[]{:S(2)}) async-start(), calls=%async_computation.10 | async-start | bytes 2621440 | tf_op jit(solution)/shard_map/all_gather | solution.py:571
  12.0 31.8 %collective-permute-start.4 = (bf16[512,1280]{1,0:T(8,128)(2,1)S(1)}, bf16[512,1280]{1,0:T(8,128)(2,1)S(1)}, u32[]{:S(2)}, u32[]{:S(2)}) collective-permute-start(bf16[512,1280]{1,0:T(8,128)(2,1)S(1)} %pad_maximum_fusion.1.refs_0_), channel_id=1, source_target_pairs={{0,2},{1,3},{2,0},{3,1},{4,6},{5,7},{6,4},{7,5},{8,10},{9,11},{10,... | collective-permute-start | bytes 3932168 | tf_op jit(solution)/shard_map/ppermute | solution.py:522
  47.7 23.8 %collective-permute-start.8 = (bf16[1024,512]{1,0:T(8,128)(2,1)S(1)}, bf16[1024,512]{1,0:T(8,128)(2,1)}, u32[]{:S(2)}, u32[]{:S(2)}) collective-permute-start(bf16[1024,512]{1,0:T(8,128)(2,1)S(1)} %copy-done.19), channel_id=1, source_target_pairs={{0,2},{1,3},{2,0},{3,1},{4,6},{5,7},{6,4},{7,5},{8,10},{9,11},{10,... | collective-permute-start | bytes 3145736 | tf_op jit(solution)/shard_map/ppermute | solution.py:522
  49.5 30.1 %collective-permute-start = (bf16[1024,512]{1,0:T(8,128)(2,1)S(1)}, bf16[1024,512]{1,0:T(8,128)(2,1)}, u32[]{:S(2)}, u32[]{:S(2)}) collective-permute-start(bf16[1024,512]{1,0:T(8,128)(2,1)S(1)} %copy-done), channel_id=1, source_target_pairs={{0,12},{4,0},{8,4},{12,8},{1,13},{5,1},{9,5},{13,9},{2,14},{6,2},{... | collective-permute-start | bytes 3145736 | tf_op jit(solution)/shard_map/ppermute | solution.py:522
  53.1 58.7 %collective-permute-start.1 = (bf16[1024,512]{1,0:T(8,128)(2,1)S(1)}, bf16[1024,512]{1,0:T(8,128)(2,1)}, u32[]{:S(2)}, u32[]{:S(2)}) collective-permute-start(bf16[1024,512]{1,0:T(8,128)(2,1)S(1)} %copy-done), channel_id=1, source_target_pairs={{0,4},{4,8},{8,12},{12,0},{1,5},{5,9},{9,13},{13,1},{2,6},{6,10},{... | collective-permute-start | bytes 3145736 | tf_op jit(solution)/shard_map/ppermute | solution.py:522
  71.5 81.4 %collective-permute-start.13 = (bf16[512,2048]{1,0:T(8,128)(2,1)}, bf16[512,2048]{1,0:T(8,128)(2,1)}, u32[]{:S(2)}, u32[]{:S(2)}) collective-permute-start(bf16[512,2048]{1,0:T(8,128)(2,1)} %all-gather.7.cloned.1.call-done.refs_2_), channel_id=1, source_target_pairs={{0,2},{1,3},{2,0},{3,1},{4,6},{5,7},{6,4},{7,5},{8,10},{9,11},{10,... | collective-permute-start | bytes 6291464 | tf_op jit(solution)/shard_map/ppermute | solution.py:522
  73.0 73.0 %collective-permute-start.3 = (bf16[512,1280]{1,0:T(8,128)(2,1)S(1)}, bf16[512,1280]{1,0:T(8,128)(2,1)}, u32[]{:S(2)}, u32[]{:S(2)}) collective-permute-start(bf16[512,1280]{1,0:T(8,128)(2,1)S(1)} %pad_maximum_fusion.1.refs_0_), channel_id=1, source_target_pairs={{0,1},{1,0},{2,3},{3,2},{4,5},{5,4},{6,7},{7,6},{8,9},{9,8},{10,11... | collective-permute-start | bytes 3932168 | tf_op jit(solution)/shard_map/ppermute | solution.py:527
  73.0 163.4 %reduce-scatter.11.cloned.1.call-start = ((), (), s32[]{:S(2)}) async-start(), calls=%async_computation.12 | async-start | bytes 2621440 | tf_op jit(solution)/shard_map/reduce_scatter | solution.py:575
  81.4 55.8 %collective-permute-start.12 = (bf16[512,512]{1,0:T(8,128)(2,1)}, bf16[512,512]{1,0:T(8,128)(2,1)}, u32[]{:S(2)}, u32[]{:S(2)}) collective-permute-start(bf16[512,512]{1,0:T(8,128)(2,1)} %slice.292), channel_id=1, source_target_pairs={{0,12},{4,0},{8,4},{12,8},{1,13},{5,1},{9,5},{13,9},{2,14},{6,2},{... | collective-permute-start | bytes 1572872 | tf_op jit(solution)/shard_map/ppermute | solution.py:522
  90.5 55.4 %collective-permute-start.5 = (bf16[512,1280]{1,0:T(8,128)(2,1)}, bf16[512,1280]{1,0:T(8,128)(2,1)}, u32[]{:S(2)}, u32[]{:S(2)}) collective-permute-start(bf16[512,1280]{1,0:T(8,128)(2,1)} %copy-done.17), channel_id=1, source_target_pairs={{0,1},{1,0},{2,3},{3,2},{4,5},{5,4},{6,7},{7,6},{8,9},{9,8},{10,11... | collective-permute-start | bytes 3932168 | tf_op jit(solution)/shard_map/ppermute | solution.py:527
  111.8 37.1 %collective-permute-start.6 = (bf16[1024,512]{1,0:T(8,128)(2,1)S(1)}, bf16[1024,512]{1,0:T(8,128)(2,1)}, u32[]{:S(2)}, u32[]{:S(2)}) collective-permute-start(bf16[1024,512]{1,0:T(8,128)(2,1)S(1)} %copy-done.19), channel_id=1, source_target_pairs={{0,1},{1,0},{2,3},{3,2},{4,5},{5,4},{6,7},{7,6},{8,9},{9,8},{10,11... | collective-permute-start | bytes 3145736 | tf_op jit(solution)/shard_map/ppermute | solution.py:527
  137.3 11.6 %collective-permute-start.9 = (bf16[1024,512]{1,0:T(8,128)(2,1)}, bf16[1024,512]{1,0:T(8,128)(2,1)}, u32[]{:S(2)}, u32[]{:S(2)}) collective-permute-start(bf16[1024,512]{1,0:T(8,128)(2,1)} %collective-permute-done.8.refs_2_), channel_id=1, source_target_pairs={{0,1},{1,0},{2,3},{3,2},{4,5},{5,4},{6,7},{7,6},{8,9},{9,8},{10,11... | collective-permute-start | bytes 3145736 | tf_op jit(solution)/shard_map/ppermute | solution.py:527
  171.8 97.9 %reduce-scatter.9.cloned.1.call-start = ((), (), s32[]{:S(2)}) async-start(), calls=%async_computation.9 | async-start | bytes 2621440 | tf_op jit(solution)/shard_map/reduce_scatter | solution.py:575
  172.9 26.2 %collective-permute-start.2 = (bf16[512,512]{1,0:T(8,128)(2,1)S(1)}, bf16[512,512]{1,0:T(8,128)(2,1)S(1)}, u32[]{:S(2)}, u32[]{:S(2)}) collective-permute-start(bf16[512,512]{1,0:T(8,128)(2,1)S(1)} %slice.286), channel_id=1, source_target_pairs={{0,4},{4,8},{8,12},{12,0},{1,5},{5,9},{9,13},{13,1},{2,6},{6,10},{... | collective-permute-start | bytes 1572872 | tf_op jit(solution)/shard_map/ppermute | solution.py:522
  218.8 99.1 %all-gather.11.cloned.1.call-start = ((), (), s32[]{:S(2)}) async-start(), calls=%async_computation.11 | async-start | bytes 2621440 | tf_op jit(solution)/shard_map/all_gather | solution.py:571
  218.8 46.8 %collective-permute-start.17 = (bf16[512,2048]{1,0:T(8,128)(2,1)}, bf16[512,2048]{1,0:T(8,128)(2,1)}, u32[]{:S(2)}, u32[]{:S(2)}) collective-permute-start(bf16[512,2048]{1,0:T(8,128)(2,1)} %all-gather.9.cloned.1.call-done.refs_2_), channel_id=1, source_target_pairs={{0,2},{1,3},{2,0},{3,1},{4,6},{5,7},{6,4},{7,5},{8,10},{9,11},{10,... | collective-permute-start | bytes 6291464 | tf_op jit(solution)/shard_map/ppermute | solution.py:522
  272.4 105.2 %all-gather.13.cloned.1.call-start = ((), (), s32[]{:S(2)}) async-start(), calls=%async_computation.13 | async-start | bytes 2621440 | tf_op jit(solution)/shard_map/all_gather | solution.py:571
  272.5 57.3 %collective-permute-start.15 = (bf16[512,2048]{1,0:T(8,128)(2,1)}, bf16[512,2048]{1,0:T(8,128)(2,1)}, u32[]{:S(2)}, u32[]{:S(2)}) collective-permute-start(bf16[512,2048]{1,0:T(8,128)(2,1)} %all-gather.7.cloned.1.call-done.refs_2_), channel_id=1, source_target_pairs={{0,1},{1,0},{2,3},{3,2},{4,5},{5,4},{6,7},{7,6},{8,9},{9,8},{10,11... | collective-permute-start | bytes 6291464 | tf_op jit(solution)/shard_map/ppermute | solution.py:527
  328.1 234.4 %reduce-scatter.13.cloned.1.call-start = ((), (), s32[]{:S(2)}) async-start(), calls=%async_computation.14 | async-start | bytes 2621440 | tf_op jit(solution)/shard_map/reduce_scatter | solution.py:575
  328.2 48.4 %collective-permute-start.19 = (bf16[512,2048]{1,0:T(8,128)(2,1)}, bf16[512,2048]{1,0:T(8,128)(2,1)}, u32[]{:S(2)}, u32[]{:S(2)}) collective-permute-start(bf16[512,2048]{1,0:T(8,128)(2,1)} %get-tuple-element.145.refs_0_), channel_id=1, source_target_pairs={{0,2},{1,3},{2,0},{3,1},{4,6},{5,7},{6,4},{7,5},{8,10},{9,11},{10,... | collective-permute-start | bytes 6291464 | tf_op jit(solution)/shard_map/ppermute | solution.py:522
  365.8 15.9 %collective-permute-start.21 = (bf16[512,2048]{1,0:T(8,128)(2,1)}, bf16[512,2048]{1,0:T(8,128)(2,1)}, u32[]{:S(2)}, u32[]{:S(2)}) collective-permute-start(bf16[512,2048]{1,0:T(8,128)(2,1)} %collective-permute-done.13.refs_2_), channel_id=1, source_target_pairs={{0,1},{1,0},{2,3},{3,2},{4,5},{5,4},{6,7},{7,6},{8,9},{9,8},{10,11... | collective-permute-start | bytes 6291464 | tf_op jit(solution)/shard_map/ppermute | solution.py:527
  380.2 48.1 %collective-permute-start.29 = (bf16[512,2048]{1,0:T(8,128)(2,1)S(1)}, bf16[512,2048]{1,0:T(8,128)(2,1)S(1)}, u32[]{:S(2)}, u32[]{:S(2)}) collective-permute-start(bf16[512,2048]{1,0:T(8,128)(2,1)S(1)} %get-tuple-element.166.refs_0_), channel_id=1, source_target_pairs={{0,2},{1,3},{2,0},{3,1},{4,6},{5,7},{6,4},{7,5},{8,10},{9,11},{10,... | collective-permute-start | bytes 6291464 | tf_op jit(solution)/shard_map/ppermute | solution.py:522
  415.2 14.5 %collective-permute-start.23 = (bf16[512,2048]{1,0:T(8,128)(2,1)}, bf16[512,2048]{1,0:T(8,128)(2,1)S(1)}, u32[]{:S(2)}, u32[]{:S(2)}) collective-permute-start(bf16[512,2048]{1,0:T(8,128)(2,1)} %get-tuple-element.155), channel_id=1, source_target_pairs={{0,1},{1,0},{2,3},{3,2},{4,5},{5,4},{6,7},{7,6},{8,9},{9,8},{10,11... | collective-permute-start | bytes 6291464 | tf_op jit(solution)/shard_map/ppermute | solution.py:527
  415.5 18.3 %collective-permute-start.25 = (bf16[512,2048]{1,0:T(8,128)(2,1)}, bf16[512,2048]{1,0:T(8,128)(2,1)S(1)}, u32[]{:S(2)}, u32[]{:S(2)}) collective-permute-start(bf16[512,2048]{1,0:T(8,128)(2,1)} %all-gather.9.cloned.1.call-done.refs_2_), channel_id=1, source_target_pairs={{0,1},{1,0},{2,3},{3,2},{4,5},{5,4},{6,7},{7,6},{8,9},{9,8},{10,11... | collective-permute-start | bytes 6291464 | tf_op jit(solution)/shard_map/ppermute | solution.py:527
  415.8 18.0 %collective-permute-start.24 = (bf16[512,2048]{1,0:T(8,128)(2,1)S(1)}, bf16[512,2048]{1,0:T(8,128)(2,1)S(1)}, u32[]{:S(2)}, u32[]{:S(2)}) collective-permute-start(bf16[512,2048]{1,0:T(8,128)(2,1)S(1)} %get-tuple-element.166.refs_0_), channel_id=1, source_target_pairs={{0,1},{1,0},{2,3},{3,2},{4,5},{5,4},{6,7},{7,6},{8,9},{9,8},{10,11... | collective-permute-start | bytes 6291464 | tf_op jit(solution)/shard_map/ppermute | solution.py:527
  425.5 53.9 %collective-permute-start.27 = (bf16[512,2048]{1,0:T(8,128)(2,1)}, bf16[512,2048]{1,0:T(8,128)(2,1)}, u32[]{:S(2)}, u32[]{:S(2)}) collective-permute-start(bf16[512,2048]{1,0:T(8,128)(2,1)} %get-tuple-element.164), channel_id=1, source_target_pairs={{0,1},{1,0},{2,3},{3,2},{4,5},{5,4},{6,7},{7,6},{8,9},{9,8},{10,11... | collective-permute-start | bytes 6291464 | tf_op jit(solution)/shard_map/ppermute | solution.py:527
  432.4 47.0 %collective-permute-start.31 = (bf16[512,2048]{1,0:T(8,128)(2,1)S(1)}, bf16[512,2048]{1,0:T(8,128)(2,1)}, u32[]{:S(2)}, u32[]{:S(2)}) collective-permute-start(bf16[512,2048]{1,0:T(8,128)(2,1)S(1)} %add_convert_fusion.8), channel_id=1, source_target_pairs={{0,2},{1,3},{2,0},{3,1},{4,6},{5,7},{6,4},{7,5},{8,10},{9,11},{10,... | collective-permute-start | bytes 6291464 | tf_op jit(solution)/shard_map/ppermute | solution.py:522
  470.0 14.3 %collective-permute-start.33 = (bf16[512,2048]{1,0:T(8,128)(2,1)}, bf16[512,2048]{1,0:T(8,128)(2,1)}, u32[]{:S(2)}, u32[]{:S(2)}) collective-permute-start(bf16[512,2048]{1,0:T(8,128)(2,1)} %collective-permute-done.17.refs_2_), channel_id=1, source_target_pairs={{0,1},{1,0},{2,3},{3,2},{4,5},{5,4},{6,7},{7,6},{8,9},{9,8},{10,11... | collective-permute-start | bytes 6291464 | tf_op jit(solution)/shard_map/ppermute | solution.py:527
  471.3 13.1 %collective-permute-start.32 = (bf16[512,2048]{1,0:T(8,128)(2,1)}, bf16[512,2048]{1,0:T(8,128)(2,1)}, u32[]{:S(2)}, u32[]{:S(2)}) collective-permute-start(bf16[512,2048]{1,0:T(8,128)(2,1)} %copy-done.92), channel_id=1, source_target_pairs={{0,1},{1,0},{2,3},{3,2},{4,5},{5,4},{6,7},{7,6},{8,9},{9,8},{10,11... | collective-permute-start | bytes 6291464 | tf_op jit(solution)/shard_map/ppermute | solution.py:527
  517.6 118.8 %reduce-scatter.15.cloned.1.call-start = ((), (), s32[]{:S(2)}) async-start(), calls=%async_computation.15 | async-start | bytes 2621440 | tf_op jit(solution)/shard_map/reduce_scatter | solution.py:575
  527.9 47.8 %collective-permute-start.37 = (bf16[512,2048]{1,0:T(8,128)(2,1)}, bf16[512,2048]{1,0:T(8,128)(2,1)}, u32[]{:S(2)}, u32[]{:S(2)}) collective-permute-start(bf16[512,2048]{1,0:T(8,128)(2,1)} %add_convert_fusion.6), channel_id=1, source_target_pairs={{0,2},{1,3},{2,0},{3,1},{4,6},{5,7},{6,4},{7,5},{8,10},{9,11},{10,... | collective-permute-start | bytes 6291464 | tf_op jit(solution)/shard_map/ppermute | solution.py:522
  528.7 47.0 %collective-permute-start.39 = (bf16[512,2048]{1,0:T(8,128)(2,1)}, bf16[512,2048]{1,0:T(8,128)(2,1)}, u32[]{:S(2)}, u32[]{:S(2)}) collective-permute-start(bf16[512,2048]{1,0:T(8,128)(2,1)} %get-tuple-element.183), channel_id=1, source_target_pairs={{0,1},{1,0},{2,3},{3,2},{4,5},{5,4},{6,7},{7,6},{8,9},{9,8},{10,11... | collective-permute-start | bytes 6291464 | tf_op jit(solution)/shard_map/ppermute | solution.py:527
  580.5 89.9 %all-gather.17.cloned.1.call-start = ((), (), s32[]{:S(2)}) async-start(), calls=%async_computation.19 | async-start | bytes 2621440 | tf_op jit(solution)/shard_map/all_gather | solution.py:571
  581.7 118.8 %collective-permute-start.16 = (bf16[512,2048]{1,0:T(8,128)(2,1)}, bf16[512,2048]{1,0:T(8,128)(2,1)}, u32[]{:S(2)}, u32[]{:S(2)}) collective-permute-start(bf16[512,2048]{1,0:T(8,128)(2,1)} %get-tuple-element.138), channel_id=1, source_target_pairs={{0,1},{1,0},{2,3},{3,2},{4,5},{5,4},{6,7},{7,6},{8,9},{9,8},{10,11... | collective-permute-start | bytes 6291464 | tf_op jit(solution)/shard_map/ppermute | solution.py:527
  594.5 122.0 %all-gather.15.cloned.1.call-start = ((), (), s32[]{:S(2)}) async-start(), calls=%async_computation.16 | async-start | bytes 2621440 | tf_op jit(solution)/shard_map/all_gather | solution.py:571
  633.7 65.4 %collective-permute-start.44 = (bf16[1024,768]{1,0:T(8,128)(2,1)}, bf16[1024,768]{1,0:T(8,128)(2,1)}, u32[]{:S(2)}, u32[]{:S(2)}) collective-permute-start(bf16[1024,768]{1,0:T(8,128)(2,1)} %get-tuple-element.293), channel_id=1, source_target_pairs={{0,16},{16,0},{1,17},{17,1},{2,18},{18,2},{3,19},{19,3},{4,20},{20... | collective-permute-start | bytes 4718600 | tf_op jit(solution)/shard_map/ppermute | solution.py:527
  635.3 65.2 %collective-permute-start.38 = (bf16[512,2048]{1,0:T(8,128)(2,1)}, bf16[512,2048]{1,0:T(8,128)(2,1)}, u32[]{:S(2)}, u32[]{:S(2)}) collective-permute-start(bf16[512,2048]{1,0:T(8,128)(2,1)} %add_convert_fusion.9), channel_id=1, source_target_pairs={{0,2},{1,3},{2,0},{3,1},{4,6},{5,7},{6,4},{7,5},{8,10},{9,11},{10,... | collective-permute-start | bytes 6291464 | tf_op jit(solution)/shard_map/ppermute | solution.py:522
  640.0 188.5 %reduce-scatter.21.cloned.1.call-start = ((), (), s32[]{:S(2)}) async-start(), calls=%async_computation.20 | async-start | bytes 2621440 | tf_op jit(solution)/shard_map/reduce_scatter | solution.py:575
  697.8 262.8 %reduce-scatter.17.cloned.1.call-start = ((), (), s32[]{:S(2)}) async-start(), calls=%async_computation.17 | async-start | bytes 2621440 | tf_op jit(solution)/shard_map/reduce_scatter | solution.py:575
  699.1 51.5 %collective-permute-start.50 = (bf16[512,2048]{1,0:T(8,128)(2,1)}, bf16[512,2048]{1,0:T(8,128)(2,1)}, u32[]{:S(2)}, u32[]{:S(2)}) collective-permute-start(bf16[512,2048]{1,0:T(8,128)(2,1)} %get-tuple-element.212), channel_id=1, source_target_pairs={{0,1},{1,0},{2,3},{3,2},{4,5},{5,4},{6,7},{7,6},{8,9},{9,8},{10,11... | collective-permute-start | bytes 6291464 | tf_op jit(solution)/shard_map/ppermute | solution.py:527
  699.1 48.9 %collective-permute-start.45 = (bf16[1024,768]{1,0:T(8,128)(2,1)}, bf16[1024,768]{1,0:T(8,128)(2,1)}, u32[]{:S(2)}, u32[]{:S(2)}) collective-permute-start(bf16[1024,768]{1,0:T(8,128)(2,1)} %get-tuple-element.204), channel_id=1, source_target_pairs={{0,16},{16,0},{1,17},{17,1},{2,18},{18,2},{3,19},{19,3},{4,20},{20... | collective-permute-start | bytes 4718600 | tf_op jit(solution)/shard_map/ppermute | solution.py:527
  744.0 218.8 %reduce-scatter.23.cloned.1.call-start = ((), (), s32[]{:S(2)}) async-start(), calls=%async_computation.21 | async-start | bytes 2621440 | tf_op jit(solution)/shard_map/reduce_scatter | solution.py:575
  748.0 36.4 %collective-permute-start.46 = (bf16[1024,768]{1,0:T(8,128)(2,1)}, bf16[1024,768]{1,0:T(8,128)(2,1)}, u32[]{:S(2)}, u32[]{:S(2)}) collective-permute-start(bf16[1024,768]{1,0:T(8,128)(2,1)} %get-tuple-element.205), channel_id=1, source_target_pairs={{0,16},{16,0},{1,17},{17,1},{2,18},{18,2},{3,19},{19,3},{4,20},{20... | collective-permute-start | bytes 4718600 | tf_op jit(solution)/shard_map/ppermute | solution.py:527
  750.6 52.1 %collective-permute-start.49 = (bf16[512,2048]{1,0:T(8,128)(2,1)}, bf16[512,2048]{1,0:T(8,128)(2,1)}, u32[]{:S(2)}, u32[]{:S(2)}) collective-permute-start(bf16[512,2048]{1,0:T(8,128)(2,1)} %get-tuple-element.210), channel_id=1, source_target_pairs={{0,1},{1,0},{2,3},{3,2},{4,5},{5,4},{6,7},{7,6},{8,9},{9,8},{10,11... | collective-permute-start | bytes 6291464 | tf_op jit(solution)/shard_map/ppermute | solution.py:527
  754.3 48.3 %collective-permute-start.51 = (bf16[512,2048]{1,0:T(8,128)(2,1)}, bf16[512,2048]{1,0:T(8,128)(2,1)}, u32[]{:S(2)}, u32[]{:S(2)}) collective-permute-start(bf16[512,2048]{1,0:T(8,128)(2,1)} %add_convert_fusion.3), channel_id=1, source_target_pairs={{0,2},{1,3},{2,0},{3,1},{4,6},{5,7},{6,4},{7,5},{8,10},{9,11},{10,... | collective-permute-start | bytes 6291464 | tf_op jit(solution)/shard_map/ppermute | solution.py:522
  767.1 24.5 %collective-permute-start.53 = (f32[512]{0:T(512)S(1)}, f32[512]{0:T(512)S(1)}, u32[]{:S(2)}, u32[]{:S(2)}) collective-permute-start(f32[512]{0:T(512)S(1)} %add.372), channel_id=1, source_target_pairs={{0,8},{4,12},{8,0},{12,4},{1,9},{5,13},{9,1},{13,5},{2,10},{6,14},... | collective-permute-start | bytes 6152 | tf_op jit(solution)/shard_map/ppermute | solution.py:527
  784.3 35.5 %collective-permute-start.47 = (bf16[1024,768]{1,0:T(8,128)(2,1)}, bf16[1024,768]{1,0:T(8,128)(2,1)}, u32[]{:S(2)}, u32[]{:S(2)}) collective-permute-start(bf16[1024,768]{1,0:T(8,128)(2,1)} %get-tuple-element.206), channel_id=1, source_target_pairs={{0,16},{16,0},{1,17},{17,1},{2,18},{18,2},{3,19},{19,3},{4,20},{20... | collective-permute-start | bytes 4718600 | tf_op jit(solution)/shard_map/ppermute | solution.py:527
  819.8 34.6 %collective-permute-start.48 = (bf16[384,2048]{1,0:T(8,128)(2,1)}, bf16[384,2048]{1,0:T(8,128)(2,1)}, u32[]{:S(2)}, u32[]{:S(2)}) collective-permute-start(bf16[384,2048]{1,0:T(8,128)(2,1)} %get-tuple-element.207), channel_id=1, source_target_pairs={{0,16},{16,0},{1,17},{17,1},{2,18},{18,2},{3,19},{19,3},{4,20},{20... | collective-permute-start | bytes 4718600 | tf_op jit(solution)/shard_map/ppermute | solution.py:527
  830.8 134.2 %reduce-scatter.19.cloned.1.call-start = ((), (), s32[]{:S(2)}) async-start(), calls=%async_computation.18 | async-start | bytes 2621440 | tf_op jit(solution)/shard_map/reduce_scatter | solution.py:575
  839.3 16.6 %collective-permute-start.62 = (bf16[1024,512]{1,0:T(8,128)(2,1)S(1)}, bf16[1024,512]{1,0:T(8,128)(2,1)S(1)}, u32[]{:S(2)}, u32[]{:S(2)}) collective-permute-start(bf16[1024,512]{1,0:T(8,128)(2,1)S(1)} %get-tuple-element.287), channel_id=1, source_target_pairs={{0,1},{1,0},{2,3},{3,2},{4,5},{5,4},{6,7},{7,6},{8,9},{9,8},{10,11... | collective-permute-start | bytes 3145736 | tf_op jit(solution)/shard_map/ppermute | solution.py:527
  839.3 43.9 %collective-permute-start.65 = (bf16[1024,512]{1,0:T(8,128)(2,1)}, bf16[1024,512]{1,0:T(8,128)(2,1)}, u32[]{:S(2)}, u32[]{:S(2)}) collective-permute-start(bf16[1024,512]{1,0:T(8,128)(2,1)} %get-tuple-element.286), channel_id=1, source_target_pairs={{0,1},{1,0},{2,3},{3,2},{4,5},{5,4},{6,7},{7,6},{8,9},{9,8},{10,11... | collective-permute-start | bytes 3145736 | tf_op jit(solution)/shard_map/ppermute | solution.py:527
  854.4 33.7 %collective-permute-start.66 = (bf16[384,2048]{1,0:T(8,128)(2,1)}, bf16[384,2048]{1,0:T(8,128)(2,1)}, u32[]{:S(2)}, u32[]{:S(2)}) collective-permute-start(bf16[384,2048]{1,0:T(8,128)(2,1)} %get-tuple-element.226), channel_id=1, source_target_pairs={{0,16},{16,0},{1,17},{17,1},{2,18},{18,2},{3,19},{19,3},{4,20},{20... | collective-permute-start | bytes 4718600 | tf_op jit(solution)/shard_map/ppermute | solution.py:527
  857.3 25.4 %collective-permute-start.63 = (bf16[1024,512]{1,0:T(8,128)(2,1)}, bf16[1024,512]{1,0:T(8,128)(2,1)}, u32[]{:S(2)}, u32[]{:S(2)}) collective-permute-start(bf16[1024,512]{1,0:T(8,128)(2,1)} %add_convert_fusion.13), channel_id=1, source_target_pairs={{0,2},{1,3},{2,0},{3,1},{4,6},{5,7},{6,4},{7,5},{8,10},{9,11},{10,... | collective-permute-start | bytes 3145736 | tf_op jit(solution)/shard_map/ppermute | solution.py:522
  864.4 37.2 %collective-permute-start.71 = (bf16[512,1024]{1,0:T(8,128)(2,1)}, bf16[512,1024]{1,0:T(8,128)(2,1)}, u32[]{:S(2)}, u32[]{:S(2)}) collective-permute-start(bf16[512,1024]{1,0:T(8,128)(2,1)} %get-tuple-element.285), channel_id=1, source_target_pairs={{0,1},{1,0},{2,3},{3,2},{4,5},{5,4},{6,7},{7,6},{8,9},{9,8},{10,11... | collective-permute-start | bytes 3145736 | tf_op jit(solution)/shard_map/ppermute | solution.py:527
  869.5 13.2 %collective-permute-start.57 = (f32[37120]{0:T(1024)S(1)}, f32[37120]{0:T(1024)S(1)}, u32[]{:S(2)}, u32[]{:S(2)}) collective-permute-start(f32[37120]{0:T(1024)S(1)} %add.384), channel_id=1, source_target_pairs={{0,2},{1,3},{2,0},{3,1},{4,6},{5,7},{6,4},{7,5},{8,10},{9,11},{10,... | collective-permute-start | bytes 445448 | tf_op jit(solution)/shard_map/ppermute | solution.py:527
  882.7 42.0 %collective-permute-start.60 = (bf16[512,256]{0,1:T(8,128)(2,1)S(1)}, bf16[512,256]{0,1:T(8,128)(2,1)S(1)}, u32[]{:S(2)}, u32[]{:S(2)}) collective-permute-start(bf16[512,256]{0,1:T(8,128)(2,1)S(1)} %get-tuple-element.300), channel_id=1, source_target_pairs={{0,1},{1,0},{2,3},{3,2},{4,5},{5,4},{6,7},{7,6},{8,9},{9,8},{10,11... | collective-permute-start | bytes 786440 | tf_op jit(solution)/shard_map/ppermute | solution.py:527
  883.3 52.2 %collective-permute-start.70 = (bf16[512,1024]{1,0:T(8,128)(2,1)}, bf16[512,1024]{1,0:T(8,128)(2,1)S(1)}, u32[]{:S(2)}, u32[]{:S(2)}) collective-permute-start(bf16[512,1024]{1,0:T(8,128)(2,1)} %get-tuple-element.284), channel_id=1, source_target_pairs={{0,1},{1,0},{2,3},{3,2},{4,5},{5,4},{6,7},{7,6},{8,9},{9,8},{10,11... | collective-permute-start | bytes 3145736 | tf_op jit(solution)/shard_map/ppermute | solution.py:527
  888.1 12.5 %collective-permute-start.58 = (f32[37120]{0:T(1024)S(1)}, f32[37120]{0:T(1024)S(1)}, u32[]{:S(2)}, u32[]{:S(2)}) collective-permute-start(f32[37120]{0:T(1024)S(1)} %add.385), channel_id=1, source_target_pairs={{0,4},{4,0},{8,12},{12,8},{1,5},{5,1},{9,13},{13,9},{2,6},{6,2},{1... | collective-permute-start | bytes 445448 | tf_op jit(solution)/shard_map/ppermute | solution.py:527
  888.1 36.7 %collective-permute-start.67 = (bf16[1024,512]{1,0:T(8,128)(2,1)S(1)}, bf16[1024,512]{1,0:T(8,128)(2,1)S(1)}, u32[]{:S(2)}, u32[]{:S(2)}) collective-permute-start(bf16[1024,512]{1,0:T(8,128)(2,1)S(1)} %add_convert_fusion.12), channel_id=1, source_target_pairs={{0,16},{16,0},{1,17},{17,1},{2,18},{18,2},{3,19},{19,3},{4,20},{20... | collective-permute-start | bytes 3145736 | tf_op jit(solution)/shard_map/ppermute | solution.py:527
  900.6 18.5 %collective-permute-start.59 = (f32[37120]{0:T(1024)S(1)}, f32[37120]{0:T(1024)S(1)}, u32[]{:S(2)}, u32[]{:S(2)}) collective-permute-start(f32[37120]{0:T(1024)S(1)} %add.386), channel_id=1, source_target_pairs={{0,8},{4,12},{8,0},{12,4},{1,9},{5,13},{9,1},{13,5},{2,10},{6,14},... | collective-permute-start | bytes 445448 | tf_op jit(solution)/shard_map/ppermute | solution.py:527
  909.6 20.8 %collective-permute-start.72 = (bf16[512,1024]{1,0:T(8,128)(2,1)S(1)}, bf16[512,1024]{1,0:T(8,128)(2,1)S(1)}, u32[]{:S(2)}, u32[]{:S(2)}) collective-permute-start(bf16[512,1024]{1,0:T(8,128)(2,1)S(1)} %add_convert_fusion.11), channel_id=1, source_target_pairs={{0,2},{1,3},{2,0},{3,1},{4,6},{5,7},{6,4},{7,5},{8,10},{9,11},{10,... | collective-permute-start | bytes 3145736 | tf_op jit(solution)/shard_map/ppermute | solution.py:522
  932.0 14.3 %collective-permute-start.74 = (bf16[512,256]{0,1:T(8,128)(2,1)S(1)}, bf16[512,256]{0,1:T(8,128)(2,1)S(1)}, u32[]{:S(2)}, u32[]{:S(2)}) collective-permute-start(bf16[512,256]{0,1:T(8,128)(2,1)S(1)} %get-tuple-element.275), channel_id=1, source_target_pairs={{0,12},{4,0},{8,4},{12,8},{1,13},{5,1},{9,5},{13,9},{2,14},{6,2},{... | collective-permute-start | bytes 786440 | tf_op jit(solution)/shard_map/ppermute | solution.py:522
  948.2 22.6 %collective-permute-start.73 = (bf16[512,1024]{1,0:T(8,128)(2,1)}, bf16[512,1024]{1,0:T(8,128)(2,1)}, u32[]{:S(2)}, u32[]{:S(2)}) collective-permute-start(bf16[512,1024]{1,0:T(8,128)(2,1)} %add_convert_fusion.10), channel_id=1, source_target_pairs={{0,16},{16,0},{1,17},{17,1},{2,18},{18,2},{3,19},{19,3},{4,20},{20... | collective-permute-start | bytes 3145736 | tf_op jit(solution)/shard_map/ppermute | solution.py:527
  (132 other events, 1820.6 us)
Sparse Core Ops, SparseCore 0:
  10.2 51.7 all-gather.6
  73.1 76.1 all-gather.8
  171.9 52.3 reduce-scatter.10
  227.2 42.5 reduce-scatter.8
  272.6 45.3 all-gather.10
  328.3 44.7 all-gather.12
  517.7 44.7 reduce-scatter.12
  580.7 42.5 reduce-scatter.14
  624.8 45.5 all-gather.16
  671.8 44.6 all-gather.14
  718.8 42.6 reduce-scatter.20
  763.7 43.1 reduce-scatter.16
  830.9 42.4 reduce-scatter.22
  876.2 49.4 reduce-scatter.18

commit v4 on v3

--- a/solution.py
+++ b/solution.py
@@ -1,4 +1,5 @@
 import functools
+import math
 
 import jax
 import jax.numpy as jnp
@@ -254,22 +255,36 @@
     y_out, x_out = refs[0:2], refs[2:4]
     small_out, logits_out, gates_out = refs[4:7]
     kept_out = refs[7:12]
-    (token, grad, gate_w, up_w, down_w, y_buf, x_buf, rows_in, rows_grad, rows_dy, rows_u, rows_da, rows_db, in_sem, grad_sem, w_sem, out_sem, kept_sem) = refs[12:]
+    (token, grad, gate_w, up_w, down_w, y_buf, x_buf, rows_in, rows_grad, rows_u, rows_da, rows_db, in_sem, grad_sem, w_sem, out_sem, kept_sem) = refs[12:]
     capacity = rows_in.shape[0] // 2
     tokens, width = token.shape[1:]
     hidden = gate_w.shape[1]
     load_tok = [pltpu.make_async_copy(token_in[g], token.at[g], in_sem.at[g]) for g in range(2)]
-    load_grad = [pltpu.make_async_copy(grad_in[g], grad.at[g], grad_sem.at[g]) for g in range(2)]
+    parts = grad_sem.shape[1]
+    strip = width // parts
+    load_grad = []
+    for g in range(2):
+        for d in range(parts):
+            there = pl.multiple_of((scalars_ref[1] + d) % parts * strip, strip)
+            load_grad.append(
+                pltpu.make_async_copy(
+                    grad_in[g].at[:, d * strip : (d + 1) * strip],
+                    grad.at[g, :, pl.ds(there, strip)],
+                    grad_sem.at[g, d],
+                )
+            )
     load_w = [
         pltpu.make_async_copy(src, dst, w_sem.at[i])
         for i, (src, dst) in enumerate(zip(weights_in, (gate_w, up_w, down_w)))
     ]
     load_tok[0].start()
-    load_grad[0].start()
+    for load in load_grad[:parts]:
+        load.start()
     for load in load_w:
         load.start()
     load_tok[1].start()
-    load_grad[1].start()
+    for load in load_grad[parts:]:
+        load.start()
     expert = scalars_ref[0]
     stores = []
     wide = min(512, width)
@@ -292,14 +307,13 @@
         pick = jnp.where(chosen, 1.0, 0.0).astype(BF16)
         here = slice(g * capacity, (g + 1) * capacity)
         gate_cols.append(slot_gates)
-        load_grad[g].wait()
+        for load in load_grad[g * parts : (g + 1) * parts]:
+            load.wait()
 
         def gather(j, _):
             at = pl.ds(pl.multiple_of(j * wide, wide), wide)
             rows_in[here, at] = mm(pick, token[g, :, at]).astype(BF16)
-            found = mm(pick, grad[g, :, at])
-            rows_grad[here, at] = found.astype(BF16)
-            rows_dy[here, at] = (slot_gates * found).astype(BF16)
+            rows_grad[here, at] = mm(pick, grad[g, :, at]).astype(BF16)
             return 0
 
         lax.fori_loop(0, width // wide, gather, 0)
@@ -307,21 +321,29 @@
         load.wait()
     slot_gates = jnp.concatenate(gate_cols, axis=0)
 
-    def middle(j, _):
+    def middle(j, carry):
+        dots, inner = carry
         at = pl.ds(pl.multiple_of(j * step, step), step)
         a = mm(rows_in[...], gate_w[:, at])
         b = mm(rows_in[...], up_w[:, at])
-        du = mm_nt(rows_dy[...], down_w[at, :]).astype(BF16).astype(F32)
+        raw = mm_nt(rows_grad[...], down_w[at, :])
         sig = 1.0 / (1.0 + jnp.exp(-a))
         silu = a * sig
-        rows_u[:, at] = (silu * b).astype(BF16)
-        rows_da[:, at] = (du * b * sig * (1.0 + a * (1.0 - sig))).astype(BF16)
-        rows_db[:, at] = (du * silu).astype(BF16)
-        return 0
-
-    lax.fori_loop(0, hidden // step, middle, 0)
+        u = (silu * b).astype(BF16).astype(F32)
+        dots = dots + jnp.sum(raw * u, axis=1, keepdims=True)
+        du = (slot_gates * raw).astype(BF16).astype(F32)
+        da = du * b * sig * (1.0 + a * (1.0 - sig))
+        db = du * silu
+        inner = inner + jnp.sum(da * a + db * b, axis=1, keepdims=True)
+        rows_u[:, at] = (slot_gates * u).astype(BF16)
+        rows_da[:, at] = da.astype(BF16)
+        rows_db[:, at] = db.astype(BF16)
+        return dots, inner
+
+    nothing = jnp.zeros((2 * capacity, 1), F32)
+    dots, inner = lax.fori_loop(0, hidden // step, middle, (nothing, nothing))
     kept_here = pl.ds(place * 2 * capacity, 2 * capacity)
-    for i, kept_rows in enumerate((rows_in, rows_dy, rows_u, rows_da, rows_db)):
+    for i, kept_rows in enumerate((rows_in, rows_grad, rows_u, rows_da, rows_db)):
         store = pltpu.make_async_copy(kept_rows, kept_out[i].at[kept_here, :], kept_sem.at[i])
         store.start()
         stores.append(store)
@@ -331,37 +353,29 @@
         ).astype(BF16)
         for g in range(2)
     ]
-
-    def back(j, carry):
-        dots, inner = carry
-        at = pl.ds(pl.multiple_of(j * wide, wide), wide)
-        y = mm(rows_u[...], down_w[:, at]).astype(BF16).astype(F32)
-        dots = dots + jnp.sum(rows_grad[:, at].astype(F32) * y, axis=1, keepdims=True)
-        low = (slot_gates * y).astype(BF16)
+    for j in range(width // wide):
+        at = slice(j * wide, (j + 1) * wide)
         dx = mm_nt(rows_da[...], gate_w[at, :]) + mm_nt(rows_db[...], up_w[at, :])
-        inner = inner + jnp.sum(rows_in[:, at].astype(F32) * dx, axis=1, keepdims=True)
-        dx_low = dx.astype(BF16)
-        for g in range(2):
-            here = slice(g * capacity, (g + 1) * capacity)
-            y_buf[g, :, at] = mm(spreads[g], low[here]).astype(BF16)
-            x_buf[g, :, at] = mm(spreads[g], dx_low[here]).astype(BF16)
-        return dots, inner
-
-    nothing = jnp.zeros((2 * capacity, 1), F32)
-    dots, inner = lax.fori_loop(0, width // wide, back, (nothing, nothing))
+        y = mm(rows_u[...], down_w[:, at])
+        for i, (rows, buf, out) in enumerate(((dx, x_buf, x_out), (y, y_buf, y_out))):
+            low = rows.astype(BF16)
+            for g in range(2):
+                here = slice(g * capacity, (g + 1) * capacity)
+                buf[g, :, at] = mm(spreads[g], low[here]).astype(BF16)
+                store = pltpu.make_async_copy(
+                    buf.at[g, :, at], out[g].at[:, at], out_sem.at[i, g, j]
+                )
+                store.start()
+                stores.append(store)
+    small_row = lax.broadcasted_iota(jnp.int32, small_out.shape[1:], 0)
     for g in range(2):
         here = slice(g * capacity, (g + 1) * capacity)
         chosen = lax.broadcasted_iota(jnp.int32, (capacity, tokens), 0) == slots_ref[g]
-        small_row = lax.broadcasted_iota(jnp.int32, small_out.shape[1:], 0)
         dots_row = jnp.sum(jnp.where(chosen, dots[here], 0.0), axis=0, keepdims=True)
         inner_row = jnp.sum(jnp.where(chosen, inner[here], 0.0), axis=0, keepdims=True)
         small_out[g] = jnp.where(small_row == expert, dots_row, 0.0) + jnp.where(
             small_row == experts, inner_row, 0.0
         )
-        for i, (buf, out) in enumerate(((x_buf, x_out), (y_buf, y_out))):
-            store = pltpu.make_async_copy(buf.at[g], out[g], out_sem.at[i, g])
-            store.start()
-            stores.append(store)
     for store in stores:
         store.wait()
 
@@ -375,6 +389,7 @@
     anywhere = pl.BlockSpec(memory_space=pl.ANY)
     inside = pl.BlockSpec(memory_space=pltpu.VMEM)
     first = kept is None
+    parts = lax.axis_size("row")
     small_rows = (experts + 8) // 8 * 8
     dense = jax.ShapeDtypeStruct((rows, width), BF16)
     kept_shapes = [jax.ShapeDtypeStruct((total, w), BF16) for w in (width, width, hidden, hidden, hidden)]
@@ -395,14 +410,13 @@
             pltpu.VMEM((2, rows, width), BF16),
             pltpu.VMEM((2 * capacity, width), BF16),
             pltpu.VMEM((2 * capacity, width), BF16),
-            pltpu.VMEM((2 * capacity, width), BF16),
             pltpu.VMEM((2 * capacity, hidden), BF16),
             pltpu.VMEM((2 * capacity, hidden), BF16),
             pltpu.VMEM((2 * capacity, hidden), BF16),
             pltpu.SemaphoreType.DMA((2,)),
-            pltpu.SemaphoreType.DMA((2,)),
+            pltpu.SemaphoreType.DMA((2, parts)),
             pltpu.SemaphoreType.DMA((3,)),
-            pltpu.SemaphoreType.DMA((2, 2)),
+            pltpu.SemaphoreType.DMA((2, 2, width // min(512, width))),
             pltpu.SemaphoreType.DMA((5,)),
         ],
         compiler_params=pltpu.CompilerParams(vmem_limit_bytes=56 << 20),
@@ -485,36 +499,82 @@
     )(starts, *pieces)
 
 
-def halves_kernel(own_ref, one_ref, two_ref, out_ref):
-    early = pl.program_id(0) < pl.num_programs(0) // 2
-
-    @pl.when(early)
-    def _():
-        out_ref[...] = own_ref[...].astype(F32) + one_ref[...].astype(F32)
-
-    @pl.when(jnp.logical_not(early))
-    def _():
-        out_ref[...] = own_ref[...].astype(F32) + two_ref[...].astype(F32)
-
-
-def halves_sum(own, one, two):
+def pieces_kernel(counts, own_ref, *refs):
+    out_ref = refs[-1]
+    step, start = pl.program_id(0), 0
+    for count, piece in zip(counts, refs[:-1]):
+
+        @pl.when(jnp.logical_and(step >= start, step < start + count))
+        def _():
+            out_ref[...] = own_ref[...].astype(F32) + piece[...].astype(F32)
+
+        start += count
+
+
+def pieces_sum(own, pieces):
     rows, width = own.shape
-    half = 2
-    block = rows // (2 * half)
+    block = math.gcd(*[piece.shape[0] for piece in pieces])
+    counts = [piece.shape[0] // block for piece in pieces]
+    specs, start = [pl.BlockSpec((block, width), lambda i: (i, 0))], 0
+    for count in counts:
+        specs.append(
+            pl.BlockSpec(
+                (block, width), lambda i, s=start, c=count: (jnp.clip(i - s, 0, c - 1), 0)
+            )
+        )
+        start += count
     return pl.pallas_call(
-        halves_kernel,
-        grid=(2 * half,),
+        functools.partial(pieces_kernel, counts),
+        grid=(rows // block,),
         out_shape=jax.ShapeDtypeStruct((rows, width), F32),
-        in_specs=[
-            pl.BlockSpec((block, width), lambda i: (i, 0)),
-            pl.BlockSpec((block, width), lambda i: (jnp.minimum(i, half - 1), 0)),
-            pl.BlockSpec((block, width), lambda i: (jnp.maximum(i - half, 0), 0)),
-        ],
+        in_specs=specs,
         out_specs=pl.BlockSpec((block, width), lambda i: (i, 0)),
         compiler_params=pltpu.CompilerParams(vmem_limit_bytes=32 << 20),
         cost_estimate=pl.CostEstimate(flops=4000000000, bytes_accessed=12000000, transcendentals=0),
-        name="halves_sum",
-    )(own, one, two)
+        name="pieces_sum",
+    )(own, *pieces)
+
+
+def grads_kernel(rows_ref, *refs):
+    half = len(refs) // 2
+    for grad_ref, out_ref in zip(refs[:half], refs[half:]):
+        out_ref[...] = mm_tn(rows_ref[...], grad_ref[...]).astype(BF16)
+
+
+def grads_of(rows_in, *grads):
+    count, width = rows_in.shape
+    hidden = grads[0].shape[1]
+    block = min(512, width)
+    return pl.pallas_call(
+        grads_kernel,
+        grid=(width // block,),
+        out_shape=[jax.ShapeDtypeStruct((width, hidden), BF16)] * len(grads),
+        in_specs=[pl.BlockSpec((count, block), lambda i: (0, i))]
+        + [pl.BlockSpec((count, hidden), lambda i: (0, 0))] * len(grads),
+        out_specs=[pl.BlockSpec((block, hidden), lambda i: (i, 0))] * len(grads),
+        compiler_params=pltpu.CompilerParams(vmem_limit_bytes=56 << 20),
+        cost_estimate=pl.CostEstimate(flops=1000000000, bytes_accessed=1000000, transcendentals=0),
+        name="grads_of",
+    )(rows_in, *grads)
+
+
+def grad_of(rows_u, rows_grad):
+    count, hidden = rows_u.shape
+    width = rows_grad.shape[1]
+    block = min(512, width)
+    return pl.pallas_call(
+        grads_kernel,
+        grid=(width // block,),
+        out_shape=[jax.ShapeDtypeStruct((hidden, width), BF16)],
+        in_specs=[
+            pl.BlockSpec((count, hidden), lambda i: (0, 0)),
+            pl.BlockSpec((count, block), lambda i: (0, i)),
+        ],
+        out_specs=[pl.BlockSpec((hidden, block), lambda i: (0, i))],
+        compiler_params=pltpu.CompilerParams(vmem_limit_bytes=56 << 20),
+        cost_estimate=pl.CostEstimate(flops=1000000000, bytes_accessed=1000000, transcendentals=0),
+        name="grad_of",
+    )(rows_u, rows_grad)[0]
 
 
 def moved(block, axis, by):
@@ -551,20 +611,19 @@
     return pieces
 
 
-def chunk_pieces(pieces, number, rows):
-    blocks, offsets = [], []
+def joined(pieces, number, rows):
+    blocks = []
     for piece in pieces:
         tall = piece[0].shape[0]
         if len(piece) == 1:
-            blocks.append(piece[0])
-            offsets.append(number * rows)
+            blocks.append(piece[0][number * rows : (number + 1) * rows])
         elif tall >= rows:
-            blocks.append(piece[number * rows // tall])
-            offsets.append(number * rows % tall)
+            start = number * rows % tall
+            blocks.append(piece[number * rows // tall][start : start + rows])
         else:
-            blocks.append(jnp.concatenate(piece, axis=0))
-            offsets.append(number * rows)
-    return blocks, offsets
+            whole = jnp.concatenate(piece, axis=0)
+            blocks.append(whole[number * rows : (number + 1) * rows])
+    return jnp.concatenate(blocks, axis=1)
 
 
 def row_gather(block):
@@ -732,16 +791,18 @@
         return array[number * rows : (number + 1) * rows]
 
     link = Link()
-    input_pieces = ring_pieces(residual)
-    grads_full = [row_gather(chunk(grad_output, n)) for n in range(chunks)]
+    inputs_full = [row_gather(chunk(residual, n)) for n in range(chunks)]
     projection = col_assemble(
         jnp.concatenate([query_weight, key_part, value_part], axis=1), 0, link
     )
     routes_all = jnp.stack(col_gather(routes, link)).reshape(col_count * chunks, rows, top_count)
     out_full = col_assemble(out_weight, 1, link)
     grads_cols = [None] * chunks
+    grad_pieces = ring_pieces(grad_output)
+    grads_near = [piece[0] for piece in grad_pieces[1:] if len(piece) == 1]
+    grads_middle = [block for piece in grad_pieces if len(piece) > 1 for block in piece]
     for n in range(chunks):
-        grads_cols[n] = col_gather(grads_full[n], link)
+        grads_cols[n] = col_gather(joined(grad_pieces, n, rows), link)
     grads_far = [[g for g in grads_cols[n][2::2]] for n in range(chunks)]
 
     gain_one = lax.dynamic_slice_in_dim(norm_attention, row_start, feature_width)
@@ -756,20 +817,14 @@
 
     for n in range(chunks):
         s = state[n]
-        s["normed_full"], s["scale_one"] = normalized_pieces(
-            *chunk_pieces(input_pieces, n, rows), rows, scalars, norm_attention[None, :]
-        )
-        normed = s["normed_full"] if n == 0 else after(s["normed_full"], *grads_far[n - 1])
+        s["normed_full"], s["scale_one"] = normalized(inputs_full[n], norm_attention[None, :])
+        normed = s["normed_full"] if n == 0 else after(s["normed_full"], *grads_near)
         s["projected"] = mm(normed, projection)
         s["mixed"] = attention_forward(
             s["projected"], heads_here, *segs[n], *tables[n], *head_gains
         )
         partial = mm(s["mixed"], out_full).astype(BF16)
-        partial = after(partial, grads_full[n])
-        summed = row_scatter(partial)
-        if n == chunks - 1:
-            summed = after(summed, *grads_far[n])
-        s["hidden"] = chunk(residual, n).astype(F32) + summed
+        s["mixed_out"] = partial
     masks, slots, slots_t = (
         table.reshape(col_count, chunks, *table.shape[1:])
         for table in route_tables(scalars, after(routes_all, partial))
@@ -809,14 +864,16 @@
         if place == 0:
             s["logits"], s["gates"] = found[5][:, :experts], found[6][:, :experts]
 
+    def hidden_of(n, ready, *others):
+        s = state[n]
+        summed = row_scatter(after(s["mixed_out"], *ready))
+        s["hidden"] = chunk(residual, n).astype(F32) + after(summed, *others)
+        s["wide"] = row_gather(after(s["hidden"].astype(BF16), masks))
+
     def second_norm(n, *others):
         s = state[n]
-        hidden_low = s["hidden"].astype(BF16)
-        if n == 0:
-            hidden_low = after(hidden_low, masks)
-        wide = row_gather(hidden_low)
         s["normed_two"], s["scale_two"] = normalized(
-            after(wide, *others), norm_experts[None, :]
+            after(s["wide"], *others), norm_experts[None, :]
         )
         own = s["normed_two"]
         s["tokens"] = [own, swapped(own, "col", 0)]
@@ -832,28 +889,42 @@
         s["small"] = butterfly(chips_total(s["small"], link), "row")
         s["total"] = chips_total(s["x"], link, *others)
 
-    second_norm(0)
+    hidden_of(0, (), *grads_middle)
+    second_norm(0, *grads_far[0], *grads_far[-1])
     for n in range(chunks):
         s = state[n]
-        run_pair(n, 0, *([state[n - 1]["x"][-1][0]] if n > 0 else []))
+        run_pair(n, 0, *([x[0] for x in state[n - 1]["x"][1:]] if n > 0 else []))
         spacer = s["small"][0][1]
+        far_tokens(n, spacer)
         if n + 1 < chunks:
-            second_norm(n + 1, spacer)
-            ahead = (state[n + 1]["normed_two"], spacer)
-        else:
-            ahead = (spacer,)
-        far_tokens(n, spacer)
+            hidden_of(n + 1, (s["wide"],), spacer)
+        for place in range(1, chips):
+            run_pair(n, place, spacer)
         if n > 0:
-            to_row(n - 1)
-            ahead += (state[n - 1]["total"],)
-        for place in range(1, chips):
-            run_pair(n, place, *ahead)
+            to_row(n - 1, s["small"][-1][0])
+        if n + 1 < chunks:
+            second_norm(n + 1, s["small"][-1][0])
+    pair = PairLink()
+    own_grads, other_grads = [], []
+
+    def expert_grads():
+        grad_down = grad_of(kept[2], kept[1])
+        grad_gate, grad_up = grads_of(after(kept[0], grad_down), kept[3], kept[4])
+        own_grads.extend((grad_gate, grad_up, grad_down))
+        wide, deep = grad_gate.shape[0], grad_down.shape[0]
+        first, middle = wide // 8, wide // 2
+        cuts = [(0, 0, first), (2, 0, deep // 2), (2, deep // 2, deep), (0, first, middle)]
+        cuts += [(0, middle, wide), (1, 0, wide // 2), (1, wide // 2, wide)]
+        for i, low, high in cuts:
+            other_grads.append(pair.swapped(own_grads[i][low:high]))
+        return other_grads[:1]
+
     acc_router = jnp.zeros((feature_width, experts), F32)
     acc_gain_two = jnp.zeros((feature_width,), F32)
     for n in range(chunks):
         s = state[n]
         if n == chunks - 1:
-            to_row(n, *([state[n - 1]["hidden_total"]] if n > 0 else []))
+            to_row(n, *expert_grads())
         normed_two_grad = row_scatter(s["total"])
         hidden = s["hidden"]
         gate_dots = s["small"][:experts].T
@@ -878,23 +949,9 @@
             + normed_two_grad * gain_two * scale_two
             - hidden * (scale_two * scale_two * inner_two / model_width)
         )
+        s["branch_full"] = row_gather(s["hidden_total"].astype(BF16))
         acc_gain_two = acc_gain_two + jnp.sum(normed_two_grad * hidden * scale_two, axis=0)
 
-    rows_in = after(kept[0], state[-1]["total"])
-    rows_u = after(kept[2], state[-1]["total"])
-    own_grads = lax.optimization_barrier(
-        (
-            lax.dot_general(rows_in, kept[3], TN, preferred_element_type=F32).astype(BF16),
-            lax.dot_general(rows_in, kept[4], TN, preferred_element_type=F32).astype(BF16),
-            lax.dot_general(rows_u, kept[1], TN, preferred_element_type=F32).astype(BF16),
-        )
-    )
-    pair = PairLink()
-    halves = [
-        pair.swapped(own[half * own.shape[0] // 2 : (half + 1) * own.shape[0] // 2])
-        for own in own_grads
-        for half in range(2)
-    ]
     for n in range(chunks):
         state[n]["mixed_total"] = chips_total(state[n]["y"], link)
 
@@ -905,9 +962,9 @@
     input_blocks = []
     for n in range(chunks):
         s = state[n]
-        branch_full = row_gather(s["hidden_total"].astype(BF16))
+        branch_full = s["branch_full"]
         if n == chunks - 1:
-            branch_full = after(branch_full, halves[0], state[0]["mixed_total"])
+            branch_full = after(branch_full, other_grads[1], state[0]["mixed_total"])
         mixed_grad = lax.dot_general(
             branch_full, out_full, NT, preferred_element_type=F32
         ).astype(BF16)
@@ -960,9 +1017,9 @@
         acc_query = query_here if n == 0 else acc_query + query_here
         scale_one = s["scale_one"]
         if n == 0:
-            normed_one_grad = after(normed_one_grad, halves[1], state[-1]["mixed_total"])
+            normed_one_grad = after(normed_one_grad, other_grads[2], other_grads[3], state[-1]["mixed_total"])
         if n == chunks - 1:
-            normed_one_grad = after(normed_one_grad, halves[3])
+            normed_one_grad = after(normed_one_grad, other_grads[4])
         input_blocks.append(
             s["hidden_total"]
             + normed_one_grad * gain_one * scale_one
@@ -970,15 +1027,19 @@
             * (scale_one * scale_one * inner_one / model_width)
         )
 
+    key_share = col_share(acc_key.astype(BF16), 0, link)
+    query_share = col_share(acc_query.astype(BF16), 0, link)
     for n in range(chunks):
         s = state[n]
         s["mixture"] = row_scatter(after(s["mixed_total"], state[-1]["partial"]))
-    state[0]["mixture"] = after(state[0]["mixture"], halves[4])
-
+    state[0]["mixture"] = after(state[0]["mixture"], *other_grads, out_share, key_share)
     out_other = pair.swapped(out_share)
-    key_share = col_share(acc_key.astype(BF16), 0, link)
     key_share = added(key_share, pair.swapped(key_share))
     shares = [jnp.concatenate(piece, axis=0) for piece in ring_pieces(key_share)]
+    query_other = pair.swapped(query_share)
+    state[-1]["mixture"] = after(
+        state[-1]["mixture"], out_other, query_share, shares[1], shares[-1]
+    )
     shares = jnp.concatenate(shares + shares, axis=1)
     shares = lax.dynamic_slice_in_dim(
         shares, (row_count - row_place) * 2 * head_size, row_count * 2 * head_size, 1
@@ -1004,16 +1065,17 @@
     )
     for axis in ("col", "row"):
         flat = butterfly(flat, axis)
+    flat = after(flat, *[s["mixture"] for s in state])
     flat = flat + pair.swapped(flat)
     totals, start = [], 0
     for size in sizes:
         totals.append(flat[start : start + size])
         start += size
-    query_share = col_share(acc_query.astype(BF16), 0, link)
-    grad_query = query_share.astype(F32) + pair.swapped(query_share).astype(F32)
+    grad_query = query_share.astype(F32) + query_other.astype(F32)
     grad_out_weight = out_share.astype(F32) + out_other.astype(F32)
     grad_gate, grad_up, grad_down = (
-        halves_sum(own, halves[2 * i], halves[2 * i + 1])[None] for i, own in enumerate(own_grads)
+        pieces_sum(own, [other_grads[j] for j in parts])[None]
+        for own, parts in zip(own_grads, ((0, 3, 4), (5, 6), (1, 2)))
     )
     output_blocks = [(s["hidden"] + s["mixture"]).astype(BF16) for s in state]
     return (

time: 991 us -> 955 us (0.964)
  matrix products: 102 us -> 60.5 us
  waiting for transfers between devices: 406 us -> 372 us
  Pallas kernels: 231 us -> 256 us
    all_gather x6, waiting for transfers between devices: 86.9 us -> 32.5 us  [row_gather(): return lax.all_gather(block, 'row', axis=block.ndim - 1, tiled=True)]
    ppermute x54 -> x55, waiting for transfers between devices: 102 us -> 141 us  [swapped(): return lax.ppermute(block, axis, [(i, i ^ 1 << bit) for i in range(count)])]
    dot_general x3 -> x0, matrix products: 36.4 us -> none  [the longest x1 14.2 us: per_device(): lax.dot_general(rows_in, kept[4], TN, preferred_element_type=F32)]
    pallas_call x5, Pallas kernels: 22.4 us -> 50.9 us  [the longest x1 22.2 us: grads_of(): pl.pallas_call(grads_kernel, grid=(width // block,), out_shape=[jax.Shape...]
    ppermute x24, waiting for transfers between devices: 196 us -> 172 us  [moved(): lax.ppermute(block, axis, [(i, (i + by) % count) for i in range(count)])]
    all_gather x6, starting transfers between devices: 0.25 us -> 10.7 us  [row_gather(): return lax.all_gather(block, 'row', axis=block.ndim - 1, tiled=True)]
    unnamed x215 -> x225, local copies, waits for them, and re-layouts: 23.5 us -> 29.2 us
    ppermute x54 -> x55, starting transfers between devices: 27.8 us -> 29.7 us  [swapped(): return lax.ppermute(block, axis, [(i, i ^ 1 << bit) for i in range(count)])]
  transfers between devices with their start and end apart: 92 -> 93, of which waited for: 43 -> 38; matrix products, arithmetic and copies ran while one was open for 23% -> 20% of each run, Pallas kernels for 20% -> 27%
where the time goes in v4:
time: 955 us; the launch traced here: 949 us
  waiting for transfers between devices  372 us (39%)
  Pallas kernels  256 us (27%)
  other arithmetic  86.9 us (9%)
  starting transfers between devices  80.1 us (8%)
  local copies, waits for them, and re-layouts  77.4 us (8%)
  matrix products  60.5 us (6%)
  between operations  16.6 us (2%)
    ppermute x24, waiting for transfers between devices, moved(): lax.ppermute(block, axis, [(i, (i + by) % count) for i in range(count)])  172 us
    ppermute x55, waiting for transfers between devices, swapped(): return lax.ppermute(block, axis, [(i, i ^ 1 << bit) for i in range(count)])  141 us
    pallas_call x4, Pallas kernels, expert_pair(): pl.pallas_call(functools.partial(pair_kernel, first, place, experts), out...  132 us
    convert_element_type x14, other arithmetic, added(): return total.astype(parts[0].dtype)  41.8 us
    ppermute x24, starting transfers between devices, moved(): lax.ppermute(block, axis, [(i, (i + by) % count) for i in range(count)])  38.6 us
    pallas_call x2, Pallas kernels, attention_backward(): pl.pallas_call(functools.partial(attention_backward_kernel, head ** (-0.5...  35.6 us
    all_gather x6, waiting for transfers between devices, row_gather(): return lax.all_gather(block, 'row', axis=block.ndim - 1, tiled=True)  32.5 us
    ppermute x55, starting transfers between devices, swapped(): return lax.ppermute(block, axis, [(i, i ^ 1 << bit) for i in range(count)])  29.7 us
  transfers between devices with their start and end apart: 93, of which 38 were waited for; matrix products, arithmetic and copies ran while one was open for 20% of the time, Pallas kernels for 27%

profile of v4, /device:TPU:0, one launch (start us, length us, event | category | flops | bytes accessed | tf_op | source)
XLA Modules:
  0.0 949.3 jit_solution(3919688399731333211)
XLA Ops:
  14.3 3.6 collective-permute-start.9
  19.1 23.4 %collective-permute-done.1.refs_2_ = bf16[512,1280]{1,0:T(8,128)(2,1)S(1)} collective-permute-done((bf16[512,1280]{1,0:T(8,128)(2,1)S(1)}, bf16[512,1280]{1,0:T(8,128)(2,1)S(1)}, u32[]{:S(2)}, u32[]{:S(2)}) %collective-permute-start.1) | collective-permute-done | bytes 1310752 | tf_op jit(solution)/shard_map/ppermute | solution.py:582
  54.4 17.8 %collective-permute-done.5.refs_2_ = bf16[1024,512]{1,0:T(8,128)(2,1)} collective-permute-done((bf16[1024,512]{1,0:T(8,128)(2,1)}, bf16[1024,512]{1,0:T(8,128)(2,1)}, u32[]{:S(2)}, u32[]{:S(2)}) %collective-permute-start.5) | collective-permute-done | bytes 1048608 | tf_op jit(solution)/shard_map/ppermute | solution.py:582
  76.6 14.1 %all-gather.7.cloned.1.call-done.in_ref = bf16[512,2048]{1,0:T(8,128)(2,1)} async-done(((bf16[512,512]{1,0:T(8,128)(2,1)}), bf16[512,2048]{1,0:T(8,128)(2,1)}) %all-gather.7.cloned.1.call-update) | async-done | bytes 2097168 | tf_op jit(solution)/shard_map/all_gather | solution.py:630
  98.6 9.0 attention_forward.2
  112.2 3.7 convolution_convert_fusion.1
  123.6 3.2 collective-permute-start.10
  128.7 17.2 %collective-permute-done.8 = bf16[512,512]{1,0:T(8,128)(2,1)S(1)} collective-permute-done((bf16[512,512]{1,0:T(8,128)(2,1)S(1)}, bf16[512,512]{1,0:T(8,128)(2,1)S(1)}, u32[]{:S(2)}, u32[]{:S(2)}) %collective-permute-start.8) | collective-permute-done | bytes 524320 | tf_op jit(solution)/shard_map/ppermute | solution.py:582
  148.7 7.7 all-gather.9.cloned.1.call-done.in_ref
  159.0 6.2 fusion.54.q_ref.k_ref.v_ref
  165.3 9.0 attention_forward.3
  174.3 3.7 convolution_convert_fusion
  179.6 10.1 %route_tables.1 = (bf16[8,512,128]{2,1,0:T(8,128)(2,1)S(1)}, s32[8,1,512]{2,1,0:T(1,128)S(1)}, s32[8,512,1]{2,1,0:T(8,128)S(1)}) custom-call(s32[2]{0:T(128)S(1)} %pad_add_fusion.2.expert_ref.scalars_ref, s32[8,512,8]{2,1,0:T(8,128)S(1)} %bitcast.139), custom_call_target="tpu_custom_call" | custom-call | flops 1000000000 | bytes 1000000 | tf_op jit(solution)/shard_map/route_tables/pallas_call | solution.py:453
  189.7 11.8 %reduce-scatter.9.cloned.1.call-done = bf16[512,512]{1,0:T(8,128)(2,1)} async-done(((bf16[512,2048]{1,0:T(8,128)(2,1)}), bf16[512,512]{1,0:T(8,128)(2,1)}) %reduce-scatter.9.cloned.1.call-update) | async-done | bytes 524304 | tf_op jit(solution)/shard_map/reduce_scatter | solution.py:634
  205.8 3.1 pad_maximum_fusion.1.refs_2_
  210.1 46.3 %collective-permute-done.14.refs_2_ = bf16[512,2048]{1,0:T(8,128)(2,1)} collective-permute-done((bf16[512,2048]{1,0:T(8,128)(2,1)}, bf16[512,2048]{1,0:T(8,128)(2,1)}, u32[]{:S(2)}, u32[]{:S(2)}) %collective-permute-start.14) | collective-permute-done | bytes 2097184 | tf_op jit(solution)/shard_map/ppermute | solution.py:582
  267.3 10.5 %all-gather.13.cloned.1.call-start = ((), (), s32[]{:S(2)}) async-start(), calls=%async_computation.13 | async-start | bytes 2621440 | tf_op jit(solution)/shard_map/all_gather | solution.py:630
  279.1 33.0 %expert_pair.4 = (bf16[512,2048]{1,0:T(8,128)(2,1)}, bf16[512,2048]{1,0:T(8,128)(2,1)}, bf16[512,2048]{1,0:T(8,128)(2,1)}, bf16[512,2048]{1,0:T(8,128)(2,1)}, f3...) custom-call(s32[2]{0:T(128)} %copy-done.62, ...), custom_call_target="tpu_custom_call" | custom-call | flops 35999997952 | bytes 10000000 | tf_op jit(solution)/shard_map/expert_pair/pallas_call | solution.py:397
  313.5 12.7 %collective-permute-done.19.refs_0_ = bf16[512,2048]{1,0:T(8,128)(2,1)} collective-permute-done((bf16[512,2048]{1,0:T(8,128)(2,1)}, bf16[512,2048]{1,0:T(8,128)(2,1)}, u32[]{:S(2)}, u32[]{:S(2)}) %collective-permute-start.19) | collective-permute-done | bytes 2097184 | tf_op jit(solution)/shard_map/ppermute | solution.py:582
  330.7 32.8 %expert_pair.5 = (bf16[512,2048]{1,0:T(8,128)(2,1)}, bf16[512,2048]{1,0:T(8,128)(2,1)}, bf16[512,2048]{1,0:T(8,128)(2,1)}, bf16[512,2048]{1,0:T(8,128)(2,1)}, f3...) custom-call(s32[2]{0:T(128)} %copy-done.62, ...), custom_call_target="tpu_custom_call", output_to_operand_aliasing={{7}: (12, {}), {8}: (13, {}), {9}: (14, {}), {10}: (15, {})... | custom-call | flops 35999997952 | bytes 10000000 | tf_op jit(solution)/shard_map/expert_pair/pallas_call | solution.py:397
  368.8 7.5 all-gather.13.cloned.1.call-done.in_ref
  385.5 32.6 %expert_pair.6 = (bf16[512,2048]{1,0:T(8,128)(2,1)}, bf16[512,2048]{1,0:T(8,128)(2,1)}, bf16[512,2048]{1,0:T(8,128)(2,1)}, bf16[512,2048]{1,0:T(8,128)(2,1)}, f3...) custom-call(s32[2]{0:T(128)} %copy-done.62, ...), custom_call_target="tpu_custom_call", output_to_operand_aliasing={{7}: (12, {}), {8}: (13, {}), {9}: (14, {}), {10}: (15, {})... | custom-call | flops 35999997952 | bytes 10000000 | tf_op jit(solution)/shard_map/expert_pair/pallas_call | solution.py:397
  419.5 11.1 %collective-permute-done.28.refs_0_ = bf16[512,2048]{1,0:T(8,128)(2,1)} collective-permute-done((bf16[512,2048]{1,0:T(8,128)(2,1)S(1)}, bf16[512,2048]{1,0:T(8,128)(2,1)}, u32[]{:S(2)}, u32[]{:S(2)}) %collective-permute-start.28) | collective-permute-done | bytes 2097184 | tf_op jit(solution)/shard_map/ppermute | solution.py:582
  438.2 33.0 %expert_pair.7 = (bf16[512,2048]{1,0:T(8,128)(2,1)}, bf16[512,2048]{1,0:T(8,128)(2,1)}, bf16[512,2048]{1,0:T(8,128)(2,1)}, bf16[512,2048]{1,0:T(8,128)(2,1)}, f3...) custom-call(s32[2]{0:T(128)} %copy-done.62, ...), custom_call_target="tpu_custom_call", output_to_operand_aliasing={{7}: (12, {}), {8}: (13, {}), {9}: (14, {}), {10}: (15, {})... | custom-call | flops 35999997952 | bytes 10000000 | tf_op jit(solution)/shard_map/expert_pair/pallas_call | solution.py:397
  476.4 5.7 collective-permute-done.34
  482.1 4.1 add_convert_fusion.4
  492.2 12.8 %grad_of.1.own_ref = bf16[768,2048]{1,0:T(8,128)(2,1)} custom-call(bf16[2560,768]{1,0:T(8,128)(2,1)} %get-tuple-element.189.rows_ref, bf16[2560,2048]{1,0:T(8,128)(2,1)} %get-tuple-element.190.refs_0_), custom_call_target="tpu_custom_call" | custom-call | flops 1000000000 | bytes 1000000 | tf_op jit(solution)/shard_map/grad_of/pallas_call | solution.py:565
  505.0 22.2 %grads_of.1 = (bf16[2048,768]{1,0:T(8,128)(2,1)}, bf16[2048,768]{1,0:T(8,128)(2,1)}) custom-call(bf16[2560,2048]{1,0:T(8,128)(2,1)} %get-tuple-element.191.rows_ref, bf16[2560,768]{1,0:T(8,128)(2,1)} %get-tuple-element.192.refs_0_, bf16[2560,768]{1,0:T(8,128)(2,1)} %get-tuple-element.193.refs_1_), custom_call_target="tpu_custom_call" | custom-call | flops 1000000000 | bytes 1000000 | tf_op jit(solution)/shard_map/grads_of/pallas_call | solution.py:548
  529.8 10.1 %collective-permute-done.39.refs_0_ = bf16[256,768]{1,0:T(8,128)(2,1)S(1)} collective-permute-done((bf16[256,768]{1,0:T(8,128)(2,1)S(1)}, bf16[256,768]{1,0:T(8,128)(2,1)S(1)}, u32[]{:S(2)}, u32[]{:S(2)}) %collective-permute-start.39) | collective-permute-done | bytes 393248 | tf_op jit(solution)/shard_map/ppermute | solution.py:587
  539.9 4.3 add_convert_fusion.5
  545.3 3.9 collective-permute-done.49
  551.2 6.4 collective-permute-done.50
  559.4 5.9 collective-permute-done.40
  566.9 7.2 collective-permute-done.41
  574.7 14.5 %reduce-scatter.13.cloned.1.call-done = bf16[512,512]{1,0:T(8,128)(2,1)} async-done(((bf16[512,2048]{1,0:T(8,128)(2,1)}), bf16[512,512]{1,0:T(8,128)(2,1)}) %reduce-scatter.13.cloned.1.call-update) | async-done | bytes 524304 | tf_op jit(solution)/shard_map/reduce_scatter | solution.py:634
  589.2 4.5 multiply_reduce_fusion.2
  600.4 31.8 %collective-permute-done.42.refs_0_ = bf16[384,2048]{1,0:T(8,128)(2,1)S(1)} collective-permute-done((bf16[384,2048]{1,0:T(8,128)(2,1)S(1)}, bf16[384,2048]{1,0:T(8,128)(2,1)S(1)}, u32[]{:S(2)}, u32[]{:S(2)}) %collective-permute-start.42) | collective-permute-done | bytes 1572896 | tf_op jit(solution)/shard_map/ppermute | solution.py:587
  636.3 3.1 all-gather.17.cloned.1.call-done
  639.5 5.3 convolution_convert_fusion.4.g_ref
  644.9 17.7 %attention_backward.3 = (bf16[512,1280]{1,0:T(8,128)(2,1)S(1)}, f32[512,128]{1,0:T(8,128)}, f32[512,128]{1,0:T(8,128)}, f32[512,1]{1,0:T(8,128)S(1)}, f32[2,128]{1,0:T(2,128)S(1)}) custom-call(f32[512,1280]{1,0:T(8,128)} %copy-done.67, f32[512,1280]{1,0:T(8,128)} %copy-done.67, f32[512,1280]{1,0:T(8,128)} %copy-done.67, ...), custom_call_target="tpu_custom_call" | custom-call | flops 20000000000 | bytes 10000000 | tf_op jit(solution)/shard_map/attention_backward/pallas_call | solution.py:157
  662.7 4.1 multiply_reduce_fusion.1
  671.3 11.0 %collective-permute-done.37 = bf16[512,2048]{1,0:T(8,128)(2,1)} collective-permute-done((bf16[512,2048]{1,0:T(8,128)(2,1)}, bf16[512,2048]{1,0:T(8,128)(2,1)}, u32[]{:S(2)}, u32[]{:S(2)}) %collective-permute-start.37) | collective-permute-done | bytes 2097184 | tf_op jit(solution)/shard_map/ppermute | solution.py:582
  682.2 4.8 add_convert_fusion.6
  687.0 5.3 convolution_convert_fusion.5.g_ref
  692.4 17.9 %attention_backward.2 = (bf16[512,1280]{1,0:T(8,128)(2,1)S(1)}, f32[512,128]{1,0:T(8,128)}, f32[512,128]{1,0:T(8,128)}, f32[512,1]{1,0:T(8,128)S(1)}, f32[2,128]{1,0:T(2,128)S(1)}) custom-call(f32[512,1280]{1,0:T(8,128)} %copy-done.68, f32[512,1280]{1,0:T(8,128)} %copy-done.68, f32[512,1280]{1,0:T(8,128)} %copy-done.68, ...), custom_call_target="tpu_custom_call" | custom-call | flops 20000000000 | bytes 10000000 | tf_op jit(solution)/shard_map/attention_backward/pallas_call | solution.py:157
  710.3 4.2 multiply_reduce_fusion
  716.7 3.9 add_convert_fusion.3
  723.9 27.2 %collective-permute-done.45.refs_2_ = bf16[1024,768]{1,0:T(8,128)(2,1)S(1)} collective-permute-done((bf16[1024,768]{1,0:T(8,128)(2,1)S(1)}, bf16[1024,768]{1,0:T(8,128)(2,1)S(1)}, u32[]{:S(2)}, u32[]{:S(2)}) %collective-permute-start.45) | collective-permute-done | bytes 1572896 | tf_op jit(solution)/shard_map/ppermute | solution.py:587
  760.8 4.6 pieces_sum.5
  765.4 6.0 pieces_sum.3
  771.5 15.3 %collective-permute-done.46.refs_0_ = bf16[1024,768]{1,0:T(8,128)(2,1)} collective-permute-done((bf16[1024,768]{1,0:T(8,128)(2,1)}, bf16[1024,768]{1,0:T(8,128)(2,1)}, u32[]{:S(2)}, u32[]{:S(2)}) %collective-permute-start.46) | collective-permute-done | bytes 1572896 | tf_op jit(solution)/shard_map/ppermute | solution.py:587
  788.7 4.8 add_convert_fusion.2
  794.7 4.2 fusion.55
  827.2 11.2 %collective-permute-done.55 = bf16[1024,512]{1,0:T(8,128)(2,1)} collective-permute-done((bf16[1024,512]{1,0:T(8,128)(2,1)}, bf16[1024,512]{1,0:T(8,128)(2,1)}, u32[]{:S(2)}, u32[]{:S(2)}) %collective-permute-start.55) | collective-permute-done | bytes 1048608 | tf_op jit(solution)/shard_map/ppermute | solution.py:582
  844.6 5.2 pieces_sum.4
  854.5 11.2 %collective-permute-done.73 = f32[37120]{0:T(1024)S(1)} collective-permute-done((f32[37120]{0:T(1024)S(1)}, f32[37120]{0:T(1024)S(1)}, u32[]{:S(2)}, u32[]{:S(2)}) %collective-permute-start.73) | collective-permute-done | bytes 148512 | tf_op jit(solution)/shard_map/ppermute | solution.py:587
  869.5 5.1 collective-permute-done.58
  880.1 9.2 collective-permute-done.74
  891.4 3.8 collective-permute-start.65
  898.1 3.0 collective-permute-done.63
  905.0 3.1 collective-permute-start.78
  908.1 3.5 add_convert_fusion.10
  929.7 5.2 collective-permute-done.75
  936.7 3.2 convert_add_fusion.1
  (542 shorter events, 232.8 us)
Async XLA Ops:
  7.2 83.5 %all-gather.7.cloned.1.call-start = ((), (), s32[]{:S(2)}) async-start(), calls=%async_computation.8 | async-start | bytes 2621440 | tf_op jit(solution)/shard_map/all_gather | solution.py:630
  9.6 146.9 %all-gather.9.cloned.1.call-start = ((), (), s32[]{:S(2)}) async-start(), calls=%async_computation.10 | async-start | bytes 2621440 | tf_op jit(solution)/shard_map/all_gather | solution.py:630
  10.8 31.8 %collective-permute-start.1 = (bf16[512,1280]{1,0:T(8,128)(2,1)S(1)}, bf16[512,1280]{1,0:T(8,128)(2,1)S(1)}, u32[]{:S(2)}, u32[]{:S(2)}) collective-permute-start(bf16[512,1280]{1,0:T(8,128)(2,1)S(1)} %pad_maximum_fusion.3.refs_0_), channel_id=1, source_target_pairs={{0,2},{1,3},{2,0},{3,1},{4,6},{5,7},{6,4},{7,5},{8,10},{9,11},{10,... | collective-permute-start | bytes 3932168 | tf_op jit(solution)/shard_map/ppermute | solution.py:582
  13.8 38.9 %collective-permute-start = (bf16[512,1280]{1,0:T(8,128)(2,1)S(1)}, bf16[512,1280]{1,0:T(8,128)(2,1)}, u32[]{:S(2)}, u32[]{:S(2)}) collective-permute-start(bf16[512,1280]{1,0:T(8,128)(2,1)S(1)} %pad_maximum_fusion.3.refs_0_), channel_id=1, source_target_pairs={{0,1},{1,0},{2,3},{3,2},{4,5},{5,4},{6,7},{7,6},{8,9},{9,8},{10,11... | collective-permute-start | bytes 3932168 | tf_op jit(solution)/shard_map/ppermute | solution.py:587
  13.8 93.8 %collective-permute-start.3 = (bf16[1024,512]{1,0:T(8,128)(2,1)}, bf16[1024,512]{1,0:T(8,128)(2,1)}, u32[]{:S(2)}, u32[]{:S(2)}) collective-permute-start(bf16[1024,512]{1,0:T(8,128)(2,1)} %refs_0_.1), channel_id=1, source_target_pairs={{0,1},{1,0},{2,3},{3,2},{4,5},{5,4},{6,7},{7,6},{8,9},{9,8},{10,11... | collective-permute-start | bytes 3145736 | tf_op jit(solution)/shard_map/ppermute | solution.py:587
  14.3 107.2 %collective-permute-start.9 = (bf16[1024,512]{1,0:T(8,128)(2,1)}, bf16[1024,512]{1,0:T(8,128)(2,1)}, u32[]{:S(2)}, u32[]{:S(2)}) collective-permute-start(bf16[1024,512]{1,0:T(8,128)(2,1)} %param.31), channel_id=1, source_target_pairs={{0,12},{4,0},{8,4},{12,8},{1,13},{5,1},{9,5},{13,9},{2,14},{6,2},{... | collective-permute-start | bytes 3145736 | tf_op jit(solution)/shard_map/ppermute | solution.py:582
  17.9 183.6 %reduce-scatter.9.cloned.1.call-start = ((), (), s32[]{:S(2)}) async-start(), calls=%async_computation.9 | async-start | bytes 2621440 | tf_op jit(solution)/shard_map/reduce_scatter | solution.py:634
  42.5 29.6 %collective-permute-start.2 = (bf16[512,1280]{1,0:T(8,128)(2,1)S(1)}, bf16[512,1280]{1,0:T(8,128)(2,1)}, u32[]{:S(2)}, u32[]{:S(2)}) collective-permute-start(bf16[512,1280]{1,0:T(8,128)(2,1)S(1)} %collective-permute-done.1.refs_2_), channel_id=1, source_target_pairs={{0,1},{1,0},{2,3},{3,2},{4,5},{5,4},{6,7},{7,6},{8,9},{9,8},{10,11... | collective-permute-start | bytes 3932168 | tf_op jit(solution)/shard_map/ppermute | solution.py:587
  47.0 25.1 %collective-permute-start.5 = (bf16[1024,512]{1,0:T(8,128)(2,1)}, bf16[1024,512]{1,0:T(8,128)(2,1)}, u32[]{:S(2)}, u32[]{:S(2)}) collective-permute-start(bf16[1024,512]{1,0:T(8,128)(2,1)} %refs_0_.1), channel_id=1, source_target_pairs={{0,2},{1,3},{2,0},{3,1},{4,6},{5,7},{6,4},{7,5},{8,10},{9,11},{10,... | collective-permute-start | bytes 3145736 | tf_op jit(solution)/shard_map/ppermute | solution.py:582
  52.7 63.3 %collective-permute-start.7 = (bf16[1024,512]{1,0:T(8,128)(2,1)}, bf16[1024,512]{1,0:T(8,128)(2,1)}, u32[]{:S(2)}, u32[]{:S(2)}) collective-permute-start(bf16[1024,512]{1,0:T(8,128)(2,1)} %param.31), channel_id=1, source_target_pairs={{0,4},{4,8},{8,12},{12,0},{1,5},{5,9},{9,13},{13,1},{2,6},{6,10},{... | collective-permute-start | bytes 3145736 | tf_op jit(solution)/shard_map/ppermute | solution.py:582
  72.1 35.5 %collective-permute-start.6 = (bf16[1024,512]{1,0:T(8,128)(2,1)}, bf16[1024,512]{1,0:T(8,128)(2,1)}, u32[]{:S(2)}, u32[]{:S(2)}) collective-permute-start(bf16[1024,512]{1,0:T(8,128)(2,1)} %collective-permute-done.5.refs_2_), channel_id=1, source_target_pairs={{0,1},{1,0},{2,3},{3,2},{4,5},{5,4},{6,7},{7,6},{8,9},{9,8},{10,11... | collective-permute-start | bytes 3145736 | tf_op jit(solution)/shard_map/ppermute | solution.py:587
  115.9 140.5 %all-gather.11.cloned.1.call-start = ((), (), s32[]{:S(2)}) async-start(), calls=%async_computation.11 | async-start | bytes 2621440 | tf_op jit(solution)/shard_map/all_gather | solution.py:630
  118.1 27.8 %collective-permute-start.8 = (bf16[512,512]{1,0:T(8,128)(2,1)S(1)}, bf16[512,512]{1,0:T(8,128)(2,1)S(1)}, u32[]{:S(2)}, u32[]{:S(2)}) collective-permute-start(bf16[512,512]{1,0:T(8,128)(2,1)S(1)} %get-tuple-element.315), channel_id=1, source_target_pairs={{0,4},{4,8},{8,12},{12,0},{1,5},{5,9},{9,13},{13,1},{2,6},{6,10},{... | collective-permute-start | bytes 1572872 | tf_op jit(solution)/shard_map/ppermute | solution.py:582
  123.6 79.1 %collective-permute-start.10 = (bf16[512,512]{1,0:T(8,128)(2,1)}, bf16[512,512]{1,0:T(8,128)(2,1)}, u32[]{:S(2)}, u32[]{:S(2)}) collective-permute-start(bf16[512,512]{1,0:T(8,128)(2,1)} %get-tuple-element.317), channel_id=1, source_target_pairs={{0,12},{4,0},{8,4},{12,8},{1,13},{5,1},{9,5},{13,9},{2,14},{6,2},{... | collective-permute-start | bytes 1572872 | tf_op jit(solution)/shard_map/ppermute | solution.py:582
  147.6 61.3 %collective-permute-start.13 = (bf16[512,2048]{1,0:T(8,128)(2,1)}, bf16[512,2048]{1,0:T(8,128)(2,1)}, u32[]{:S(2)}, u32[]{:S(2)}) collective-permute-start(bf16[512,2048]{1,0:T(8,128)(2,1)} %pad_maximum_fusion.refs_2_), channel_id=1, source_target_pairs={{0,2},{1,3},{2,0},{3,1},{4,6},{5,7},{6,4},{7,5},{8,10},{9,11},{10,... | collective-permute-start | bytes 6291464 | tf_op jit(solution)/shard_map/ppermute | solution.py:582
  205.7 121.5 %reduce-scatter.11.cloned.1.call-start = ((), (), s32[]{:S(2)}) async-start(), calls=%async_computation.12 | async-start | bytes 2621440 | tf_op jit(solution)/shard_map/reduce_scatter | solution.py:634
  208.9 47.5 %collective-permute-start.14 = (bf16[512,2048]{1,0:T(8,128)(2,1)}, bf16[512,2048]{1,0:T(8,128)(2,1)}, u32[]{:S(2)}, u32[]{:S(2)}) collective-permute-start(bf16[512,2048]{1,0:T(8,128)(2,1)} %pad_maximum_fusion.1.refs_2_), channel_id=1, source_target_pairs={{0,2},{1,3},{2,0},{3,1},{4,6},{5,7},{6,4},{7,5},{8,10},{9,11},{10,... | collective-permute-start | bytes 6291464 | tf_op jit(solution)/shard_map/ppermute | solution.py:582
  210.1 69.0 %collective-permute-start.16 = (bf16[512,2048]{1,0:T(8,128)(2,1)}, bf16[512,2048]{1,0:T(8,128)(2,1)}, u32[]{:S(2)}, u32[]{:S(2)}) collective-permute-start(bf16[512,2048]{1,0:T(8,128)(2,1)} %pad_maximum_fusion.refs_2_), channel_id=1, source_target_pairs={{0,1},{1,0},{2,3},{3,2},{4,5},{5,4},{6,7},{7,6},{8,9},{9,8},{10,11... | collective-permute-start | bytes 6291464 | tf_op jit(solution)/shard_map/ppermute | solution.py:587
  261.0 18.1 %collective-permute-start.15 = (bf16[512,2048]{1,0:T(8,128)(2,1)}, bf16[512,2048]{1,0:T(8,128)(2,1)}, u32[]{:S(2)}, u32[]{:S(2)}) collective-permute-start(bf16[512,2048]{1,0:T(8,128)(2,1)} %get-tuple-element.146.refs_0_), channel_id=1, source_target_pairs={{0,1},{1,0},{2,3},{3,2},{4,5},{5,4},{6,7},{7,6},{8,9},{9,8},{10,11... | collective-permute-start | bytes 6291464 | tf_op jit(solution)/shard_map/ppermute | solution.py:587
  267.3 109.0 %all-gather.13.cloned.1.call-start = ((), (), s32[]{:S(2)}) async-start(), calls=%async_computation.13 | async-start | bytes 2621440 | tf_op jit(solution)/shard_map/all_gather | solution.py:630
  277.8 48.4 %collective-permute-start.19 = (bf16[512,2048]{1,0:T(8,128)(2,1)}, bf16[512,2048]{1,0:T(8,128)(2,1)}, u32[]{:S(2)}, u32[]{:S(2)}) collective-permute-start(bf16[512,2048]{1,0:T(8,128)(2,1)} %get-tuple-element.146.refs_0_), channel_id=1, source_target_pairs={{0,2},{1,3},{2,0},{3,1},{4,6},{5,7},{6,4},{7,5},{8,10},{9,11},{10,... | collective-permute-start | bytes 6291464 | tf_op jit(solution)/shard_map/ppermute | solution.py:582
  313.2 17.2 %collective-permute-start.21 = (bf16[512,2048]{1,0:T(8,128)(2,1)}, bf16[512,2048]{1,0:T(8,128)(2,1)}, u32[]{:S(2)}, u32[]{:S(2)}) collective-permute-start(bf16[512,2048]{1,0:T(8,128)(2,1)} %collective-permute-done.13.refs_2_), channel_id=1, source_target_pairs={{0,1},{1,0},{2,3},{3,2},{4,5},{5,4},{6,7},{7,6},{8,9},{9,8},{10,11... | collective-permute-start | bytes 6291464 | tf_op jit(solution)/shard_map/ppermute | solution.py:587
  330.4 244.3 %reduce-scatter.17.cloned.1.call-start = ((), (), s32[]{:S(2)}) async-start(), calls=%async_computation.17 | async-start | bytes 2621440 | tf_op jit(solution)/shard_map/reduce_scatter | solution.py:634
  363.6 16.6 %collective-permute-start.23 = (bf16[512,2048]{1,0:T(8,128)(2,1)}, bf16[512,2048]{1,0:T(8,128)(2,1)}, u32[]{:S(2)}, u32[]{:S(2)}) collective-permute-start(bf16[512,2048]{1,0:T(8,128)(2,1)} %get-tuple-element.156), channel_id=1, source_target_pairs={{0,1},{1,0},{2,3},{3,2},{4,5},{5,4},{6,7},{7,6},{8,9},{9,8},{10,11... | collective-permute-start | bytes 6291464 | tf_op jit(solution)/shard_map/ppermute | solution.py:587
  365.0 19.3 %collective-permute-start.26 = (bf16[512,2048]{1,0:T(8,128)(2,1)}, bf16[512,2048]{1,0:T(8,128)(2,1)}, u32[]{:S(2)}, u32[]{:S(2)}) collective-permute-start(bf16[512,2048]{1,0:T(8,128)(2,1)} %pad_maximum_fusion.1.refs_2_), channel_id=1, source_target_pairs={{0,1},{1,0},{2,3},{3,2},{4,5},{5,4},{6,7},{7,6},{8,9},{9,8},{10,11... | collective-permute-start | bytes 6291464 | tf_op jit(solution)/shard_map/ppermute | solution.py:587
  382.7 47.9 %collective-permute-start.28 = (bf16[512,2048]{1,0:T(8,128)(2,1)S(1)}, bf16[512,2048]{1,0:T(8,128)(2,1)}, u32[]{:S(2)}, u32[]{:S(2)}) collective-permute-start(bf16[512,2048]{1,0:T(8,128)(2,1)S(1)} %get-tuple-element.171.refs_0_), channel_id=1, source_target_pairs={{0,2},{1,3},{2,0},{3,1},{4,6},{5,7},{6,4},{7,5},{8,10},{9,11},{10,... | collective-permute-start | bytes 6291464 | tf_op jit(solution)/shard_map/ppermute | solution.py:582
  419.0 17.2 %collective-permute-start.30 = (bf16[512,2048]{1,0:T(8,128)(2,1)}, bf16[512,2048]{1,0:T(8,128)(2,1)S(1)}, u32[]{:S(2)}, u32[]{:S(2)}) collective-permute-start(bf16[512,2048]{1,0:T(8,128)(2,1)} %collective-permute-done.14.refs_2_), channel_id=1, source_target_pairs={{0,1},{1,0},{2,3},{3,2},{4,5},{5,4},{6,7},{7,6},{8,9},{9,8},{10,11... | collective-permute-start | bytes 6291464 | tf_op jit(solution)/shard_map/ppermute | solution.py:587
  433.1 49.1 %collective-permute-start.48 = (bf16[512,2048]{1,0:T(8,128)(2,1)}, bf16[512,2048]{1,0:T(8,128)(2,1)S(1)}, u32[]{:S(2)}, u32[]{:S(2)}) collective-permute-start(bf16[512,2048]{1,0:T(8,128)(2,1)} %get-tuple-element.210), channel_id=1, source_target_pairs={{0,1},{1,0},{2,3},{3,2},{4,5},{5,4},{6,7},{7,6},{8,9},{9,8},{10,11... | collective-permute-start | bytes 6291464 | tf_op jit(solution)/shard_map/ppermute | solution.py:587
  434.8 47.4 %collective-permute-start.34 = (bf16[512,2048]{1,0:T(8,128)(2,1)S(1)}, bf16[512,2048]{1,0:T(8,128)(2,1)}, u32[]{:S(2)}, u32[]{:S(2)}) collective-permute-start(bf16[512,2048]{1,0:T(8,128)(2,1)S(1)} %add_convert_fusion.8), channel_id=1, source_target_pairs={{0,2},{1,3},{2,0},{3,1},{4,6},{5,7},{6,4},{7,5},{8,10},{9,11},{10,... | collective-permute-start | bytes 6291464 | tf_op jit(solution)/shard_map/ppermute | solution.py:582
  471.3 16.8 %collective-permute-start.31 = (bf16[512,2048]{1,0:T(8,128)(2,1)}, bf16[512,2048]{1,0:T(8,128)(2,1)}, u32[]{:S(2)}, u32[]{:S(2)}) collective-permute-start(bf16[512,2048]{1,0:T(8,128)(2,1)} %get-tuple-element.179), channel_id=1, source_target_pairs={{0,1},{1,0},{2,3},{3,2},{4,5},{5,4},{6,7},{7,6},{8,9},{9,8},{10,11... | collective-permute-start | bytes 6291464 | tf_op jit(solution)/shard_map/ppermute | solution.py:587
  486.3 102.9 %reduce-scatter.13.cloned.1.call-start = ((), (), s32[]{:S(2)}) async-start(), calls=%async_computation.14 | async-start | bytes 2621440 | tf_op jit(solution)/shard_map/reduce_scatter | solution.py:634
  490.7 49.2 %collective-permute-start.36 = (bf16[512,2048]{1,0:T(8,128)(2,1)S(1)}, bf16[512,2048]{1,0:T(8,128)(2,1)S(1)}, u32[]{:S(2)}, u32[]{:S(2)}) collective-permute-start(bf16[512,2048]{1,0:T(8,128)(2,1)S(1)} %add_convert_fusion.7), channel_id=1, source_target_pairs={{0,2},{1,3},{2,0},{3,1},{4,6},{5,7},{6,4},{7,5},{8,10},{9,11},{10,... | collective-permute-start | bytes 6291464 | tf_op jit(solution)/shard_map/ppermute | solution.py:582
  492.2 47.7 %collective-permute-start.38 = (bf16[512,2048]{1,0:T(8,128)(2,1)}, bf16[512,2048]{1,0:T(8,128)(2,1)}, u32[]{:S(2)}, u32[]{:S(2)}) collective-permute-start(bf16[512,2048]{1,0:T(8,128)(2,1)} %get-tuple-element.187), channel_id=1, source_target_pairs={{0,1},{1,0},{2,3},{3,2},{4,5},{5,4},{6,7},{7,6},{8,9},{9,8},{10,11... | collective-permute-start | bytes 6291464 | tf_op jit(solution)/shard_map/ppermute | solution.py:587
  544.3 95.2 %all-gather.17.cloned.1.call-start = ((), (), s32[]{:S(2)}) async-start(), calls=%async_computation.18 | async-start | bytes 2621440 | tf_op jit(solution)/shard_map/all_gather | solution.py:630
  593.8 93.2 %all-gather.15.cloned.1.call-start = ((), (), s32[]{:S(2)}) async-start(), calls=%async_computation.15 | async-start | bytes 2621440 | tf_op jit(solution)/shard_map/all_gather | solution.py:630
  595.4 36.8 %collective-permute-start.42 = (bf16[384,2048]{1,0:T(8,128)(2,1)S(1)}, bf16[384,2048]{1,0:T(8,128)(2,1)S(1)}, u32[]{:S(2)}, u32[]{:S(2)}) collective-permute-start(bf16[384,2048]{1,0:T(8,128)(2,1)S(1)} %get-tuple-element.199), channel_id=1, source_target_pairs={{0,16},{16,0},{1,17},{17,1},{2,18},{18,2},{3,19},{19,3},{4,20},{20... | collective-permute-start | bytes 4718600 | tf_op jit(solution)/shard_map/ppermute | solution.py:587
  596.9 85.3 %collective-permute-start.17 = (bf16[512,2048]{1,0:T(8,128)(2,1)}, bf16[512,2048]{1,0:T(8,128)(2,1)}, u32[]{:S(2)}, u32[]{:S(2)}) collective-permute-start(bf16[512,2048]{1,0:T(8,128)(2,1)} %get-tuple-element.143), channel_id=1, source_target_pairs={{0,1},{1,0},{2,3},{3,2},{4,5},{5,4},{6,7},{7,6},{8,9},{9,8},{10,11... | collective-permute-start | bytes 6291464 | tf_op jit(solution)/shard_map/ppermute | solution.py:587
  633.3 36.5 %collective-permute-start.43 = (bf16[384,2048]{1,0:T(8,128)(2,1)}, bf16[384,2048]{1,0:T(8,128)(2,1)}, u32[]{:S(2)}, u32[]{:S(2)}) collective-permute-start(bf16[384,2048]{1,0:T(8,128)(2,1)} %get-tuple-element.203), channel_id=1, source_target_pairs={{0,16},{16,0},{1,17},{17,1},{2,18},{18,2},{3,19},{19,3},{4,20},{20... | collective-permute-start | bytes 4718600 | tf_op jit(solution)/shard_map/ppermute | solution.py:587
  634.8 47.4 %collective-permute-start.37 = (bf16[512,2048]{1,0:T(8,128)(2,1)}, bf16[512,2048]{1,0:T(8,128)(2,1)}, u32[]{:S(2)}, u32[]{:S(2)}) collective-permute-start(bf16[512,2048]{1,0:T(8,128)(2,1)} %add_convert_fusion.9), channel_id=1, source_target_pairs={{0,2},{1,3},{2,0},{3,1},{4,6},{5,7},{6,4},{7,5},{8,10},{9,11},{10,... | collective-permute-start | bytes 6291464 | tf_op jit(solution)/shard_map/ppermute | solution.py:582
  636.3 280.0 %reduce-scatter.21.cloned.1.call-start = ((), (), s32[]{:S(2)}) async-start(), calls=%async_computation.20 | async-start | bytes 2621440 | tf_op jit(solution)/shard_map/reduce_scatter | solution.py:634
  666.8 251.6 %reduce-scatter.23.cloned.1.call-start = ((), (), s32[]{:S(2)}) async-start(), calls=%async_computation.21 | async-start | bytes 2621440 | tf_op jit(solution)/shard_map/reduce_scatter | solution.py:634
  669.8 46.9 %collective-permute-start.53 = (bf16[512,2048]{1,0:T(8,128)(2,1)}, bf16[512,2048]{1,0:T(8,128)(2,1)}, u32[]{:S(2)}, u32[]{:S(2)}) collective-permute-start(bf16[512,2048]{1,0:T(8,128)(2,1)} %get-tuple-element.216), channel_id=1, source_target_pairs={{0,1},{1,0},{2,3},{3,2},{4,5},{5,4},{6,7},{7,6},{8,9},{9,8},{10,11... | collective-permute-start | bytes 6291464 | tf_op jit(solution)/shard_map/ppermute | solution.py:587
  669.8 46.4 %collective-permute-start.44 = (bf16[768,768]{1,0:T(8,128)(2,1)}, bf16[768,768]{1,0:T(8,128)(2,1)}, u32[]{:S(2)}, u32[]{:S(2)}) collective-permute-start(bf16[768,768]{1,0:T(8,128)(2,1)} %slice.275), channel_id=1, source_target_pairs={{0,16},{16,0},{1,17},{17,1},{2,18},{18,2},{3,19},{19,3},{4,20},{20... | collective-permute-start | bytes 3538952 | tf_op jit(solution)/shard_map/ppermute | solution.py:587
  714.5 206.3 %reduce-scatter.15.cloned.1.call-start = ((), (), s32[]{:S(2)}) async-start(), calls=%async_computation.16 | async-start | bytes 2621440 | tf_op jit(solution)/shard_map/reduce_scatter | solution.py:634
  716.2 34.8 %collective-permute-start.45 = (bf16[1024,768]{1,0:T(8,128)(2,1)S(1)}, bf16[1024,768]{1,0:T(8,128)(2,1)S(1)}, u32[]{:S(2)}, u32[]{:S(2)}) collective-permute-start(bf16[1024,768]{1,0:T(8,128)(2,1)S(1)} %slice.276), channel_id=1, source_target_pairs={{0,16},{16,0},{1,17},{17,1},{2,18},{18,2},{3,19},{19,3},{4,20},{20... | collective-permute-start | bytes 4718600 | tf_op jit(solution)/shard_map/ppermute | solution.py:587
  716.7 72.0 %collective-permute-start.59 = (bf16[512,2048]{1,0:T(8,128)(2,1)}, bf16[512,2048]{1,0:T(8,128)(2,1)}, u32[]{:S(2)}, u32[]{:S(2)}) collective-permute-start(bf16[512,2048]{1,0:T(8,128)(2,1)} %get-tuple-element.223), channel_id=1, source_target_pairs={{0,1},{1,0},{2,3},{3,2},{4,5},{5,4},{6,7},{7,6},{8,9},{9,8},{10,11... | collective-permute-start | bytes 6291464 | tf_op jit(solution)/shard_map/ppermute | solution.py:587
  720.6 68.1 %collective-permute-start.54 = (bf16[512,2048]{1,0:T(8,128)(2,1)}, bf16[512,2048]{1,0:T(8,128)(2,1)}, u32[]{:S(2)}, u32[]{:S(2)}) collective-permute-start(bf16[512,2048]{1,0:T(8,128)(2,1)} %add_convert_fusion.3), channel_id=1, source_target_pairs={{0,2},{1,3},{2,0},{3,1},{4,6},{5,7},{6,4},{7,5},{8,10},{9,11},{10,... | collective-permute-start | bytes 6291464 | tf_op jit(solution)/shard_map/ppermute | solution.py:582
  752.2 34.6 %collective-permute-start.46 = (bf16[1024,768]{1,0:T(8,128)(2,1)}, bf16[1024,768]{1,0:T(8,128)(2,1)}, u32[]{:S(2)}, u32[]{:S(2)}) collective-permute-start(bf16[1024,768]{1,0:T(8,128)(2,1)} %get-tuple-element.207), channel_id=1, source_target_pairs={{0,16},{16,0},{1,17},{17,1},{2,18},{18,2},{3,19},{19,3},{4,20},{20... | collective-permute-start | bytes 4718600 | tf_op jit(solution)/shard_map/ppermute | solution.py:587
  786.8 54.9 %collective-permute-start.47 = (bf16[1024,768]{1,0:T(8,128)(2,1)}, bf16[1024,768]{1,0:T(8,128)(2,1)}, u32[]{:S(2)}, u32[]{:S(2)}) collective-permute-start(bf16[1024,768]{1,0:T(8,128)(2,1)} %get-tuple-element.208), channel_id=1, source_target_pairs={{0,16},{16,0},{1,17},{17,1},{2,18},{18,2},{3,19},{19,3},{4,20},{20... | collective-permute-start | bytes 4718600 | tf_op jit(solution)/shard_map/ppermute | solution.py:587
  793.6 27.7 %collective-permute-start.67 = (f32[512]{0:T(512)S(1)}, f32[512]{0:T(512)S(1)}, u32[]{:S(2)}, u32[]{:S(2)}) collective-permute-start(f32[512]{0:T(512)S(1)} %reduce.12), channel_id=1, source_target_pairs={{0,4},{4,0},{8,12},{12,8},{1,5},{5,1},{9,13},{13,9},{2,6},{6,2},{1... | collective-permute-start | bytes 6152 | tf_op jit(solution)/shard_map/ppermute | solution.py:587
  793.7 129.2 %reduce-scatter.19.cloned.1.call-start = ((), (), s32[]{:S(2)}) async-start(), calls=%async_computation.19 | async-start | bytes 2621440 | tf_op jit(solution)/shard_map/reduce_scatter | solution.py:634
  808.6 16.3 %collective-permute-start.71 = (f32[37120]{0:T(1024)}, f32[37120]{0:T(1024)}, u32[]{:S(2)}, u32[]{:S(2)}) collective-permute-start(f32[37120]{0:T(1024)} %constant_dynamic-update-slice_fusion.8), channel_id=1, source_target_pairs={{0,1},{1,0},{2,3},{3,2},{4,5},{5,4},{6,7},{7,6},{8,9},{9,8},{10,11... | collective-permute-start | bytes 445448 | tf_op jit(solution)/shard_map/ppermute | solution.py:587
  808.7 29.8 %collective-permute-start.51 = (bf16[1024,512]{1,0:T(8,128)(2,1)}, bf16[1024,512]{1,0:T(8,128)(2,1)}, u32[]{:S(2)}, u32[]{:S(2)}) collective-permute-start(bf16[1024,512]{1,0:T(8,128)(2,1)} %get-tuple-element.294), channel_id=1, source_target_pairs={{0,1},{1,0},{2,3},{3,2},{4,5},{5,4},{6,7},{7,6},{8,9},{9,8},{10,11... | collective-permute-start | bytes 3145736 | tf_op jit(solution)/shard_map/ppermute | solution.py:587
  813.0 25.5 %collective-permute-start.55 = (bf16[1024,512]{1,0:T(8,128)(2,1)}, bf16[1024,512]{1,0:T(8,128)(2,1)}, u32[]{:S(2)}, u32[]{:S(2)}) collective-permute-start(bf16[1024,512]{1,0:T(8,128)(2,1)} %add_convert_fusion.13), channel_id=1, source_target_pairs={{0,2},{1,3},{2,0},{3,1},{4,6},{5,7},{6,4},{7,5},{8,10},{9,11},{10,... | collective-permute-start | bytes 3145736 | tf_op jit(solution)/shard_map/ppermute | solution.py:582
  821.4 45.1 %collective-permute-start.62 = (bf16[512,1024]{1,0:T(8,128)(2,1)}, bf16[512,1024]{1,0:T(8,128)(2,1)}, u32[]{:S(2)}, u32[]{:S(2)}) collective-permute-start(bf16[512,1024]{1,0:T(8,128)(2,1)} %get-tuple-element.293), channel_id=1, source_target_pairs={{0,1},{1,0},{2,3},{3,2},{4,5},{5,4},{6,7},{7,6},{8,9},{9,8},{10,11... | collective-permute-start | bytes 3145736 | tf_op jit(solution)/shard_map/ppermute | solution.py:587
  824.9 18.4 %collective-permute-start.69 = (f32[512]{0:T(512)S(1)}, f32[512]{0:T(512)S(1)}, u32[]{:S(2)}, u32[]{:S(2)}) collective-permute-start(f32[512]{0:T(512)S(1)} %reduce.15), channel_id=1, source_target_pairs={{0,4},{4,0},{8,12},{12,8},{1,5},{5,1},{9,13},{13,9},{2,6},{6,2},{1... | collective-permute-start | bytes 6152 | tf_op jit(solution)/shard_map/ppermute | solution.py:587
  838.5 13.8 %collective-permute-start.57 = (bf16[512,256]{0,1:T(8,128)(2,1)}, bf16[512,256]{0,1:T(8,128)(2,1)}, u32[]{:S(2)}, u32[]{:S(2)}) collective-permute-start(bf16[512,256]{0,1:T(8,128)(2,1)} %get-tuple-element.311), channel_id=1, source_target_pairs={{0,1},{1,0},{2,3},{3,2},{4,5},{5,4},{6,7},{7,6},{8,9},{9,8},{10,11... | collective-permute-start | bytes 786440 | tf_op jit(solution)/shard_map/ppermute | solution.py:587
  843.3 36.0 %collective-permute-start.60 = (bf16[1024,512]{1,0:T(8,128)(2,1)S(1)}, bf16[1024,512]{1,0:T(8,128)(2,1)}, u32[]{:S(2)}, u32[]{:S(2)}) collective-permute-start(bf16[1024,512]{1,0:T(8,128)(2,1)S(1)} %add_convert_fusion.12), channel_id=1, source_target_pairs={{0,16},{16,0},{1,17},{17,1},{2,18},{18,2},{3,19},{19,3},{4,20},{20... | collective-permute-start | bytes 3145736 | tf_op jit(solution)/shard_map/ppermute | solution.py:587
  849.9 27.4 %collective-permute-start.56 = (bf16[512,256]{0,1:T(8,128)(2,1)}, bf16[512,256]{0,1:T(8,128)(2,1)}, u32[]{:S(2)}, u32[]{:S(2)}) collective-permute-start(bf16[512,256]{0,1:T(8,128)(2,1)} %get-tuple-element.310), channel_id=1, source_target_pairs={{0,1},{1,0},{2,3},{3,2},{4,5},{5,4},{6,7},{7,6},{8,9},{9,8},{10,11... | collective-permute-start | bytes 786440 | tf_op jit(solution)/shard_map/ppermute | solution.py:587
  850.8 57.3 %collective-permute-start.61 = (bf16[512,1024]{1,0:T(8,128)(2,1)S(1)}, bf16[512,1024]{1,0:T(8,128)(2,1)}, u32[]{:S(2)}, u32[]{:S(2)}) collective-permute-start(bf16[512,1024]{1,0:T(8,128)(2,1)S(1)} %copy-done.86), channel_id=1, source_target_pairs={{0,1},{1,0},{2,3},{3,2},{4,5},{5,4},{6,7},{7,6},{8,9},{9,8},{10,11... | collective-permute-start | bytes 3145736 | tf_op jit(solution)/shard_map/ppermute | solution.py:587
  865.7 14.0 %collective-permute-start.70 = (f32[512]{0:T(512)S(1)}, f32[512]{0:T(512)S(1)}, u32[]{:S(2)}, u32[]{:S(2)}) collective-permute-start(f32[512]{0:T(512)S(1)} %add.392), channel_id=1, source_target_pairs={{0,8},{4,12},{8,0},{12,4},{1,9},{5,13},{9,1},{13,5},{2,10},{6,14},... | collective-permute-start | bytes 6152 | tf_op jit(solution)/shard_map/ppermute | solution.py:587
  874.6 14.7 %collective-permute-start.74 = (f32[37120]{0:T(1024)}, f32[37120]{0:T(1024)}, u32[]{:S(2)}, u32[]{:S(2)}) collective-permute-start(f32[37120]{0:T(1024)} %add.403), channel_id=1, source_target_pairs={{0,8},{4,12},{8,0},{12,4},{1,9},{5,13},{9,1},{13,5},{2,10},{6,14},... | collective-permute-start | bytes 445448 | tf_op jit(solution)/shard_map/ppermute | solution.py:587
  877.2 23.9 %collective-permute-start.63 = (bf16[512,1024]{1,0:T(8,128)(2,1)}, bf16[512,1024]{1,0:T(8,128)(2,1)}, u32[]{:S(2)}, u32[]{:S(2)}) collective-permute-start(bf16[512,1024]{1,0:T(8,128)(2,1)} %add_convert_fusion.11), channel_id=1, source_target_pairs={{0,2},{1,3},{2,0},{3,1},{4,6},{5,7},{6,4},{7,5},{8,10},{9,11},{10,... | collective-permute-start | bytes 3145736 | tf_op jit(solution)/shard_map/ppermute | solution.py:582
  911.6 23.3 %collective-permute-start.75 = (bf16[512,1024]{1,0:T(8,128)(2,1)}, bf16[512,1024]{1,0:T(8,128)(2,1)}, u32[]{:S(2)}, u32[]{:S(2)}) collective-permute-start(bf16[512,1024]{1,0:T(8,128)(2,1)} %add_convert_fusion.10), channel_id=1, source_target_pairs={{0,16},{16,0},{1,17},{17,1},{2,18},{18,2},{3,19},{19,3},{4,20},{20... | collective-permute-start | bytes 3145736 | tf_op jit(solution)/shard_map/ppermute | solution.py:587
  (138 other events, 1591.7 us)
Sparse Core Ops, SparseCore 0:
  10.2 80.4 all-gather.6
  92.8 63.5 all-gather.8
  159.3 42.1 reduce-scatter.8
  205.9 45.3 all-gather.10
  267.4 43.6 reduce-scatter.10
  330.5 45.7 all-gather.12
  486.4 42.5 reduce-scatter.16
  544.4 44.8 reduce-scatter.12
  593.9 45.5 all-gather.16
  640.9 44.5 all-gather.14
  688.4 42.6 reduce-scatter.20
  733.3 43.1 reduce-scatter.22
  793.9 43.3 reduce-scatter.14
  840.1 49.5 reduce-scatter.18

commit v5 on v4

--- a/solution.py
+++ b/solution.py
@@ -631,7 +631,7 @@
 
 
 def row_scatter(partial):
-    return lax.psum_scatter(partial, "row", scatter_dimension=1, tiled=True).astype(F32)
+    return lax.psum_scatter(partial, "row", scatter_dimension=1, tiled=True)
 
 
 def after(value, *others):
@@ -867,7 +867,7 @@
     def hidden_of(n, ready, *others):
         s = state[n]
         summed = row_scatter(after(s["mixed_out"], *ready))
-        s["hidden"] = chunk(residual, n).astype(F32) + after(summed, *others)
+        s["hidden"] = chunk(residual, n).astype(F32) + after(summed, *others).astype(F32)
         s["wide"] = row_gather(after(s["hidden"].astype(BF16), masks))
 
     def second_norm(n, *others):
@@ -937,7 +937,7 @@
         acc_router = acc_router + lax.dot_general(
             shard, logit_grad, TN, preferred_element_type=F32
         )
-        normed_two_grad = normed_two_grad + lax.dot_general(
+        normed_two_grad = normed_two_grad.astype(F32) + lax.dot_general(
             logit_grad, router_rows, NT, preferred_element_type=F32
         )
         inner_two = slot_inner[:, None] + jnp.sum(
@@ -1022,7 +1022,7 @@
             normed_one_grad = after(normed_one_grad, other_grads[4])
         input_blocks.append(
             s["hidden_total"]
-            + normed_one_grad * gain_one * scale_one
+            + normed_one_grad.astype(F32) * gain_one * scale_one
             - chunk(residual, n).astype(F32)
             * (scale_one * scale_one * inner_one / model_width)
         )
@@ -1077,7 +1077,7 @@
         pieces_sum(own, [other_grads[j] for j in parts])[None]
         for own, parts in zip(own_grads, ((0, 3, 4), (5, 6), (1, 2)))
     )
-    output_blocks = [(s["hidden"] + s["mixture"]).astype(BF16) for s in state]
+    output_blocks = [(s["hidden"] + s["mixture"].astype(F32)).astype(BF16) for s in state]
     return (
         jnp.concatenate(output_blocks, axis=0),
         jnp.concatenate(input_blocks, axis=0),

time: 955 us -> 945 us (0.990)
  starting transfers between devices: 80.1 us -> 68.7 us
  other arithmetic: 86.9 us -> 76.7 us
  Pallas kernels: 256 us -> 266 us
    ppermute x24, waiting for transfers between devices: 172 us -> 161 us  [moved(): lax.ppermute(block, axis, [(i, (i + by) % count) for i in range(count)])]
    all_gather x6, starting transfers between devices: 10.7 us -> 0.25 us  [row_gather(): return lax.all_gather(block, 'row', axis=block.ndim - 1, tiled=True)]
    convert_element_type x6 -> x0, other arithmetic: 10.2 us -> none  [row_scatter(): lax.psum_scatter(partial, 'row', scatter_dimension=1, tiled=True)]
    pallas_call x4, Pallas kernels: 132 us -> 142 us  [expert_pair(): pl.pallas_call(functools.partial(pair_kernel, first, place, experts), out...]
    unnamed x225 -> x215, local copies, waits for them, and re-layouts: 29.2 us -> 27.1 us
  transfers between devices with their start and end apart: 93 -> 93, of which waited for: 38 -> 38; matrix products, arithmetic and copies ran while one was open for 20% -> 19% of each run, Pallas kernels for 27% -> 28%
where the time goes in v5:
time: 945 us; the launch traced here: 934 us
  waiting for transfers between devices  369 us (39%)
  Pallas kernels  266 us (28%)
  local copies, waits for them, and re-layouts  77.5 us (8%)
  other arithmetic  76.7 us (8%)
  starting transfers between devices  68.7 us (7%)
  matrix products  60.3 us (6%)
  between operations  16.5 us (2%)
    ppermute x24, waiting for transfers between devices, moved(): lax.ppermute(block, axis, [(i, (i + by) % count) for i in range(count)])  161 us
    ppermute x55, waiting for transfers between devices, swapped(): return lax.ppermute(block, axis, [(i, i ^ 1 << bit) for i in range(count)])  150 us
    pallas_call x4, Pallas kernels, expert_pair(): pl.pallas_call(functools.partial(pair_kernel, first, place, experts), out...  142 us
    convert_element_type x14, other arithmetic, added(): return total.astype(parts[0].dtype)  40.7 us
    ppermute x24, starting transfers between devices, moved(): lax.ppermute(block, axis, [(i, (i + by) % count) for i in range(count)])  40.2 us
    pallas_call x2, Pallas kernels, attention_backward(): pl.pallas_call(functools.partial(attention_backward_kernel, head ** (-0.5...  35.6 us
    all_gather x6, waiting for transfers between devices, row_gather(): return lax.all_gather(block, 'row', axis=block.ndim - 1, tiled=True)  31.2 us
    ppermute x55, starting transfers between devices, swapped(): return lax.ppermute(block, axis, [(i, i ^ 1 << bit) for i in range(count)])  27.2 us
  transfers between devices with their start and end apart: 93, of which 38 were waited for; matrix products, arithmetic and copies ran while one was open for 19% of the time, Pallas kernels for 28%

profile of v5, /device:TPU:0, one launch (start us, length us, event | category | flops | bytes accessed | tf_op | source)
XLA Modules:
  0.0 934.1 jit_solution(17417391147999313426)
XLA Ops:
  10.8 3.0 collective-permute-start.1
  14.3 3.6 collective-permute-start.9
  19.1 23.4 %collective-permute-done.1.refs_2_ = bf16[512,1280]{1,0:T(8,128)(2,1)S(1)} collective-permute-done((bf16[512,1280]{1,0:T(8,128)(2,1)S(1)}, bf16[512,1280]{1,0:T(8,128)(2,1)S(1)}, u32[]{:S(2)}, u32[]{:S(2)}) %collective-permute-start.1) | collective-permute-done | bytes 1310752 | tf_op jit(solution)/shard_map/ppermute | solution.py:582
  54.4 17.8 %collective-permute-done.5.refs_2_ = bf16[1024,512]{1,0:T(8,128)(2,1)} collective-permute-done((bf16[1024,512]{1,0:T(8,128)(2,1)}, bf16[1024,512]{1,0:T(8,128)(2,1)}, u32[]{:S(2)}, u32[]{:S(2)}) %collective-permute-start.5) | collective-permute-done | bytes 1048608 | tf_op jit(solution)/shard_map/ppermute | solution.py:582
  76.6 14.1 %all-gather.7.cloned.1.call-done.in_ref = bf16[512,2048]{1,0:T(8,128)(2,1)} async-done(((bf16[512,512]{1,0:T(8,128)(2,1)}), bf16[512,2048]{1,0:T(8,128)(2,1)}) %all-gather.7.cloned.1.call-update) | async-done | bytes 2097168 | tf_op jit(solution)/shard_map/all_gather | solution.py:630
  98.6 9.0 attention_forward.2
  112.2 3.7 convolution_convert_fusion.1
  123.6 3.2 collective-permute-start.10
  128.7 17.2 %collective-permute-done.8 = bf16[512,512]{1,0:T(8,128)(2,1)S(1)} collective-permute-done((bf16[512,512]{1,0:T(8,128)(2,1)S(1)}, bf16[512,512]{1,0:T(8,128)(2,1)S(1)}, u32[]{:S(2)}, u32[]{:S(2)}) %collective-permute-start.8) | collective-permute-done | bytes 524320 | tf_op jit(solution)/shard_map/ppermute | solution.py:582
  148.7 7.8 all-gather.9.cloned.1.call-done.in_ref
  159.0 6.2 fusion.54.q_ref.k_ref.v_ref
  165.3 9.0 attention_forward.3
  174.3 3.7 convolution_convert_fusion
  179.6 10.1 %route_tables.1 = (bf16[8,512,128]{2,1,0:T(8,128)(2,1)S(1)}, s32[8,1,512]{2,1,0:T(1,128)S(1)}, s32[8,512,1]{2,1,0:T(8,128)S(1)}) custom-call(s32[2]{0:T(128)S(1)} %pad_add_fusion.2.expert_ref.scalars_ref, s32[8,512,8]{2,1,0:T(8,128)S(1)} %bitcast.139), custom_call_target="tpu_custom_call" | custom-call | flops 1000000000 | bytes 1000000 | tf_op jit(solution)/shard_map/route_tables/pallas_call | solution.py:453
  189.7 11.8 %reduce-scatter.9.cloned.1.call-done = bf16[512,512]{1,0:T(8,128)(2,1)} async-done(((bf16[512,2048]{1,0:T(8,128)(2,1)}), bf16[512,512]{1,0:T(8,128)(2,1)}) %reduce-scatter.9.cloned.1.call-update) | async-done | bytes 524304 | tf_op jit(solution)/shard_map/reduce_scatter | solution.py:634
  203.7 3.1 pad_maximum_fusion.1.refs_2_
  208.3 46.0 %collective-permute-done.14.refs_2_ = bf16[512,2048]{1,0:T(8,128)(2,1)} collective-permute-done((bf16[512,2048]{1,0:T(8,128)(2,1)}, bf16[512,2048]{1,0:T(8,128)(2,1)}, u32[]{:S(2)}, u32[]{:S(2)}) %collective-permute-start.14) | collective-permute-done | bytes 2097184 | tf_op jit(solution)/shard_map/ppermute | solution.py:582
  266.8 43.1 %expert_pair.4 = (bf16[512,2048]{1,0:T(8,128)(2,1)}, bf16[512,2048]{1,0:T(8,128)(2,1)}, bf16[512,2048]{1,0:T(8,128)(2,1)}, bf16[512,2048]{1,0:T(8,128)(2,1)}, f3...) custom-call(s32[2]{0:T(128)} %copy-done.62, ...), custom_call_target="tpu_custom_call" | custom-call | flops 35999997952 | bytes 10000000 | tf_op jit(solution)/shard_map/expert_pair/pallas_call | solution.py:397
  318.5 32.9 %expert_pair.5 = (bf16[512,2048]{1,0:T(8,128)(2,1)}, bf16[512,2048]{1,0:T(8,128)(2,1)}, bf16[512,2048]{1,0:T(8,128)(2,1)}, bf16[512,2048]{1,0:T(8,128)(2,1)}, f3...) custom-call(s32[2]{0:T(128)} %copy-done.62, ...), custom_call_target="tpu_custom_call", output_to_operand_aliasing={{7}: (12, {}), {8}: (13, {}), {9}: (14, {}), {10}: (15, {})... | custom-call | flops 35999997952 | bytes 10000000 | tf_op jit(solution)/shard_map/expert_pair/pallas_call | solution.py:397
  356.6 5.9 all-gather.13.cloned.1.call-done.in_ref
  371.8 32.6 %expert_pair.6 = (bf16[512,2048]{1,0:T(8,128)(2,1)}, bf16[512,2048]{1,0:T(8,128)(2,1)}, bf16[512,2048]{1,0:T(8,128)(2,1)}, bf16[512,2048]{1,0:T(8,128)(2,1)}, f3...) custom-call(s32[2]{0:T(128)} %copy-done.62, ...), custom_call_target="tpu_custom_call", output_to_operand_aliasing={{7}: (12, {}), {8}: (13, {}), {9}: (14, {}), {10}: (15, {})... | custom-call | flops 35999997952 | bytes 10000000 | tf_op jit(solution)/shard_map/expert_pair/pallas_call | solution.py:397
  405.7 11.1 %collective-permute-done.28.refs_0_ = bf16[512,2048]{1,0:T(8,128)(2,1)} collective-permute-done((bf16[512,2048]{1,0:T(8,128)(2,1)S(1)}, bf16[512,2048]{1,0:T(8,128)(2,1)}, u32[]{:S(2)}, u32[]{:S(2)}) %collective-permute-start.28) | collective-permute-done | bytes 2097184 | tf_op jit(solution)/shard_map/ppermute | solution.py:582
  424.5 33.0 %expert_pair.7 = (bf16[512,2048]{1,0:T(8,128)(2,1)}, bf16[512,2048]{1,0:T(8,128)(2,1)}, bf16[512,2048]{1,0:T(8,128)(2,1)}, bf16[512,2048]{1,0:T(8,128)(2,1)}, f3...) custom-call(s32[2]{0:T(128)} %copy-done.62, ...), custom_call_target="tpu_custom_call", output_to_operand_aliasing={{7}: (12, {}), {8}: (13, {}), {9}: (14, {}), {10}: (15, {})... | custom-call | flops 35999997952 | bytes 10000000 | tf_op jit(solution)/shard_map/expert_pair/pallas_call | solution.py:397
  458.9 2.9 collective-permute-done.32
  462.6 5.8 collective-permute-done.34
  468.4 4.1 add_convert_fusion.4
  478.4 12.8 %grad_of.1.own_ref = bf16[768,2048]{1,0:T(8,128)(2,1)} custom-call(bf16[2560,768]{1,0:T(8,128)(2,1)} %get-tuple-element.189.rows_ref, bf16[2560,2048]{1,0:T(8,128)(2,1)} %get-tuple-element.190.refs_0_), custom_call_target="tpu_custom_call" | custom-call | flops 1000000000 | bytes 1000000 | tf_op jit(solution)/shard_map/grad_of/pallas_call | solution.py:565
  491.2 22.2 %grads_of.1 = (bf16[2048,768]{1,0:T(8,128)(2,1)}, bf16[2048,768]{1,0:T(8,128)(2,1)}) custom-call(bf16[2560,2048]{1,0:T(8,128)(2,1)} %get-tuple-element.191.rows_ref, bf16[2560,768]{1,0:T(8,128)(2,1)} %get-tuple-element.192.refs_0_, bf16[2560,768]{1,0:T(8,128)(2,1)} %get-tuple-element.193.refs_1_), custom_call_target="tpu_custom_call" | custom-call | flops 1000000000 | bytes 1000000 | tf_op jit(solution)/shard_map/grads_of/pallas_call | solution.py:548
  516.0 10.1 %collective-permute-done.39.refs_0_ = bf16[256,768]{1,0:T(8,128)(2,1)S(1)} collective-permute-done((bf16[256,768]{1,0:T(8,128)(2,1)S(1)}, bf16[256,768]{1,0:T(8,128)(2,1)S(1)}, u32[]{:S(2)}, u32[]{:S(2)}) %collective-permute-start.39) | collective-permute-done | bytes 393248 | tf_op jit(solution)/shard_map/ppermute | solution.py:587
  526.1 4.3 add_convert_fusion.5
  531.5 3.9 collective-permute-done.49
  537.4 6.5 collective-permute-done.50
  545.6 5.6 collective-permute-done.40
  551.7 8.3 collective-permute-done.41
  560.6 14.6 %reduce-scatter.13.cloned.1.call-done = bf16[512,512]{1,0:T(8,128)(2,1)} async-done(((bf16[512,2048]{1,0:T(8,128)(2,1)}), bf16[512,512]{1,0:T(8,128)(2,1)}) %reduce-scatter.13.cloned.1.call-update) | async-done | bytes 524304 | tf_op jit(solution)/shard_map/reduce_scatter | solution.py:634
  575.2 4.3 multiply_reduce_fusion.2
  586.1 31.8 %collective-permute-done.42.refs_0_ = bf16[384,2048]{1,0:T(8,128)(2,1)S(1)} collective-permute-done((bf16[384,2048]{1,0:T(8,128)(2,1)S(1)}, bf16[384,2048]{1,0:T(8,128)(2,1)S(1)}, u32[]{:S(2)}, u32[]{:S(2)}) %collective-permute-start.42) | collective-permute-done | bytes 1572896 | tf_op jit(solution)/shard_map/ppermute | solution.py:587
  622.1 3.4 all-gather.17.cloned.1.call-done
  625.4 5.3 convolution_convert_fusion.4.g_ref
  630.8 17.7 %attention_backward.3 = (bf16[512,1280]{1,0:T(8,128)(2,1)S(1)}, f32[512,128]{1,0:T(8,128)}, f32[512,128]{1,0:T(8,128)}, f32[512,1]{1,0:T(8,128)S(1)}, f32[2,128]{1,0:T(2,128)S(1)}) custom-call(f32[512,1280]{1,0:T(8,128)} %copy-done.67, f32[512,1280]{1,0:T(8,128)} %copy-done.67, f32[512,1280]{1,0:T(8,128)} %copy-done.67, ...), custom_call_target="tpu_custom_call" | custom-call | flops 20000000000 | bytes 10000000 | tf_op jit(solution)/shard_map/attention_backward/pallas_call | solution.py:157
  648.6 4.1 multiply_reduce_fusion.1
  657.2 10.8 %collective-permute-done.37 = bf16[512,2048]{1,0:T(8,128)(2,1)} collective-permute-done((bf16[512,2048]{1,0:T(8,128)(2,1)}, bf16[512,2048]{1,0:T(8,128)(2,1)}, u32[]{:S(2)}, u32[]{:S(2)}) %collective-permute-start.37) | collective-permute-done | bytes 2097184 | tf_op jit(solution)/shard_map/ppermute | solution.py:582
  668.0 4.8 add_convert_fusion.6
  672.8 5.3 convolution_convert_fusion.5.g_ref
  678.2 17.9 %attention_backward.2 = (bf16[512,1280]{1,0:T(8,128)(2,1)S(1)}, f32[512,128]{1,0:T(8,128)}, f32[512,128]{1,0:T(8,128)}, f32[512,1]{1,0:T(8,128)S(1)}, f32[2,128]{1,0:T(2,128)S(1)}) custom-call(f32[512,1280]{1,0:T(8,128)} %copy-done.68, f32[512,1280]{1,0:T(8,128)} %copy-done.68, f32[512,1280]{1,0:T(8,128)} %copy-done.68, ...), custom_call_target="tpu_custom_call" | custom-call | flops 20000000000 | bytes 10000000 | tf_op jit(solution)/shard_map/attention_backward/pallas_call | solution.py:157
  696.1 4.2 multiply_reduce_fusion
  702.5 3.9 add_convert_fusion.3
  709.6 27.2 %collective-permute-done.45.refs_2_ = bf16[1024,768]{1,0:T(8,128)(2,1)S(1)} collective-permute-done((bf16[1024,768]{1,0:T(8,128)(2,1)S(1)}, bf16[1024,768]{1,0:T(8,128)(2,1)S(1)}, u32[]{:S(2)}, u32[]{:S(2)}) %collective-permute-start.45) | collective-permute-done | bytes 1572896 | tf_op jit(solution)/shard_map/ppermute | solution.py:587
  746.8 4.6 pieces_sum.5
  751.4 6.0 pieces_sum.3
  757.4 15.5 %collective-permute-done.46.refs_0_ = bf16[1024,768]{1,0:T(8,128)(2,1)} collective-permute-done((bf16[1024,768]{1,0:T(8,128)(2,1)}, bf16[1024,768]{1,0:T(8,128)(2,1)}, u32[]{:S(2)}, u32[]{:S(2)}) %collective-permute-start.46) | collective-permute-done | bytes 1572896 | tf_op jit(solution)/shard_map/ppermute | solution.py:587
  774.8 4.8 add_convert_fusion.2
  780.9 4.2 fusion.55
  813.4 11.3 %collective-permute-done.55 = bf16[1024,512]{1,0:T(8,128)(2,1)} collective-permute-done((bf16[1024,512]{1,0:T(8,128)(2,1)}, bf16[1024,512]{1,0:T(8,128)(2,1)}, u32[]{:S(2)}, u32[]{:S(2)}) %collective-permute-start.55) | collective-permute-done | bytes 1048608 | tf_op jit(solution)/shard_map/ppermute | solution.py:582
  830.6 5.0 pieces_sum.4
  840.1 11.2 %collective-permute-done.73 = f32[37120]{0:T(1024)S(1)} collective-permute-done((f32[37120]{0:T(1024)S(1)}, f32[37120]{0:T(1024)S(1)}, u32[]{:S(2)}, u32[]{:S(2)}) %collective-permute-start.73) | collective-permute-done | bytes 148512 | tf_op jit(solution)/shard_map/ppermute | solution.py:587
  853.3 2.9 add_convert_fusion.11
  856.3 4.1 collective-permute-done.58
  865.7 9.2 collective-permute-done.74
  877.0 3.8 collective-permute-start.65
  883.6 3.5 collective-permute-done.63
  903.3 3.3 fusion.1
  909.1 10.6 %collective-permute-done.75 = bf16[512,1024]{1,0:T(8,128)(2,1)} collective-permute-done((bf16[512,1024]{1,0:T(8,128)(2,1)S(1)}, bf16[512,1024]{1,0:T(8,128)(2,1)}, u32[]{:S(2)}, u32[]{:S(2)}) %collective-permute-start.75) | collective-permute-done | bytes 1048608 | tf_op jit(solution)/shard_map/ppermute | solution.py:587
  920.2 2.9 convert_add_fusion.1
  (526 shorter events, 221.7 us)
Async XLA Ops:
  7.2 83.5 %all-gather.7.cloned.1.call-start = ((), (), s32[]{:S(2)}) async-start(), calls=%async_computation.8 | async-start | bytes 2621440 | tf_op jit(solution)/shard_map/all_gather | solution.py:630
  9.6 146.9 %all-gather.9.cloned.1.call-start = ((), (), s32[]{:S(2)}) async-start(), calls=%async_computation.10 | async-start | bytes 2621440 | tf_op jit(solution)/shard_map/all_gather | solution.py:630
  10.8 31.8 %collective-permute-start.1 = (bf16[512,1280]{1,0:T(8,128)(2,1)S(1)}, bf16[512,1280]{1,0:T(8,128)(2,1)S(1)}, u32[]{:S(2)}, u32[]{:S(2)}) collective-permute-start(bf16[512,1280]{1,0:T(8,128)(2,1)S(1)} %pad_maximum_fusion.3.refs_0_), channel_id=1, source_target_pairs={{0,2},{1,3},{2,0},{3,1},{4,6},{5,7},{6,4},{7,5},{8,10},{9,11},{10,... | collective-permute-start | bytes 3932168 | tf_op jit(solution)/shard_map/ppermute | solution.py:582
  13.8 38.9 %collective-permute-start = (bf16[512,1280]{1,0:T(8,128)(2,1)S(1)}, bf16[512,1280]{1,0:T(8,128)(2,1)}, u32[]{:S(2)}, u32[]{:S(2)}) collective-permute-start(bf16[512,1280]{1,0:T(8,128)(2,1)S(1)} %pad_maximum_fusion.3.refs_0_), channel_id=1, source_target_pairs={{0,1},{1,0},{2,3},{3,2},{4,5},{5,4},{6,7},{7,6},{8,9},{9,8},{10,11... | collective-permute-start | bytes 3932168 | tf_op jit(solution)/shard_map/ppermute | solution.py:587
  13.8 93.8 %collective-permute-start.3 = (bf16[1024,512]{1,0:T(8,128)(2,1)}, bf16[1024,512]{1,0:T(8,128)(2,1)}, u32[]{:S(2)}, u32[]{:S(2)}) collective-permute-start(bf16[1024,512]{1,0:T(8,128)(2,1)} %refs_0_.1), channel_id=1, source_target_pairs={{0,1},{1,0},{2,3},{3,2},{4,5},{5,4},{6,7},{7,6},{8,9},{9,8},{10,11... | collective-permute-start | bytes 3145736 | tf_op jit(solution)/shard_map/ppermute | solution.py:587
  14.3 107.2 %collective-permute-start.9 = (bf16[1024,512]{1,0:T(8,128)(2,1)}, bf16[1024,512]{1,0:T(8,128)(2,1)}, u32[]{:S(2)}, u32[]{:S(2)}) collective-permute-start(bf16[1024,512]{1,0:T(8,128)(2,1)} %param.31), channel_id=1, source_target_pairs={{0,12},{4,0},{8,4},{12,8},{1,13},{5,1},{9,5},{13,9},{2,14},{6,2},{... | collective-permute-start | bytes 3145736 | tf_op jit(solution)/shard_map/ppermute | solution.py:582
  17.9 183.6 %reduce-scatter.9.cloned.1.call-start = ((), (), s32[]{:S(2)}) async-start(), calls=%async_computation.9 | async-start | bytes 2621440 | tf_op jit(solution)/shard_map/reduce_scatter | solution.py:634
  42.5 29.6 %collective-permute-start.2 = (bf16[512,1280]{1,0:T(8,128)(2,1)S(1)}, bf16[512,1280]{1,0:T(8,128)(2,1)}, u32[]{:S(2)}, u32[]{:S(2)}) collective-permute-start(bf16[512,1280]{1,0:T(8,128)(2,1)S(1)} %collective-permute-done.1.refs_2_), channel_id=1, source_target_pairs={{0,1},{1,0},{2,3},{3,2},{4,5},{5,4},{6,7},{7,6},{8,9},{9,8},{10,11... | collective-permute-start | bytes 3932168 | tf_op jit(solution)/shard_map/ppermute | solution.py:587
  47.0 25.1 %collective-permute-start.5 = (bf16[1024,512]{1,0:T(8,128)(2,1)}, bf16[1024,512]{1,0:T(8,128)(2,1)}, u32[]{:S(2)}, u32[]{:S(2)}) collective-permute-start(bf16[1024,512]{1,0:T(8,128)(2,1)} %refs_0_.1), channel_id=1, source_target_pairs={{0,2},{1,3},{2,0},{3,1},{4,6},{5,7},{6,4},{7,5},{8,10},{9,11},{10,... | collective-permute-start | bytes 3145736 | tf_op jit(solution)/shard_map/ppermute | solution.py:582
  52.7 63.3 %collective-permute-start.7 = (bf16[1024,512]{1,0:T(8,128)(2,1)}, bf16[1024,512]{1,0:T(8,128)(2,1)}, u32[]{:S(2)}, u32[]{:S(2)}) collective-permute-start(bf16[1024,512]{1,0:T(8,128)(2,1)} %param.31), channel_id=1, source_target_pairs={{0,4},{4,8},{8,12},{12,0},{1,5},{5,9},{9,13},{13,1},{2,6},{6,10},{... | collective-permute-start | bytes 3145736 | tf_op jit(solution)/shard_map/ppermute | solution.py:582
  72.1 35.5 %collective-permute-start.6 = (bf16[1024,512]{1,0:T(8,128)(2,1)}, bf16[1024,512]{1,0:T(8,128)(2,1)}, u32[]{:S(2)}, u32[]{:S(2)}) collective-permute-start(bf16[1024,512]{1,0:T(8,128)(2,1)} %collective-permute-done.5.refs_2_), channel_id=1, source_target_pairs={{0,1},{1,0},{2,3},{3,2},{4,5},{5,4},{6,7},{7,6},{8,9},{9,8},{10,11... | collective-permute-start | bytes 3145736 | tf_op jit(solution)/shard_map/ppermute | solution.py:587
  115.9 138.4 %all-gather.11.cloned.1.call-start = ((), (), s32[]{:S(2)}) async-start(), calls=%async_computation.11 | async-start | bytes 2621440 | tf_op jit(solution)/shard_map/all_gather | solution.py:630
  118.1 27.8 %collective-permute-start.8 = (bf16[512,512]{1,0:T(8,128)(2,1)S(1)}, bf16[512,512]{1,0:T(8,128)(2,1)S(1)}, u32[]{:S(2)}, u32[]{:S(2)}) collective-permute-start(bf16[512,512]{1,0:T(8,128)(2,1)S(1)} %get-tuple-element.315), channel_id=1, source_target_pairs={{0,4},{4,8},{8,12},{12,0},{1,5},{5,9},{9,13},{13,1},{2,6},{6,10},{... | collective-permute-start | bytes 1572872 | tf_op jit(solution)/shard_map/ppermute | solution.py:582
  123.6 66.2 %collective-permute-start.10 = (bf16[512,512]{1,0:T(8,128)(2,1)}, bf16[512,512]{1,0:T(8,128)(2,1)}, u32[]{:S(2)}, u32[]{:S(2)}) collective-permute-start(bf16[512,512]{1,0:T(8,128)(2,1)} %get-tuple-element.317), channel_id=1, source_target_pairs={{0,12},{4,0},{8,4},{12,8},{1,13},{5,1},{9,5},{13,9},{2,14},{6,2},{... | collective-permute-start | bytes 1572872 | tf_op jit(solution)/shard_map/ppermute | solution.py:582
  147.6 59.2 %collective-permute-start.13 = (bf16[512,2048]{1,0:T(8,128)(2,1)}, bf16[512,2048]{1,0:T(8,128)(2,1)}, u32[]{:S(2)}, u32[]{:S(2)}) collective-permute-start(bf16[512,2048]{1,0:T(8,128)(2,1)} %pad_maximum_fusion.refs_2_), channel_id=1, source_target_pairs={{0,2},{1,3},{2,0},{3,1},{4,6},{5,7},{6,4},{7,5},{8,10},{9,11},{10,... | collective-permute-start | bytes 6291464 | tf_op jit(solution)/shard_map/ppermute | solution.py:582
  203.6 111.1 %reduce-scatter.11.cloned.1.call-start = ((), (), s32[]{:S(2)}) async-start(), calls=%async_computation.12 | async-start | bytes 2621440 | tf_op jit(solution)/shard_map/reduce_scatter | solution.py:634
  206.8 47.5 %collective-permute-start.14 = (bf16[512,2048]{1,0:T(8,128)(2,1)}, bf16[512,2048]{1,0:T(8,128)(2,1)}, u32[]{:S(2)}, u32[]{:S(2)}) collective-permute-start(bf16[512,2048]{1,0:T(8,128)(2,1)} %pad_maximum_fusion.1.refs_2_), channel_id=1, source_target_pairs={{0,2},{1,3},{2,0},{3,1},{4,6},{5,7},{6,4},{7,5},{8,10},{9,11},{10,... | collective-permute-start | bytes 6291464 | tf_op jit(solution)/shard_map/ppermute | solution.py:582
  208.3 58.5 %collective-permute-start.16 = (bf16[512,2048]{1,0:T(8,128)(2,1)}, bf16[512,2048]{1,0:T(8,128)(2,1)}, u32[]{:S(2)}, u32[]{:S(2)}) collective-permute-start(bf16[512,2048]{1,0:T(8,128)(2,1)} %pad_maximum_fusion.refs_2_), channel_id=1, source_target_pairs={{0,1},{1,0},{2,3},{3,2},{4,5},{5,4},{6,7},{7,6},{8,9},{9,8},{10,11... | collective-permute-start | bytes 6291464 | tf_op jit(solution)/shard_map/ppermute | solution.py:587
  265.2 97.3 %all-gather.13.cloned.1.call-start = ((), (), s32[]{:S(2)}) async-start(), calls=%async_computation.13 | async-start | bytes 2621440 | tf_op jit(solution)/shard_map/all_gather | solution.py:630
  265.3 48.4 %collective-permute-start.19 = (bf16[512,2048]{1,0:T(8,128)(2,1)}, bf16[512,2048]{1,0:T(8,128)(2,1)}, u32[]{:S(2)}, u32[]{:S(2)}) collective-permute-start(bf16[512,2048]{1,0:T(8,128)(2,1)} %get-tuple-element.146.refs_0_), channel_id=1, source_target_pairs={{0,2},{1,3},{2,0},{3,1},{4,6},{5,7},{6,4},{7,5},{8,10},{9,11},{10,... | collective-permute-start | bytes 6291464 | tf_op jit(solution)/shard_map/ppermute | solution.py:582
  316.7 243.9 %reduce-scatter.17.cloned.1.call-start = ((), (), s32[]{:S(2)}) async-start(), calls=%async_computation.17 | async-start | bytes 2621440 | tf_op jit(solution)/shard_map/reduce_scatter | solution.py:634
  351.4 15.0 %collective-permute-start.23 = (bf16[512,2048]{1,0:T(8,128)(2,1)}, bf16[512,2048]{1,0:T(8,128)(2,1)}, u32[]{:S(2)}, u32[]{:S(2)}) collective-permute-start(bf16[512,2048]{1,0:T(8,128)(2,1)} %get-tuple-element.156), channel_id=1, source_target_pairs={{0,1},{1,0},{2,3},{3,2},{4,5},{5,4},{6,7},{7,6},{8,9},{9,8},{10,11... | collective-permute-start | bytes 6291464 | tf_op jit(solution)/shard_map/ppermute | solution.py:587
  352.8 17.6 %collective-permute-start.26 = (bf16[512,2048]{1,0:T(8,128)(2,1)}, bf16[512,2048]{1,0:T(8,128)(2,1)}, u32[]{:S(2)}, u32[]{:S(2)}) collective-permute-start(bf16[512,2048]{1,0:T(8,128)(2,1)} %pad_maximum_fusion.1.refs_2_), channel_id=1, source_target_pairs={{0,1},{1,0},{2,3},{3,2},{4,5},{5,4},{6,7},{7,6},{8,9},{9,8},{10,11... | collective-permute-start | bytes 6291464 | tf_op jit(solution)/shard_map/ppermute | solution.py:587
  368.9 47.9 %collective-permute-start.28 = (bf16[512,2048]{1,0:T(8,128)(2,1)S(1)}, bf16[512,2048]{1,0:T(8,128)(2,1)}, u32[]{:S(2)}, u32[]{:S(2)}) collective-permute-start(bf16[512,2048]{1,0:T(8,128)(2,1)S(1)} %get-tuple-element.171.refs_0_), channel_id=1, source_target_pairs={{0,2},{1,3},{2,0},{3,1},{4,6},{5,7},{6,4},{7,5},{8,10},{9,11},{10,... | collective-permute-start | bytes 6291464 | tf_op jit(solution)/shard_map/ppermute | solution.py:582
  405.2 17.3 %collective-permute-start.30 = (bf16[512,2048]{1,0:T(8,128)(2,1)}, bf16[512,2048]{1,0:T(8,128)(2,1)S(1)}, u32[]{:S(2)}, u32[]{:S(2)}) collective-permute-start(bf16[512,2048]{1,0:T(8,128)(2,1)} %collective-permute-done.14.refs_2_), channel_id=1, source_target_pairs={{0,1},{1,0},{2,3},{3,2},{4,5},{5,4},{6,7},{7,6},{8,9},{9,8},{10,11... | collective-permute-start | bytes 6291464 | tf_op jit(solution)/shard_map/ppermute | solution.py:587
  419.3 49.1 %collective-permute-start.48 = (bf16[512,2048]{1,0:T(8,128)(2,1)}, bf16[512,2048]{1,0:T(8,128)(2,1)S(1)}, u32[]{:S(2)}, u32[]{:S(2)}) collective-permute-start(bf16[512,2048]{1,0:T(8,128)(2,1)} %get-tuple-element.210), channel_id=1, source_target_pairs={{0,1},{1,0},{2,3},{3,2},{4,5},{5,4},{6,7},{7,6},{8,9},{9,8},{10,11... | collective-permute-start | bytes 6291464 | tf_op jit(solution)/shard_map/ppermute | solution.py:587
  421.0 47.4 %collective-permute-start.34 = (bf16[512,2048]{1,0:T(8,128)(2,1)S(1)}, bf16[512,2048]{1,0:T(8,128)(2,1)}, u32[]{:S(2)}, u32[]{:S(2)}) collective-permute-start(bf16[512,2048]{1,0:T(8,128)(2,1)S(1)} %add_convert_fusion.8), channel_id=1, source_target_pairs={{0,2},{1,3},{2,0},{3,1},{4,6},{5,7},{6,4},{7,5},{8,10},{9,11},{10,... | collective-permute-start | bytes 6291464 | tf_op jit(solution)/shard_map/ppermute | solution.py:582
  457.5 16.8 %collective-permute-start.31 = (bf16[512,2048]{1,0:T(8,128)(2,1)}, bf16[512,2048]{1,0:T(8,128)(2,1)}, u32[]{:S(2)}, u32[]{:S(2)}) collective-permute-start(bf16[512,2048]{1,0:T(8,128)(2,1)} %get-tuple-element.179), channel_id=1, source_target_pairs={{0,1},{1,0},{2,3},{3,2},{4,5},{5,4},{6,7},{7,6},{8,9},{9,8},{10,11... | collective-permute-start | bytes 6291464 | tf_op jit(solution)/shard_map/ppermute | solution.py:587
  472.5 102.7 %reduce-scatter.13.cloned.1.call-start = ((), (), s32[]{:S(2)}) async-start(), calls=%async_computation.14 | async-start | bytes 2621440 | tf_op jit(solution)/shard_map/reduce_scatter | solution.py:634
  476.9 49.2 %collective-permute-start.36 = (bf16[512,2048]{1,0:T(8,128)(2,1)S(1)}, bf16[512,2048]{1,0:T(8,128)(2,1)S(1)}, u32[]{:S(2)}, u32[]{:S(2)}) collective-permute-start(bf16[512,2048]{1,0:T(8,128)(2,1)S(1)} %add_convert_fusion.7), channel_id=1, source_target_pairs={{0,2},{1,3},{2,0},{3,1},{4,6},{5,7},{6,4},{7,5},{8,10},{9,11},{10,... | collective-permute-start | bytes 6291464 | tf_op jit(solution)/shard_map/ppermute | solution.py:582
  478.4 47.7 %collective-permute-start.38 = (bf16[512,2048]{1,0:T(8,128)(2,1)}, bf16[512,2048]{1,0:T(8,128)(2,1)}, u32[]{:S(2)}, u32[]{:S(2)}) collective-permute-start(bf16[512,2048]{1,0:T(8,128)(2,1)} %get-tuple-element.187), channel_id=1, source_target_pairs={{0,1},{1,0},{2,3},{3,2},{4,5},{5,4},{6,7},{7,6},{8,9},{9,8},{10,11... | collective-permute-start | bytes 6291464 | tf_op jit(solution)/shard_map/ppermute | solution.py:587
  530.5 95.0 %all-gather.17.cloned.1.call-start = ((), (), s32[]{:S(2)}) async-start(), calls=%async_computation.18 | async-start | bytes 2621440 | tf_op jit(solution)/shard_map/all_gather | solution.py:630
  579.5 93.2 %all-gather.15.cloned.1.call-start = ((), (), s32[]{:S(2)}) async-start(), calls=%async_computation.15 | async-start | bytes 2621440 | tf_op jit(solution)/shard_map/all_gather | solution.py:630
  581.1 36.8 %collective-permute-start.42 = (bf16[384,2048]{1,0:T(8,128)(2,1)S(1)}, bf16[384,2048]{1,0:T(8,128)(2,1)S(1)}, u32[]{:S(2)}, u32[]{:S(2)}) collective-permute-start(bf16[384,2048]{1,0:T(8,128)(2,1)S(1)} %get-tuple-element.199), channel_id=1, source_target_pairs={{0,16},{16,0},{1,17},{17,1},{2,18},{18,2},{3,19},{19,3},{4,20},{20... | collective-permute-start | bytes 4718600 | tf_op jit(solution)/shard_map/ppermute | solution.py:587
  582.6 85.3 %collective-permute-start.17 = (bf16[512,2048]{1,0:T(8,128)(2,1)}, bf16[512,2048]{1,0:T(8,128)(2,1)}, u32[]{:S(2)}, u32[]{:S(2)}) collective-permute-start(bf16[512,2048]{1,0:T(8,128)(2,1)} %get-tuple-element.143), channel_id=1, source_target_pairs={{0,1},{1,0},{2,3},{3,2},{4,5},{5,4},{6,7},{7,6},{8,9},{9,8},{10,11... | collective-permute-start | bytes 6291464 | tf_op jit(solution)/shard_map/ppermute | solution.py:587
  619.1 36.7 %collective-permute-start.43 = (bf16[384,2048]{1,0:T(8,128)(2,1)}, bf16[384,2048]{1,0:T(8,128)(2,1)}, u32[]{:S(2)}, u32[]{:S(2)}) collective-permute-start(bf16[384,2048]{1,0:T(8,128)(2,1)} %get-tuple-element.203), channel_id=1, source_target_pairs={{0,16},{16,0},{1,17},{17,1},{2,18},{18,2},{3,19},{19,3},{4,20},{20... | collective-permute-start | bytes 4718600 | tf_op jit(solution)/shard_map/ppermute | solution.py:587
  620.6 47.4 %collective-permute-start.37 = (bf16[512,2048]{1,0:T(8,128)(2,1)}, bf16[512,2048]{1,0:T(8,128)(2,1)}, u32[]{:S(2)}, u32[]{:S(2)}) collective-permute-start(bf16[512,2048]{1,0:T(8,128)(2,1)} %add_convert_fusion.9), channel_id=1, source_target_pairs={{0,2},{1,3},{2,0},{3,1},{4,6},{5,7},{6,4},{7,5},{8,10},{9,11},{10,... | collective-permute-start | bytes 6291464 | tf_op jit(solution)/shard_map/ppermute | solution.py:582
  622.0 281.2 %reduce-scatter.21.cloned.1.call-start = ((), (), s32[]{:S(2)}) async-start(), calls=%async_computation.20 | async-start | bytes 2621440 | tf_op jit(solution)/shard_map/reduce_scatter | solution.py:634
  652.8 250.5 %reduce-scatter.23.cloned.1.call-start = ((), (), s32[]{:S(2)}) async-start(), calls=%async_computation.21 | async-start | bytes 2621440 | tf_op jit(solution)/shard_map/reduce_scatter | solution.py:634
  655.8 46.7 %collective-permute-start.53 = (bf16[512,2048]{1,0:T(8,128)(2,1)}, bf16[512,2048]{1,0:T(8,128)(2,1)}, u32[]{:S(2)}, u32[]{:S(2)}) collective-permute-start(bf16[512,2048]{1,0:T(8,128)(2,1)} %get-tuple-element.216), channel_id=1, source_target_pairs={{0,1},{1,0},{2,3},{3,2},{4,5},{5,4},{6,7},{7,6},{8,9},{9,8},{10,11... | collective-permute-start | bytes 6291464 | tf_op jit(solution)/shard_map/ppermute | solution.py:587
  655.8 46.3 %collective-permute-start.44 = (bf16[768,768]{1,0:T(8,128)(2,1)}, bf16[768,768]{1,0:T(8,128)(2,1)}, u32[]{:S(2)}, u32[]{:S(2)}) collective-permute-start(bf16[768,768]{1,0:T(8,128)(2,1)} %slice.275), channel_id=1, source_target_pairs={{0,16},{16,0},{1,17},{17,1},{2,18},{18,2},{3,19},{19,3},{4,20},{20... | collective-permute-start | bytes 3538952 | tf_op jit(solution)/shard_map/ppermute | solution.py:587
  700.3 202.9 %reduce-scatter.15.cloned.1.call-start = ((), (), s32[]{:S(2)}) async-start(), calls=%async_computation.16 | async-start | bytes 2621440 | tf_op jit(solution)/shard_map/reduce_scatter | solution.py:634
  702.1 34.8 %collective-permute-start.45 = (bf16[1024,768]{1,0:T(8,128)(2,1)S(1)}, bf16[1024,768]{1,0:T(8,128)(2,1)S(1)}, u32[]{:S(2)}, u32[]{:S(2)}) collective-permute-start(bf16[1024,768]{1,0:T(8,128)(2,1)S(1)} %slice.276), channel_id=1, source_target_pairs={{0,16},{16,0},{1,17},{17,1},{2,18},{18,2},{3,19},{19,3},{4,20},{20... | collective-permute-start | bytes 4718600 | tf_op jit(solution)/shard_map/ppermute | solution.py:587
  702.5 72.3 %collective-permute-start.59 = (bf16[512,2048]{1,0:T(8,128)(2,1)}, bf16[512,2048]{1,0:T(8,128)(2,1)}, u32[]{:S(2)}, u32[]{:S(2)}) collective-permute-start(bf16[512,2048]{1,0:T(8,128)(2,1)} %get-tuple-element.223), channel_id=1, source_target_pairs={{0,1},{1,0},{2,3},{3,2},{4,5},{5,4},{6,7},{7,6},{8,9},{9,8},{10,11... | collective-permute-start | bytes 6291464 | tf_op jit(solution)/shard_map/ppermute | solution.py:587
  706.4 68.4 %collective-permute-start.54 = (bf16[512,2048]{1,0:T(8,128)(2,1)}, bf16[512,2048]{1,0:T(8,128)(2,1)}, u32[]{:S(2)}, u32[]{:S(2)}) collective-permute-start(bf16[512,2048]{1,0:T(8,128)(2,1)} %add_convert_fusion.3), channel_id=1, source_target_pairs={{0,2},{1,3},{2,0},{3,1},{4,6},{5,7},{6,4},{7,5},{8,10},{9,11},{10,... | collective-permute-start | bytes 6291464 | tf_op jit(solution)/shard_map/ppermute | solution.py:582
  738.0 35.0 %collective-permute-start.46 = (bf16[1024,768]{1,0:T(8,128)(2,1)}, bf16[1024,768]{1,0:T(8,128)(2,1)}, u32[]{:S(2)}, u32[]{:S(2)}) collective-permute-start(bf16[1024,768]{1,0:T(8,128)(2,1)} %get-tuple-element.207), channel_id=1, source_target_pairs={{0,16},{16,0},{1,17},{17,1},{2,18},{18,2},{3,19},{19,3},{4,20},{20... | collective-permute-start | bytes 4718600 | tf_op jit(solution)/shard_map/ppermute | solution.py:587
  772.9 55.0 %collective-permute-start.47 = (bf16[1024,768]{1,0:T(8,128)(2,1)}, bf16[1024,768]{1,0:T(8,128)(2,1)}, u32[]{:S(2)}, u32[]{:S(2)}) collective-permute-start(bf16[1024,768]{1,0:T(8,128)(2,1)} %get-tuple-element.208), channel_id=1, source_target_pairs={{0,16},{16,0},{1,17},{17,1},{2,18},{18,2},{3,19},{19,3},{4,20},{20... | collective-permute-start | bytes 4718600 | tf_op jit(solution)/shard_map/ppermute | solution.py:587
  779.8 27.7 %collective-permute-start.67 = (f32[512]{0:T(512)S(1)}, f32[512]{0:T(512)S(1)}, u32[]{:S(2)}, u32[]{:S(2)}) collective-permute-start(f32[512]{0:T(512)S(1)} %reduce.12), channel_id=1, source_target_pairs={{0,4},{4,0},{8,12},{12,8},{1,5},{5,1},{9,13},{13,9},{2,6},{6,2},{1... | collective-permute-start | bytes 6152 | tf_op jit(solution)/shard_map/ppermute | solution.py:587
  779.9 123.4 %reduce-scatter.19.cloned.1.call-start = ((), (), s32[]{:S(2)}) async-start(), calls=%async_computation.19 | async-start | bytes 2621440 | tf_op jit(solution)/shard_map/reduce_scatter | solution.py:634
  794.8 16.3 %collective-permute-start.71 = (f32[37120]{0:T(1024)}, f32[37120]{0:T(1024)}, u32[]{:S(2)}, u32[]{:S(2)}) collective-permute-start(f32[37120]{0:T(1024)} %constant_dynamic-update-slice_fusion.8), channel_id=1, source_target_pairs={{0,1},{1,0},{2,3},{3,2},{4,5},{5,4},{6,7},{7,6},{8,9},{9,8},{10,11... | collective-permute-start | bytes 445448 | tf_op jit(solution)/shard_map/ppermute | solution.py:587
  794.9 29.8 %collective-permute-start.51 = (bf16[1024,512]{1,0:T(8,128)(2,1)}, bf16[1024,512]{1,0:T(8,128)(2,1)}, u32[]{:S(2)}, u32[]{:S(2)}) collective-permute-start(bf16[1024,512]{1,0:T(8,128)(2,1)} %get-tuple-element.294), channel_id=1, source_target_pairs={{0,1},{1,0},{2,3},{3,2},{4,5},{5,4},{6,7},{7,6},{8,9},{9,8},{10,11... | collective-permute-start | bytes 3145736 | tf_op jit(solution)/shard_map/ppermute | solution.py:587
  799.1 25.5 %collective-permute-start.55 = (bf16[1024,512]{1,0:T(8,128)(2,1)}, bf16[1024,512]{1,0:T(8,128)(2,1)}, u32[]{:S(2)}, u32[]{:S(2)}) collective-permute-start(bf16[1024,512]{1,0:T(8,128)(2,1)} %add_convert_fusion.13), channel_id=1, source_target_pairs={{0,2},{1,3},{2,0},{3,1},{4,6},{5,7},{6,4},{7,5},{8,10},{9,11},{10,... | collective-permute-start | bytes 3145736 | tf_op jit(solution)/shard_map/ppermute | solution.py:582
  807.5 44.5 %collective-permute-start.62 = (bf16[512,1024]{1,0:T(8,128)(2,1)}, bf16[512,1024]{1,0:T(8,128)(2,1)}, u32[]{:S(2)}, u32[]{:S(2)}) collective-permute-start(bf16[512,1024]{1,0:T(8,128)(2,1)} %get-tuple-element.293), channel_id=1, source_target_pairs={{0,1},{1,0},{2,3},{3,2},{4,5},{5,4},{6,7},{7,6},{8,9},{9,8},{10,11... | collective-permute-start | bytes 3145736 | tf_op jit(solution)/shard_map/ppermute | solution.py:587
  811.0 18.4 %collective-permute-start.69 = (f32[512]{0:T(512)S(1)}, f32[512]{0:T(512)S(1)}, u32[]{:S(2)}, u32[]{:S(2)}) collective-permute-start(f32[512]{0:T(512)S(1)} %reduce.15), channel_id=1, source_target_pairs={{0,4},{4,0},{8,12},{12,8},{1,5},{5,1},{9,13},{13,9},{2,6},{6,2},{1... | collective-permute-start | bytes 6152 | tf_op jit(solution)/shard_map/ppermute | solution.py:587
  824.6 13.4 %collective-permute-start.57 = (bf16[512,256]{0,1:T(8,128)(2,1)}, bf16[512,256]{0,1:T(8,128)(2,1)}, u32[]{:S(2)}, u32[]{:S(2)}) collective-permute-start(bf16[512,256]{0,1:T(8,128)(2,1)} %get-tuple-element.311), channel_id=1, source_target_pairs={{0,1},{1,0},{2,3},{3,2},{4,5},{5,4},{6,7},{7,6},{8,9},{9,8},{10,11... | collective-permute-start | bytes 786440 | tf_op jit(solution)/shard_map/ppermute | solution.py:587
  829.5 35.6 %collective-permute-start.60 = (bf16[1024,512]{1,0:T(8,128)(2,1)S(1)}, bf16[1024,512]{1,0:T(8,128)(2,1)}, u32[]{:S(2)}, u32[]{:S(2)}) collective-permute-start(bf16[1024,512]{1,0:T(8,128)(2,1)S(1)} %add_convert_fusion.12), channel_id=1, source_target_pairs={{0,16},{16,0},{1,17},{17,1},{2,18},{18,2},{3,19},{19,3},{4,20},{20... | collective-permute-start | bytes 3145736 | tf_op jit(solution)/shard_map/ppermute | solution.py:587
  835.7 27.3 %collective-permute-start.56 = (bf16[512,256]{0,1:T(8,128)(2,1)}, bf16[512,256]{0,1:T(8,128)(2,1)}, u32[]{:S(2)}, u32[]{:S(2)}) collective-permute-start(bf16[512,256]{0,1:T(8,128)(2,1)} %get-tuple-element.310), channel_id=1, source_target_pairs={{0,1},{1,0},{2,3},{3,2},{4,5},{5,4},{6,7},{7,6},{8,9},{9,8},{10,11... | collective-permute-start | bytes 786440 | tf_op jit(solution)/shard_map/ppermute | solution.py:587
  836.6 57.0 %collective-permute-start.61 = (bf16[512,1024]{1,0:T(8,128)(2,1)S(1)}, bf16[512,1024]{1,0:T(8,128)(2,1)}, u32[]{:S(2)}, u32[]{:S(2)}) collective-permute-start(bf16[512,1024]{1,0:T(8,128)(2,1)S(1)} %copy-done.81), channel_id=1, source_target_pairs={{0,1},{1,0},{2,3},{3,2},{4,5},{5,4},{6,7},{7,6},{8,9},{9,8},{10,11... | collective-permute-start | bytes 3145736 | tf_op jit(solution)/shard_map/ppermute | solution.py:587
  838.1 13.2 %collective-permute-start.73 = (f32[37120]{0:T(1024)S(1)}, f32[37120]{0:T(1024)S(1)}, u32[]{:S(2)}, u32[]{:S(2)}) collective-permute-start(f32[37120]{0:T(1024)S(1)} %add.402), channel_id=1, source_target_pairs={{0,4},{4,0},{8,12},{12,8},{1,5},{5,1},{9,13},{13,9},{2,6},{6,2},{1... | collective-permute-start | bytes 445448 | tf_op jit(solution)/shard_map/ppermute | solution.py:587
  851.3 14.0 %collective-permute-start.70 = (f32[512]{0:T(512)S(1)}, f32[512]{0:T(512)S(1)}, u32[]{:S(2)}, u32[]{:S(2)}) collective-permute-start(f32[512]{0:T(512)S(1)} %add.392), channel_id=1, source_target_pairs={{0,8},{4,12},{8,0},{12,4},{1,9},{5,13},{9,1},{13,5},{2,10},{6,14},... | collective-permute-start | bytes 6152 | tf_op jit(solution)/shard_map/ppermute | solution.py:587
  860.4 14.5 %collective-permute-start.74 = (f32[37120]{0:T(1024)}, f32[37120]{0:T(1024)}, u32[]{:S(2)}, u32[]{:S(2)}) collective-permute-start(f32[37120]{0:T(1024)} %add.403), channel_id=1, source_target_pairs={{0,8},{4,12},{8,0},{12,4},{1,9},{5,13},{9,1},{13,5},{2,10},{6,14},... | collective-permute-start | bytes 445448 | tf_op jit(solution)/shard_map/ppermute | solution.py:587
  863.0 24.1 %collective-permute-start.63 = (bf16[512,1024]{1,0:T(8,128)(2,1)}, bf16[512,1024]{1,0:T(8,128)(2,1)}, u32[]{:S(2)}, u32[]{:S(2)}) collective-permute-start(bf16[512,1024]{1,0:T(8,128)(2,1)} %add_convert_fusion.11), channel_id=1, source_target_pairs={{0,2},{1,3},{2,0},{3,1},{4,6},{5,7},{6,4},{7,5},{8,10},{9,11},{10,... | collective-permute-start | bytes 3145736 | tf_op jit(solution)/shard_map/ppermute | solution.py:582
  877.0 13.8 %collective-permute-start.65 = (bf16[512,256]{0,1:T(8,128)(2,1)S(1)}, bf16[512,256]{0,1:T(8,128)(2,1)S(1)}, u32[]{:S(2)}, u32[]{:S(2)}) collective-permute-start(bf16[512,256]{0,1:T(8,128)(2,1)S(1)} %get-tuple-element.283), channel_id=1, source_target_pairs={{0,12},{4,0},{8,4},{12,8},{1,13},{5,1},{9,5},{13,9},{2,14},{6,2},{... | collective-permute-start | bytes 786440 | tf_op jit(solution)/shard_map/ppermute | solution.py:582
  896.1 23.6 %collective-permute-start.75 = (bf16[512,1024]{1,0:T(8,128)(2,1)S(1)}, bf16[512,1024]{1,0:T(8,128)(2,1)}, u32[]{:S(2)}, u32[]{:S(2)}) collective-permute-start(bf16[512,1024]{1,0:T(8,128)(2,1)S(1)} %add_convert_fusion.10), channel_id=1, source_target_pairs={{0,16},{16,0},{1,17},{17,1},{2,18},{18,2},{3,19},{19,3},{4,20},{20... | collective-permute-start | bytes 3145736 | tf_op jit(solution)/shard_map/ppermute | solution.py:587
  (133 other events, 1578.1 us)
Sparse Core Ops, SparseCore 0:
  10.2 80.4 all-gather.6
  92.8 63.5 all-gather.8
  159.3 42.1 reduce-scatter.8
  203.8 45.2 all-gather.10
  265.4 43.5 reduce-scatter.10
  316.8 45.6 all-gather.12
  472.7 42.5 reduce-scatter.16
  530.6 44.5 reduce-scatter.12
  579.6 45.7 all-gather.16
  626.8 44.5 all-gather.14
  674.4 42.6 reduce-scatter.20
  719.3 43.2 reduce-scatter.22
  780.0 42.7 reduce-scatter.14
  825.6 49.5 reduce-scatter.18

commit v6 on v5

--- a/solution.py
+++ b/solution.py
@@ -280,10 +280,10 @@
     load_tok[0].start()
     for load in load_grad[:parts]:
         load.start()
-    for load in load_w:
-        load.start()
     load_tok[1].start()
     for load in load_grad[parts:]:
+        load.start()
+    for load in load_w:
         load.start()
     expert = scalars_ref[0]
     stores = []

time: 945 us -> 945 us (level)
  no operation moved by 1% of the time
where the time goes in v6:
time: 945 us; the launch traced here: 934 us
  waiting for transfers between devices  369 us (39%)
  Pallas kernels  266 us (28%)
  local copies, waits for them, and re-layouts  77.5 us (8%)
  other arithmetic  76.8 us (8%)
  starting transfers between devices  68.6 us (7%)
  matrix products  60.4 us (6%)
  between operations  16.5 us (2%)
    ppermute x24, waiting for transfers between devices, moved(): lax.ppermute(block, axis, [(i, (i + by) % count) for i in range(count)])  161 us
    ppermute x55, waiting for transfers between devices, swapped(): return lax.ppermute(block, axis, [(i, i ^ 1 << bit) for i in range(count)])  150 us
    pallas_call x4, Pallas kernels, expert_pair(): pl.pallas_call(functools.partial(pair_kernel, first, place, experts), out...  142 us
    convert_element_type x14, other arithmetic, added(): return total.astype(parts[0].dtype)  40.8 us
    ppermute x24, starting transfers between devices, moved(): lax.ppermute(block, axis, [(i, (i + by) % count) for i in range(count)])  39.8 us
    pallas_call x2, Pallas kernels, attention_backward(): pl.pallas_call(functools.partial(attention_backward_kernel, head ** (-0.5...  35.6 us
    all_gather x6, waiting for transfers between devices, row_gather(): return lax.all_gather(block, 'row', axis=block.ndim - 1, tiled=True)  31.1 us
    ppermute x55, starting transfers between devices, swapped(): return lax.ppermute(block, axis, [(i, i ^ 1 << bit) for i in range(count)])  27.4 us
  transfers between devices with their start and end apart: 93, of which 38 were waited for; matrix products, arithmetic and copies ran while one was open for 19% of the time, Pallas kernels for 28%

profile of v6, /device:TPU:0, one launch (start us, length us, event | category | flops | bytes accessed | tf_op | source)
XLA Modules:
  0.0 934.2 jit_solution(10794253356378016985)
XLA Ops:
  10.8 3.0 collective-permute-start.1
  14.3 3.6 collective-permute-start.9
  19.1 23.4 %collective-permute-done.1.refs_2_ = bf16[512,1280]{1,0:T(8,128)(2,1)S(1)} collective-permute-done((bf16[512,1280]{1,0:T(8,128)(2,1)S(1)}, bf16[512,1280]{1,0:T(8,128)(2,1)S(1)}, u32[]{:S(2)}, u32[]{:S(2)}) %collective-permute-start.1) | collective-permute-done | bytes 1310752 | tf_op jit(solution)/shard_map/ppermute | solution.py:582
  54.4 17.8 %collective-permute-done.5.refs_2_ = bf16[1024,512]{1,0:T(8,128)(2,1)} collective-permute-done((bf16[1024,512]{1,0:T(8,128)(2,1)}, bf16[1024,512]{1,0:T(8,128)(2,1)}, u32[]{:S(2)}, u32[]{:S(2)}) %collective-permute-start.5) | collective-permute-done | bytes 1048608 | tf_op jit(solution)/shard_map/ppermute | solution.py:582
  76.6 14.1 %all-gather.7.cloned.1.call-done.in_ref = bf16[512,2048]{1,0:T(8,128)(2,1)} async-done(((bf16[512,512]{1,0:T(8,128)(2,1)}), bf16[512,2048]{1,0:T(8,128)(2,1)}) %all-gather.7.cloned.1.call-update) | async-done | bytes 2097168 | tf_op jit(solution)/shard_map/all_gather | solution.py:630
  98.6 9.0 attention_forward.2
  112.2 3.7 convolution_convert_fusion.1
  123.6 3.2 collective-permute-start.10
  128.7 17.2 %collective-permute-done.8 = bf16[512,512]{1,0:T(8,128)(2,1)S(1)} collective-permute-done((bf16[512,512]{1,0:T(8,128)(2,1)S(1)}, bf16[512,512]{1,0:T(8,128)(2,1)S(1)}, u32[]{:S(2)}, u32[]{:S(2)}) %collective-permute-start.8) | collective-permute-done | bytes 524320 | tf_op jit(solution)/shard_map/ppermute | solution.py:582
  148.7 7.8 all-gather.9.cloned.1.call-done.in_ref
  159.0 6.2 fusion.54.q_ref.k_ref.v_ref
  165.3 9.0 attention_forward.3
  174.3 3.7 convolution_convert_fusion
  179.6 10.1 %route_tables.1 = (bf16[8,512,128]{2,1,0:T(8,128)(2,1)S(1)}, s32[8,1,512]{2,1,0:T(1,128)S(1)}, s32[8,512,1]{2,1,0:T(8,128)S(1)}) custom-call(s32[2]{0:T(128)S(1)} %pad_add_fusion.2.expert_ref.scalars_ref, s32[8,512,8]{2,1,0:T(8,128)S(1)} %bitcast.139), custom_call_target="tpu_custom_call" | custom-call | flops 1000000000 | bytes 1000000 | tf_op jit(solution)/shard_map/route_tables/pallas_call | solution.py:453
  189.7 11.8 %reduce-scatter.9.cloned.1.call-done = bf16[512,512]{1,0:T(8,128)(2,1)} async-done(((bf16[512,2048]{1,0:T(8,128)(2,1)}), bf16[512,512]{1,0:T(8,128)(2,1)}) %reduce-scatter.9.cloned.1.call-update) | async-done | bytes 524304 | tf_op jit(solution)/shard_map/reduce_scatter | solution.py:634
  203.7 3.1 pad_maximum_fusion.1.refs_2_
  208.3 46.0 %collective-permute-done.14.refs_2_ = bf16[512,2048]{1,0:T(8,128)(2,1)} collective-permute-done((bf16[512,2048]{1,0:T(8,128)(2,1)}, bf16[512,2048]{1,0:T(8,128)(2,1)}, u32[]{:S(2)}, u32[]{:S(2)}) %collective-permute-start.14) | collective-permute-done | bytes 2097184 | tf_op jit(solution)/shard_map/ppermute | solution.py:582
  266.8 43.2 %expert_pair.4 = (bf16[512,2048]{1,0:T(8,128)(2,1)}, bf16[512,2048]{1,0:T(8,128)(2,1)}, bf16[512,2048]{1,0:T(8,128)(2,1)}, bf16[512,2048]{1,0:T(8,128)(2,1)}, f3...) custom-call(s32[2]{0:T(128)} %copy-done.62, ...), custom_call_target="tpu_custom_call" | custom-call | flops 35999997952 | bytes 10000000 | tf_op jit(solution)/shard_map/expert_pair/pallas_call | solution.py:397
  318.6 32.9 %expert_pair.5 = (bf16[512,2048]{1,0:T(8,128)(2,1)}, bf16[512,2048]{1,0:T(8,128)(2,1)}, bf16[512,2048]{1,0:T(8,128)(2,1)}, bf16[512,2048]{1,0:T(8,128)(2,1)}, f3...) custom-call(s32[2]{0:T(128)} %copy-done.62, ...), custom_call_target="tpu_custom_call", output_to_operand_aliasing={{7}: (12, {}), {8}: (13, {}), {9}: (14, {}), {10}: (15, {})... | custom-call | flops 35999997952 | bytes 10000000 | tf_op jit(solution)/shard_map/expert_pair/pallas_call | solution.py:397
  356.7 5.8 all-gather.13.cloned.1.call-done.in_ref
  371.8 32.6 %expert_pair.6 = (bf16[512,2048]{1,0:T(8,128)(2,1)}, bf16[512,2048]{1,0:T(8,128)(2,1)}, bf16[512,2048]{1,0:T(8,128)(2,1)}, bf16[512,2048]{1,0:T(8,128)(2,1)}, f3...) custom-call(s32[2]{0:T(128)} %copy-done.62, ...), custom_call_target="tpu_custom_call", output_to_operand_aliasing={{7}: (12, {}), {8}: (13, {}), {9}: (14, {}), {10}: (15, {})... | custom-call | flops 35999997952 | bytes 10000000 | tf_op jit(solution)/shard_map/expert_pair/pallas_call | solution.py:397
  405.7 11.2 %collective-permute-done.28.refs_0_ = bf16[512,2048]{1,0:T(8,128)(2,1)} collective-permute-done((bf16[512,2048]{1,0:T(8,128)(2,1)S(1)}, bf16[512,2048]{1,0:T(8,128)(2,1)}, u32[]{:S(2)}, u32[]{:S(2)}) %collective-permute-start.28) | collective-permute-done | bytes 2097184 | tf_op jit(solution)/shard_map/ppermute | solution.py:582
  424.5 33.0 %expert_pair.7 = (bf16[512,2048]{1,0:T(8,128)(2,1)}, bf16[512,2048]{1,0:T(8,128)(2,1)}, bf16[512,2048]{1,0:T(8,128)(2,1)}, bf16[512,2048]{1,0:T(8,128)(2,1)}, f3...) custom-call(s32[2]{0:T(128)} %copy-done.62, ...), custom_call_target="tpu_custom_call", output_to_operand_aliasing={{7}: (12, {}), {8}: (13, {}), {9}: (14, {}), {10}: (15, {})... | custom-call | flops 35999997952 | bytes 10000000 | tf_op jit(solution)/shard_map/expert_pair/pallas_call | solution.py:397
  458.8 2.9 collective-permute-done.32
  462.5 5.9 collective-permute-done.34
  468.4 4.1 add_convert_fusion.4
  478.4 12.8 %grad_of.1.own_ref = bf16[768,2048]{1,0:T(8,128)(2,1)} custom-call(bf16[2560,768]{1,0:T(8,128)(2,1)} %get-tuple-element.189.rows_ref, bf16[2560,2048]{1,0:T(8,128)(2,1)} %get-tuple-element.190.refs_0_), custom_call_target="tpu_custom_call" | custom-call | flops 1000000000 | bytes 1000000 | tf_op jit(solution)/shard_map/grad_of/pallas_call | solution.py:565
  491.2 22.2 %grads_of.1 = (bf16[2048,768]{1,0:T(8,128)(2,1)}, bf16[2048,768]{1,0:T(8,128)(2,1)}) custom-call(bf16[2560,2048]{1,0:T(8,128)(2,1)} %get-tuple-element.191.rows_ref, bf16[2560,768]{1,0:T(8,128)(2,1)} %get-tuple-element.192.refs_0_, bf16[2560,768]{1,0:T(8,128)(2,1)} %get-tuple-element.193.refs_1_), custom_call_target="tpu_custom_call" | custom-call | flops 1000000000 | bytes 1000000 | tf_op jit(solution)/shard_map/grads_of/pallas_call | solution.py:548
  516.0 10.1 %collective-permute-done.39.refs_0_ = bf16[256,768]{1,0:T(8,128)(2,1)S(1)} collective-permute-done((bf16[256,768]{1,0:T(8,128)(2,1)S(1)}, bf16[256,768]{1,0:T(8,128)(2,1)S(1)}, u32[]{:S(2)}, u32[]{:S(2)}) %collective-permute-start.39) | collective-permute-done | bytes 393248 | tf_op jit(solution)/shard_map/ppermute | solution.py:587
  526.1 4.3 add_convert_fusion.5
  531.5 3.9 collective-permute-done.49
  537.4 6.5 collective-permute-done.50
  545.6 5.7 collective-permute-done.40
  551.8 8.3 collective-permute-done.41
  560.7 14.6 %reduce-scatter.13.cloned.1.call-done = bf16[512,512]{1,0:T(8,128)(2,1)} async-done(((bf16[512,2048]{1,0:T(8,128)(2,1)}), bf16[512,512]{1,0:T(8,128)(2,1)}) %reduce-scatter.13.cloned.1.call-update) | async-done | bytes 524304 | tf_op jit(solution)/shard_map/reduce_scatter | solution.py:634
  575.2 4.3 multiply_reduce_fusion.2
  586.2 31.8 %collective-permute-done.42.refs_0_ = bf16[384,2048]{1,0:T(8,128)(2,1)S(1)} collective-permute-done((bf16[384,2048]{1,0:T(8,128)(2,1)S(1)}, bf16[384,2048]{1,0:T(8,128)(2,1)S(1)}, u32[]{:S(2)}, u32[]{:S(2)}) %collective-permute-start.42) | collective-permute-done | bytes 1572896 | tf_op jit(solution)/shard_map/ppermute | solution.py:587
  622.1 3.4 all-gather.17.cloned.1.call-done
  625.5 5.3 convolution_convert_fusion.4.g_ref
  630.9 17.7 %attention_backward.3 = (bf16[512,1280]{1,0:T(8,128)(2,1)S(1)}, f32[512,128]{1,0:T(8,128)}, f32[512,128]{1,0:T(8,128)}, f32[512,1]{1,0:T(8,128)S(1)}, f32[2,128]{1,0:T(2,128)S(1)}) custom-call(f32[512,1280]{1,0:T(8,128)} %copy-done.67, f32[512,1280]{1,0:T(8,128)} %copy-done.67, f32[512,1280]{1,0:T(8,128)} %copy-done.67, ...), custom_call_target="tpu_custom_call" | custom-call | flops 20000000000 | bytes 10000000 | tf_op jit(solution)/shard_map/attention_backward/pallas_call | solution.py:157
  648.7 4.1 multiply_reduce_fusion.1
  657.2 10.7 %collective-permute-done.37 = bf16[512,2048]{1,0:T(8,128)(2,1)} collective-permute-done((bf16[512,2048]{1,0:T(8,128)(2,1)}, bf16[512,2048]{1,0:T(8,128)(2,1)}, u32[]{:S(2)}, u32[]{:S(2)}) %collective-permute-start.37) | collective-permute-done | bytes 2097184 | tf_op jit(solution)/shard_map/ppermute | solution.py:582
  668.0 4.8 add_convert_fusion.6
  672.8 5.3 convolution_convert_fusion.5.g_ref
  678.2 17.9 %attention_backward.2 = (bf16[512,1280]{1,0:T(8,128)(2,1)S(1)}, f32[512,128]{1,0:T(8,128)}, f32[512,128]{1,0:T(8,128)}, f32[512,1]{1,0:T(8,128)S(1)}, f32[2,128]{1,0:T(2,128)S(1)}) custom-call(f32[512,1280]{1,0:T(8,128)} %copy-done.68, f32[512,1280]{1,0:T(8,128)} %copy-done.68, f32[512,1280]{1,0:T(8,128)} %copy-done.68, ...), custom_call_target="tpu_custom_call" | custom-call | flops 20000000000 | bytes 10000000 | tf_op jit(solution)/shard_map/attention_backward/pallas_call | solution.py:157
  696.1 4.2 multiply_reduce_fusion
  702.5 3.9 add_convert_fusion.3
  709.7 27.2 %collective-permute-done.45.refs_2_ = bf16[1024,768]{1,0:T(8,128)(2,1)S(1)} collective-permute-done((bf16[1024,768]{1,0:T(8,128)(2,1)S(1)}, bf16[1024,768]{1,0:T(8,128)(2,1)S(1)}, u32[]{:S(2)}, u32[]{:S(2)}) %collective-permute-start.45) | collective-permute-done | bytes 1572896 | tf_op jit(solution)/shard_map/ppermute | solution.py:587
  746.8 4.6 pieces_sum.5
  751.4 6.0 pieces_sum.3
  757.5 15.6 %collective-permute-done.46.refs_0_ = bf16[1024,768]{1,0:T(8,128)(2,1)} collective-permute-done((bf16[1024,768]{1,0:T(8,128)(2,1)}, bf16[1024,768]{1,0:T(8,128)(2,1)}, u32[]{:S(2)}, u32[]{:S(2)}) %collective-permute-start.46) | collective-permute-done | bytes 1572896 | tf_op jit(solution)/shard_map/ppermute | solution.py:587
  774.9 4.8 add_convert_fusion.2
  780.9 4.2 fusion.55
  813.4 11.3 %collective-permute-done.55 = bf16[1024,512]{1,0:T(8,128)(2,1)} collective-permute-done((bf16[1024,512]{1,0:T(8,128)(2,1)}, bf16[1024,512]{1,0:T(8,128)(2,1)}, u32[]{:S(2)}, u32[]{:S(2)}) %collective-permute-start.55) | collective-permute-done | bytes 1048608 | tf_op jit(solution)/shard_map/ppermute | solution.py:582
  830.7 5.1 pieces_sum.4
  840.2 11.2 %collective-permute-done.73 = f32[37120]{0:T(1024)S(1)} collective-permute-done((f32[37120]{0:T(1024)S(1)}, f32[37120]{0:T(1024)S(1)}, u32[]{:S(2)}, u32[]{:S(2)}) %collective-permute-start.73) | collective-permute-done | bytes 148512 | tf_op jit(solution)/shard_map/ppermute | solution.py:587
  853.3 2.9 add_convert_fusion.11
  856.2 4.2 collective-permute-done.58
  865.8 9.1 collective-permute-done.74
  877.1 3.8 collective-permute-start.65
  883.7 3.5 collective-permute-done.63
  903.4 3.3 fusion.1
  909.2 10.6 %collective-permute-done.75 = bf16[512,1024]{1,0:T(8,128)(2,1)} collective-permute-done((bf16[512,1024]{1,0:T(8,128)(2,1)S(1)}, bf16[512,1024]{1,0:T(8,128)(2,1)}, u32[]{:S(2)}, u32[]{:S(2)}) %collective-permute-start.75) | collective-permute-done | bytes 1048608 | tf_op jit(solution)/shard_map/ppermute | solution.py:587
  920.5 2.9 convert_add_fusion.1
  (526 shorter events, 221.6 us)
Async XLA Ops:
  7.2 83.5 %all-gather.7.cloned.1.call-start = ((), (), s32[]{:S(2)}) async-start(), calls=%async_computation.8 | async-start | bytes 2621440 | tf_op jit(solution)/shard_map/all_gather | solution.py:630
  9.6 146.9 %all-gather.9.cloned.1.call-start = ((), (), s32[]{:S(2)}) async-start(), calls=%async_computation.10 | async-start | bytes 2621440 | tf_op jit(solution)/shard_map/all_gather | solution.py:630
  10.8 31.8 %collective-permute-start.1 = (bf16[512,1280]{1,0:T(8,128)(2,1)S(1)}, bf16[512,1280]{1,0:T(8,128)(2,1)S(1)}, u32[]{:S(2)}, u32[]{:S(2)}) collective-permute-start(bf16[512,1280]{1,0:T(8,128)(2,1)S(1)} %pad_maximum_fusion.3.refs_0_), channel_id=1, source_target_pairs={{0,2},{1,3},{2,0},{3,1},{4,6},{5,7},{6,4},{7,5},{8,10},{9,11},{10,... | collective-permute-start | bytes 3932168 | tf_op jit(solution)/shard_map/ppermute | solution.py:582
  13.8 38.9 %collective-permute-start = (bf16[512,1280]{1,0:T(8,128)(2,1)S(1)}, bf16[512,1280]{1,0:T(8,128)(2,1)}, u32[]{:S(2)}, u32[]{:S(2)}) collective-permute-start(bf16[512,1280]{1,0:T(8,128)(2,1)S(1)} %pad_maximum_fusion.3.refs_0_), channel_id=1, source_target_pairs={{0,1},{1,0},{2,3},{3,2},{4,5},{5,4},{6,7},{7,6},{8,9},{9,8},{10,11... | collective-permute-start | bytes 3932168 | tf_op jit(solution)/shard_map/ppermute | solution.py:587
  13.8 93.8 %collective-permute-start.3 = (bf16[1024,512]{1,0:T(8,128)(2,1)}, bf16[1024,512]{1,0:T(8,128)(2,1)}, u32[]{:S(2)}, u32[]{:S(2)}) collective-permute-start(bf16[1024,512]{1,0:T(8,128)(2,1)} %refs_0_.1), channel_id=1, source_target_pairs={{0,1},{1,0},{2,3},{3,2},{4,5},{5,4},{6,7},{7,6},{8,9},{9,8},{10,11... | collective-permute-start | bytes 3145736 | tf_op jit(solution)/shard_map/ppermute | solution.py:587
  14.3 107.2 %collective-permute-start.9 = (bf16[1024,512]{1,0:T(8,128)(2,1)}, bf16[1024,512]{1,0:T(8,128)(2,1)}, u32[]{:S(2)}, u32[]{:S(2)}) collective-permute-start(bf16[1024,512]{1,0:T(8,128)(2,1)} %param.31), channel_id=1, source_target_pairs={{0,12},{4,0},{8,4},{12,8},{1,13},{5,1},{9,5},{13,9},{2,14},{6,2},{... | collective-permute-start | bytes 3145736 | tf_op jit(solution)/shard_map/ppermute | solution.py:582
  17.9 183.6 %reduce-scatter.9.cloned.1.call-start = ((), (), s32[]{:S(2)}) async-start(), calls=%async_computation.9 | async-start | bytes 2621440 | tf_op jit(solution)/shard_map/reduce_scatter | solution.py:634
  42.5 29.6 %collective-permute-start.2 = (bf16[512,1280]{1,0:T(8,128)(2,1)S(1)}, bf16[512,1280]{1,0:T(8,128)(2,1)}, u32[]{:S(2)}, u32[]{:S(2)}) collective-permute-start(bf16[512,1280]{1,0:T(8,128)(2,1)S(1)} %collective-permute-done.1.refs_2_), channel_id=1, source_target_pairs={{0,1},{1,0},{2,3},{3,2},{4,5},{5,4},{6,7},{7,6},{8,9},{9,8},{10,11... | collective-permute-start | bytes 3932168 | tf_op jit(solution)/shard_map/ppermute | solution.py:587
  47.0 25.1 %collective-permute-start.5 = (bf16[1024,512]{1,0:T(8,128)(2,1)}, bf16[1024,512]{1,0:T(8,128)(2,1)}, u32[]{:S(2)}, u32[]{:S(2)}) collective-permute-start(bf16[1024,512]{1,0:T(8,128)(2,1)} %refs_0_.1), channel_id=1, source_target_pairs={{0,2},{1,3},{2,0},{3,1},{4,6},{5,7},{6,4},{7,5},{8,10},{9,11},{10,... | collective-permute-start | bytes 3145736 | tf_op jit(solution)/shard_map/ppermute | solution.py:582
  52.7 63.3 %collective-permute-start.7 = (bf16[1024,512]{1,0:T(8,128)(2,1)}, bf16[1024,512]{1,0:T(8,128)(2,1)}, u32[]{:S(2)}, u32[]{:S(2)}) collective-permute-start(bf16[1024,512]{1,0:T(8,128)(2,1)} %param.31), channel_id=1, source_target_pairs={{0,4},{4,8},{8,12},{12,0},{1,5},{5,9},{9,13},{13,1},{2,6},{6,10},{... | collective-permute-start | bytes 3145736 | tf_op jit(solution)/shard_map/ppermute | solution.py:582
  72.1 35.5 %collective-permute-start.6 = (bf16[1024,512]{1,0:T(8,128)(2,1)}, bf16[1024,512]{1,0:T(8,128)(2,1)}, u32[]{:S(2)}, u32[]{:S(2)}) collective-permute-start(bf16[1024,512]{1,0:T(8,128)(2,1)} %collective-permute-done.5.refs_2_), channel_id=1, source_target_pairs={{0,1},{1,0},{2,3},{3,2},{4,5},{5,4},{6,7},{7,6},{8,9},{9,8},{10,11... | collective-permute-start | bytes 3145736 | tf_op jit(solution)/shard_map/ppermute | solution.py:587
  115.9 138.4 %all-gather.11.cloned.1.call-start = ((), (), s32[]{:S(2)}) async-start(), calls=%async_computation.11 | async-start | bytes 2621440 | tf_op jit(solution)/shard_map/all_gather | solution.py:630
  118.1 27.8 %collective-permute-start.8 = (bf16[512,512]{1,0:T(8,128)(2,1)S(1)}, bf16[512,512]{1,0:T(8,128)(2,1)S(1)}, u32[]{:S(2)}, u32[]{:S(2)}) collective-permute-start(bf16[512,512]{1,0:T(8,128)(2,1)S(1)} %get-tuple-element.315), channel_id=1, source_target_pairs={{0,4},{4,8},{8,12},{12,0},{1,5},{5,9},{9,13},{13,1},{2,6},{6,10},{... | collective-permute-start | bytes 1572872 | tf_op jit(solution)/shard_map/ppermute | solution.py:582
  123.6 66.2 %collective-permute-start.10 = (bf16[512,512]{1,0:T(8,128)(2,1)}, bf16[512,512]{1,0:T(8,128)(2,1)}, u32[]{:S(2)}, u32[]{:S(2)}) collective-permute-start(bf16[512,512]{1,0:T(8,128)(2,1)} %get-tuple-element.317), channel_id=1, source_target_pairs={{0,12},{4,0},{8,4},{12,8},{1,13},{5,1},{9,5},{13,9},{2,14},{6,2},{... | collective-permute-start | bytes 1572872 | tf_op jit(solution)/shard_map/ppermute | solution.py:582
  147.6 59.2 %collective-permute-start.13 = (bf16[512,2048]{1,0:T(8,128)(2,1)}, bf16[512,2048]{1,0:T(8,128)(2,1)}, u32[]{:S(2)}, u32[]{:S(2)}) collective-permute-start(bf16[512,2048]{1,0:T(8,128)(2,1)} %pad_maximum_fusion.refs_2_), channel_id=1, source_target_pairs={{0,2},{1,3},{2,0},{3,1},{4,6},{5,7},{6,4},{7,5},{8,10},{9,11},{10,... | collective-permute-start | bytes 6291464 | tf_op jit(solution)/shard_map/ppermute | solution.py:582
  203.6 111.1 %reduce-scatter.11.cloned.1.call-start = ((), (), s32[]{:S(2)}) async-start(), calls=%async_computation.12 | async-start | bytes 2621440 | tf_op jit(solution)/shard_map/reduce_scatter | solution.py:634
  206.8 47.5 %collective-permute-start.14 = (bf16[512,2048]{1,0:T(8,128)(2,1)}, bf16[512,2048]{1,0:T(8,128)(2,1)}, u32[]{:S(2)}, u32[]{:S(2)}) collective-permute-start(bf16[512,2048]{1,0:T(8,128)(2,1)} %pad_maximum_fusion.1.refs_2_), channel_id=1, source_target_pairs={{0,2},{1,3},{2,0},{3,1},{4,6},{5,7},{6,4},{7,5},{8,10},{9,11},{10,... | collective-permute-start | bytes 6291464 | tf_op jit(solution)/shard_map/ppermute | solution.py:582
  208.3 58.5 %collective-permute-start.16 = (bf16[512,2048]{1,0:T(8,128)(2,1)}, bf16[512,2048]{1,0:T(8,128)(2,1)}, u32[]{:S(2)}, u32[]{:S(2)}) collective-permute-start(bf16[512,2048]{1,0:T(8,128)(2,1)} %pad_maximum_fusion.refs_2_), channel_id=1, source_target_pairs={{0,1},{1,0},{2,3},{3,2},{4,5},{5,4},{6,7},{7,6},{8,9},{9,8},{10,11... | collective-permute-start | bytes 6291464 | tf_op jit(solution)/shard_map/ppermute | solution.py:587
  265.2 97.3 %all-gather.13.cloned.1.call-start = ((), (), s32[]{:S(2)}) async-start(), calls=%async_computation.13 | async-start | bytes 2621440 | tf_op jit(solution)/shard_map/all_gather | solution.py:630
  265.3 48.4 %collective-permute-start.19 = (bf16[512,2048]{1,0:T(8,128)(2,1)}, bf16[512,2048]{1,0:T(8,128)(2,1)}, u32[]{:S(2)}, u32[]{:S(2)}) collective-permute-start(bf16[512,2048]{1,0:T(8,128)(2,1)} %get-tuple-element.146.refs_0_), channel_id=1, source_target_pairs={{0,2},{1,3},{2,0},{3,1},{4,6},{5,7},{6,4},{7,5},{8,10},{9,11},{10,... | collective-permute-start | bytes 6291464 | tf_op jit(solution)/shard_map/ppermute | solution.py:582
  316.7 243.9 %reduce-scatter.17.cloned.1.call-start = ((), (), s32[]{:S(2)}) async-start(), calls=%async_computation.17 | async-start | bytes 2621440 | tf_op jit(solution)/shard_map/reduce_scatter | solution.py:634
  351.5 14.9 %collective-permute-start.23 = (bf16[512,2048]{1,0:T(8,128)(2,1)}, bf16[512,2048]{1,0:T(8,128)(2,1)}, u32[]{:S(2)}, u32[]{:S(2)}) collective-permute-start(bf16[512,2048]{1,0:T(8,128)(2,1)} %get-tuple-element.156), channel_id=1, source_target_pairs={{0,1},{1,0},{2,3},{3,2},{4,5},{5,4},{6,7},{7,6},{8,9},{9,8},{10,11... | collective-permute-start | bytes 6291464 | tf_op jit(solution)/shard_map/ppermute | solution.py:587
  352.9 17.5 %collective-permute-start.26 = (bf16[512,2048]{1,0:T(8,128)(2,1)}, bf16[512,2048]{1,0:T(8,128)(2,1)}, u32[]{:S(2)}, u32[]{:S(2)}) collective-permute-start(bf16[512,2048]{1,0:T(8,128)(2,1)} %pad_maximum_fusion.1.refs_2_), channel_id=1, source_target_pairs={{0,1},{1,0},{2,3},{3,2},{4,5},{5,4},{6,7},{7,6},{8,9},{9,8},{10,11... | collective-permute-start | bytes 6291464 | tf_op jit(solution)/shard_map/ppermute | solution.py:587
  369.0 47.9 %collective-permute-start.28 = (bf16[512,2048]{1,0:T(8,128)(2,1)S(1)}, bf16[512,2048]{1,0:T(8,128)(2,1)}, u32[]{:S(2)}, u32[]{:S(2)}) collective-permute-start(bf16[512,2048]{1,0:T(8,128)(2,1)S(1)} %get-tuple-element.171.refs_0_), channel_id=1, source_target_pairs={{0,2},{1,3},{2,0},{3,1},{4,6},{5,7},{6,4},{7,5},{8,10},{9,11},{10,... | collective-permute-start | bytes 6291464 | tf_op jit(solution)/shard_map/ppermute | solution.py:582
  405.2 17.3 %collective-permute-start.30 = (bf16[512,2048]{1,0:T(8,128)(2,1)}, bf16[512,2048]{1,0:T(8,128)(2,1)S(1)}, u32[]{:S(2)}, u32[]{:S(2)}) collective-permute-start(bf16[512,2048]{1,0:T(8,128)(2,1)} %collective-permute-done.14.refs_2_), channel_id=1, source_target_pairs={{0,1},{1,0},{2,3},{3,2},{4,5},{5,4},{6,7},{7,6},{8,9},{9,8},{10,11... | collective-permute-start | bytes 6291464 | tf_op jit(solution)/shard_map/ppermute | solution.py:587
  419.3 49.1 %collective-permute-start.48 = (bf16[512,2048]{1,0:T(8,128)(2,1)}, bf16[512,2048]{1,0:T(8,128)(2,1)S(1)}, u32[]{:S(2)}, u32[]{:S(2)}) collective-permute-start(bf16[512,2048]{1,0:T(8,128)(2,1)} %get-tuple-element.210), channel_id=1, source_target_pairs={{0,1},{1,0},{2,3},{3,2},{4,5},{5,4},{6,7},{7,6},{8,9},{9,8},{10,11... | collective-permute-start | bytes 6291464 | tf_op jit(solution)/shard_map/ppermute | solution.py:587
  421.0 47.4 %collective-permute-start.34 = (bf16[512,2048]{1,0:T(8,128)(2,1)S(1)}, bf16[512,2048]{1,0:T(8,128)(2,1)}, u32[]{:S(2)}, u32[]{:S(2)}) collective-permute-start(bf16[512,2048]{1,0:T(8,128)(2,1)S(1)} %add_convert_fusion.8), channel_id=1, source_target_pairs={{0,2},{1,3},{2,0},{3,1},{4,6},{5,7},{6,4},{7,5},{8,10},{9,11},{10,... | collective-permute-start | bytes 6291464 | tf_op jit(solution)/shard_map/ppermute | solution.py:582
  457.4 16.9 %collective-permute-start.31 = (bf16[512,2048]{1,0:T(8,128)(2,1)}, bf16[512,2048]{1,0:T(8,128)(2,1)}, u32[]{:S(2)}, u32[]{:S(2)}) collective-permute-start(bf16[512,2048]{1,0:T(8,128)(2,1)} %get-tuple-element.179), channel_id=1, source_target_pairs={{0,1},{1,0},{2,3},{3,2},{4,5},{5,4},{6,7},{7,6},{8,9},{9,8},{10,11... | collective-permute-start | bytes 6291464 | tf_op jit(solution)/shard_map/ppermute | solution.py:587
  472.6 102.6 %reduce-scatter.13.cloned.1.call-start = ((), (), s32[]{:S(2)}) async-start(), calls=%async_computation.14 | async-start | bytes 2621440 | tf_op jit(solution)/shard_map/reduce_scatter | solution.py:634
  477.0 49.1 %collective-permute-start.36 = (bf16[512,2048]{1,0:T(8,128)(2,1)S(1)}, bf16[512,2048]{1,0:T(8,128)(2,1)S(1)}, u32[]{:S(2)}, u32[]{:S(2)}) collective-permute-start(bf16[512,2048]{1,0:T(8,128)(2,1)S(1)} %add_convert_fusion.7), channel_id=1, source_target_pairs={{0,2},{1,3},{2,0},{3,1},{4,6},{5,7},{6,4},{7,5},{8,10},{9,11},{10,... | collective-permute-start | bytes 6291464 | tf_op jit(solution)/shard_map/ppermute | solution.py:582
  478.4 47.7 %collective-permute-start.38 = (bf16[512,2048]{1,0:T(8,128)(2,1)}, bf16[512,2048]{1,0:T(8,128)(2,1)}, u32[]{:S(2)}, u32[]{:S(2)}) collective-permute-start(bf16[512,2048]{1,0:T(8,128)(2,1)} %get-tuple-element.187), channel_id=1, source_target_pairs={{0,1},{1,0},{2,3},{3,2},{4,5},{5,4},{6,7},{7,6},{8,9},{9,8},{10,11... | collective-permute-start | bytes 6291464 | tf_op jit(solution)/shard_map/ppermute | solution.py:587
  530.5 95.0 %all-gather.17.cloned.1.call-start = ((), (), s32[]{:S(2)}) async-start(), calls=%async_computation.18 | async-start | bytes 2621440 | tf_op jit(solution)/shard_map/all_gather | solution.py:630
  579.6 93.2 %all-gather.15.cloned.1.call-start = ((), (), s32[]{:S(2)}) async-start(), calls=%async_computation.15 | async-start | bytes 2621440 | tf_op jit(solution)/shard_map/all_gather | solution.py:630
  581.2 36.8 %collective-permute-start.42 = (bf16[384,2048]{1,0:T(8,128)(2,1)S(1)}, bf16[384,2048]{1,0:T(8,128)(2,1)S(1)}, u32[]{:S(2)}, u32[]{:S(2)}) collective-permute-start(bf16[384,2048]{1,0:T(8,128)(2,1)S(1)} %get-tuple-element.199), channel_id=1, source_target_pairs={{0,16},{16,0},{1,17},{17,1},{2,18},{18,2},{3,19},{19,3},{4,20},{20... | collective-permute-start | bytes 4718600 | tf_op jit(solution)/shard_map/ppermute | solution.py:587
  582.6 85.3 %collective-permute-start.17 = (bf16[512,2048]{1,0:T(8,128)(2,1)}, bf16[512,2048]{1,0:T(8,128)(2,1)}, u32[]{:S(2)}, u32[]{:S(2)}) collective-permute-start(bf16[512,2048]{1,0:T(8,128)(2,1)} %get-tuple-element.143), channel_id=1, source_target_pairs={{0,1},{1,0},{2,3},{3,2},{4,5},{5,4},{6,7},{7,6},{8,9},{9,8},{10,11... | collective-permute-start | bytes 6291464 | tf_op jit(solution)/shard_map/ppermute | solution.py:587
  619.1 36.7 %collective-permute-start.43 = (bf16[384,2048]{1,0:T(8,128)(2,1)}, bf16[384,2048]{1,0:T(8,128)(2,1)}, u32[]{:S(2)}, u32[]{:S(2)}) collective-permute-start(bf16[384,2048]{1,0:T(8,128)(2,1)} %get-tuple-element.203), channel_id=1, source_target_pairs={{0,16},{16,0},{1,17},{17,1},{2,18},{18,2},{3,19},{19,3},{4,20},{20... | collective-permute-start | bytes 4718600 | tf_op jit(solution)/shard_map/ppermute | solution.py:587
  620.6 47.4 %collective-permute-start.37 = (bf16[512,2048]{1,0:T(8,128)(2,1)}, bf16[512,2048]{1,0:T(8,128)(2,1)}, u32[]{:S(2)}, u32[]{:S(2)}) collective-permute-start(bf16[512,2048]{1,0:T(8,128)(2,1)} %add_convert_fusion.9), channel_id=1, source_target_pairs={{0,2},{1,3},{2,0},{3,1},{4,6},{5,7},{6,4},{7,5},{8,10},{9,11},{10,... | collective-permute-start | bytes 6291464 | tf_op jit(solution)/shard_map/ppermute | solution.py:582
  622.0 281.3 %reduce-scatter.21.cloned.1.call-start = ((), (), s32[]{:S(2)}) async-start(), calls=%async_computation.20 | async-start | bytes 2621440 | tf_op jit(solution)/shard_map/reduce_scatter | solution.py:634
  652.8 250.5 %reduce-scatter.23.cloned.1.call-start = ((), (), s32[]{:S(2)}) async-start(), calls=%async_computation.21 | async-start | bytes 2621440 | tf_op jit(solution)/shard_map/reduce_scatter | solution.py:634
  655.8 46.7 %collective-permute-start.53 = (bf16[512,2048]{1,0:T(8,128)(2,1)}, bf16[512,2048]{1,0:T(8,128)(2,1)}, u32[]{:S(2)}, u32[]{:S(2)}) collective-permute-start(bf16[512,2048]{1,0:T(8,128)(2,1)} %get-tuple-element.216), channel_id=1, source_target_pairs={{0,1},{1,0},{2,3},{3,2},{4,5},{5,4},{6,7},{7,6},{8,9},{9,8},{10,11... | collective-permute-start | bytes 6291464 | tf_op jit(solution)/shard_map/ppermute | solution.py:587
  655.8 46.3 %collective-permute-start.44 = (bf16[768,768]{1,0:T(8,128)(2,1)}, bf16[768,768]{1,0:T(8,128)(2,1)}, u32[]{:S(2)}, u32[]{:S(2)}) collective-permute-start(bf16[768,768]{1,0:T(8,128)(2,1)} %slice.275), channel_id=1, source_target_pairs={{0,16},{16,0},{1,17},{17,1},{2,18},{18,2},{3,19},{19,3},{4,20},{20... | collective-permute-start | bytes 3538952 | tf_op jit(solution)/shard_map/ppermute | solution.py:587
  700.3 203.0 %reduce-scatter.15.cloned.1.call-start = ((), (), s32[]{:S(2)}) async-start(), calls=%async_computation.16 | async-start | bytes 2621440 | tf_op jit(solution)/shard_map/reduce_scatter | solution.py:634
  702.1 34.8 %collective-permute-start.45 = (bf16[1024,768]{1,0:T(8,128)(2,1)S(1)}, bf16[1024,768]{1,0:T(8,128)(2,1)S(1)}, u32[]{:S(2)}, u32[]{:S(2)}) collective-permute-start(bf16[1024,768]{1,0:T(8,128)(2,1)S(1)} %slice.276), channel_id=1, source_target_pairs={{0,16},{16,0},{1,17},{17,1},{2,18},{18,2},{3,19},{19,3},{4,20},{20... | collective-permute-start | bytes 4718600 | tf_op jit(solution)/shard_map/ppermute | solution.py:587
  702.5 72.4 %collective-permute-start.59 = (bf16[512,2048]{1,0:T(8,128)(2,1)}, bf16[512,2048]{1,0:T(8,128)(2,1)}, u32[]{:S(2)}, u32[]{:S(2)}) collective-permute-start(bf16[512,2048]{1,0:T(8,128)(2,1)} %get-tuple-element.223), channel_id=1, source_target_pairs={{0,1},{1,0},{2,3},{3,2},{4,5},{5,4},{6,7},{7,6},{8,9},{9,8},{10,11... | collective-permute-start | bytes 6291464 | tf_op jit(solution)/shard_map/ppermute | solution.py:587
  706.4 68.5 %collective-permute-start.54 = (bf16[512,2048]{1,0:T(8,128)(2,1)}, bf16[512,2048]{1,0:T(8,128)(2,1)}, u32[]{:S(2)}, u32[]{:S(2)}) collective-permute-start(bf16[512,2048]{1,0:T(8,128)(2,1)} %add_convert_fusion.3), channel_id=1, source_target_pairs={{0,2},{1,3},{2,0},{3,1},{4,6},{5,7},{6,4},{7,5},{8,10},{9,11},{10,... | collective-permute-start | bytes 6291464 | tf_op jit(solution)/shard_map/ppermute | solution.py:582
  738.0 35.0 %collective-permute-start.46 = (bf16[1024,768]{1,0:T(8,128)(2,1)}, bf16[1024,768]{1,0:T(8,128)(2,1)}, u32[]{:S(2)}, u32[]{:S(2)}) collective-permute-start(bf16[1024,768]{1,0:T(8,128)(2,1)} %get-tuple-element.207), channel_id=1, source_target_pairs={{0,16},{16,0},{1,17},{17,1},{2,18},{18,2},{3,19},{19,3},{4,20},{20... | collective-permute-start | bytes 4718600 | tf_op jit(solution)/shard_map/ppermute | solution.py:587
  773.0 54.9 %collective-permute-start.47 = (bf16[1024,768]{1,0:T(8,128)(2,1)}, bf16[1024,768]{1,0:T(8,128)(2,1)}, u32[]{:S(2)}, u32[]{:S(2)}) collective-permute-start(bf16[1024,768]{1,0:T(8,128)(2,1)} %get-tuple-element.208), channel_id=1, source_target_pairs={{0,16},{16,0},{1,17},{17,1},{2,18},{18,2},{3,19},{19,3},{4,20},{20... | collective-permute-start | bytes 4718600 | tf_op jit(solution)/shard_map/ppermute | solution.py:587
  779.8 27.7 %collective-permute-start.67 = (f32[512]{0:T(512)S(1)}, f32[512]{0:T(512)S(1)}, u32[]{:S(2)}, u32[]{:S(2)}) collective-permute-start(f32[512]{0:T(512)S(1)} %reduce.12), channel_id=1, source_target_pairs={{0,4},{4,0},{8,12},{12,8},{1,5},{5,1},{9,13},{13,9},{2,6},{6,2},{1... | collective-permute-start | bytes 6152 | tf_op jit(solution)/shard_map/ppermute | solution.py:587
  780.0 123.4 %reduce-scatter.19.cloned.1.call-start = ((), (), s32[]{:S(2)}) async-start(), calls=%async_computation.19 | async-start | bytes 2621440 | tf_op jit(solution)/shard_map/reduce_scatter | solution.py:634
  794.8 16.2 %collective-permute-start.71 = (f32[37120]{0:T(1024)}, f32[37120]{0:T(1024)}, u32[]{:S(2)}, u32[]{:S(2)}) collective-permute-start(f32[37120]{0:T(1024)} %constant_dynamic-update-slice_fusion.8), channel_id=1, source_target_pairs={{0,1},{1,0},{2,3},{3,2},{4,5},{5,4},{6,7},{7,6},{8,9},{9,8},{10,11... | collective-permute-start | bytes 445448 | tf_op jit(solution)/shard_map/ppermute | solution.py:587
  795.0 29.8 %collective-permute-start.51 = (bf16[1024,512]{1,0:T(8,128)(2,1)}, bf16[1024,512]{1,0:T(8,128)(2,1)}, u32[]{:S(2)}, u32[]{:S(2)}) collective-permute-start(bf16[1024,512]{1,0:T(8,128)(2,1)} %get-tuple-element.294), channel_id=1, source_target_pairs={{0,1},{1,0},{2,3},{3,2},{4,5},{5,4},{6,7},{7,6},{8,9},{9,8},{10,11... | collective-permute-start | bytes 3145736 | tf_op jit(solution)/shard_map/ppermute | solution.py:587
  799.2 25.5 %collective-permute-start.55 = (bf16[1024,512]{1,0:T(8,128)(2,1)}, bf16[1024,512]{1,0:T(8,128)(2,1)}, u32[]{:S(2)}, u32[]{:S(2)}) collective-permute-start(bf16[1024,512]{1,0:T(8,128)(2,1)} %add_convert_fusion.13), channel_id=1, source_target_pairs={{0,2},{1,3},{2,0},{3,1},{4,6},{5,7},{6,4},{7,5},{8,10},{9,11},{10,... | collective-permute-start | bytes 3145736 | tf_op jit(solution)/shard_map/ppermute | solution.py:582
  807.5 44.6 %collective-permute-start.62 = (bf16[512,1024]{1,0:T(8,128)(2,1)}, bf16[512,1024]{1,0:T(8,128)(2,1)}, u32[]{:S(2)}, u32[]{:S(2)}) collective-permute-start(bf16[512,1024]{1,0:T(8,128)(2,1)} %get-tuple-element.293), channel_id=1, source_target_pairs={{0,1},{1,0},{2,3},{3,2},{4,5},{5,4},{6,7},{7,6},{8,9},{9,8},{10,11... | collective-permute-start | bytes 3145736 | tf_op jit(solution)/shard_map/ppermute | solution.py:587
  811.1 18.4 %collective-permute-start.69 = (f32[512]{0:T(512)S(1)}, f32[512]{0:T(512)S(1)}, u32[]{:S(2)}, u32[]{:S(2)}) collective-permute-start(f32[512]{0:T(512)S(1)} %reduce.15), channel_id=1, source_target_pairs={{0,4},{4,0},{8,12},{12,8},{1,5},{5,1},{9,13},{13,9},{2,6},{6,2},{1... | collective-permute-start | bytes 6152 | tf_op jit(solution)/shard_map/ppermute | solution.py:587
  824.7 13.4 %collective-permute-start.57 = (bf16[512,256]{0,1:T(8,128)(2,1)}, bf16[512,256]{0,1:T(8,128)(2,1)}, u32[]{:S(2)}, u32[]{:S(2)}) collective-permute-start(bf16[512,256]{0,1:T(8,128)(2,1)} %get-tuple-element.311), channel_id=1, source_target_pairs={{0,1},{1,0},{2,3},{3,2},{4,5},{5,4},{6,7},{7,6},{8,9},{9,8},{10,11... | collective-permute-start | bytes 786440 | tf_op jit(solution)/shard_map/ppermute | solution.py:587
  829.5 35.6 %collective-permute-start.60 = (bf16[1024,512]{1,0:T(8,128)(2,1)S(1)}, bf16[1024,512]{1,0:T(8,128)(2,1)}, u32[]{:S(2)}, u32[]{:S(2)}) collective-permute-start(bf16[1024,512]{1,0:T(8,128)(2,1)S(1)} %add_convert_fusion.12), channel_id=1, source_target_pairs={{0,16},{16,0},{1,17},{17,1},{2,18},{18,2},{3,19},{19,3},{4,20},{20... | collective-permute-start | bytes 3145736 | tf_op jit(solution)/shard_map/ppermute | solution.py:587
  835.7 27.3 %collective-permute-start.56 = (bf16[512,256]{0,1:T(8,128)(2,1)}, bf16[512,256]{0,1:T(8,128)(2,1)}, u32[]{:S(2)}, u32[]{:S(2)}) collective-permute-start(bf16[512,256]{0,1:T(8,128)(2,1)} %get-tuple-element.310), channel_id=1, source_target_pairs={{0,1},{1,0},{2,3},{3,2},{4,5},{5,4},{6,7},{7,6},{8,9},{9,8},{10,11... | collective-permute-start | bytes 786440 | tf_op jit(solution)/shard_map/ppermute | solution.py:587
  836.7 57.0 %collective-permute-start.61 = (bf16[512,1024]{1,0:T(8,128)(2,1)S(1)}, bf16[512,1024]{1,0:T(8,128)(2,1)}, u32[]{:S(2)}, u32[]{:S(2)}) collective-permute-start(bf16[512,1024]{1,0:T(8,128)(2,1)S(1)} %copy-done.81), channel_id=1, source_target_pairs={{0,1},{1,0},{2,3},{3,2},{4,5},{5,4},{6,7},{7,6},{8,9},{9,8},{10,11... | collective-permute-start | bytes 3145736 | tf_op jit(solution)/shard_map/ppermute | solution.py:587
  838.1 13.3 %collective-permute-start.73 = (f32[37120]{0:T(1024)S(1)}, f32[37120]{0:T(1024)S(1)}, u32[]{:S(2)}, u32[]{:S(2)}) collective-permute-start(f32[37120]{0:T(1024)S(1)} %add.402), channel_id=1, source_target_pairs={{0,4},{4,0},{8,12},{12,8},{1,5},{5,1},{9,13},{13,9},{2,6},{6,2},{1... | collective-permute-start | bytes 445448 | tf_op jit(solution)/shard_map/ppermute | solution.py:587
  851.4 14.1 %collective-permute-start.70 = (f32[512]{0:T(512)S(1)}, f32[512]{0:T(512)S(1)}, u32[]{:S(2)}, u32[]{:S(2)}) collective-permute-start(f32[512]{0:T(512)S(1)} %add.392), channel_id=1, source_target_pairs={{0,8},{4,12},{8,0},{12,4},{1,9},{5,13},{9,1},{13,5},{2,10},{6,14},... | collective-permute-start | bytes 6152 | tf_op jit(solution)/shard_map/ppermute | solution.py:587
  860.4 14.5 %collective-permute-start.74 = (f32[37120]{0:T(1024)}, f32[37120]{0:T(1024)}, u32[]{:S(2)}, u32[]{:S(2)}) collective-permute-start(f32[37120]{0:T(1024)} %add.403), channel_id=1, source_target_pairs={{0,8},{4,12},{8,0},{12,4},{1,9},{5,13},{9,1},{13,5},{2,10},{6,14},... | collective-permute-start | bytes 445448 | tf_op jit(solution)/shard_map/ppermute | solution.py:587
  863.1 24.1 %collective-permute-start.63 = (bf16[512,1024]{1,0:T(8,128)(2,1)}, bf16[512,1024]{1,0:T(8,128)(2,1)}, u32[]{:S(2)}, u32[]{:S(2)}) collective-permute-start(bf16[512,1024]{1,0:T(8,128)(2,1)} %add_convert_fusion.11), channel_id=1, source_target_pairs={{0,2},{1,3},{2,0},{3,1},{4,6},{5,7},{6,4},{7,5},{8,10},{9,11},{10,... | collective-permute-start | bytes 3145736 | tf_op jit(solution)/shard_map/ppermute | solution.py:582
  877.1 13.8 %collective-permute-start.65 = (bf16[512,256]{0,1:T(8,128)(2,1)S(1)}, bf16[512,256]{0,1:T(8,128)(2,1)S(1)}, u32[]{:S(2)}, u32[]{:S(2)}) collective-permute-start(bf16[512,256]{0,1:T(8,128)(2,1)S(1)} %get-tuple-element.283), channel_id=1, source_target_pairs={{0,12},{4,0},{8,4},{12,8},{1,13},{5,1},{9,5},{13,9},{2,14},{6,2},{... | collective-permute-start | bytes 786440 | tf_op jit(solution)/shard_map/ppermute | solution.py:582
  896.2 23.6 %collective-permute-start.75 = (bf16[512,1024]{1,0:T(8,128)(2,1)S(1)}, bf16[512,1024]{1,0:T(8,128)(2,1)}, u32[]{:S(2)}, u32[]{:S(2)}) collective-permute-start(bf16[512,1024]{1,0:T(8,128)(2,1)S(1)} %add_convert_fusion.10), channel_id=1, source_target_pairs={{0,16},{16,0},{1,17},{17,1},{2,18},{18,2},{3,19},{19,3},{4,20},{20... | collective-permute-start | bytes 3145736 | tf_op jit(solution)/shard_map/ppermute | solution.py:587
  (133 other events, 1578.3 us)
Sparse Core Ops, SparseCore 0:
  10.2 80.4 all-gather.6
  92.8 63.5 all-gather.8
  159.3 42.1 reduce-scatter.8
  203.8 45.2 all-gather.10
  265.4 43.5 reduce-scatter.10
  316.8 45.6 all-gather.12
  472.7 42.5 reduce-scatter.16
  530.6 44.6 reduce-scatter.12
  579.7 45.7 all-gather.16
  626.9 44.5 all-gather.14
  674.4 42.6 reduce-scatter.20
  719.3 43.2 reduce-scatter.22
  780.1 42.7 reduce-scatter.14
  825.7 49.5 reduce-scatter.18
